TPU v7x, 512 devices: a whole 4x4x16 slice. The times are simulated.
512 devices in a mesh: wide: 64 (over z, x), narrow: 8 (over y, core).
Axes of the slice: x: 4, y: 4, z: 16, core: 2. Of those that a mesh axis runs over, the one named last changes fastest.
Arguments:
- phase: int32 [1024, 128, 256], P('wide', 'narrow'), may hold values 0 or 1
- distance: float32 [1024, 128, 256], P('wide', 'narrow'), may hold values from 0.05 to 3
- velocity: float32 [3, 1024, 128, 256], P(None, 'wide', 'narrow'), may hold values from -3 to 3
Outputs:
- moved: float32 [1024, 128, 256], P('wide', 'narrow')
- pressure: float32 [1024, 128, 256], P('wide', 'narrow')
All inputs are finite; a program needn't handle non-finite values. No bound on the sum of `phase` on one device may be relied on, other than what follows from the above.
Results may differ from a plain program's by a relative error of at most 0.0001.
Values sent between devices are 32-bit elements; how exact they have to be, the bound alone decides.
No kernel may reach another device: no remote copies, remote signals or barrier semaphores. Data moves between devices by JAX's collectives and lax.ppermute only.
A program may use at most 128 MiB of HBM per device.

v0:
```python
import jax
import jax.numpy as jnp
from jax import lax
from jax.sharding import PartitionSpec as P

LEVELS = 4
PRE = 2
POST = 2
COARSE = 4
CYCLES = 2


TIME_STEP = 0.25
TENSION = 4.0
DELTA_SQ = 0.0025
WENO_EPS = 0.01
RELAX_WEIGHT = 0.8


def extended_2(cells, sides, width):
    for axis, dim in sides:
        count = lax.axis_size(axis)
        ends = count - 1
        head = lax.slice_in_dim(cells, 0, width, axis=dim)
        tail = lax.slice_in_dim(cells, cells.shape[dim] - width, cells.shape[dim], axis=dim)
        cells = jnp.concatenate(
            [
                lax.ppermute(tail, axis, [(i, (i + 1) % count) for i in range(ends)]),
                cells,
                lax.ppermute(head, axis, [((i + 1) % count, i) for i in range(ends)]),
            ],
            axis=dim,
        )
    return cells


def reconstruct(far_up, upwind, centre, downwind, far_down):
    smooth_zero = (
        13.0 / 12.0 * (far_up - 2.0 * upwind + centre) ** 2
        + 0.25 * (far_up - 4.0 * upwind + 3.0 * centre) ** 2
    )
    smooth_one = (
        13.0 / 12.0 * (upwind - 2.0 * centre + downwind) ** 2 + 0.25 * (upwind - downwind) ** 2
    )
    smooth_two = (
        13.0 / 12.0 * (centre - 2.0 * downwind + far_down) ** 2
        + 0.25 * (3.0 * centre - 4.0 * downwind + far_down) ** 2
    )
    weight_zero = 0.1 / (WENO_EPS + smooth_zero) ** 2
    weight_one = 0.6 / (WENO_EPS + smooth_one) ** 2
    weight_two = 0.3 / (WENO_EPS + smooth_two) ** 2
    guess_zero = (2.0 * far_up - 7.0 * upwind + 11.0 * centre) / 6.0
    guess_one = (-upwind + 5.0 * centre + 2.0 * downwind) / 6.0
    guess_two = (2.0 * centre + 5.0 * downwind - far_down) / 6.0
    return (weight_zero * guess_zero + weight_one * guess_one + weight_two * guess_two) / (
        weight_zero + weight_one + weight_two
    )


def weno_divergence(values, speeds, dimension, length):
    layers = [
        lax.slice_in_dim(values, offset, offset + length + 1, axis=dimension) for offset in range(6)
    ]
    face_speed = 0.5 * (
        lax.slice_in_dim(speeds, 0, length + 1, axis=dimension)
        + lax.slice_in_dim(speeds, 1, length + 2, axis=dimension)
    )
    left_value = reconstruct(layers[0], layers[1], layers[2], layers[3], layers[4])
    right_value = reconstruct(layers[5], layers[4], layers[3], layers[2], layers[1])
    flux = jnp.maximum(face_speed, 0.0) * left_value + jnp.minimum(face_speed, 0.0) * right_value
    return lax.slice_in_dim(flux, 1, length + 1, axis=dimension) - lax.slice_in_dim(
        flux, 0, length, axis=dimension
    )


def advect(psi_pad, vel_pad):
    count_x = psi_pad.shape[0] - 6
    count_y = psi_pad.shape[1] - 6
    count_z = psi_pad.shape[2] - 6
    centre = psi_pad[3:-3, 3:-3, 3:-3]
    change = weno_divergence(psi_pad[:, 3:-3, 3:-3], vel_pad[0][:, 1:-1, 1:-1], 0, count_x)
    change = change + weno_divergence(psi_pad[3:-3, :, 3:-3], vel_pad[1][1:-1, :, 1:-1], 1, count_y)
    change = change + weno_divergence(psi_pad[3:-3, 3:-3, :], vel_pad[2][1:-1, 1:-1, :], 2, count_z)
    return centre - TIME_STEP * change


def gradient(padded):
    grad_x = 0.5 * (padded[2:, 1:-1, 1:-1] - padded[:-2, 1:-1, 1:-1])
    grad_y = 0.5 * (padded[1:-1, 2:, 1:-1] - padded[1:-1, :-2, 1:-1])
    grad_z = 0.5 * (padded[1:-1, 1:-1, 2:] - padded[1:-1, 1:-1, :-2])
    return (grad_x, grad_y, grad_z)


def curvature(padded):
    grad_x, grad_y, grad_z = gradient(padded)
    inverse = 1.0 / jnp.sqrt(grad_x * grad_x + grad_y * grad_y + grad_z * grad_z + DELTA_SQ)
    normal = jnp.stack((grad_x * inverse, grad_y * inverse, grad_z * inverse))
    bending = -(
        0.5 * (normal[0][2:, 1:-1, 1:-1] - normal[0][:-2, 1:-1, 1:-1])
        + 0.5 * (normal[1][1:-1, 2:, 1:-1] - normal[1][1:-1, :-2, 1:-1])
        + 0.5 * (normal[2][1:-1, 1:-1, 2:] - normal[2][1:-1, 1:-1, :-2])
    )
    inner_grad = jnp.stack(
        (grad_x[1:-1, 1:-1, 1:-1], grad_y[1:-1, 1:-1, 1:-1], grad_z[1:-1, 1:-1, 1:-1])
    )
    return (bending, inner_grad)


def source_term(star_pad):
    return -(
        0.5 * (star_pad[0][2:, 1:-1, 1:-1] - star_pad[0][:-2, 1:-1, 1:-1])
        + 0.5 * (star_pad[1][1:-1, 2:, 1:-1] - star_pad[1][1:-1, :-2, 1:-1])
        + 0.5 * (star_pad[2][1:-1, 1:-1, 2:] - star_pad[2][1:-1, 1:-1, :-2])
    )


def apply_padded(padded, spacing_sq):
    centre = padded[1:-1, 1:-1, 1:-1]
    beside = (
        padded[2:, 1:-1, 1:-1]
        + padded[:-2, 1:-1, 1:-1]
        + padded[1:-1, 2:, 1:-1]
        + padded[1:-1, :-2, 1:-1]
        + padded[1:-1, 1:-1, 2:]
        + padded[1:-1, 1:-1, :-2]
    )
    return (6.0 * centre - beside) / spacing_sq


def pad_depth(values, margin):
    return jnp.pad(values, ((0, 0), (0, 0), (margin, margin)))


def pad_components(values, margin):
    return jnp.pad(values, ((0, 0), (0, 0), (0, 0), (margin, margin)))


def smooth_step(estimate, source, spacing_sq):
    border = extended_2(estimate, (("wide", 0), ("narrow", 1)), 1)
    return estimate + RELAX_WEIGHT * spacing_sq / 6.0 * (
        source - apply_padded(pad_depth(border, 1), spacing_sq)
    )


def coarse_step(estimate, source, spacing_sq):
    border = extended_2(estimate, (("wide", 0), ("narrow", 1)), 1)
    return estimate + RELAX_WEIGHT * spacing_sq / 6.0 * (
        source - apply_padded(pad_depth(border, 1), spacing_sq)
    )


def leftover_of(estimate, source, spacing_sq):
    border = extended_2(estimate, (("wide", 0), ("narrow", 1)), 1)
    return source - apply_padded(pad_depth(border, 1), spacing_sq)


def coarsen(values):
    size_x, size_y, size_z = values.shape
    return values.reshape(size_x // 2, 2, size_y // 2, 2, size_z // 2, 2).mean(axis=(1, 3, 5))


def refine(values):
    return jnp.repeat(jnp.repeat(jnp.repeat(values, 2, axis=0), 2, axis=1), 2, axis=2)


def coarsest_solve(source):
    coarse_spacing = 4.0 ** (LEVELS - 1)
    estimate = jnp.zeros_like(source)
    for sweep_index in range(COARSE):
        estimate = coarse_step(estimate, source, coarse_spacing)
    return estimate


def v_cycle(estimate, source):
    sources = [source]
    stored = []
    for level_index in range(LEVELS - 1):
        spacing_sq = 4.0**level_index
        for sweep_index in range(PRE):
            estimate = smooth_step(estimate, sources[level_index], spacing_sq)
        stored.append(estimate)
        leftover = leftover_of(estimate, sources[level_index], spacing_sq)
        sources.append(coarsen(leftover))
        estimate = jnp.zeros_like(sources[level_index + 1])
    estimate = coarsest_solve(sources[LEVELS - 1])
    for level_index in reversed(range(LEVELS - 1)):
        spacing_sq = 4.0**level_index
        estimate = stored[level_index] + refine(estimate)
        for sweep_index in range(POST):
            estimate = smooth_step(estimate, sources[level_index], spacing_sq)
    return estimate


def on_device(phase, distance, velocity):
    orient = 2.0 * phase.astype(jnp.float32) - 1.0
    level_set = 1.0 / (1.0 + jnp.exp(-orient * distance))
    border = extended_2(
        jnp.concatenate((level_set[None], velocity), 0), (("wide", 1), ("narrow", 2)), 3
    )
    psi_pad = pad_depth(border[0], 3)
    vel_pad = pad_components(border[1:, 2:-2, 2:-2], 1)
    moved = advect(psi_pad, vel_pad)
    extended = extended_2(moved, (("wide", 0), ("narrow", 1)), 2)
    bending, inner_grad = curvature(pad_depth(extended, 2))
    provisional = velocity + TIME_STEP * TENSION * bending[None] * inner_grad
    star_pad = pad_components(extended_2(provisional, (("wide", 1), ("narrow", 2)), 1), 1)
    source = source_term(star_pad)
    pressure = jnp.zeros_like(source)
    for cycle_index in range(CYCLES):
        pressure = v_cycle(pressure, source)
    return (moved, pressure)


def solution(mesh):
    in_specs = (
        P("wide", "narrow", None),
        P("wide", "narrow", None),
        P(None, "wide", "narrow", None),
    )
    out_specs = (P("wide", "narrow", None), P("wide", "narrow", None))
    return jax.shard_map(
        on_device, mesh=mesh, in_specs=in_specs, out_specs=out_specs, check_vma=False
    )
```

profile of v0, /device:TPU:408, one launch (start us, length us, event | category | flops | bytes accessed | tf_op | source)
XLA Modules:
  0.0 746.5 jit_solution(1445947347911336470)
XLA Ops:
  6.3 5.8 collective-permute-start.1
  34.8 7.6 %collective-permute-start.5 = (f32[2,16,256]{2,1,0:T(8,128)S(1)}, f32[2,16,256]{2,1,0:T(8,128)S(1)}, u32[]{:S(2)}, u32[]{:S(2)}) collective-permute-start(f32[2,16,256]{2,1,0:T(8,128)S(1)} %get-tuple-element.84), channel_id=1, source_target_pairs={{8,0},{16,8},{24,16},{32,24},{40,32},{48,40},{56,48},{64,56},{72,6... | collective-permute-start | bytes 98312 | tf_op jit(solution)/shard_map/ppermute | solution.py:30
  49.6 7.5 %collective-permute-start.12 = (f32[1,16,256]{2,1,0:T(8,128)S(1)}, f32[1,16,256]{2,1,0:T(8,128)S(1)}, u32[]{:S(2)}, u32[]{:S(2)}) collective-permute-start(f32[1,16,256]{2,1,0:T(8,128)S(1)} %broadcast.413), channel_id=1, source_target_pairs={{8,0},{16,8},{24,16},{32,24},{40,32},{48,40},{56,48},{64,56},{72,6... | collective-permute-start | bytes 49160 | tf_op jit(solution)/shard_map/ppermute | solution.py:30
  63.7 7.2 collective-permute-start.9
  84.6 4.8 collective-permute-start.16
  91.4 7.0 collective-permute-done.17
  109.3 5.2 collective-permute-start.20
  131.1 18.1 %reshape.78 = f32[8,2,8,2,128,2]{5,4,3,2,1,0:T(8,128)} reshape(f32[16,16,256]{2,1,0:T(8,128)S(1)} %fusion.137) | data formatting | bytes 524288 | tf_op jit(solution)/shard_map/reshape | solution.py:159
  149.2 7.0 reduce_sum.54
  156.2 6.7 collective-permute-start.28
  164.9 6.9 collective-permute-done.29
  182.3 5.2 collective-permute-start.32
  205.9 6.4 collective-permute-start.40
  214.3 7.2 collective-permute-start.48
  230.5 7.2 collective-permute-start.44
  254.1 6.0 collective-permute-start.52
  262.0 6.8 collective-permute-done.53
  281.7 4.8 collective-permute-done.57
  299.4 4.8 collective-permute-done.61
  313.5 3.9 collective-permute-start.65
  317.4 4.9 collective-permute-done.65
  335.4 4.9 collective-permute-done.69
  353.6 4.9 collective-permute-done.73
  371.5 4.9 collective-permute-done.77
  389.4 3.9 collective-permute-start.81
  393.3 5.0 collective-permute-done.81
  407.9 3.9 collective-permute-start.85
  411.8 5.0 collective-permute-done.85
  426.4 3.9 collective-permute-start.89
  430.4 5.0 collective-permute-done.89
  444.9 3.9 collective-permute-start.93
  448.9 5.0 collective-permute-done.93
  467.4 5.0 collective-permute-done.97
  480.0 18.1 %reshape.90 = f32[8,2,8,2,128,2]{5,4,3,2,1,0:T(8,128)} reshape(f32[16,16,256]{2,1,0:T(8,128)S(1)} %fusion.104) | data formatting | bytes 524288 | tf_op jit(solution)/shard_map/reshape | solution.py:159
  498.1 7.0 reduce_sum.57
  511.0 4.9 collective-permute-done.101
  528.9 4.9 collective-permute-done.105
  549.1 4.9 collective-permute-done.109
  566.9 4.9 collective-permute-done.113
  585.0 4.8 collective-permute-done.117
  602.8 4.8 collective-permute-done.121
  620.5 4.8 collective-permute-done.125
  638.5 4.9 collective-permute-done.129
  656.3 4.9 collective-permute-done.133
  674.5 4.9 collective-permute-done.137
  692.4 4.9 collective-permute-done.141
  714.1 5.0 collective-permute-done.145
  732.7 5.0 collective-permute-done.149
  (495 shorter events, 457.2 us)
Async XLA Ops:
  2.9 11.9 %collective-permute-start = (f32[4,3,16,256]{3,2,1,0:T(8,128)S(1)}, f32[4,3,16,256]{3,2,1,0:T(8,128)S(1)}, u32[]{:S(2)}, u32[]{:S(2)}) collective-permute-start(f32[4,3,16,256]{3,2,1,0:T(8,128)S(1)} %get-tuple-element.37), channel_id=1, source_target_pairs={{0,8},{8,16},{16,24},{24,32},{32,40},{40,48},{48,56},{56,64},{64,7... | collective-permute-start | bytes 589832 | tf_op jit(solution)/shard_map/ppermute | solution.py:28
  6.3 9.6 %collective-permute-start.1 = (f32[4,3,16,256]{3,2,1,0:T(8,128)S(1)}, f32[4,3,16,256]{3,2,1,0:T(8,128)S(1)}, u32[]{:S(2)}, u32[]{:S(2)}) collective-permute-start(f32[4,3,16,256]{3,2,1,0:T(8,128)S(1)} %get-tuple-element.38), channel_id=1, source_target_pairs={{8,0},{16,8},{24,16},{32,24},{40,32},{48,40},{56,48},{64,56},{72,6... | collective-permute-start | bytes 589832 | tf_op jit(solution)/shard_map/ppermute | solution.py:30
  32.7 9.6 %collective-permute-start.4 = (f32[2,16,256]{2,1,0:T(8,128)S(1)}, f32[2,16,256]{2,1,0:T(8,128)S(1)}, u32[]{:S(2)}, u32[]{:S(2)}) collective-permute-start(f32[2,16,256]{2,1,0:T(8,128)S(1)} %get-tuple-element.83), channel_id=1, source_target_pairs={{0,8},{8,16},{16,24},{24,32},{32,40},{40,48},{48,56},{56,64},{64,7... | collective-permute-start | bytes 98312 | tf_op jit(solution)/shard_map/ppermute | solution.py:28
  34.8 9.2 %collective-permute-start.5 = (f32[2,16,256]{2,1,0:T(8,128)S(1)}, f32[2,16,256]{2,1,0:T(8,128)S(1)}, u32[]{:S(2)}, u32[]{:S(2)}) collective-permute-start(f32[2,16,256]{2,1,0:T(8,128)S(1)} %get-tuple-element.84), channel_id=1, source_target_pairs={{8,0},{16,8},{24,16},{32,24},{40,32},{48,40},{56,48},{64,56},{72,6... | collective-permute-start | bytes 98312 | tf_op jit(solution)/shard_map/ppermute | solution.py:30
  44.0 15.1 %collective-permute-start.6 = (f32[20,2,256]{2,1,0:T(2,128)S(1)}, f32[20,2,256]{2,1,0:T(2,128)S(1)}, u32[]{:S(2)}, u32[]{:S(2)}) collective-permute-start(f32[20,2,256]{2,1,0:T(2,128)S(1)} %get-tuple-element.43), channel_id=1, source_target_pairs={{0,1},{1,2},{2,3},{3,4},{4,5},{5,6},{6,7},{8,9},{9,10},{10,11},{11... | collective-permute-start | bytes 122888 | tf_op jit(solution)/shard_map/ppermute | solution.py:28
  45.9 13.2 %collective-permute-start.7 = (f32[20,2,256]{2,1,0:T(2,128)S(1)}, f32[20,2,256]{2,1,0:T(2,128)S(1)}, u32[]{:S(2)}, u32[]{:S(2)}) collective-permute-start(f32[20,2,256]{2,1,0:T(2,128)S(1)} %get-tuple-element.44), channel_id=1, source_target_pairs={{1,0},{2,1},{3,2},{4,3},{5,4},{6,5},{7,6},{9,8},{10,9},{11,10},{12... | collective-permute-start | bytes 122888 | tf_op jit(solution)/shard_map/ppermute | solution.py:30
  49.6 21.3 %collective-permute-start.12 = (f32[1,16,256]{2,1,0:T(8,128)S(1)}, f32[1,16,256]{2,1,0:T(8,128)S(1)}, u32[]{:S(2)}, u32[]{:S(2)}) collective-permute-start(f32[1,16,256]{2,1,0:T(8,128)S(1)} %broadcast.413), channel_id=1, source_target_pairs={{8,0},{16,8},{24,16},{32,24},{40,32},{48,40},{56,48},{64,56},{72,6... | collective-permute-start | bytes 49160 | tf_op jit(solution)/shard_map/ppermute | solution.py:30
  57.1 13.8 %collective-permute-start.13 = (f32[1,16,256]{2,1,0:T(8,128)S(1)}, f32[1,16,256]{2,1,0:T(8,128)S(1)}, u32[]{:S(2)}, u32[]{:S(2)}) collective-permute-start(f32[1,16,256]{2,1,0:T(8,128)S(1)} %broadcast.413), channel_id=1, source_target_pairs={{0,8},{8,16},{16,24},{24,32},{32,40},{40,48},{48,56},{56,64},{64,7... | collective-permute-start | bytes 49160 | tf_op jit(solution)/shard_map/ppermute | solution.py:28
  61.7 13.6 %collective-permute-start.8 = (f32[3,1,16,256]{3,2,1,0:T(8,128)S(1)}, f32[3,1,16,256]{3,2,1,0:T(8,128)S(1)}, u32[]{:S(2)}, u32[]{:S(2)}) collective-permute-start(f32[3,1,16,256]{3,2,1,0:T(8,128)S(1)} %get-tuple-element.41), channel_id=1, source_target_pairs={{0,8},{8,16},{16,24},{24,32},{32,40},{40,48},{48,56},{56,64},{64,7... | collective-permute-start | bytes 147464 | tf_op jit(solution)/shard_map/ppermute | solution.py:28
  63.7 11.7 %collective-permute-start.9 = (f32[3,1,16,256]{3,2,1,0:T(8,128)S(1)}, f32[3,1,16,256]{3,2,1,0:T(8,128)S(1)}, u32[]{:S(2)}, u32[]{:S(2)}) collective-permute-start(f32[3,1,16,256]{3,2,1,0:T(8,128)S(1)} %get-tuple-element.42), channel_id=1, source_target_pairs={{8,0},{16,8},{24,16},{32,24},{40,32},{48,40},{56,48},{64,56},{72,6... | collective-permute-start | bytes 147464 | tf_op jit(solution)/shard_map/ppermute | solution.py:30
  71.0 10.2 %collective-permute-start.14 = (f32[18,1,256]{2,1,0:T(1,128)S(1)}, f32[18,1,256]{2,1,0:T(1,128)S(1)}, u32[]{:S(2)}, u32[]{:S(2)}) collective-permute-start(f32[18,1,256]{2,1,0:T(1,128)S(1)} %get-tuple-element.64), channel_id=1, source_target_pairs={{1,0},{2,1},{3,2},{4,3},{5,4},{6,5},{7,6},{9,8},{10,9},{11,10},{12... | collective-permute-start | bytes 55304 | tf_op jit(solution)/shard_map/ppermute | solution.py:30
  89.4 9.0 %collective-permute-start.17 = (f32[1,16,256]{2,1,0:T(8,128)S(1)}, f32[1,16,256]{2,1,0:T(8,128)S(1)}, u32[]{:S(2)}, u32[]{:S(2)}) collective-permute-start(f32[1,16,256]{2,1,0:T(8,128)S(1)} %get-tuple-element.81), channel_id=1, source_target_pairs={{0,8},{8,16},{16,24},{24,32},{32,40},{40,48},{48,56},{56,64},{64,7... | collective-permute-start | bytes 49160 | tf_op jit(solution)/shard_map/ppermute | solution.py:28
  98.4 10.2 %collective-permute-start.18 = (f32[18,1,256]{2,1,0:T(1,128)S(1)}, f32[18,1,256]{2,1,0:T(1,128)S(1)}, u32[]{:S(2)}, u32[]{:S(2)}) collective-permute-start(f32[18,1,256]{2,1,0:T(1,128)S(1)} %get-tuple-element.62), channel_id=1, source_target_pairs={{1,0},{2,1},{3,2},{4,3},{5,4},{6,5},{7,6},{9,8},{10,9},{11,10},{12... | collective-permute-start | bytes 55304 | tf_op jit(solution)/shard_map/ppermute | solution.py:30
  102.8 13.7 %collective-permute-start.24 = (f32[1,8,128]{2,1,0:T(8,128)S(1)}, f32[1,8,128]{2,1,0:T(8,128)S(1)}, u32[]{:S(2)}, u32[]{:S(2)}) collective-permute-start(f32[1,8,128]{2,1,0:T(8,128)S(1)} %broadcast.418), channel_id=1, source_target_pairs={{8,0},{16,8},{24,16},{32,24},{40,32},{48,40},{56,48},{64,56},{72,6... | collective-permute-start | bytes 12296 | tf_op jit(solution)/shard_map/ppermute | solution.py:30
  104.7 11.8 %collective-permute-start.25 = (f32[1,8,128]{2,1,0:T(8,128)S(1)}, f32[1,8,128]{2,1,0:T(8,128)S(1)}, u32[]{:S(2)}, u32[]{:S(2)}) collective-permute-start(f32[1,8,128]{2,1,0:T(8,128)S(1)} %broadcast.418), channel_id=1, source_target_pairs={{0,8},{8,16},{16,24},{24,32},{32,40},{40,48},{48,56},{56,64},{64,7... | collective-permute-start | bytes 12296 | tf_op jit(solution)/shard_map/ppermute | solution.py:28
  109.3 12.2 %collective-permute-start.20 = (f32[1,16,256]{2,1,0:T(8,128)S(1)}, f32[1,16,256]{2,1,0:T(8,128)S(1)}, u32[]{:S(2)}, u32[]{:S(2)}) collective-permute-start(f32[1,16,256]{2,1,0:T(8,128)S(1)} %get-tuple-element.80), channel_id=1, source_target_pairs={{8,0},{16,8},{24,16},{32,24},{40,32},{48,40},{56,48},{64,56},{72,6... | collective-permute-start | bytes 49160 | tf_op jit(solution)/shard_map/ppermute | solution.py:30
  114.5 9.0 %collective-permute-start.21 = (f32[1,16,256]{2,1,0:T(8,128)S(1)}, f32[1,16,256]{2,1,0:T(8,128)S(1)}, u32[]{:S(2)}, u32[]{:S(2)}) collective-permute-start(f32[1,16,256]{2,1,0:T(8,128)S(1)} %get-tuple-element.79), channel_id=1, source_target_pairs={{0,8},{8,16},{16,24},{24,32},{32,40},{40,48},{48,56},{56,64},{64,7... | collective-permute-start | bytes 49160 | tf_op jit(solution)/shard_map/ppermute | solution.py:28
  116.5 11.3 %collective-permute-start.26 = (f32[10,1,128]{2,1,0:T(1,128)S(1)}, f32[10,1,128]{2,1,0:T(1,128)S(1)}, u32[]{:S(2)}, u32[]{:S(2)}) collective-permute-start(f32[10,1,128]{2,1,0:T(1,128)S(1)} %get-tuple-element.102), channel_id=1, source_target_pairs={{1,0},{2,1},{3,2},{4,3},{5,4},{6,5},{7,6},{9,8},{10,9},{11,10},{12... | collective-permute-start | bytes 15368 | tf_op jit(solution)/shard_map/ppermute | solution.py:30
  163.0 8.8 %collective-permute-start.29 = (f32[1,8,128]{2,1,0:T(8,128)S(1)}, f32[1,8,128]{2,1,0:T(8,128)S(1)}, u32[]{:S(2)}, u32[]{:S(2)}) collective-permute-start(f32[1,8,128]{2,1,0:T(8,128)S(1)} %get-tuple-element.117), channel_id=1, source_target_pairs={{0,8},{8,16},{16,24},{24,32},{32,40},{40,48},{48,56},{56,64},{64,7... | collective-permute-start | bytes 12296 | tf_op jit(solution)/shard_map/ppermute | solution.py:28
  171.8 10.2 %collective-permute-start.30 = (f32[10,1,128]{2,1,0:T(1,128)S(1)}, f32[10,1,128]{2,1,0:T(1,128)S(1)}, u32[]{:S(2)}, u32[]{:S(2)}) collective-permute-start(f32[10,1,128]{2,1,0:T(1,128)S(1)} %get-tuple-element.100), channel_id=1, source_target_pairs={{1,0},{2,1},{3,2},{4,3},{5,4},{6,5},{7,6},{9,8},{10,9},{11,10},{12... | collective-permute-start | bytes 15368 | tf_op jit(solution)/shard_map/ppermute | solution.py:30
  176.2 13.3 %collective-permute-start.36 = (f32[1,4,64]{2,1,0:T(4,128)S(1)}, f32[1,4,64]{2,1,0:T(4,128)S(1)}, u32[]{:S(2)}, u32[]{:S(2)}) collective-permute-start(f32[1,4,64]{2,1,0:T(4,128)S(1)} %broadcast.424), channel_id=1, source_target_pairs={{8,0},{16,8},{24,16},{32,24},{40,32},{48,40},{56,48},{64,56},{72,6... | collective-permute-start | bytes 3080 | tf_op jit(solution)/shard_map/ppermute | solution.py:30
  178.1 11.4 %collective-permute-start.37 = (f32[1,4,64]{2,1,0:T(4,128)S(1)}, f32[1,4,64]{2,1,0:T(4,128)S(1)}, u32[]{:S(2)}, u32[]{:S(2)}) collective-permute-start(f32[1,4,64]{2,1,0:T(4,128)S(1)} %broadcast.424), channel_id=1, source_target_pairs={{0,8},{8,16},{16,24},{24,32},{32,40},{40,48},{48,56},{56,64},{64,7... | collective-permute-start | bytes 3080 | tf_op jit(solution)/shard_map/ppermute | solution.py:28
  182.3 11.8 %collective-permute-start.32 = (f32[1,8,128]{2,1,0:T(8,128)S(1)}, f32[1,8,128]{2,1,0:T(8,128)S(1)}, u32[]{:S(2)}, u32[]{:S(2)}) collective-permute-start(f32[1,8,128]{2,1,0:T(8,128)S(1)} %get-tuple-element.116), channel_id=1, source_target_pairs={{8,0},{16,8},{24,16},{32,24},{40,32},{48,40},{56,48},{64,56},{72,6... | collective-permute-start | bytes 12296 | tf_op jit(solution)/shard_map/ppermute | solution.py:30
  187.6 8.8 %collective-permute-start.33 = (f32[1,8,128]{2,1,0:T(8,128)S(1)}, f32[1,8,128]{2,1,0:T(8,128)S(1)}, u32[]{:S(2)}, u32[]{:S(2)}) collective-permute-start(f32[1,8,128]{2,1,0:T(8,128)S(1)} %get-tuple-element.115), channel_id=1, source_target_pairs={{0,8},{8,16},{16,24},{24,32},{32,40},{40,48},{48,56},{56,64},{64,7... | collective-permute-start | bytes 12296 | tf_op jit(solution)/shard_map/ppermute | solution.py:28
  189.5 11.2 %collective-permute-start.38 = (f32[6,1,64]{2,1,0:T(1,128)S(1)}, f32[6,1,64]{2,1,0:T(1,128)S(1)}, u32[]{:S(2)}, u32[]{:S(2)}) collective-permute-start(f32[6,1,64]{2,1,0:T(1,128)S(1)} %get-tuple-element.136), channel_id=1, source_target_pairs={{1,0},{2,1},{3,2},{4,3},{5,4},{6,5},{7,6},{9,8},{10,9},{11,10},{12... | collective-permute-start | bytes 4616 | tf_op jit(solution)/shard_map/ppermute | solution.py:30
  205.9 17.5 %collective-permute-start.40 = (f32[1,4,64]{2,1,0:T(4,128)S(1)}, f32[1,4,64]{2,1,0:T(4,128)S(1)}, u32[]{:S(2)}, u32[]{:S(2)}) collective-permute-start(f32[1,4,64]{2,1,0:T(4,128)S(1)} %get-tuple-element.152), channel_id=1, source_target_pairs={{8,0},{16,8},{24,16},{32,24},{40,32},{48,40},{56,48},{64,56},{72,6... | collective-permute-start | bytes 3080 | tf_op jit(solution)/shard_map/ppermute | solution.py:30
  212.3 11.1 %collective-permute-start.41 = (f32[1,4,64]{2,1,0:T(4,128)S(1)}, f32[1,4,64]{2,1,0:T(4,128)S(1)}, u32[]{:S(2)}, u32[]{:S(2)}) collective-permute-start(f32[1,4,64]{2,1,0:T(4,128)S(1)} %get-tuple-element.151), channel_id=1, source_target_pairs={{0,8},{8,16},{16,24},{24,32},{32,40},{40,48},{48,56},{56,64},{64,7... | collective-permute-start | bytes 3080 | tf_op jit(solution)/shard_map/ppermute | solution.py:28
  214.3 13.6 %collective-permute-start.48 = (f32[1,2,32]{2,1,0:T(2,128)S(1)}, f32[1,2,32]{2,1,0:T(2,128)S(1)}, u32[]{:S(2)}, u32[]{:S(2)}) collective-permute-start(f32[1,2,32]{2,1,0:T(2,128)S(1)} %broadcast.430), channel_id=1, source_target_pairs={{8,0},{16,8},{24,16},{32,24},{40,32},{48,40},{56,48},{64,56},{72,6... | collective-permute-start | bytes 776 | tf_op jit(solution)/shard_map/ppermute | solution.py:30
  230.5 13.5 %collective-permute-start.44 = (f32[1,4,64]{2,1,0:T(4,128)S(1)}, f32[1,4,64]{2,1,0:T(4,128)S(1)}, u32[]{:S(2)}, u32[]{:S(2)}) collective-permute-start(f32[1,4,64]{2,1,0:T(4,128)S(1)} %get-tuple-element.150), channel_id=1, source_target_pairs={{8,0},{16,8},{24,16},{32,24},{40,32},{48,40},{56,48},{64,56},{72,6... | collective-permute-start | bytes 3080 | tf_op jit(solution)/shard_map/ppermute | solution.py:30
  239.7 11.2 %collective-permute-start.50 = (f32[4,1,32]{2,1,0:T(1,128)S(1)}, f32[4,1,32]{2,1,0:T(1,128)S(1)}, u32[]{:S(2)}, u32[]{:S(2)}) collective-permute-start(f32[4,1,32]{2,1,0:T(1,128)S(1)} %get-tuple-element.166), channel_id=1, source_target_pairs={{1,0},{2,1},{3,2},{4,3},{5,4},{6,5},{7,6},{9,8},{10,9},{11,10},{12... | collective-permute-start | bytes 1544 | tf_op jit(solution)/shard_map/ppermute | solution.py:30
  241.6 9.3 %collective-permute-start.51 = (f32[4,1,32]{2,1,0:T(1,128)S(1)}, f32[4,1,32]{2,1,0:T(1,128)S(1)}, u32[]{:S(2)}, u32[]{:S(2)}) collective-permute-start(f32[4,1,32]{2,1,0:T(1,128)S(1)} %get-tuple-element.165), channel_id=1, source_target_pairs={{0,1},{1,2},{2,3},{3,4},{4,5},{5,6},{6,7},{8,9},{9,10},{10,11},{11... | collective-permute-start | bytes 1544 | tf_op jit(solution)/shard_map/ppermute | solution.py:28
  313.5 8.8 %collective-permute-start.65 = (f32[1,4,64]{2,1,0:T(4,128)S(1)}, f32[1,4,64]{2,1,0:T(4,128)S(1)}, u32[]{:S(2)}, u32[]{:S(2)}) collective-permute-start(f32[1,4,64]{2,1,0:T(4,128)S(1)} %get-tuple-element.147), channel_id=1, source_target_pairs={{0,8},{8,16},{16,24},{24,32},{32,40},{40,48},{48,56},{56,64},{64,7... | collective-permute-start | bytes 3080 | tf_op jit(solution)/shard_map/ppermute | solution.py:28
  349.7 8.8 %collective-permute-start.73 = (f32[1,8,128]{2,1,0:T(8,128)S(1)}, f32[1,8,128]{2,1,0:T(8,128)S(1)}, u32[]{:S(2)}, u32[]{:S(2)}) collective-permute-start(f32[1,8,128]{2,1,0:T(8,128)S(1)} %get-tuple-element.113), channel_id=1, source_target_pairs={{0,8},{8,16},{16,24},{24,32},{32,40},{40,48},{48,56},{56,64},{64,7... | collective-permute-start | bytes 12296 | tf_op jit(solution)/shard_map/ppermute | solution.py:28
  367.6 8.8 %collective-permute-start.77 = (f32[1,8,128]{2,1,0:T(8,128)S(1)}, f32[1,8,128]{2,1,0:T(8,128)S(1)}, u32[]{:S(2)}, u32[]{:S(2)}) collective-permute-start(f32[1,8,128]{2,1,0:T(8,128)S(1)} %get-tuple-element.111), channel_id=1, source_target_pairs={{0,8},{8,16},{16,24},{24,32},{32,40},{40,48},{48,56},{56,64},{64,7... | collective-permute-start | bytes 12296 | tf_op jit(solution)/shard_map/ppermute | solution.py:28
  389.4 9.0 %collective-permute-start.81 = (f32[1,16,256]{2,1,0:T(8,128)S(1)}, f32[1,16,256]{2,1,0:T(8,128)S(1)}, u32[]{:S(2)}, u32[]{:S(2)}) collective-permute-start(f32[1,16,256]{2,1,0:T(8,128)S(1)} %get-tuple-element.77), channel_id=1, source_target_pairs={{0,8},{8,16},{16,24},{24,32},{32,40},{40,48},{48,56},{56,64},{64,7... | collective-permute-start | bytes 49160 | tf_op jit(solution)/shard_map/ppermute | solution.py:28
  407.9 9.0 %collective-permute-start.85 = (f32[1,16,256]{2,1,0:T(8,128)S(1)}, f32[1,16,256]{2,1,0:T(8,128)S(1)}, u32[]{:S(2)}, u32[]{:S(2)}) collective-permute-start(f32[1,16,256]{2,1,0:T(8,128)S(1)} %get-tuple-element.75), channel_id=1, source_target_pairs={{0,8},{8,16},{16,24},{24,32},{32,40},{40,48},{48,56},{56,64},{64,7... | collective-permute-start | bytes 49160 | tf_op jit(solution)/shard_map/ppermute | solution.py:28
  426.4 9.0 %collective-permute-start.89 = (f32[1,16,256]{2,1,0:T(8,128)S(1)}, f32[1,16,256]{2,1,0:T(8,128)S(1)}, u32[]{:S(2)}, u32[]{:S(2)}) collective-permute-start(f32[1,16,256]{2,1,0:T(8,128)S(1)} %get-tuple-element.73), channel_id=1, source_target_pairs={{0,8},{8,16},{16,24},{24,32},{32,40},{40,48},{48,56},{56,64},{64,7... | collective-permute-start | bytes 49160 | tf_op jit(solution)/shard_map/ppermute | solution.py:28
  444.9 9.0 %collective-permute-start.93 = (f32[1,16,256]{2,1,0:T(8,128)S(1)}, f32[1,16,256]{2,1,0:T(8,128)S(1)}, u32[]{:S(2)}, u32[]{:S(2)}) collective-permute-start(f32[1,16,256]{2,1,0:T(8,128)S(1)} %get-tuple-element.71), channel_id=1, source_target_pairs={{0,8},{8,16},{16,24},{24,32},{32,40},{40,48},{48,56},{56,64},{64,7... | collective-permute-start | bytes 49160 | tf_op jit(solution)/shard_map/ppermute | solution.py:28
  463.5 9.0 %collective-permute-start.97 = (f32[1,16,256]{2,1,0:T(8,128)S(1)}, f32[1,16,256]{2,1,0:T(8,128)S(1)}, u32[]{:S(2)}, u32[]{:S(2)}) collective-permute-start(f32[1,16,256]{2,1,0:T(8,128)S(1)} %get-tuple-element.69), channel_id=1, source_target_pairs={{0,8},{8,16},{16,24},{24,32},{32,40},{40,48},{48,56},{56,64},{64,7... | collective-permute-start | bytes 49160 | tf_op jit(solution)/shard_map/ppermute | solution.py:28
  507.1 8.8 %collective-permute-start.101 = (f32[1,8,128]{2,1,0:T(8,128)S(1)}, f32[1,8,128]{2,1,0:T(8,128)S(1)}, u32[]{:S(2)}, u32[]{:S(2)}) collective-permute-start(f32[1,8,128]{2,1,0:T(8,128)S(1)} %get-tuple-element.109), channel_id=1, source_target_pairs={{0,8},{8,16},{16,24},{24,32},{32,40},{40,48},{48,56},{56,64},{64,7... | collective-permute-start | bytes 12296 | tf_op jit(solution)/shard_map/ppermute | solution.py:28
  525.0 8.8 %collective-permute-start.105 = (f32[1,8,128]{2,1,0:T(8,128)S(1)}, f32[1,8,128]{2,1,0:T(8,128)S(1)}, u32[]{:S(2)}, u32[]{:S(2)}) collective-permute-start(f32[1,8,128]{2,1,0:T(8,128)S(1)} %get-tuple-element.107), channel_id=1, source_target_pairs={{0,8},{8,16},{16,24},{24,32},{32,40},{40,48},{48,56},{56,64},{64,7... | collective-permute-start | bytes 12296 | tf_op jit(solution)/shard_map/ppermute | solution.py:28
  545.2 8.8 %collective-permute-start.109 = (f32[1,4,64]{2,1,0:T(4,128)S(1)}, f32[1,4,64]{2,1,0:T(4,128)S(1)}, u32[]{:S(2)}, u32[]{:S(2)}) collective-permute-start(f32[1,4,64]{2,1,0:T(4,128)S(1)} %get-tuple-element.143), channel_id=1, source_target_pairs={{0,8},{8,16},{16,24},{24,32},{32,40},{40,48},{48,56},{56,64},{64,7... | collective-permute-start | bytes 3080 | tf_op jit(solution)/shard_map/ppermute | solution.py:28
  562.9 8.8 %collective-permute-start.113 = (f32[1,4,64]{2,1,0:T(4,128)S(1)}, f32[1,4,64]{2,1,0:T(4,128)S(1)}, u32[]{:S(2)}, u32[]{:S(2)}) collective-permute-start(f32[1,4,64]{2,1,0:T(4,128)S(1)} %get-tuple-element.141), channel_id=1, source_target_pairs={{0,8},{8,16},{16,24},{24,32},{32,40},{40,48},{48,56},{56,64},{64,7... | collective-permute-start | bytes 3080 | tf_op jit(solution)/shard_map/ppermute | solution.py:28
  634.6 8.8 %collective-permute-start.129 = (f32[1,4,64]{2,1,0:T(4,128)S(1)}, f32[1,4,64]{2,1,0:T(4,128)S(1)}, u32[]{:S(2)}, u32[]{:S(2)}) collective-permute-start(f32[1,4,64]{2,1,0:T(4,128)S(1)} %get-tuple-element.139), channel_id=1, source_target_pairs={{0,8},{8,16},{16,24},{24,32},{32,40},{40,48},{48,56},{56,64},{64,7... | collective-permute-start | bytes 3080 | tf_op jit(solution)/shard_map/ppermute | solution.py:28
  670.5 8.8 %collective-permute-start.137 = (f32[1,8,128]{2,1,0:T(8,128)S(1)}, f32[1,8,128]{2,1,0:T(8,128)S(1)}, u32[]{:S(2)}, u32[]{:S(2)}) collective-permute-start(f32[1,8,128]{2,1,0:T(8,128)S(1)} %get-tuple-element.105), channel_id=1, source_target_pairs={{0,8},{8,16},{16,24},{24,32},{32,40},{40,48},{48,56},{56,64},{64,7... | collective-permute-start | bytes 12296 | tf_op jit(solution)/shard_map/ppermute | solution.py:28
  688.4 8.8 %collective-permute-start.141 = (f32[1,8,128]{2,1,0:T(8,128)S(1)}, f32[1,8,128]{2,1,0:T(8,128)S(1)}, u32[]{:S(2)}, u32[]{:S(2)}) collective-permute-start(f32[1,8,128]{2,1,0:T(8,128)S(1)} %get-tuple-element.103), channel_id=1, source_target_pairs={{0,8},{8,16},{16,24},{24,32},{32,40},{40,48},{48,56},{56,64},{64,7... | collective-permute-start | bytes 12296 | tf_op jit(solution)/shard_map/ppermute | solution.py:28
  710.2 9.0 %collective-permute-start.145 = (f32[1,16,256]{2,1,0:T(8,128)S(1)}, f32[1,16,256]{2,1,0:T(8,128)S(1)}, u32[]{:S(2)}, u32[]{:S(2)}) collective-permute-start(f32[1,16,256]{2,1,0:T(8,128)S(1)} %get-tuple-element.67), channel_id=1, source_target_pairs={{0,8},{8,16},{16,24},{24,32},{32,40},{40,48},{48,56},{56,64},{64,7... | collective-permute-start | bytes 49160 | tf_op jit(solution)/shard_map/ppermute | solution.py:28
  728.7 9.0 %collective-permute-start.149 = (f32[1,16,256]{2,1,0:T(8,128)S(1)}, f32[1,16,256]{2,1,0:T(8,128)S(1)}, u32[]{:S(2)}, u32[]{:S(2)}) collective-permute-start(f32[1,16,256]{2,1,0:T(8,128)S(1)} %get-tuple-element.65), channel_id=1, source_target_pairs={{0,8},{8,16},{16,24},{24,32},{32,40},{40,48},{48,56},{56,64},{64,7... | collective-permute-start | bytes 49160 | tf_op jit(solution)/shard_map/ppermute | solution.py:28
  (106 other events, 636.4 us)
where the time goes:
time: 759 us; the launch traced here: 746 us
  starting transfers between devices  423 us (56%)
  waiting for transfers between devices  229 us (30%)
  local copies, waits for them, and re-layouts  51.7 us (7%)
  other arithmetic  38.8 us (5%)
    ppermute x76, waiting for transfers between devices, extended_2(): lax.ppermute(tail, axis, [(i, (i + 1) % count) for i in range(ends)])  223 us
    ppermute x76, starting transfers between devices, extended_2(): lax.ppermute(tail, axis, [(i, (i + 1) % count) for i in range(ends)])  215 us
    ppermute x76, starting transfers between devices, extended_2(): lax.ppermute(head, axis, [((i + 1) % count, i) for i in range(ends)])  208 us
    reshape x6, local copies, waits for them, and re-layouts, coarsen(): values.reshape(size_x // 2, 2, size_y // 2, 2, size_z // 2, 2)  40.9 us
  transfers between devices with their start and end apart: 152, of which 65 were waited for; matrix products, arithmetic and copies ran while one was open for 1% of the time, Pallas kernels for 0%

commit v1 on v0

v1 whole, which is shorter than its diff:
```python
import functools

import jax
import jax.numpy as jnp
from jax import lax
from jax.experimental import pallas as pl
from jax.experimental.pallas import tpu as pltpu
from jax.sharding import PartitionSpec as P

DELTA_SQ = 0.0025
WENO_EPS = 0.01
SIDE = 0.8 / 6.0
F32 = jnp.float32
HIGHEST = lax.Precision.HIGHEST
VMEM_LIMIT = 56 * 1024 * 1024

HALO = 10
ROWS = 12
GROUP = 4


def iota(shape, dim):
    return lax.broadcasted_iota(jnp.int32, shape, dim)


def roll(v, shift, axis):
    return pltpu.roll(v, shift % v.shape[axis], axis)


def z_shifted(v):
    lane = iota(v.shape, 1)
    last = v.shape[1] - 1
    lower = jnp.where(lane == 0, 0.0, roll(v, 1, 1))
    upper = jnp.where(lane == last, 0.0, roll(v, -1, 1))
    return lower, upper


def z_pair(v):
    lower, upper = z_shifted(v)
    return lower + upper


def y_pair(v):
    return roll(v, 1, 0) + roll(v, -1, 0)


def beside(ref, i):
    c = ref[i]
    return c, (ref[i - 1] + ref[i + 1]) + y_pair(c) + z_pair(c)


def inside(first, count):
    return jnp.logical_and(first >= 0, first < count)


def row_mask(shape, first, count):
    rows = iota(shape, 0) + first
    return jnp.where(inside(rows, count), 1.0, 0.0).astype(F32)


def plane_factor(index, count):
    return jnp.where(inside(index, count), 1.0, 0.0).astype(F32)


def dot(a, b):
    return lax.dot_general(
        a, b, (((1,), (0,)), ((), ())), precision=HIGHEST, preferred_element_type=F32
    )


def pair_matrix(rows, cols, value):
    return jnp.where((iota((rows, cols), 0) >> 1) == iota((rows, cols), 1), value, 0.0).astype(F32)


def copy_matrix(rows, cols):
    return jnp.where(iota((rows, cols), 0) == (iota((rows, cols), 1) >> 1), 1.0, 0.0).astype(F32)


def call(body, outs, scratch, args, flops):
    vmem = pl.BlockSpec(memory_space=pltpu.VMEM)
    smem = pl.BlockSpec(memory_space=pltpu.SMEM)
    return pl.pallas_call(
        body,
        out_shape=[jax.ShapeDtypeStruct(s, F32) for s in outs],
        in_specs=[smem if a.dtype == jnp.int32 and a.ndim == 1 else vmem for a in args],
        out_specs=[vmem] * len(outs),
        scratch_shapes=[pltpu.VMEM(s, F32) for s in scratch],
        compiler_params=pltpu.CompilerParams(vmem_limit_bytes=VMEM_LIMIT),
        cost_estimate=pl.CostEstimate(flops=flops, bytes_accessed=4000000, transcendentals=0),
    )(*args)


def prepare_body(phase, distance, velocity, psi, x_low, x_high, y_low, y_high):
    def plane(i, carry):
        orient = 2.0 * phase[i].astype(F32) - 1.0
        psi[i] = 1.0 / (1.0 + jnp.exp(-orient * distance[i]))
        y_low[i, 0:3, :] = psi[i, 0:3, :]
        y_low[i, 3:4, :] = velocity[1, i, 0:1, :]
        y_high[i, 0:3, :] = psi[i, 13:16, :]
        y_high[i, 3:4, :] = velocity[1, i, 15:16, :]
        return carry

    lax.fori_loop(0, 16, plane, 0)
    for k in range(3):
        x_low[k] = psi[k]
        x_high[k] = psi[13 + k]
    x_low[3] = velocity[0, 0]
    x_high[3] = velocity[0, 15]


def prepare(phase, distance, velocity):
    outs = [(16, 16, 256), (4, 16, 256), (4, 16, 256), (16, 4, 256), (16, 4, 256)]
    return call(prepare_body, outs, [], [phase, distance, velocity], 1000000)


def indicators(a, b, c):
    d = a - c
    curve = (a + c) - 2.0 * b
    twice = 2.0 * curve
    base = (13.0 / 12.0) * (curve * curve) + WENO_EPS
    up, down = twice - d, twice + d
    p = base + 0.25 * (up * up)
    q = base + 0.25 * (d * d)
    r = base + 0.25 * (down * down)
    return p * p, q * q, r * r


def upwind_flux(s, l, p_left, q_left, r_left, p_right, q_right, r_right):
    ahead = s > 0.0
    pick = lambda x, y: jnp.where(ahead, x, y)
    a, b, c, e, f = pick(l[0], l[5]), pick(l[1], l[4]), pick(l[2], l[3]), pick(l[3], l[2]), pick(l[4], l[1])
    p, q, r = pick(p_left, r_right), pick(q_left, q_right), pick(r_left, p_right)
    w0, w1, w2 = 0.1 * (q * r), 0.6 * (p * r), 0.3 * (p * q)
    g0 = 2.0 * a - 7.0 * b + 11.0 * c
    g1 = 5.0 * c + 2.0 * e - b
    g2 = 2.0 * c + 5.0 * e - f
    top = w0 * g0 + w1 * g1 + w2 * g2
    return (s * top) / (6.0 * (w0 + w1 + w2))


def transport_body(psi, velocity, xl, xh, yl, yh, moved, ext, p_x, q_x, r_x, rows, speed):
    for k in range(3):
        ext[k] = xl[k]
        ext[19 + k] = xh[k]

    def fill(i, carry):
        ext[3 + i] = psi[i]
        return carry

    lax.fori_loop(0, 16, fill, 0)

    def marks(i, carry):
        p, q, r = indicators(ext[i], ext[i + 1], ext[i + 2])
        p_x[i], q_x[i], r_x[i] = p, q, r
        return carry

    lax.fori_loop(0, 20, marks, 0, unroll=2)

    def x_flux(j, v_low, v_high):
        s = 0.5 * (v_low + v_high)
        l = [ext[j + k] for k in range(6)]
        return upwind_flux(
            s, l, p_x[j], q_x[j + 1], r_x[j + 2], p_x[j + 1], q_x[j + 2], r_x[j + 3]
        )

    def plane(i, below):
        here = velocity[0, i]
        following = jnp.where(i == 15, xh[3], velocity[0, jnp.minimum(i + 1, 15)])
        above = x_flux(i + 1, here, following)
        change = above - below
        rows[1:4, :] = yl[i, 0:3, :]
        rows[4:20, :] = psi[i]
        rows[20:23, :] = yh[i, 0:3, :]
        speed[3:4, :] = yl[i, 3:4, :]
        speed[4:20, :] = velocity[1, i]
        speed[20:21, :] = yh[i, 3:4, :]
        v = rows[...]
        u = speed[...]
        s = 0.5 * (u + roll(u, -1, 0))
        l = [roll(v, 2 - k, 0) for k in range(6)]
        p, q, r = indicators(l[1], l[2], l[3])
        q_next, r_next = roll(q, -1, 0), roll(r, -1, 0)
        flux = upwind_flux(s, l, roll(p, 1, 0), q, r_next, p, q_next, roll(r, -2, 0))
        rows_change = flux - roll(flux, 1, 0)
        change = change + rows_change[4:20, :]
        v = psi[i]
        w = velocity[2, i]
        lane = iota(v.shape, 1)

        def ahead(x, k):
            return jnp.where(lane > 255 - k, 0.0, roll(x, -k, 1))

        def behind(x, k):
            return jnp.where(lane < k, 0.0, roll(x, k, 1))

        l = [behind(v, 2), behind(v, 1), v, ahead(v, 1), ahead(v, 2), ahead(v, 3)]
        s = 0.5 * (w + ahead(w, 1))
        p, q, r = indicators(l[1], l[2], l[3])
        p1, q1, r1 = indicators(l[2], l[3], l[4])
        _, _, r2 = indicators(l[3], l[4], l[5])
        p0, _, _ = indicators(l[0], l[1], l[2])
        flux = upwind_flux(s, l, p0, q, r1, p, q1, r2)
        low = v[:, 0:128]
        none = jnp.zeros_like(low)
        l = [none, none, none, low, roll(low, -1, 1), roll(low, -2, 1)]
        p, q, r = indicators(l[1], l[2], l[3])
        p1, q1, r1 = indicators(l[2], l[3], l[4])
        _, _, r2 = indicators(l[3], l[4], l[5])
        p0, _, _ = indicators(none, none, none)
        wall = upwind_flux(0.5 * w[:, 0:128], l, p0, q, r1, p, q1, r2)
        wall = jnp.concatenate([wall, wall], axis=1)
        change = change + (flux - jnp.where(lane == 0, wall, roll(flux, 1, 1)))
        moved[i] = v - 0.25 * change
        return above

    rows[...] = jnp.zeros_like(rows)
    speed[...] = jnp.zeros_like(speed)
    lax.fori_loop(0, 16, plane, x_flux(0, xl[3], velocity[0, 0]))


def transport(psi, velocity, xl, xh, yl, yh):
    planes = (20, 16, 256)
    scratch = [(22, 16, 256), planes, planes, planes, (24, 256), (24, 256)]
    return call(
        transport_body, [(16, 16, 256)], scratch, [psi, velocity, xl, xh, yl, yh], 10000000
    )[0]


def force_body(nx, ny, at, mid, yl, yh, velocity, xl, xh, vyl, vyh, source, m, n_x, n_y, n_z, s_x, part, pad):
    x0, y0 = at[0] * 16, at[1] * 16
    shape = (32, 256)
    lane = iota(shape, 1)

    def fill(i, carry):
        m[i] = jnp.zeros(shape, F32)
        m[i, 5:8, :] = yl[i]
        m[i, 8:24, :] = mid[i]
        m[i, 24:27, :] = yh[i]
        return carry

    lax.fori_loop(0, 22, fill, 0)

    def gradient(i):
        c = m[i]
        lower, upper = z_shifted(c)
        gx = 0.5 * (m[i + 1] - m[i - 1])
        gy = 0.5 * (roll(c, -1, 0) - roll(c, 1, 0))
        return gx, gy, 0.5 * (upper - lower)

    def normals(i, carry):
        gx, gy, gz = gradient(i + 1)
        inverse = lax.rsqrt(gx * gx + gy * gy + gz * gz + DELTA_SQ)
        n_x[i], n_y[i], n_z[i] = gx * inverse, gy * inverse, gz * inverse
        return carry

    lax.fori_loop(0, 20, normals, 0)
    mask_y = row_mask(shape, y0 - 8, ny)

    def stars(i, carry):
        gx, gy, gz = gradient(i + 2)
        c = m[i + 2]
        edge = 0.5 * c
        edge = edge * lax.rsqrt(edge * edge + DELTA_SQ)
        nz = n_z[i + 1]
        upper = jnp.where(lane == 255, -edge, roll(nz, -1, 1))
        lower = jnp.where(lane == 0, edge, roll(nz, 1, 1))
        nn = n_y[i + 1]
        bending = -0.5 * (
            (n_x[i + 2] - n_x[i]) + (roll(nn, -1, 0) - roll(nn, 1, 0)) + (upper - lower)
        )
        keep = mask_y * plane_factor(x0 + i - 1, nx)
        bending = bending * keep
        fx, fy, fz = bending * gx, bending * gy, bending * gz
        k = jnp.clip(i - 1, 0, 15)
        vx = jnp.where(i == 0, xl[0], jnp.where(i == 17, xh[0], velocity[0, k]))
        s_x[i] = fx[8:24, :] + vx
        pad[7:8, :] = vyl[k]
        pad[8:24, :] = velocity[1, k]
        pad[24:25, :] = vyh[k]
        sy = fy + pad[...]
        dy = roll(sy, -1, 0) - roll(sy, 1, 0)
        sz = fz[8:24, :] + velocity[2, k]
        below, above = z_shifted(sz)
        part[i] = dy[8:24, :] + (above - below)
        return carry

    pad[...] = jnp.zeros_like(pad)
    lax.fori_loop(0, 18, stars, 0)

    def finish(i, carry):
        source[i] = -0.5 * (part[i + 1] + (s_x[i + 2] - s_x[i]))
        return carry

    lax.fori_loop(0, 16, finish, 0)


def force(nx, ny, at, mid, yl, yh, velocity, xl, xh, vyl, vyh):
    n = (20, 32, 256)
    scratch = [(22, 32, 256), n, n, n, (18, 16, 256), (18, 16, 256), (32, 256)]
    args = [at, mid, yl, yh, velocity, xl, xh, vyl, vyh]
    return call(functools.partial(force_body, nx, ny), [(16, 16, 256)], scratch, args, 10000000)[0]


def assemble(ext, mid, yl, yh, planes):
    def fill(i, carry):
        ext[i, 0:12, :] = yl[i]
        ext[i, 12:28, :] = mid[i]
        ext[i, 28:40, :] = yh[i]
        return carry

    lax.fori_loop(0, planes, fill, 0)


def descend(nx, ny, at, b, v, v_out, b1_out, u_out, b2_out, wide_rows, t, s1, t1):
    x1, y1 = at[0] * 8, at[1] * 8

    def keep_v(i, carry):
        v_out[i] = v[i + 7]
        return carry

    lax.fori_loop(0, 20, keep_v, 0)

    def residual(i):
        c, around = beside(v, i)
        return b[i + 1] - (6.0 * c - around)

    def pairs(i, carry):
        total = residual(2 * i + 1) + residual(2 * i + 2)
        for half in range(2):
            wide_rows[half] = total[:, 128 * half : 128 * half + 128]
            even = wide_rows[half, pl.ds(0, 20, stride=2), :]
            odd = wide_rows[half, pl.ds(1, 20, stride=2), :]
            t[i, 0:20, 128 * half : 128 * half + 128] = even + odd
        return carry

    lax.fori_loop(0, 16, pairs, 0)
    full = dot(t[...].reshape(16 * 24, 256), pair_matrix(256, 128, 0.125)).reshape(16, 24, 128)
    rows = iota((24, 128), 0)
    good = jnp.logical_and(inside(rows + (y1 - 6), ny // 2), rows < 20)
    for i in range(16):
        ok = jnp.logical_and(good, inside(x1 + i - 4, nx // 2))
        b1_out[i] = jnp.where(ok, full[i], 0.0)
    mask = jnp.where(good, 1.0, 0.0).astype(F32)
    weight = 4.0 * SIDE

    def smooth(i, carry):
        c, around = beside(b1_out, i + 1)
        u_out[i] = (weight * plane_factor(x1 + i - 3, nx // 2)) * mask * (1.2 * c + SIDE * around)
        return carry

    lax.fori_loop(0, 14, smooth, 0)
    t1[...] = jnp.zeros_like(t1)
    for k in range(4):
        total = 0.0
        for j in (2 * k, 2 * k + 1):
            c, around = beside(u_out, j + 3)
            total = total + (b1_out[j + 4] - 0.25 * (6.0 * c - around))
        s1[k] = total
        t1[k, 0:4, :] = s1[k, pl.ds(6, 4, stride=2), :] + s1[k, pl.ds(7, 4, stride=2), :]
    small = dot(t1[...].reshape(32, 128), pair_matrix(128, 128, 0.125)).reshape(4, 8, 128)
    for k in range(4):
        b2_out[k] = small[k, 0:4, 0:64]


DOWN_OUTS = [(20, 40, 256), (16, 24, 128), (14, 24, 128), (4, 4, 64)]
DOWN_SCRATCH = [(34, 40, 256), (2, 40, 128), (16, 24, 256), (4, 24, 128), (4, 8, 128)]


def first_down_body(nx, ny, at, mid, yl, yh, b, v_out, b1_out, u_out, b2_out, v, *scratch):
    assemble(b, mid, yl, yh, 36)
    mask = row_mask((40, 256), at[1] * 16 - ROWS, ny)

    def smooth(i, carry):
        c, around = beside(b, i + 1)
        keep = mask * plane_factor(at[0] * 16 + i - 9, nx)
        v[i] = SIDE * keep * (1.2 * c + SIDE * around)
        return carry

    lax.fori_loop(0, 34, smooth, 0)
    descend(nx, ny, at, b, v, v_out, b1_out, u_out, b2_out, *scratch)


def first_down(nx, ny, at, mid, yl, yh):
    return call(
        functools.partial(first_down_body, nx, ny),
        [(36, 40, 256)] + DOWN_OUTS,
        DOWN_SCRATCH,
        [at, mid, yl, yh],
        20000000,
    )


def next_down_body(nx, ny, at, mid, yl, yh, b, v_out, b1_out, u_out, b2_out, v, wide_rows, t, s1, t1, start, once):
    assemble(start, mid, yl, yh, 38)
    mask = row_mask((40, 256), at[1] * 16 - ROWS, ny)

    def sweep(src, dst, first, shift):
        def plane(i, carry):
            c, around = beside(src, i + 1)
            keep = mask * plane_factor(at[0] * 16 + i + first, nx)
            dst[i] = keep * (0.2 * c + SIDE * (around + b[i + shift]))
            return carry

        return plane

    lax.fori_loop(0, 36, sweep(start, once, -10, 0), 0)
    lax.fori_loop(0, 34, sweep(once, v, -9, 1), 0)
    descend(nx, ny, at, b, v, v_out, b1_out, u_out, b2_out, wide_rows, t, s1, t1)


def next_down(nx, ny, at, mid, yl, yh, b):
    return call(
        functools.partial(next_down_body, nx, ny),
        DOWN_OUTS,
        DOWN_SCRATCH + [(38, 40, 256), (36, 40, 256)],
        [at, mid, yl, yh, b],
        30000000,
    )


def up_body(nx, ny, at, b2_all, b1, u, b, v_down, out, s2, v2, w2, t3, b3, c3, d3, dup, row2, m1, n1, m0, n0):
    wide, narrow = at[0], at[1]
    spot = wide % GROUP
    rows2 = s2.shape[1]
    rows3 = rows2 // 2
    count = rows2 // 4
    s2[...] = jnp.zeros_like(s2)

    def gather(j, carry):
        block = spot + 1 + j
        layer, place = block // GROUP, block % GROUP
        for n in range(count):
            for k in range(4):
                s2[4 * j + k, 4 * n : 4 * n + 4, 0:64] = b2_all[place * count + n, layer, k]
        return carry

    lax.fori_loop(0, 7, gather, 0)

    def walled(c, rows, lanes):
        row, lane = iota(c.shape, 0), iota(c.shape, 1)
        lower = jnp.where(row == 0, 0.0, roll(c, 1, 0))
        upper = jnp.where(row == rows - 1, 0.0, roll(c, -1, 0))
        return (lower + upper) + (roll(c, 1, 1) + roll(c, -1, 1))

    def around(ref, i, rows, lanes):
        c = ref[i]
        return c, (ref[i - 1] + ref[i + 1]) + walled(c, rows, lanes)

    def lanes_below(rows, lanes):
        return jnp.where(iota((rows, 128), 1) < lanes, 1.0, 0.0).astype(F32)

    x2 = wide * 4
    mask2 = lanes_below(rows2, 64)
    weight2 = 16.0 * SIDE

    def smooth2(i, carry):
        c, near = around(s2, i, rows2, 64)
        v2[i] = (weight2 * plane_factor(x2 + i - 12, nx // 4)) * mask2 * (1.2 * c + SIDE * near)
        return carry

    lax.fori_loop(1, 27, smooth2, 0)

    def residual2(i):
        c, near = around(v2, i, rows2, 64)
        return s2[i] - (1.0 / 16.0) * (6.0 * c - near)

    def pairs2(i, carry):
        row2[...] = residual2(2 * i + 2) + residual2(2 * i + 3)
        t3[i] = row2[pl.ds(0, rows3, stride=2), :] + row2[pl.ds(1, rows3, stride=2), :]
        return carry

    lax.fori_loop(0, 12, pairs2, 0)
    full = dot(t3[...].reshape(12 * rows3, 128), pair_matrix(128, 128, 0.125)).reshape(12, rows3, 128)
    x3 = wide * 2
    mask3 = lanes_below(rows3, 32)
    weight3 = 64.0 * SIDE
    for i in range(12):
        value = full[i] * mask3 * (weight3 * plane_factor(x3 + i - 5, nx // 8))
        b3[i] = value
        c3[i] = value

    def sweep3(src, dst):
        def plane(i, carry):
            c, near = around(src, i, rows3, 32)
            dst[i] = mask3 * plane_factor(x3 + i - 5, nx // 8) * (0.2 * c + SIDE * near) + b3[i]
            return carry

        return plane

    lax.fori_loop(1, 11, sweep3(c3, d3), 0)
    lax.fori_loop(2, 10, sweep3(d3, c3), 0)
    lax.fori_loop(3, 9, sweep3(c3, d3), 0)
    spread = dot(d3[3:9].reshape(6 * rows3, 128), copy_matrix(128, 128)).reshape(6, rows3, 128)
    for i in range(6):
        dup[pl.ds(0, rows3, stride=2), :] = spread[i]
        dup[pl.ds(1, rows3, stride=2), :] = spread[i]
        for k in (8 + 2 * i, 9 + 2 * i):
            v2[k] = v2[k] + dup[0:rows2, :] * mask2 * plane_factor(x2 + k - 12, nx // 4)

    def sweep2(src, dst):
        def plane(i, carry):
            c, near = around(src, i, rows2, 64)
            keep = mask2 * plane_factor(x2 + i - 12, nx // 4)
            dst[i] = keep * (0.2 * c + SIDE * (near + 16.0 * s2[i]))
            return carry

        return plane

    lax.fori_loop(9, 19, sweep2(v2, w2), 0)
    lax.fori_loop(10, 18, sweep2(w2, v2), 0)
    turn = lax.rem(rows2 + 3 - 4 * narrow + rows2, rows2)
    picked = [pltpu.roll(v2[10 + i], turn, 0)[0:16, :] for i in range(8)]
    spread = dot(jnp.concatenate(picked, axis=0), copy_matrix(128, 128)).reshape(8, 16, 128)
    x1, y1 = wide * 8, narrow * 8
    mask1 = row_mask((24, 128), y1 - 6, ny // 2)
    for i in range(8):
        dup[pl.ds(0, 12, stride=2), :] = spread[i, 0:12, :]
        dup[pl.ds(1, 12, stride=2), :] = spread[i, 0:12, :]
        for k in (2 * i - 1, 2 * i):
            if 0 <= k < 14:
                m1[k] = (u[k] + dup[0:24, :]) * mask1 * plane_factor(x1 + k - 3, nx // 2)

    def sweep1(src, dst):
        def plane(i, carry):
            c, near = beside(src, i)
            keep = mask1 * plane_factor(x1 + i - 3, nx // 2)
            dst[i] = keep * (0.2 * c + SIDE * (near + 4.0 * b1[i + 1]))
            return carry

        return plane

    lax.fori_loop(1, 13, sweep1(m1, n1), 0)
    lax.fori_loop(2, 12, sweep1(n1, m1), 0)
    spread = dot(m1[2:12].reshape(10 * 24, 128), copy_matrix(128, 256)).reshape(10, 24, 256)
    x0, y0 = wide * 16, narrow * 16
    mask0 = row_mask((40, 256), y0 - ROWS, ny)
    for i in range(10):
        for half in range(2):
            value = spread[i, 0:20, 128 * half : 128 * half + 128]
            dup[pl.ds(0, 20, stride=2), :] = value
            dup[pl.ds(1, 20, stride=2), :] = value
            for k in (2 * i, 2 * i + 1):
                n0[k, :, 128 * half : 128 * half + 128] = dup[0:40, :]

    def add0(i, carry):
        m0[i] = (v_down[i] + n0[i]) * mask0 * plane_factor(x0 + i - 2, nx)
        return carry

    lax.fori_loop(0, 20, add0, 0)

    def sweep0(i, carry):
        c, near = beside(m0, i)
        keep = mask0 * plane_factor(x0 + i - 2, nx)
        n0[i] = keep * (0.2 * c + SIDE * (near + b[i + 8]))
        return carry

    lax.fori_loop(1, 19, sweep0, 0)

    def last0(i, carry):
        c, near = beside(n0, i + 2)
        value = 0.2 * c + SIDE * (near + b[i + 10])
        out[i] = value[12:28, :]
        return carry

    lax.fori_loop(0, 16, last0, 0)


def up(nx, ny, at, b2_all, b1, u, b, v_down):
    rows2 = ny // 4
    rows3 = rows2 // 2
    wide_part = (28, rows2, 128)
    small = (12, rows3, 128)
    scratch = [
        wide_part, wide_part, wide_part, small, small, small, small,
        (48, 128), (rows2, 128), (14, 24, 128), (14, 24, 128), (20, 40, 256), (20, 40, 256),
    ]
    return call(
        functools.partial(up_body, nx, ny),
        [(16, 16, 256)],
        scratch,
        [at, b2_all, b1, u, b, v_down],
        20000000,
    )[0]


def shifted(array, axis, step):
    count = lax.axis_size(axis)
    return lax.ppermute(
        array, axis, [(i, i + step) for i in range(count) if 0 <= i + step < count]
    )


def surround(array, planes, rows):
    low = shifted(array[16 - planes :], "wide", 1)
    high = shifted(array[:planes], "wide", -1)
    mid = jnp.concatenate([low, array, high], axis=0)
    y_low = shifted(mid[:, 16 - rows :, :], "narrow", 1)
    y_high = shifted(mid[:, :rows, :], "narrow", -1)
    return mid, y_low, y_high


def spread_coarse(b2):
    wide, narrow = lax.axis_size("wide"), lax.axis_size("narrow")
    before = shifted(b2, "wide", GROUP)
    after = shifted(b2, "wide", -GROUP)
    three = jnp.stack([before, b2, after])
    size = GROUP * narrow
    pieces = jnp.broadcast_to(three[None], (size,) + three.shape)
    groups = [[g * size + k for k in range(size)] for g in range(wide // GROUP)]
    return lax.all_to_all(pieces, ("wide", "narrow"), 0, 0, axis_index_groups=groups)


def on_device(phase, distance, velocity):
    nx, ny = 16 * lax.axis_size("wide"), 16 * lax.axis_size("narrow")
    at = jnp.stack([lax.axis_index("wide"), lax.axis_index("narrow")]).astype(jnp.int32)
    psi, x_low, x_high, y_low, y_high = prepare(phase, distance, velocity)
    xl = shifted(x_high, "wide", 1)
    xh = shifted(x_low, "wide", -1)
    yl = shifted(y_high, "narrow", 1)
    yh = shifted(y_low, "narrow", -1)
    moved = transport(psi, velocity, xl, xh, yl, yh)
    mid, m_low, m_high = surround(moved, 3, 3)
    source = force(
        nx, ny, at, mid, m_low, m_high, velocity, xl[3:], xh[3:], yl[:, 3:, :], yh[:, 3:, :]
    )
    b, v, b1, u, b2 = first_down(nx, ny, at, *surround(source, HALO, ROWS))
    pressure = up(nx, ny, at, spread_coarse(b2), b1, u, b, v)
    v, b1, u, b2 = next_down(nx, ny, at, *surround(pressure, HALO + 1, ROWS), b)
    pressure = up(nx, ny, at, spread_coarse(b2), b1, u, b, v)
    return (moved, pressure)


def solution(mesh):
    blocks = P("wide", "narrow", None)
    return jax.shard_map(
        on_device,
        mesh=mesh,
        in_specs=(blocks, blocks, P(None, "wide", "narrow", None)),
        out_specs=(blocks, blocks),
        check_vma=False,
    )
```

time: 759 us -> 244 us (0.32)
  the two profiles are of different devices: /device:TPU:408 before, /device:TPU:257 now
where the time goes in v1:
time: 244 us; the launch traced here: 243 us
  Pallas kernels  73.2 us (30%)
  starting transfers between devices  67.5 us (28%)
  blocking collectives  40.1 us (16%)
  waiting for transfers between devices  31.3 us (13%)
  local copies, waits for them, and re-layouts  21.4 us (9%)
  other arithmetic  8.12 us (3%)
    pallas_call x7, Pallas kernels, call(): pl.pallas_call(body, out_shape=[jax.ShapeDtypeStruct(s, F32) for s in out...  73.2 us
    ppermute x20, starting transfers between devices, shifted(): lax.ppermute(array, axis, [(i, i + step) for i in range(count) if 0 <= i...  67.5 us
    all_to_all x2, blocking collectives, spread_coarse(): lax.all_to_all(pieces, ('wide', 'narrow'), 0, 0, axis_index_groups=groups)  40.1 us
    ppermute x20, waiting for transfers between devices, shifted(): lax.ppermute(array, axis, [(i, i + step) for i in range(count) if 0 <= i...  31.3 us
    unnamed x22, local copies, waits for them, and re-layouts  7.04 us
  transfers between devices with their start and end apart: 20, of which 12 were waited for; matrix products, arithmetic and copies ran while one was open for 4% of the time, Pallas kernels for 0%

profile of v1, /device:TPU:257, one launch (start us, length us, event | category | flops | bytes accessed | tf_op | source)
XLA Modules:
  0.0 242.7 jit_solution(7899789469613738370)
XLA Ops:
  0.6 2.6 %shard_map.50 = (f32[16,16,256]{2,1,0:T(8,128)}, f32[4,16,256]{2,1,0:T(8,128)}, f32[4,16,256]{2,1,0:T(8,128)}, f32[16,4,256]{2,1,0:T(4,128)}, f32[16,4,256]{2,1,0:T(4,128)}) custom-call(s32[16,16,256]{2,1,0:T(8,128)} %phase.1, f32[16,16,256]{2,1,0:T(8,128)} %distance.1, f32[3,16,16,256]{3,2,1,0:T(8,128)} %velocity.5), custom_call_target="tpu_custom_call" | custom-call | flops 1000000 | bytes 4000000 | tf_op jit(solution)/shard_map/pallas_call | solution.py:82
  3.2 3.1 %collective-permute-start = (f32[4,16,256]{2,1,0:T(8,128)}, f32[4,16,256]{2,1,0:T(8,128)S(1)}, u32[]{:S(2)}, u32[]{:S(2)}) collective-permute-start(f32[4,16,256]{2,1,0:T(8,128)} %get-tuple-element.17), channel_id=1, source_target_pairs={{0,8},{8,16},{16,24},{24,32},{32,40},{40,48},{48,56},{56,64},{64,7... | collective-permute-start | bytes 196616 | tf_op jit(solution)/shard_map/ppermute | solution.py:588
  6.3 5.5 %collective-permute-start.1 = (f32[4,16,256]{2,1,0:T(8,128)}, f32[4,16,256]{2,1,0:T(8,128)S(1)}, u32[]{:S(2)}, u32[]{:S(2)}) collective-permute-start(f32[4,16,256]{2,1,0:T(8,128)} %get-tuple-element.18), channel_id=1, source_target_pairs={{8,0},{16,8},{24,16},{32,24},{40,32},{48,40},{56,48},{64,56},{72,6... | collective-permute-start | bytes 196616 | tf_op jit(solution)/shard_map/ppermute | solution.py:588
  11.8 4.3 %collective-permute-start.2 = (f32[16,4,256]{2,1,0:T(4,128)}, f32[16,4,256]{2,1,0:T(4,128)S(1)}, u32[]{:S(2)}, u32[]{:S(2)}) collective-permute-start(f32[16,4,256]{2,1,0:T(4,128)} %get-tuple-element.19), channel_id=1, source_target_pairs={{0,1},{1,2},{2,3},{3,4},{4,5},{5,6},{6,7},{8,9},{9,10},{10,11},{11... | collective-permute-start | bytes 196616 | tf_op jit(solution)/shard_map/ppermute | solution.py:588
  16.1 1.9 collective-permute-start.3
  18.1 3.8 %collective-permute-done.3.yh = f32[16,4,256]{2,1,0:T(4,128)S(1)} collective-permute-done((f32[16,4,256]{2,1,0:T(4,128)}, f32[16,4,256]{2,1,0:T(4,128)S(1)}, u32[]{:S(2)}, u32[]{:S(2)}) %collective-permute-start.3) | collective-permute-done | bytes 65568 | tf_op jit(solution)/shard_map/ppermute | solution.py:588
  22.5 6.6 %shard_map.51 = f32[16,16,256]{2,1,0:T(8,128)} custom-call(f32[16,16,256]{2,1,0:T(8,128)} %get-tuple-element.16.psi, f32[3,16,16,256]{3,2,1,0:T(8,128)} %velocity.5, f32[4,16,256]{2,1,0:T(8,128)} %copy-done.3, f32[4,16,256]{2,1,0:T(8,128)} %copy-done.4, f32[16,4,256]{2,1,0:T(4,128)} %copy-done.5, f32[16,4,256]{2,1,0:T(4,128)} %copy-done.6), custom_call_target="tpu_custom_call" | custom-call | flops 10000000 | bytes 4000000 | tf_op jit(solution)/shard_map/pallas_call | solution.py:82
  30.0 1.9 collective-permute-start.4
  31.9 6.7 %collective-permute-start.5 = (f32[3,16,256]{2,1,0:T(8,128)S(1)}, f32[3,16,256]{2,1,0:T(8,128)S(1)}, u32[]{:S(2)}, u32[]{:S(2)}) collective-permute-start(f32[3,16,256]{2,1,0:T(8,128)S(1)} %get-tuple-element.41), channel_id=1, source_target_pairs={{8,0},{16,8},{24,16},{32,24},{40,32},{48,40},{56,48},{64,56},{72,6... | collective-permute-start | bytes 147464 | tf_op jit(solution)/shard_map/ppermute | solution.py:588
  38.6 1.1 collective-permute-done.5
  40.8 1.9 collective-permute-start.7
  42.7 3.6 %collective-permute-start.6 = (f32[22,3,256]{2,1,0:T(4,128)S(1)}, f32[22,3,256]{2,1,0:T(4,128)S(1)}, u32[]{:S(2)}, u32[]{:S(2)}) collective-permute-start(f32[22,3,256]{2,1,0:T(4,128)S(1)} %get-tuple-element.35), channel_id=1, source_target_pairs={{0,1},{1,2},{2,3},{3,4},{4,5},{5,6},{6,7},{8,9},{9,10},{10,11},{11... | collective-permute-start | bytes 202760 | tf_op jit(solution)/shard_map/ppermute | solution.py:588
  47.0 1.3 slice.68.xl
  48.3 1.3 slice.69.xh
  49.6 1.5 slice.70.vyl
  51.1 1.5 slice.71.vyh
  53.8 7.3 %shard_map.52 = f32[16,16,256]{2,1,0:T(8,128)} custom-call(s32[2]{0:T(128)} %pad_add_fusion.at, f32[22,16,256]{2,1,0:T(8,128)} %copy-done.2, f32[22,3,256]{2,1,0:T(4,128)} %copy-done.8, f32[22,3,256]{2,1,0:T(4,128)} %copy-done.7, f32[3,16,16,256]{3,2,1,0:T(8,128)} %velocity.5, f32[1,16,256]{2,1,0:T(8,128)} %slice.68.xl, f32[1,16,256]{2,1,0:T(8,128)} %slice.69.xh, ...), custom_call_target="tpu_custom_call" | custom-call | flops 10000000 | bytes 4000000 | tf_op jit(solution)/shard_map/pallas_call | solution.py:82
  62.2 1.9 collective-permute-start.8
  64.1 7.0 %collective-permute-start.9 = (f32[10,16,256]{2,1,0:T(8,128)S(1)}, f32[10,16,256]{2,1,0:T(8,128)S(1)}, u32[]{:S(2)}, u32[]{:S(2)}) collective-permute-start(f32[10,16,256]{2,1,0:T(8,128)S(1)} %get-tuple-element.39), channel_id=1, source_target_pairs={{8,0},{16,8},{24,16},{32,24},{40,32},{48,40},{56,48},{64,56},{72,6... | collective-permute-start | bytes 491528 | tf_op jit(solution)/shard_map/ppermute | solution.py:588
  71.1 1.5 collective-permute-done.8
  72.6 1.8 collective-permute-done.9
  76.1 3.7 %collective-permute-start.10 = (f32[36,12,256]{2,0,1:T(8,128)S(1)}, f32[36,12,256]{2,0,1:T(8,128)S(1)}, u32[]{:S(2)}, u32[]{:S(2)}) collective-permute-start(f32[36,12,256]{2,0,1:T(8,128)S(1)} %copy.5), channel_id=1, source_target_pairs={{0,1},{1,2},{2,3},{3,4},{4,5},{5,6},{6,7},{8,9},{9,10},{10,11},{11... | collective-permute-start | bytes 1327112 | tf_op jit(solution)/shard_map/ppermute | solution.py:588
  80.1 1.9 collective-permute-start.11
  82.0 3.6 %collective-permute-done.10 = f32[36,12,256]{2,0,1:T(8,128)S(1)} collective-permute-done((f32[36,12,256]{2,0,1:T(8,128)S(1)}, f32[36,12,256]{2,0,1:T(8,128)S(1)}, u32[]{:S(2)}, u32[]{:S(2)}) %collective-permute-start.10) | collective-permute-done | bytes 442400 | tf_op jit(solution)/shard_map/ppermute | solution.py:588
  86.5 3.7 %collective-permute-done.11 = f32[36,12,256]{2,0,1:T(8,128)S(1)} collective-permute-done((f32[36,12,256]{2,0,1:T(8,128)S(1)}, f32[36,12,256]{2,0,1:T(8,128)S(1)}, u32[]{:S(2)}, u32[]{:S(2)}) %collective-permute-start.11) | collective-permute-done | bytes 442400 | tf_op jit(solution)/shard_map/ppermute | solution.py:588
  91.2 10.4 %shard_map.53 = (f32[36,40,256]{2,1,0:T(8,128)}, f32[20,40,256]{2,1,0:T(8,128)}, f32[16,24,128]{2,1,0:T(8,128)}, f32[14,24,128]{2,1,0:T(8,128)}, f32[4,4,64]{2,1,0:T(4,128)}) custom-call(s32[2]{0:T(128)} %pad_add_fusion.at, f32[36,16,256]{2,1,0:T(8,128)} %copy-done.1, f32[36,12,256]{2,1,0:T(8,128)} %copy.7.yl, f32[36,12,256]{2,1,0:T(8,128)} %copy.8.yh), custom_call_target="tpu_custom_call" | custom-call | flops 20000000 | bytes 4000000 | tf_op jit(solution)/shard_map/pallas_call | solution.py:82
  101.6 1.9 collective-permute-start.13
  103.5 3.4 %collective-permute-start.12 = (f32[4,4,64]{2,1,0:T(4,128)}, f32[4,4,64]{2,1,0:T(4,128)S(1)}, u32[]{:S(2)}, u32[]{:S(2)}) collective-permute-start(f32[4,4,64]{2,1,0:T(4,128)} %get-tuple-element.21), channel_id=1, source_target_pairs={{0,32},{8,40},{16,48},{24,56},{32,64},{40,72},{48,80},{56,88},{64,... | collective-permute-start | bytes 12296 | tf_op jit(solution)/shard_map/ppermute | solution.py:588
  106.9 2.4 %collective-permute-done.12 = f32[4,4,64]{2,1,0:T(4,128)S(1)} collective-permute-done((f32[4,4,64]{2,1,0:T(4,128)}, f32[4,4,64]{2,1,0:T(4,128)S(1)}, u32[]{:S(2)}, u32[]{:S(2)}) %collective-permute-start.12) | collective-permute-done | bytes 4128 | tf_op jit(solution)/shard_map/ppermute | solution.py:588
  110.9 20.6 %all_to_all.10 = f32[32,1,3072]{2,1,0:T(1,128)S(1)} all-to-all(f32[32,1,3072]{2,1,0:T(1,128)S(1)} %reshape.6), channel_id=1, replica_groups={{0,1,2,3,4,5,6,7,8,9,10,11,12,13,14,15,16,17,18,19,20,21,22,23,24,25,26..., dimensions={0} | all-to-all | bytes 786432 | tf_op jit(solution)/shard_map/all_to_all | solution.py:610
  132.0 1.6 reduce
  133.6 1.4 reshape.7.b2_all
  135.0 16.2 %shard_map.54 = f32[16,16,256]{2,1,0:T(8,128)} custom-call(s32[2]{0:T(128)} %pad_add_fusion.at, f32[32,3,4,4,64]{4,3,2,1,0:T(4,128)} %reshape.7.b2_all, f32[16,24,128]{2,1,0:T(8,128)} %get-tuple-element.22.b1, f32[14,24,128]{2,1,0:T(8,128)} %get-tuple-element.23.u, f32[36,40,256]{2,1,0:T(8,128)} %get-tuple-element.24.b, f32[20,40,256]{2,1,0:T(8,128)} %get-tuple-element.25.v_down), custom_call_target="tpu_custom_call" | custom-call | flops 20000000 | bytes 4000000 | tf_op jit(solution)/shard_map/pallas_call | solution.py:82
  152.2 2.1 collective-permute-start.14
  154.3 6.5 %collective-permute-start.15 = (f32[11,16,256]{2,1,0:T(8,128)S(1)}, f32[11,16,256]{2,1,0:T(8,128)S(1)}, u32[]{:S(2)}, u32[]{:S(2)}) collective-permute-start(f32[11,16,256]{2,1,0:T(8,128)S(1)} %get-tuple-element.37), channel_id=1, source_target_pairs={{8,0},{16,8},{24,16},{32,24},{40,32},{48,40},{56,48},{64,56},{72,6... | collective-permute-start | bytes 540680 | tf_op jit(solution)/shard_map/ppermute | solution.py:588
  160.8 2.8 %collective-permute-done.14 = f32[11,16,256]{2,1,0:T(8,128)S(1)} collective-permute-done((f32[11,16,256]{2,1,0:T(8,128)S(1)}, f32[11,16,256]{2,1,0:T(8,128)S(1)}, u32[]{:S(2)}, u32[]{:S(2)}) %collective-permute-start.14) | collective-permute-done | bytes 180256 | tf_op jit(solution)/shard_map/ppermute | solution.py:588
  166.4 2.9 %collective-permute-start.16 = (f32[38,12,256]{2,0,1:T(8,128)S(1)}, f32[38,12,256]{2,0,1:T(8,128)S(1)}, u32[]{:S(2)}, u32[]{:S(2)}) collective-permute-start(f32[38,12,256]{2,0,1:T(8,128)S(1)} %copy.9), channel_id=1, source_target_pairs={{0,1},{1,2},{2,3},{3,4},{4,5},{5,6},{6,7},{8,9},{9,10},{10,11},{11... | collective-permute-start | bytes 1400840 | tf_op jit(solution)/shard_map/ppermute | solution.py:588
  169.6 1.9 collective-permute-start.17
  171.5 3.5 %collective-permute-done.16 = f32[38,12,256]{2,0,1:T(8,128)S(1)} collective-permute-done((f32[38,12,256]{2,0,1:T(8,128)S(1)}, f32[38,12,256]{2,0,1:T(8,128)S(1)}, u32[]{:S(2)}, u32[]{:S(2)}) %collective-permute-start.16) | collective-permute-done | bytes 466976 | tf_op jit(solution)/shard_map/ppermute | solution.py:588
  176.1 3.7 %collective-permute-done.17 = f32[38,12,256]{2,0,1:T(8,128)S(1)} collective-permute-done((f32[38,12,256]{2,0,1:T(8,128)S(1)}, f32[38,12,256]{2,0,1:T(8,128)S(1)}, u32[]{:S(2)}, u32[]{:S(2)}) %collective-permute-start.17) | collective-permute-done | bytes 466976 | tf_op jit(solution)/shard_map/ppermute | solution.py:588
  180.7 14.0 %shard_map.55 = (f32[20,40,256]{2,1,0:T(8,128)}, f32[16,24,128]{2,1,0:T(8,128)}, f32[14,24,128]{2,1,0:T(8,128)}, f32[4,4,64]{2,1,0:T(4,128)}) custom-call(s32[2]{0:T(128)} %pad_add_fusion.at, f32[38,16,256]{2,1,0:T(8,128)} %copy-done, f32[38,12,256]{2,1,0:T(8,128)} %copy.11.yl, f32[38,12,256]{2,1,0:T(8,128)} %copy.12.yh, f32[36,40,256]{2,1,0:T(8,128)} %get-tuple-element.24.b), custom_call_target="tpu_custom_call" | custom-call | flops 30000000 | bytes 4000000 | tf_op jit(solution)/shard_map/pallas_call | solution.py:82
  194.8 1.9 collective-permute-start.19
  196.7 3.4 %collective-permute-start.18 = (f32[4,4,64]{2,1,0:T(4,128)}, f32[4,4,64]{2,1,0:T(4,128)S(1)}, u32[]{:S(2)}, u32[]{:S(2)}) collective-permute-start(f32[4,4,64]{2,1,0:T(4,128)} %get-tuple-element.26), channel_id=1, source_target_pairs={{0,32},{8,40},{16,48},{24,56},{32,64},{40,72},{48,80},{56,88},{64,... | collective-permute-start | bytes 12296 | tf_op jit(solution)/shard_map/ppermute | solution.py:588
  200.1 2.4 %collective-permute-done.18 = f32[4,4,64]{2,1,0:T(4,128)S(1)} collective-permute-done((f32[4,4,64]{2,1,0:T(4,128)}, f32[4,4,64]{2,1,0:T(4,128)S(1)}, u32[]{:S(2)}, u32[]{:S(2)}) %collective-permute-start.18) | collective-permute-done | bytes 4128 | tf_op jit(solution)/shard_map/ppermute | solution.py:588
  204.0 19.5 %all_to_all.11 = f32[32,1,3072]{2,1,0:T(1,128)S(1)} all-to-all(f32[32,1,3072]{2,1,0:T(1,128)S(1)} %reshape.8), channel_id=1, replica_groups={{0,1,2,3,4,5,6,7,8,9,10,11,12,13,14,15,16,17,18,19,20,21,22,23,24,25,26..., dimensions={0} | all-to-all | bytes 786432 | tf_op jit(solution)/shard_map/all_to_all | solution.py:610
  223.6 1.6 reduce.1
  225.2 1.4 reshape.9.b2_all
  226.6 16.2 %shard_map.56 = f32[16,16,256]{2,1,0:T(8,128)} custom-call(s32[2]{0:T(128)} %pad_add_fusion.at, f32[32,3,4,4,64]{4,3,2,1,0:T(4,128)} %reshape.9.b2_all, f32[16,24,128]{2,1,0:T(8,128)} %get-tuple-element.27.b1, f32[14,24,128]{2,1,0:T(8,128)} %get-tuple-element.28.u, f32[36,40,256]{2,1,0:T(8,128)} %get-tuple-element.24.b, f32[20,40,256]{2,1,0:T(8,128)} %get-tuple-element.29.v_down), custom_call_target="tpu_custom_call" | custom-call | flops 20000000 | bytes 4000000 | tf_op jit(solution)/shard_map/pallas_call | solution.py:82
  (52 shorter events, 19.0 us)
Async XLA Ops:
  3.2 14.9 %collective-permute-start = (f32[4,16,256]{2,1,0:T(8,128)}, f32[4,16,256]{2,1,0:T(8,128)S(1)}, u32[]{:S(2)}, u32[]{:S(2)}) collective-permute-start(f32[4,16,256]{2,1,0:T(8,128)} %get-tuple-element.17), channel_id=1, source_target_pairs={{0,8},{8,16},{16,24},{24,32},{32,40},{40,48},{48,56},{56,64},{64,7... | collective-permute-start | bytes 196616 | tf_op jit(solution)/shard_map/ppermute | solution.py:588
  6.3 11.8 %collective-permute-start.1 = (f32[4,16,256]{2,1,0:T(8,128)}, f32[4,16,256]{2,1,0:T(8,128)S(1)}, u32[]{:S(2)}, u32[]{:S(2)}) collective-permute-start(f32[4,16,256]{2,1,0:T(8,128)} %get-tuple-element.18), channel_id=1, source_target_pairs={{8,0},{16,8},{24,16},{32,24},{40,32},{48,40},{56,48},{64,56},{72,6... | collective-permute-start | bytes 196616 | tf_op jit(solution)/shard_map/ppermute | solution.py:588
  11.8 6.3 %collective-permute-start.2 = (f32[16,4,256]{2,1,0:T(4,128)}, f32[16,4,256]{2,1,0:T(4,128)S(1)}, u32[]{:S(2)}, u32[]{:S(2)}) collective-permute-start(f32[16,4,256]{2,1,0:T(4,128)} %get-tuple-element.19), channel_id=1, source_target_pairs={{0,1},{1,2},{2,3},{3,4},{4,5},{5,6},{6,7},{8,9},{9,10},{10,11},{11... | collective-permute-start | bytes 196616 | tf_op jit(solution)/shard_map/ppermute | solution.py:588
  16.1 5.8 %collective-permute-start.3 = (f32[16,4,256]{2,1,0:T(4,128)}, f32[16,4,256]{2,1,0:T(4,128)S(1)}, u32[]{:S(2)}, u32[]{:S(2)}) collective-permute-start(f32[16,4,256]{2,1,0:T(4,128)} %get-tuple-element.20), channel_id=1, source_target_pairs={{1,0},{2,1},{3,2},{4,3},{5,4},{6,5},{7,6},{9,8},{10,9},{11,10},{12... | collective-permute-start | bytes 196616 | tf_op jit(solution)/shard_map/ppermute | solution.py:588
  18.1 3.9 %copy-start.3 = (f32[4,16,256]{2,1,0:T(8,128)}, f32[4,16,256]{2,1,0:T(8,128)S(1)}, u32[]{:S(2)}) copy-start(f32[4,16,256]{2,1,0:T(8,128)S(1)} %collective-permute-done.xl) | copy-start | bytes 196612
  18.1 3.8 %copy-start.4 = (f32[4,16,256]{2,1,0:T(8,128)}, f32[4,16,256]{2,1,0:T(8,128)S(1)}, u32[]{:S(2)}) copy-start(f32[4,16,256]{2,1,0:T(8,128)S(1)} %collective-permute-done.1.xh) | copy-start | bytes 196612
  18.1 3.8 %copy-start.5 = (f32[16,4,256]{2,1,0:T(4,128)}, f32[16,4,256]{2,1,0:T(4,128)S(1)}, u32[]{:S(2)}) copy-start(f32[16,4,256]{2,1,0:T(4,128)S(1)} %collective-permute-done.2.yl) | copy-start | bytes 196612
  21.9 0.6 copy-start.6
  30.0 8.6 %collective-permute-start.4 = (f32[3,16,256]{2,1,0:T(8,128)S(1)}, f32[3,16,256]{2,1,0:T(8,128)S(1)}, u32[]{:S(2)}, u32[]{:S(2)}) collective-permute-start(f32[3,16,256]{2,1,0:T(8,128)S(1)} %get-tuple-element.40), channel_id=1, source_target_pairs={{0,8},{8,16},{16,24},{24,32},{32,40},{40,48},{48,56},{56,64},{64,7... | collective-permute-start | bytes 147464 | tf_op jit(solution)/shard_map/ppermute | solution.py:588
  31.9 7.8 %collective-permute-start.5 = (f32[3,16,256]{2,1,0:T(8,128)S(1)}, f32[3,16,256]{2,1,0:T(8,128)S(1)}, u32[]{:S(2)}, u32[]{:S(2)}) collective-permute-start(f32[3,16,256]{2,1,0:T(8,128)S(1)} %get-tuple-element.41), channel_id=1, source_target_pairs={{8,0},{16,8},{24,16},{32,24},{40,32},{48,40},{56,48},{64,56},{72,6... | collective-permute-start | bytes 147464 | tf_op jit(solution)/shard_map/ppermute | solution.py:588
  40.7 11.8 %copy-start.2 = (f32[22,16,256]{2,1,0:T(8,128)}, f32[22,16,256]{2,1,0:T(8,128)S(1)}, u32[]{:S(2)}) copy-start(f32[22,16,256]{2,1,0:T(8,128)S(1)} %pad_maximum_fusion.2.mid) | copy-start | bytes 1081348
  40.8 11.8 %collective-permute-start.7 = (f32[22,3,256]{2,1,0:T(4,128)S(1)}, f32[22,3,256]{2,1,0:T(4,128)S(1)}, u32[]{:S(2)}, u32[]{:S(2)}) collective-permute-start(f32[22,3,256]{2,1,0:T(4,128)S(1)} %get-tuple-element.34), channel_id=1, source_target_pairs={{1,0},{2,1},{3,2},{4,3},{5,4},{6,5},{7,6},{9,8},{10,9},{11,10},{12... | collective-permute-start | bytes 202760 | tf_op jit(solution)/shard_map/ppermute | solution.py:588
  42.7 9.9 %collective-permute-start.6 = (f32[22,3,256]{2,1,0:T(4,128)S(1)}, f32[22,3,256]{2,1,0:T(4,128)S(1)}, u32[]{:S(2)}, u32[]{:S(2)}) collective-permute-start(f32[22,3,256]{2,1,0:T(4,128)S(1)} %get-tuple-element.35), channel_id=1, source_target_pairs={{0,1},{1,2},{2,3},{3,4},{4,5},{5,6},{6,7},{8,9},{9,10},{10,11},{11... | collective-permute-start | bytes 202760 | tf_op jit(solution)/shard_map/ppermute | solution.py:588
  52.6 0.6 copy-start.7
  53.2 0.6 copy-start.8
  62.2 10.4 %collective-permute-start.8 = (f32[10,16,256]{2,1,0:T(8,128)S(1)}, f32[10,16,256]{2,1,0:T(8,128)S(1)}, u32[]{:S(2)}, u32[]{:S(2)}) collective-permute-start(f32[10,16,256]{2,1,0:T(8,128)S(1)} %get-tuple-element.38), channel_id=1, source_target_pairs={{0,8},{8,16},{16,24},{24,32},{32,40},{40,48},{48,56},{56,64},{64,7... | collective-permute-start | bytes 491528 | tf_op jit(solution)/shard_map/ppermute | solution.py:588
  64.1 10.2 %collective-permute-start.9 = (f32[10,16,256]{2,1,0:T(8,128)S(1)}, f32[10,16,256]{2,1,0:T(8,128)S(1)}, u32[]{:S(2)}, u32[]{:S(2)}) collective-permute-start(f32[10,16,256]{2,1,0:T(8,128)S(1)} %get-tuple-element.39), channel_id=1, source_target_pairs={{8,0},{16,8},{24,16},{32,24},{40,32},{48,40},{56,48},{64,56},{72,6... | collective-permute-start | bytes 491528 | tf_op jit(solution)/shard_map/ppermute | solution.py:588
  75.3 0.8 copy-start.1
  76.1 9.4 %collective-permute-start.10 = (f32[36,12,256]{2,0,1:T(8,128)S(1)}, f32[36,12,256]{2,0,1:T(8,128)S(1)}, u32[]{:S(2)}, u32[]{:S(2)}) collective-permute-start(f32[36,12,256]{2,0,1:T(8,128)S(1)} %copy.5), channel_id=1, source_target_pairs={{0,1},{1,2},{2,3},{3,4},{4,5},{5,6},{6,7},{8,9},{9,10},{10,11},{11... | collective-permute-start | bytes 1327112 | tf_op jit(solution)/shard_map/ppermute | solution.py:588
  80.1 10.1 %collective-permute-start.11 = (f32[36,12,256]{2,0,1:T(8,128)S(1)}, f32[36,12,256]{2,0,1:T(8,128)S(1)}, u32[]{:S(2)}, u32[]{:S(2)}) collective-permute-start(f32[36,12,256]{2,0,1:T(8,128)S(1)} %copy.6), channel_id=1, source_target_pairs={{1,0},{2,1},{3,2},{4,3},{5,4},{6,5},{7,6},{9,8},{10,9},{11,10},{12... | collective-permute-start | bytes 1327112 | tf_op jit(solution)/shard_map/ppermute | solution.py:588
  101.6 5.3 %collective-permute-start.13 = (f32[4,4,64]{2,1,0:T(4,128)}, f32[4,4,64]{2,1,0:T(4,128)S(1)}, u32[]{:S(2)}, u32[]{:S(2)}) collective-permute-start(f32[4,4,64]{2,1,0:T(4,128)} %get-tuple-element.21), channel_id=1, source_target_pairs={{32,0},{40,8},{48,16},{56,24},{64,32},{72,40},{80,48},{88,56},{96,... | collective-permute-start | bytes 12296 | tf_op jit(solution)/shard_map/ppermute | solution.py:588
  103.5 5.8 %collective-permute-start.12 = (f32[4,4,64]{2,1,0:T(4,128)}, f32[4,4,64]{2,1,0:T(4,128)S(1)}, u32[]{:S(2)}, u32[]{:S(2)}) collective-permute-start(f32[4,4,64]{2,1,0:T(4,128)} %get-tuple-element.21), channel_id=1, source_target_pairs={{0,32},{8,40},{16,48},{24,56},{32,64},{40,72},{48,80},{56,88},{64,... | collective-permute-start | bytes 12296 | tf_op jit(solution)/shard_map/ppermute | solution.py:588
  152.2 11.4 %collective-permute-start.14 = (f32[11,16,256]{2,1,0:T(8,128)S(1)}, f32[11,16,256]{2,1,0:T(8,128)S(1)}, u32[]{:S(2)}, u32[]{:S(2)}) collective-permute-start(f32[11,16,256]{2,1,0:T(8,128)S(1)} %get-tuple-element.36), channel_id=1, source_target_pairs={{0,8},{8,16},{16,24},{24,32},{32,40},{40,48},{48,56},{56,64},{64,7... | collective-permute-start | bytes 540680 | tf_op jit(solution)/shard_map/ppermute | solution.py:588
  154.3 10.3 %collective-permute-start.15 = (f32[11,16,256]{2,1,0:T(8,128)S(1)}, f32[11,16,256]{2,1,0:T(8,128)S(1)}, u32[]{:S(2)}, u32[]{:S(2)}) collective-permute-start(f32[11,16,256]{2,1,0:T(8,128)S(1)} %get-tuple-element.37), channel_id=1, source_target_pairs={{8,0},{16,8},{24,16},{32,24},{40,32},{48,40},{56,48},{64,56},{72,6... | collective-permute-start | bytes 540680 | tf_op jit(solution)/shard_map/ppermute | solution.py:588
  165.6 0.8 copy-start
  166.4 8.7 %collective-permute-start.16 = (f32[38,12,256]{2,0,1:T(8,128)S(1)}, f32[38,12,256]{2,0,1:T(8,128)S(1)}, u32[]{:S(2)}, u32[]{:S(2)}) collective-permute-start(f32[38,12,256]{2,0,1:T(8,128)S(1)} %copy.9), channel_id=1, source_target_pairs={{0,1},{1,2},{2,3},{3,4},{4,5},{5,6},{6,7},{8,9},{9,10},{10,11},{11... | collective-permute-start | bytes 1400840 | tf_op jit(solution)/shard_map/ppermute | solution.py:588
  169.6 10.1 %collective-permute-start.17 = (f32[38,12,256]{2,0,1:T(8,128)S(1)}, f32[38,12,256]{2,0,1:T(8,128)S(1)}, u32[]{:S(2)}, u32[]{:S(2)}) collective-permute-start(f32[38,12,256]{2,0,1:T(8,128)S(1)} %copy.10), channel_id=1, source_target_pairs={{1,0},{2,1},{3,2},{4,3},{5,4},{6,5},{7,6},{9,8},{10,9},{11,10},{12... | collective-permute-start | bytes 1400840 | tf_op jit(solution)/shard_map/ppermute | solution.py:588
  194.8 5.3 %collective-permute-start.19 = (f32[4,4,64]{2,1,0:T(4,128)}, f32[4,4,64]{2,1,0:T(4,128)S(1)}, u32[]{:S(2)}, u32[]{:S(2)}) collective-permute-start(f32[4,4,64]{2,1,0:T(4,128)} %get-tuple-element.26), channel_id=1, source_target_pairs={{32,0},{40,8},{48,16},{56,24},{64,32},{72,40},{80,48},{88,56},{96,... | collective-permute-start | bytes 12296 | tf_op jit(solution)/shard_map/ppermute | solution.py:588
  196.7 5.8 %collective-permute-start.18 = (f32[4,4,64]{2,1,0:T(4,128)}, f32[4,4,64]{2,1,0:T(4,128)S(1)}, u32[]{:S(2)}, u32[]{:S(2)}) collective-permute-start(f32[4,4,64]{2,1,0:T(4,128)} %get-tuple-element.26), channel_id=1, source_target_pairs={{0,32},{8,40},{16,48},{24,56},{32,64},{40,72},{48,80},{56,88},{64,... | collective-permute-start | bytes 12296 | tf_op jit(solution)/shard_map/ppermute | solution.py:588

commit v2 on v1

--- a/solution.py
+++ b/solution.py
@@ -90,6 +90,18 @@
     )(*args)
 
 
+def send_shapes(planes):
+    return [(16 + 2 * planes, 16, 256), (planes, 16, 256), (planes, 16, 256)]
+
+
+def send(block, wider, low, high, planes):
+    for i in range(16):
+        wider[planes + i] = block[i]
+    for i in range(planes):
+        low[i] = block[i]
+        high[i] = block[16 - planes + i]
+
+
 def prepare_body(phase, distance, velocity, psi, x_low, x_high, y_low, y_high):
     def plane(i, carry):
         orient = 2.0 * phase[i].astype(F32) - 1.0
@@ -100,7 +112,7 @@
         y_high[i, 3:4, :] = velocity[1, i, 15:16, :]
         return carry
 
-    lax.fori_loop(0, 16, plane, 0)
+    lax.fori_loop(0, 16, plane, 0, unroll=True)
     for k in range(3):
         x_low[k] = psi[k]
         x_high[k] = psi[13 + k]
@@ -138,7 +150,7 @@
     return (s * top) / (6.0 * (w0 + w1 + w2))
 
 
-def transport_body(psi, velocity, xl, xh, yl, yh, moved, ext, p_x, q_x, r_x, rows, speed):
+def transport_body(psi, velocity, xl, xh, yl, yh, moved, wider, low, high, ext, p_x, q_x, r_x, rows, speed):
     for k in range(3):
         ext[k] = xl[k]
         ext[19 + k] = xh[k]
@@ -147,14 +159,14 @@
         ext[3 + i] = psi[i]
         return carry
 
-    lax.fori_loop(0, 16, fill, 0)
+    lax.fori_loop(0, 16, fill, 0, unroll=True)
 
     def marks(i, carry):
         p, q, r = indicators(ext[i], ext[i + 1], ext[i + 2])
         p_x[i], q_x[i], r_x[i] = p, q, r
         return carry
 
-    lax.fori_loop(0, 20, marks, 0, unroll=2)
+    lax.fori_loop(0, 20, marks, 0, unroll=True)
 
     def x_flux(j, v_low, v_high):
         s = 0.5 * (v_low + v_high)
@@ -215,18 +227,18 @@
 
     rows[...] = jnp.zeros_like(rows)
     speed[...] = jnp.zeros_like(speed)
-    lax.fori_loop(0, 16, plane, x_flux(0, xl[3], velocity[0, 0]))
+    lax.fori_loop(0, 16, plane, x_flux(0, xl[3], velocity[0, 0]), unroll=True)
+    send(moved, wider, low, high, 3)
 
 
 def transport(psi, velocity, xl, xh, yl, yh):
     planes = (20, 16, 256)
     scratch = [(22, 16, 256), planes, planes, planes, (24, 256), (24, 256)]
-    return call(
-        transport_body, [(16, 16, 256)], scratch, [psi, velocity, xl, xh, yl, yh], 10000000
-    )[0]
-
-
-def force_body(nx, ny, at, mid, yl, yh, velocity, xl, xh, vyl, vyh, source, m, n_x, n_y, n_z, s_x, part, pad):
+    outs = [(16, 16, 256)] + send_shapes(3)
+    return call(transport_body, outs, scratch, [psi, velocity, xl, xh, yl, yh], 10000000)
+
+
+def force_body(nx, ny, at, mid, yl, yh, velocity, xl, xh, vyl, vyh, wider, low, high, m, n_x, n_y, n_z, s_x, part, pad, source):
     x0, y0 = at[0] * 16, at[1] * 16
     shape = (32, 256)
     lane = iota(shape, 1)
@@ -238,7 +250,7 @@
         m[i, 24:27, :] = yh[i]
         return carry
 
-    lax.fori_loop(0, 22, fill, 0)
+    lax.fori_loop(0, 22, fill, 0, unroll=True)
 
     def gradient(i):
         c = m[i]
@@ -253,7 +265,7 @@
         n_x[i], n_y[i], n_z[i] = gx * inverse, gy * inverse, gz * inverse
         return carry
 
-    lax.fori_loop(0, 20, normals, 0)
+    lax.fori_loop(0, 20, normals, 0, unroll=True)
     mask_y = row_mask(shape, y0 - 8, ny)
 
     def stars(i, carry):
@@ -272,11 +284,11 @@
         bending = bending * keep
         fx, fy, fz = bending * gx, bending * gy, bending * gz
         k = jnp.clip(i - 1, 0, 15)
-        vx = jnp.where(i == 0, xl[0], jnp.where(i == 17, xh[0], velocity[0, k]))
+        vx = jnp.where(i == 0, xl[3], jnp.where(i == 17, xh[3], velocity[0, k]))
         s_x[i] = fx[8:24, :] + vx
-        pad[7:8, :] = vyl[k]
+        pad[7:8, :] = vyl[k, 3:4, :]
         pad[8:24, :] = velocity[1, k]
-        pad[24:25, :] = vyh[k]
+        pad[24:25, :] = vyh[k, 3:4, :]
         sy = fy + pad[...]
         dy = roll(sy, -1, 0) - roll(sy, 1, 0)
         sz = fz[8:24, :] + velocity[2, k]
@@ -285,30 +297,31 @@
         return carry
 
     pad[...] = jnp.zeros_like(pad)
-    lax.fori_loop(0, 18, stars, 0)
+    lax.fori_loop(0, 18, stars, 0, unroll=True)
 
     def finish(i, carry):
         source[i] = -0.5 * (part[i + 1] + (s_x[i + 2] - s_x[i]))
         return carry
 
-    lax.fori_loop(0, 16, finish, 0)
+    lax.fori_loop(0, 16, finish, 0, unroll=True)
+    send(source, wider, low, high, HALO)
 
 
 def force(nx, ny, at, mid, yl, yh, velocity, xl, xh, vyl, vyh):
     n = (20, 32, 256)
-    scratch = [(22, 32, 256), n, n, n, (18, 16, 256), (18, 16, 256), (32, 256)]
+    scratch = [(22, 32, 256), n, n, n, (18, 16, 256), (18, 16, 256), (32, 256), (16, 16, 256)]
     args = [at, mid, yl, yh, velocity, xl, xh, vyl, vyh]
-    return call(functools.partial(force_body, nx, ny), [(16, 16, 256)], scratch, args, 10000000)[0]
+    return call(functools.partial(force_body, nx, ny), send_shapes(HALO), scratch, args, 10000000)
 
 
 def assemble(ext, mid, yl, yh, planes):
     def fill(i, carry):
-        ext[i, 0:12, :] = yl[i]
+        ext[i, 0:12, :] = yl[i, 4:16, :]
         ext[i, 12:28, :] = mid[i]
-        ext[i, 28:40, :] = yh[i]
-        return carry
-
-    lax.fori_loop(0, planes, fill, 0)
+        ext[i, 28:40, :] = yh[i, 0:12, :]
+        return carry
+
+    lax.fori_loop(0, planes, fill, 0, unroll=True)
 
 
 def descend(nx, ny, at, b, v, v_out, b1_out, u_out, b2_out, wide_rows, t, s1, t1):
@@ -318,7 +331,7 @@
         v_out[i] = v[i + 7]
         return carry
 
-    lax.fori_loop(0, 20, keep_v, 0)
+    lax.fori_loop(0, 20, keep_v, 0, unroll=True)
 
     def residual(i):
         c, around = beside(v, i)
@@ -333,7 +346,7 @@
             t[i, 0:20, 128 * half : 128 * half + 128] = even + odd
         return carry
 
-    lax.fori_loop(0, 16, pairs, 0)
+    lax.fori_loop(0, 16, pairs, 0, unroll=True)
     full = dot(t[...].reshape(16 * 24, 256), pair_matrix(256, 128, 0.125)).reshape(16, 24, 128)
     rows = iota((24, 128), 0)
     good = jnp.logical_and(inside(rows + (y1 - 6), ny // 2), rows < 20)
@@ -348,7 +361,7 @@
         u_out[i] = (weight * plane_factor(x1 + i - 3, nx // 2)) * mask * (1.2 * c + SIDE * around)
         return carry
 
-    lax.fori_loop(0, 14, smooth, 0)
+    lax.fori_loop(0, 14, smooth, 0, unroll=True)
     t1[...] = jnp.zeros_like(t1)
     for k in range(4):
         total = 0.0
@@ -358,11 +371,17 @@
         s1[k] = total
         t1[k, 0:4, :] = s1[k, pl.ds(6, 4, stride=2), :] + s1[k, pl.ds(7, 4, stride=2), :]
     small = dot(t1[...].reshape(32, 128), pair_matrix(128, 128, 0.125)).reshape(4, 8, 128)
-    for k in range(4):
-        b2_out[k] = small[k, 0:4, 0:64]
-
-
-DOWN_OUTS = [(20, 40, 256), (16, 24, 128), (14, 24, 128), (4, 4, 64)]
+    tile = jnp.concatenate([small[0, 0:4], small[1, 0:4]], axis=0) + roll(
+        jnp.concatenate([small[2, 0:4], small[3, 0:4]], axis=0), 64, 1
+    )
+    for k in range(b2_out.shape[0]):
+        b2_out[k] = tile
+
+
+def down_outs(ny):
+    return [(20, 40, 256), (16, 24, 128), (14, 24, 128), (GROUP * ny // 16, 8, 128)]
+
+
 DOWN_SCRATCH = [(34, 40, 256), (2, 40, 128), (16, 24, 256), (4, 24, 128), (4, 8, 128)]
 
 
@@ -376,14 +395,14 @@
         v[i] = SIDE * keep * (1.2 * c + SIDE * around)
         return carry
 
-    lax.fori_loop(0, 34, smooth, 0)
+    lax.fori_loop(0, 34, smooth, 0, unroll=True)
     descend(nx, ny, at, b, v, v_out, b1_out, u_out, b2_out, *scratch)
 
 
 def first_down(nx, ny, at, mid, yl, yh):
     return call(
         functools.partial(first_down_body, nx, ny),
-        [(36, 40, 256)] + DOWN_OUTS,
+        [(36, 40, 256)] + down_outs(ny),
         DOWN_SCRATCH,
         [at, mid, yl, yh],
         20000000,
@@ -403,38 +422,45 @@
 
         return plane
 
-    lax.fori_loop(0, 36, sweep(start, once, -10, 0), 0)
-    lax.fori_loop(0, 34, sweep(once, v, -9, 1), 0)
+    lax.fori_loop(0, 36, sweep(start, once, -10, 0), 0, unroll=True)
+    lax.fori_loop(0, 34, sweep(once, v, -9, 1), 0, unroll=True)
     descend(nx, ny, at, b, v, v_out, b1_out, u_out, b2_out, wide_rows, t, s1, t1)
 
 
 def next_down(nx, ny, at, mid, yl, yh, b):
     return call(
         functools.partial(next_down_body, nx, ny),
-        DOWN_OUTS,
+        down_outs(ny),
         DOWN_SCRATCH + [(38, 40, 256), (36, 40, 256)],
         [at, mid, yl, yh, b],
         30000000,
     )
 
 
-def up_body(nx, ny, at, b2_all, b1, u, b, v_down, out, s2, v2, w2, t3, b3, c3, d3, dup, row2, m1, n1, m0, n0):
+def up_body(nx, ny, last, at, b2_all, before, after, b1, u, b, v_down, *refs):
+    if last:
+        out, *refs = refs
+    else:
+        wider, low, high, *refs = refs
+        out = refs.pop()
+    s2, v2, w2, t3, b3, c3, d3, dup, row2, m1, n1, m0, n0 = refs
     wide, narrow = at[0], at[1]
     spot = wide % GROUP
     rows2 = s2.shape[1]
     rows3 = rows2 // 2
     count = rows2 // 4
-    s2[...] = jnp.zeros_like(s2)
-
-    def gather(j, carry):
+    lower = iota((8, 128), 1) < 64
+    for j in range(7):
         block = spot + 1 + j
         layer, place = block // GROUP, block % GROUP
         for n in range(count):
-            for k in range(4):
-                s2[4 * j + k, 4 * n : 4 * n + 4, 0:64] = b2_all[place * count + n, layer, k]
-        return carry
-
-    lax.fori_loop(0, 7, gather, 0)
+            k = place * count + n
+            tile = jnp.where(layer == 0, before[k], jnp.where(layer == 1, b2_all[k], after[k]))
+            first = jnp.where(lower, tile, 0.0)
+            second = jnp.where(lower, roll(tile, 64, 1), 0.0)
+            for p in range(4):
+                part = (first, second)[p // 2]
+                s2[4 * j + p, 4 * n : 4 * n + 4, :] = part[4 * (p % 2) : 4 * (p % 2) + 4, :]
 
     def walled(c, rows, lanes):
         row, lane = iota(c.shape, 0), iota(c.shape, 1)
@@ -458,7 +484,7 @@
         v2[i] = (weight2 * plane_factor(x2 + i - 12, nx // 4)) * mask2 * (1.2 * c + SIDE * near)
         return carry
 
-    lax.fori_loop(1, 27, smooth2, 0)
+    lax.fori_loop(1, 27, smooth2, 0, unroll=True)
 
     def residual2(i):
         c, near = around(v2, i, rows2, 64)
@@ -469,7 +495,7 @@
         t3[i] = row2[pl.ds(0, rows3, stride=2), :] + row2[pl.ds(1, rows3, stride=2), :]
         return carry
 
-    lax.fori_loop(0, 12, pairs2, 0)
+    lax.fori_loop(0, 12, pairs2, 0, unroll=True)
     full = dot(t3[...].reshape(12 * rows3, 128), pair_matrix(128, 128, 0.125)).reshape(12, rows3, 128)
     x3 = wide * 2
     mask3 = lanes_below(rows3, 32)
@@ -487,9 +513,9 @@
 
         return plane
 
-    lax.fori_loop(1, 11, sweep3(c3, d3), 0)
-    lax.fori_loop(2, 10, sweep3(d3, c3), 0)
-    lax.fori_loop(3, 9, sweep3(c3, d3), 0)
+    lax.fori_loop(1, 11, sweep3(c3, d3), 0, unroll=True)
+    lax.fori_loop(2, 10, sweep3(d3, c3), 0, unroll=True)
+    lax.fori_loop(3, 9, sweep3(c3, d3), 0, unroll=True)
     spread = dot(d3[3:9].reshape(6 * rows3, 128), copy_matrix(128, 128)).reshape(6, rows3, 128)
     for i in range(6):
         dup[pl.ds(0, rows3, stride=2), :] = spread[i]
@@ -506,8 +532,8 @@
 
         return plane
 
-    lax.fori_loop(9, 19, sweep2(v2, w2), 0)
-    lax.fori_loop(10, 18, sweep2(w2, v2), 0)
+    lax.fori_loop(9, 19, sweep2(v2, w2), 0, unroll=True)
+    lax.fori_loop(10, 18, sweep2(w2, v2), 0, unroll=True)
     turn = lax.rem(rows2 + 3 - 4 * narrow + rows2, rows2)
     picked = [pltpu.roll(v2[10 + i], turn, 0)[0:16, :] for i in range(8)]
     spread = dot(jnp.concatenate(picked, axis=0), copy_matrix(128, 128)).reshape(8, 16, 128)
@@ -529,8 +555,8 @@
 
         return plane
 
-    lax.fori_loop(1, 13, sweep1(m1, n1), 0)
-    lax.fori_loop(2, 12, sweep1(n1, m1), 0)
+    lax.fori_loop(1, 13, sweep1(m1, n1), 0, unroll=True)
+    lax.fori_loop(2, 12, sweep1(n1, m1), 0, unroll=True)
     spread = dot(m1[2:12].reshape(10 * 24, 128), copy_matrix(128, 256)).reshape(10, 24, 256)
     x0, y0 = wide * 16, narrow * 16
     mask0 = row_mask((40, 256), y0 - ROWS, ny)
@@ -546,7 +572,7 @@
         m0[i] = (v_down[i] + n0[i]) * mask0 * plane_factor(x0 + i - 2, nx)
         return carry
 
-    lax.fori_loop(0, 20, add0, 0)
+    lax.fori_loop(0, 20, add0, 0, unroll=True)
 
     def sweep0(i, carry):
         c, near = beside(m0, i)
@@ -554,7 +580,7 @@
         n0[i] = keep * (0.2 * c + SIDE * (near + b[i + 8]))
         return carry
 
-    lax.fori_loop(1, 19, sweep0, 0)
+    lax.fori_loop(1, 19, sweep0, 0, unroll=True)
 
     def last0(i, carry):
         c, near = beside(n0, i + 2)
@@ -562,25 +588,28 @@
         out[i] = value[12:28, :]
         return carry
 
-    lax.fori_loop(0, 16, last0, 0)
-
-
-def up(nx, ny, at, b2_all, b1, u, b, v_down):
+    lax.fori_loop(0, 16, last0, 0, unroll=True)
+    if not last:
+        send(out, wider, low, high, HALO + 1)
+
+
+def up(nx, ny, last, at, coarse, b1, u, b, v_down):
     rows2 = ny // 4
     rows3 = rows2 // 2
     wide_part = (28, rows2, 128)
     small = (12, rows3, 128)
+    block = (16, 16, 256)
     scratch = [
         wide_part, wide_part, wide_part, small, small, small, small,
         (48, 128), (rows2, 128), (14, 24, 128), (14, 24, 128), (20, 40, 256), (20, 40, 256),
     ]
     return call(
-        functools.partial(up_body, nx, ny),
-        [(16, 16, 256)],
-        scratch,
-        [at, b2_all, b1, u, b, v_down],
+        functools.partial(up_body, nx, ny, last),
+        [block] if last else send_shapes(HALO + 1),
+        scratch if last else scratch + [block],
+        [at, *coarse, b1, u, b, v_down],
         20000000,
-    )[0]
+    )
 
 
 def shifted(array, axis, step):
@@ -590,24 +619,22 @@
     )
 
 
-def surround(array, planes, rows):
-    low = shifted(array[16 - planes :], "wide", 1)
-    high = shifted(array[:planes], "wide", -1)
-    mid = jnp.concatenate([low, array, high], axis=0)
-    y_low = shifted(mid[:, 16 - rows :, :], "narrow", 1)
-    y_high = shifted(mid[:, :rows, :], "narrow", -1)
-    return mid, y_low, y_high
+def widen(wider, low, high):
+    planes = low.shape[0]
+    wider = lax.dynamic_update_slice(wider, shifted(high, "wide", 1), (0, 0, 0))
+    return lax.dynamic_update_slice(wider, shifted(low, "wide", -1), (16 + planes, 0, 0))
+
+
+def surround(wider, low, high):
+    mid = widen(wider, low, high)
+    return mid, shifted(mid, "narrow", 1), shifted(mid, "narrow", -1)
 
 
 def spread_coarse(b2):
-    wide, narrow = lax.axis_size("wide"), lax.axis_size("narrow")
-    before = shifted(b2, "wide", GROUP)
-    after = shifted(b2, "wide", -GROUP)
-    three = jnp.stack([before, b2, after])
-    size = GROUP * narrow
-    pieces = jnp.broadcast_to(three[None], (size,) + three.shape)
+    wide, size = lax.axis_size("wide"), b2.shape[0]
     groups = [[g * size + k for k in range(size)] for g in range(wide // GROUP)]
-    return lax.all_to_all(pieces, ("wide", "narrow"), 0, 0, axis_index_groups=groups)
+    here = lax.all_to_all(b2, ("wide", "narrow"), 0, 0, axis_index_groups=groups)
+    return here, shifted(here, "wide", GROUP), shifted(here, "wide", -GROUP)
 
 
 def on_device(phase, distance, velocity):
@@ -618,15 +645,15 @@
     xh = shifted(x_low, "wide", -1)
     yl = shifted(y_high, "narrow", 1)
     yh = shifted(y_low, "narrow", -1)
-    moved = transport(psi, velocity, xl, xh, yl, yh)
-    mid, m_low, m_high = surround(moved, 3, 3)
-    source = force(
-        nx, ny, at, mid, m_low, m_high, velocity, xl[3:], xh[3:], yl[:, 3:, :], yh[:, 3:, :]
-    )
-    b, v, b1, u, b2 = first_down(nx, ny, at, *surround(source, HALO, ROWS))
-    pressure = up(nx, ny, at, spread_coarse(b2), b1, u, b, v)
-    v, b1, u, b2 = next_down(nx, ny, at, *surround(pressure, HALO + 1, ROWS), b)
-    pressure = up(nx, ny, at, spread_coarse(b2), b1, u, b, v)
+    moved, *sends = transport(psi, velocity, xl, xh, yl, yh)
+    mid = widen(*sends)
+    m_low = shifted(mid[:, 13:, :], "narrow", 1)
+    m_high = shifted(mid[:, :3, :], "narrow", -1)
+    sends = force(nx, ny, at, mid, m_low, m_high, velocity, xl, xh, yl, yh)
+    b, v, b1, u, b2 = first_down(nx, ny, at, *surround(*sends))
+    sends = up(nx, ny, False, at, spread_coarse(b2), b1, u, b, v)
+    v, b1, u, b2 = next_down(nx, ny, at, *surround(*sends), b)
+    (pressure,) = up(nx, ny, True, at, spread_coarse(b2), b1, u, b, v)
     return (moved, pressure)
 
 

time: 244 us -> 188 us (0.77)
  the two profiles are of different devices: /device:TPU:257 before, /device:TPU:128 now
where the time goes in v2:
time: 188 us; the launch traced here: 187 us
  starting transfers between devices  72.2 us (38%)
  blocking collectives  40.9 us (22%)
  Pallas kernels  35.4 us (19%)
  waiting for transfers between devices  27.6 us (15%)
  local copies, waits for them, and re-layouts  9.68 us (5%)
    ppermute x20, starting transfers between devices, shifted(): lax.ppermute(array, axis, [(i, i + step) for i in range(count) if 0 <= i...  72.2 us
    all_to_all x2, blocking collectives, spread_coarse(): lax.all_to_all(b2, ('wide', 'narrow'), 0, 0, axis_index_groups=groups)  40.9 us
    pallas_call x7, Pallas kernels, call(): pl.pallas_call(body, out_shape=[jax.ShapeDtypeStruct(s, F32) for s in out...  35.4 us
    ppermute x20, waiting for transfers between devices, shifted(): lax.ppermute(array, axis, [(i, i + step) for i in range(count) if 0 <= i...  27.6 us
    unnamed x32, local copies, waits for them, and re-layouts  4.62 us
  transfers between devices with their start and end apart: 20, of which 14 were waited for; matrix products, arithmetic and copies ran while one was open for 1% of the time, Pallas kernels for 0%

profile of v2, /device:TPU:128, one launch (start us, length us, event | category | flops | bytes accessed | tf_op | source)
XLA Modules:
  0.0 187.3 jit_solution(8915779343391994664)
XLA Ops:
  0.6 2.1 %shard_map.50 = (f32[16,16,256]{2,1,0:T(8,128)}, f32[4,16,256]{2,1,0:T(8,128)}, f32[4,16,256]{2,1,0:T(8,128)}, f32[16,4,256]{2,1,0:T(4,128)}, f32[16,4,256]{2,1,0:T(4,128)}) custom-call(s32[16,16,256]{2,1,0:T(8,128)} %phase.1, f32[16,16,256]{2,1,0:T(8,128)} %distance.1, f32[3,16,16,256]{3,2,1,0:T(8,128)} %velocity.5), custom_call_target="tpu_custom_call" | custom-call | flops 1000000 | bytes 4000000 | tf_op jit(solution)/shard_map/pallas_call | solution.py:82
  2.8 3.4 %collective-permute-start = (f32[4,16,256]{2,1,0:T(8,128)}, f32[4,16,256]{2,1,0:T(8,128)S(1)}, u32[]{:S(2)}, u32[]{:S(2)}) collective-permute-start(f32[4,16,256]{2,1,0:T(8,128)} %get-tuple-element.27), channel_id=1, source_target_pairs={{0,8},{8,16},{16,24},{24,32},{32,40},{40,48},{48,56},{56,64},{64,7... | collective-permute-start | bytes 196616 | tf_op jit(solution)/shard_map/ppermute | solution.py:617
  6.2 5.8 %collective-permute-start.1 = (f32[4,16,256]{2,1,0:T(8,128)}, f32[4,16,256]{2,1,0:T(8,128)S(1)}, u32[]{:S(2)}, u32[]{:S(2)}) collective-permute-start(f32[4,16,256]{2,1,0:T(8,128)} %get-tuple-element.28), channel_id=1, source_target_pairs={{8,0},{16,8},{24,16},{32,24},{40,32},{48,40},{56,48},{64,56},{72,6... | collective-permute-start | bytes 196616 | tf_op jit(solution)/shard_map/ppermute | solution.py:617
  11.9 1.3 collective-permute-start.2
  13.2 1.3 collective-permute-start.3
  14.6 3.8 %collective-permute-done.3.yh.vyh = f32[16,4,256]{2,1,0:T(4,128)S(1)} collective-permute-done((f32[16,4,256]{2,1,0:T(4,128)}, f32[16,4,256]{2,1,0:T(4,128)S(1)}, u32[]{:S(2)}, u32[]{:S(2)}) %collective-permute-start.3) | collective-permute-done | bytes 65568 | tf_op jit(solution)/shard_map/ppermute | solution.py:617
  19.0 5.5 %shard_map.51 = (f32[16,16,256]{2,1,0:T(8,128)}, f32[22,16,256]{2,1,0:T(8,128)}, f32[3,16,256]{2,1,0:T(8,128)}, f32[3,16,256]{2,1,0:T(8,128)}) custom-call(f32[16,16,256]{2,1,0:T(8,128)} %get-tuple-element.26.psi, f32[3,16,16,256]{3,2,1,0:T(8,128)} %velocity.5, f32[4,16,256]{2,1,0:T(8,128)} %copy-done.6, f32[4,16,256]{2,1,0:T(8,128)} %copy-done.7, ...), custom_call_target="tpu_custom_call" | custom-call | flops 10000000 | bytes 4000000 | tf_op jit(solution)/shard_map/pallas_call | solution.py:82
  24.5 1.9 %collective-permute-start.4 = (f32[3,16,256]{2,1,0:T(8,128)}, f32[3,16,256]{2,1,0:T(8,128)S(1)}, u32[]{:S(2)}, u32[]{:S(2)}) collective-permute-start(f32[3,16,256]{2,1,0:T(8,128)} %get-tuple-element.33), channel_id=1, source_target_pairs={{0,8},{8,16},{16,24},{24,32},{32,40},{40,48},{48,56},{56,64},{64,7... | collective-permute-start | bytes 147464 | tf_op jit(solution)/shard_map/ppermute | solution.py:617
  26.5 7.2 %collective-permute-start.5 = (f32[3,16,256]{2,1,0:T(8,128)}, f32[3,16,256]{2,1,0:T(8,128)S(1)}, u32[]{:S(2)}, u32[]{:S(2)}) collective-permute-start(f32[3,16,256]{2,1,0:T(8,128)} %get-tuple-element.34), channel_id=1, source_target_pairs={{8,0},{16,8},{24,16},{32,24},{40,32},{48,40},{56,48},{64,56},{72,6... | collective-permute-start | bytes 147464 | tf_op jit(solution)/shard_map/ppermute | solution.py:617
  34.7 1.1 collective-permute-done.5
  36.4 1.0 fusion
  37.4 1.3 collective-permute-start.7
  38.7 4.3 %collective-permute-start.6 = (f32[22,3,256]{2,1,0:T(4,128)S(1)}, f32[22,3,256]{2,1,0:T(4,128)S(1)}, u32[]{:S(2)}, u32[]{:S(2)}) collective-permute-start(f32[22,3,256]{2,1,0:T(4,128)S(1)} %get-tuple-element.51), channel_id=1, source_target_pairs={{0,1},{1,2},{2,3},{3,4},{4,5},{5,6},{6,7},{8,9},{9,10},{10,11},{11... | collective-permute-start | bytes 202760 | tf_op jit(solution)/shard_map/ppermute | solution.py:617
  45.0 4.4 %shard_map.52 = (f32[36,16,256]{2,1,0:T(8,128)}, f32[10,16,256]{2,1,0:T(8,128)}, f32[10,16,256]{2,1,0:T(8,128)}) custom-call(s32[2]{0:T(128)} %pad_add_fusion.at, f32[22,16,256]{2,1,0:T(8,128)} %constant_dynamic-update-slice_fusion.4.mid, f32[22,3,256]{2,1,0:T(4,128)} %copy-done.15, f32[22,3,256]{2,1,0:T(4,128)} %copy-done.14, f32[3,16,16,256]{3,2,1,0:T(8,128)} %velocity.5, ...), custom_call_target="tpu_custom_call" | custom-call | flops 10000000 | bytes 4000000 | tf_op jit(solution)/shard_map/pallas_call | solution.py:82
  49.3 1.9 %collective-permute-start.8 = (f32[10,16,256]{2,1,0:T(8,128)}, f32[10,16,256]{2,1,0:T(8,128)S(1)}, u32[]{:S(2)}, u32[]{:S(2)}) collective-permute-start(f32[10,16,256]{2,1,0:T(8,128)} %get-tuple-element.36), channel_id=1, source_target_pairs={{0,8},{8,16},{16,24},{24,32},{32,40},{40,48},{48,56},{56,64},{64,7... | collective-permute-start | bytes 491528 | tf_op jit(solution)/shard_map/ppermute | solution.py:617
  51.2 7.2 %collective-permute-start.9 = (f32[10,16,256]{2,1,0:T(8,128)}, f32[10,16,256]{2,1,0:T(8,128)S(1)}, u32[]{:S(2)}, u32[]{:S(2)}) collective-permute-start(f32[10,16,256]{2,1,0:T(8,128)} %get-tuple-element.37), channel_id=1, source_target_pairs={{8,0},{16,8},{24,16},{32,24},{40,32},{48,40},{56,48},{64,56},{72,6... | collective-permute-start | bytes 491528 | tf_op jit(solution)/shard_map/ppermute | solution.py:617
  58.5 2.0 %collective-permute-done.8 = f32[10,16,256]{2,1,0:T(8,128)S(1)} collective-permute-done((f32[10,16,256]{2,1,0:T(8,128)}, f32[10,16,256]{2,1,0:T(8,128)S(1)}, u32[]{:S(2)}, u32[]{:S(2)}) %collective-permute-start.8) | collective-permute-done | bytes 163872 | tf_op jit(solution)/shard_map/ppermute | solution.py:617
  60.5 0.7 constant_dynamic-update-slice_fusion.3
  61.2 1.2 collective-permute-done.9
  62.4 0.7 constant_dynamic-update-slice_fusion.2.mid
  63.1 1.3 collective-permute-start.11
  64.4 3.7 %collective-permute-start.10 = (f32[36,16,256]{2,1,0:T(8,128)}, f32[36,16,256]{2,1,0:T(8,128)S(1)}, u32[]{:S(2)}, u32[]{:S(2)}) collective-permute-start(f32[36,16,256]{2,1,0:T(8,128)} %constant_dynamic-update-slice_fusion.2.mid), channel_id=1, source_target_pairs={{0,1},{1,2},{2,3},{3,4},{4,5},{5,6},{6,7},{8,9},{9,10},{10,11},{11... | collective-permute-start | bytes 1769480 | tf_op jit(solution)/shard_map/ppermute | solution.py:617
  68.1 1.8 collective-permute-done.10.yl
  69.8 0.8 copy-done.3
  70.7 5.4 %shard_map.53 = (f32[36,40,256]{2,1,0:T(8,128)}, f32[20,40,256]{2,1,0:T(8,128)}, f32[16,24,128]{2,1,0:T(8,128)}, f32[14,24,128]{2,1,0:T(8,128)}, f32[32,8,128]{2,1,0:T(8,128)}) custom-call(s32[2]{0:T(128)} %pad_add_fusion.at, f32[36,16,256]{2,1,0:T(8,128)} %constant_dynamic-update-slice_fusion.2.mid, f32[36,16,256]{2,1,0:T(8,128)} %copy-done.3, ...), custom_call_target="tpu_custom_call" | custom-call | flops 20000000 | bytes 4000000 | tf_op jit(solution)/shard_map/pallas_call | solution.py:82
  76.1 22.4 %all_to_all.10.b2_all = f32[32,8,128]{2,1,0:T(8,128)S(1)} all-to-all(f32[32,8,128]{2,1,0:T(8,128)} %get-tuple-element.38), channel_id=1, replica_groups={{0,1,2,3,4,5,6,7,8,9,10,11,12,13,14,15,16,17,18,19,20,21,22,23,24,25,26..., dimensions={0} | all-to-all | bytes 262144 | tf_op jit(solution)/shard_map/all_to_all | solution.py:636
  98.5 6.8 %collective-permute-start.13 = (f32[32,8,128]{2,1,0:T(8,128)S(1)}, f32[32,8,128]{2,1,0:T(8,128)S(1)}, u32[]{:S(2)}, u32[]{:S(2)}) collective-permute-start(f32[32,8,128]{2,1,0:T(8,128)S(1)} %all_to_all.10.b2_all), channel_id=1, source_target_pairs={{32,0},{40,8},{48,16},{56,24},{64,32},{72,40},{80,48},{88,56},{96,... | collective-permute-start | bytes 393224 | tf_op jit(solution)/shard_map/ppermute | solution.py:617
  105.3 2.1 %collective-permute-start.12 = (f32[32,8,128]{2,1,0:T(8,128)S(1)}, f32[32,8,128]{2,1,0:T(8,128)S(1)}, u32[]{:S(2)}, u32[]{:S(2)}) collective-permute-start(f32[32,8,128]{2,1,0:T(8,128)S(1)} %all_to_all.10.b2_all), channel_id=1, source_target_pairs={{0,32},{8,40},{16,48},{24,56},{32,64},{40,72},{48,80},{56,88},{64,... | collective-permute-start | bytes 393224 | tf_op jit(solution)/shard_map/ppermute | solution.py:617
  107.4 0.9 collective-permute-done.13.after
  108.3 5.3 %collective-permute-done.12.before = f32[32,8,128]{2,1,0:T(8,128)S(1)} collective-permute-done((f32[32,8,128]{2,1,0:T(8,128)S(1)}, f32[32,8,128]{2,1,0:T(8,128)S(1)}, u32[]{:S(2)}, u32[]{:S(2)}) %collective-permute-start.12) | collective-permute-done | bytes 131104 | tf_op jit(solution)/shard_map/ppermute | solution.py:617
  114.3 5.9 %shard_map.54 = (f32[38,16,256]{2,1,0:T(8,128)}, f32[11,16,256]{2,1,0:T(8,128)}, f32[11,16,256]{2,1,0:T(8,128)}) custom-call(s32[2]{0:T(128)} %pad_add_fusion.at, f32[32,8,128]{2,1,0:T(8,128)} %copy-done.4, f32[32,8,128]{2,1,0:T(8,128)} %copy-done.12, f32[32,8,128]{2,1,0:T(8,128)} %copy-done.10, f32[16,24,128]{2,1,0:T(8,128)} %get-tuple-element.39.b1, ...), custom_call_target="tpu_custom_call" | custom-call | flops 20000000 | bytes 4000000 | tf_op jit(solution)/shard_map/pallas_call | solution.py:82
  120.2 2.5 %collective-permute-start.14 = (f32[11,16,256]{2,1,0:T(8,128)}, f32[11,16,256]{2,1,0:T(8,128)S(1)}, u32[]{:S(2)}, u32[]{:S(2)}) collective-permute-start(f32[11,16,256]{2,1,0:T(8,128)} %get-tuple-element.44), channel_id=1, source_target_pairs={{0,8},{8,16},{16,24},{24,32},{32,40},{40,48},{48,56},{56,64},{64,7... | collective-permute-start | bytes 540680 | tf_op jit(solution)/shard_map/ppermute | solution.py:617
  122.7 6.7 %collective-permute-start.15 = (f32[11,16,256]{2,1,0:T(8,128)}, f32[11,16,256]{2,1,0:T(8,128)S(1)}, u32[]{:S(2)}, u32[]{:S(2)}) collective-permute-start(f32[11,16,256]{2,1,0:T(8,128)} %get-tuple-element.45), channel_id=1, source_target_pairs={{8,0},{16,8},{24,16},{32,24},{40,32},{48,40},{56,48},{64,56},{72,6... | collective-permute-start | bytes 540680 | tf_op jit(solution)/shard_map/ppermute | solution.py:617
  129.3 1.7 collective-permute-done.14
  131.1 0.7 constant_dynamic-update-slice_fusion.1
  131.8 0.9 collective-permute-done.15
  132.6 0.7 constant_dynamic-update-slice_fusion.mid
  133.3 1.3 collective-permute-start.17
  134.6 3.1 %collective-permute-start.16 = (f32[38,16,256]{2,1,0:T(8,128)}, f32[38,16,256]{2,1,0:T(8,128)S(1)}, u32[]{:S(2)}, u32[]{:S(2)}) collective-permute-start(f32[38,16,256]{2,1,0:T(8,128)} %constant_dynamic-update-slice_fusion.mid), channel_id=1, source_target_pairs={{0,1},{1,2},{2,3},{3,4},{4,5},{5,6},{6,7},{8,9},{9,10},{10,11},{11... | collective-permute-start | bytes 1867784 | tf_op jit(solution)/shard_map/ppermute | solution.py:617
  137.7 1.8 collective-permute-done.16.yl
  139.5 0.8 copy-done.1
  140.4 6.4 %shard_map.55 = (f32[20,40,256]{2,1,0:T(8,128)}, f32[16,24,128]{2,1,0:T(8,128)}, f32[14,24,128]{2,1,0:T(8,128)}, f32[32,8,128]{2,1,0:T(8,128)}) custom-call(s32[2]{0:T(128)} %pad_add_fusion.at, f32[38,16,256]{2,1,0:T(8,128)} %constant_dynamic-update-slice_fusion.mid, f32[38,16,256]{2,1,0:T(8,128)} %copy-done.1, f32[38,16,256]{2,1,0:T(8,128)} %copy-done, ...), custom_call_target="tpu_custom_call" | custom-call | flops 30000000 | bytes 4000000 | tf_op jit(solution)/shard_map/pallas_call | solution.py:82
  146.8 18.5 %all_to_all.11.b2_all = f32[32,8,128]{2,1,0:T(8,128)S(1)} all-to-all(f32[32,8,128]{2,1,0:T(8,128)} %get-tuple-element.46), channel_id=1, replica_groups={{0,1,2,3,4,5,6,7,8,9,10,11,12,13,14,15,16,17,18,19,20,21,22,23,24,25,26..., dimensions={0} | all-to-all | bytes 262144 | tf_op jit(solution)/shard_map/all_to_all | solution.py:636
  165.3 7.3 %collective-permute-start.19 = (f32[32,8,128]{2,1,0:T(8,128)S(1)}, f32[32,8,128]{2,1,0:T(8,128)S(1)}, u32[]{:S(2)}, u32[]{:S(2)}) collective-permute-start(f32[32,8,128]{2,1,0:T(8,128)S(1)} %all_to_all.11.b2_all), channel_id=1, source_target_pairs={{32,0},{40,8},{48,16},{56,24},{64,32},{72,40},{80,48},{88,56},{96,... | collective-permute-start | bytes 393224 | tf_op jit(solution)/shard_map/ppermute | solution.py:617
  172.6 1.9 %collective-permute-start.18 = (f32[32,8,128]{2,1,0:T(8,128)S(1)}, f32[32,8,128]{2,1,0:T(8,128)S(1)}, u32[]{:S(2)}, u32[]{:S(2)}) collective-permute-start(f32[32,8,128]{2,1,0:T(8,128)S(1)} %all_to_all.11.b2_all), channel_id=1, source_target_pairs={{0,32},{8,40},{16,48},{24,56},{32,64},{40,72},{48,80},{56,88},{64,... | collective-permute-start | bytes 393224 | tf_op jit(solution)/shard_map/ppermute | solution.py:617
  174.5 1.1 collective-permute-done.19.after
  175.6 5.3 %collective-permute-done.18.before = f32[32,8,128]{2,1,0:T(8,128)S(1)} collective-permute-done((f32[32,8,128]{2,1,0:T(8,128)S(1)}, f32[32,8,128]{2,1,0:T(8,128)S(1)}, u32[]{:S(2)}, u32[]{:S(2)}) %collective-permute-start.18) | collective-permute-done | bytes 131104 | tf_op jit(solution)/shard_map/ppermute | solution.py:617
  181.6 5.7 %shard_map.56 = f32[16,16,256]{2,1,0:T(8,128)} custom-call(s32[2]{0:T(128)} %pad_add_fusion.at, f32[32,8,128]{2,1,0:T(8,128)} %copy-done.5, f32[32,8,128]{2,1,0:T(8,128)} %copy-done.13, f32[32,8,128]{2,1,0:T(8,128)} %copy-done.11, f32[16,24,128]{2,1,0:T(8,128)} %get-tuple-element.47.b1, f32[14,24,128]{2,1,0:T(8,128)} %get-tuple-element.48.u, ...), custom_call_target="tpu_custom_call" | custom-call | flops 20000000 | bytes 4000000 | tf_op jit(solution)/shard_map/pallas_call | solution.py:82
  (41 shorter events, 5.5 us)
Async XLA Ops:
  2.8 11.8 %collective-permute-start = (f32[4,16,256]{2,1,0:T(8,128)}, f32[4,16,256]{2,1,0:T(8,128)S(1)}, u32[]{:S(2)}, u32[]{:S(2)}) collective-permute-start(f32[4,16,256]{2,1,0:T(8,128)} %get-tuple-element.27), channel_id=1, source_target_pairs={{0,8},{8,16},{16,24},{24,32},{32,40},{40,48},{48,56},{56,64},{64,7... | collective-permute-start | bytes 196616 | tf_op jit(solution)/shard_map/ppermute | solution.py:617
  6.2 8.4 %collective-permute-start.1 = (f32[4,16,256]{2,1,0:T(8,128)}, f32[4,16,256]{2,1,0:T(8,128)S(1)}, u32[]{:S(2)}, u32[]{:S(2)}) collective-permute-start(f32[4,16,256]{2,1,0:T(8,128)} %get-tuple-element.28), channel_id=1, source_target_pairs={{8,0},{16,8},{24,16},{32,24},{40,32},{48,40},{56,48},{64,56},{72,6... | collective-permute-start | bytes 196616 | tf_op jit(solution)/shard_map/ppermute | solution.py:617
  11.9 2.6 %collective-permute-start.2 = (f32[16,4,256]{2,1,0:T(4,128)}, f32[16,4,256]{2,1,0:T(4,128)S(1)}, u32[]{:S(2)}, u32[]{:S(2)}) collective-permute-start(f32[16,4,256]{2,1,0:T(4,128)} %get-tuple-element.29), channel_id=1, source_target_pairs={{0,1},{1,2},{2,3},{3,4},{4,5},{5,6},{6,7},{8,9},{9,10},{10,11},{11... | collective-permute-start | bytes 196616 | tf_op jit(solution)/shard_map/ppermute | solution.py:617
  13.2 5.2 %collective-permute-start.3 = (f32[16,4,256]{2,1,0:T(4,128)}, f32[16,4,256]{2,1,0:T(4,128)S(1)}, u32[]{:S(2)}, u32[]{:S(2)}) collective-permute-start(f32[16,4,256]{2,1,0:T(4,128)} %get-tuple-element.30), channel_id=1, source_target_pairs={{1,0},{2,1},{3,2},{4,3},{5,4},{6,5},{7,6},{9,8},{10,9},{11,10},{12... | collective-permute-start | bytes 196616 | tf_op jit(solution)/shard_map/ppermute | solution.py:617
  14.5 3.9 %copy-start.6 = (f32[4,16,256]{2,1,0:T(8,128)}, f32[4,16,256]{2,1,0:T(8,128)S(1)}, u32[]{:S(2)}) copy-start(f32[4,16,256]{2,1,0:T(8,128)S(1)} %collective-permute-done.xl) | copy-start | bytes 196612
  14.6 3.8 %copy-start.7 = (f32[4,16,256]{2,1,0:T(8,128)}, f32[4,16,256]{2,1,0:T(8,128)S(1)}, u32[]{:S(2)}) copy-start(f32[4,16,256]{2,1,0:T(8,128)S(1)} %collective-permute-done.1.xh) | copy-start | bytes 196612
  14.6 3.8 %copy-start.8 = (f32[16,4,256]{2,1,0:T(4,128)}, f32[16,4,256]{2,1,0:T(4,128)S(1)}, u32[]{:S(2)}) copy-start(f32[16,4,256]{2,1,0:T(4,128)S(1)} %collective-permute-done.2.yl.vyl) | copy-start | bytes 196612
  18.4 0.6 copy-start.9
  24.5 9.5 %collective-permute-start.4 = (f32[3,16,256]{2,1,0:T(8,128)}, f32[3,16,256]{2,1,0:T(8,128)S(1)}, u32[]{:S(2)}, u32[]{:S(2)}) collective-permute-start(f32[3,16,256]{2,1,0:T(8,128)} %get-tuple-element.33), channel_id=1, source_target_pairs={{0,8},{8,16},{16,24},{24,32},{32,40},{40,48},{48,56},{56,64},{64,7... | collective-permute-start | bytes 147464 | tf_op jit(solution)/shard_map/ppermute | solution.py:617
  26.5 9.3 %collective-permute-start.5 = (f32[3,16,256]{2,1,0:T(8,128)}, f32[3,16,256]{2,1,0:T(8,128)S(1)}, u32[]{:S(2)}, u32[]{:S(2)}) collective-permute-start(f32[3,16,256]{2,1,0:T(8,128)} %get-tuple-element.34), channel_id=1, source_target_pairs={{8,0},{16,8},{24,16},{32,24},{40,32},{48,40},{56,48},{64,56},{72,6... | collective-permute-start | bytes 147464 | tf_op jit(solution)/shard_map/ppermute | solution.py:617
  37.4 6.3 %collective-permute-start.7 = (f32[22,3,256]{2,1,0:T(4,128)S(1)}, f32[22,3,256]{2,1,0:T(4,128)S(1)}, u32[]{:S(2)}, u32[]{:S(2)}) collective-permute-start(f32[22,3,256]{2,1,0:T(4,128)S(1)} %get-tuple-element.50), channel_id=1, source_target_pairs={{1,0},{2,1},{3,2},{4,3},{5,4},{6,5},{7,6},{9,8},{10,9},{11,10},{12... | collective-permute-start | bytes 202760 | tf_op jit(solution)/shard_map/ppermute | solution.py:617
  38.7 5.3 %collective-permute-start.6 = (f32[22,3,256]{2,1,0:T(4,128)S(1)}, f32[22,3,256]{2,1,0:T(4,128)S(1)}, u32[]{:S(2)}, u32[]{:S(2)}) collective-permute-start(f32[22,3,256]{2,1,0:T(4,128)S(1)} %get-tuple-element.51), channel_id=1, source_target_pairs={{0,1},{1,2},{2,3},{3,4},{4,5},{5,6},{6,7},{8,9},{9,10},{10,11},{11... | collective-permute-start | bytes 202760 | tf_op jit(solution)/shard_map/ppermute | solution.py:617
  43.7 0.6 copy-start.14
  44.3 0.7 copy-start.15
  49.3 11.2 %collective-permute-start.8 = (f32[10,16,256]{2,1,0:T(8,128)}, f32[10,16,256]{2,1,0:T(8,128)S(1)}, u32[]{:S(2)}, u32[]{:S(2)}) collective-permute-start(f32[10,16,256]{2,1,0:T(8,128)} %get-tuple-element.36), channel_id=1, source_target_pairs={{0,8},{8,16},{16,24},{24,32},{32,40},{40,48},{48,56},{56,64},{64,7... | collective-permute-start | bytes 491528 | tf_op jit(solution)/shard_map/ppermute | solution.py:617
  51.2 11.2 %collective-permute-start.9 = (f32[10,16,256]{2,1,0:T(8,128)}, f32[10,16,256]{2,1,0:T(8,128)S(1)}, u32[]{:S(2)}, u32[]{:S(2)}) collective-permute-start(f32[10,16,256]{2,1,0:T(8,128)} %get-tuple-element.37), channel_id=1, source_target_pairs={{8,0},{16,8},{24,16},{32,24},{40,32},{48,40},{56,48},{64,56},{72,6... | collective-permute-start | bytes 491528 | tf_op jit(solution)/shard_map/ppermute | solution.py:617
  63.1 4.9 %collective-permute-start.11 = (f32[36,16,256]{2,1,0:T(8,128)}, f32[36,16,256]{2,1,0:T(8,128)S(1)}, u32[]{:S(2)}, u32[]{:S(2)}) collective-permute-start(f32[36,16,256]{2,1,0:T(8,128)} %constant_dynamic-update-slice_fusion.2.mid), channel_id=1, source_target_pairs={{1,0},{2,1},{3,2},{4,3},{5,4},{6,5},{7,6},{9,8},{10,9},{11,10},{12... | collective-permute-start | bytes 1769480 | tf_op jit(solution)/shard_map/ppermute | solution.py:617
  64.4 5.4 %collective-permute-start.10 = (f32[36,16,256]{2,1,0:T(8,128)}, f32[36,16,256]{2,1,0:T(8,128)S(1)}, u32[]{:S(2)}, u32[]{:S(2)}) collective-permute-start(f32[36,16,256]{2,1,0:T(8,128)} %constant_dynamic-update-slice_fusion.2.mid), channel_id=1, source_target_pairs={{0,1},{1,2},{2,3},{3,4},{4,5},{5,6},{6,7},{8,9},{9,10},{10,11},{11... | collective-permute-start | bytes 1769480 | tf_op jit(solution)/shard_map/ppermute | solution.py:617
  68.0 1.8 copy-start.2
  69.8 0.8 copy-start.3
  98.5 15.2 %copy-start.4 = (f32[32,8,128]{2,1,0:T(8,128)}, f32[32,8,128]{2,1,0:T(8,128)S(1)}, u32[]{:S(2)}) copy-start(f32[32,8,128]{2,1,0:T(8,128)S(1)} %all_to_all.10.b2_all) | copy-start | bytes 393220
  98.5 9.9 %collective-permute-start.13 = (f32[32,8,128]{2,1,0:T(8,128)S(1)}, f32[32,8,128]{2,1,0:T(8,128)S(1)}, u32[]{:S(2)}, u32[]{:S(2)}) collective-permute-start(f32[32,8,128]{2,1,0:T(8,128)S(1)} %all_to_all.10.b2_all), channel_id=1, source_target_pairs={{32,0},{40,8},{48,16},{56,24},{64,32},{72,40},{80,48},{88,56},{96,... | collective-permute-start | bytes 393224 | tf_op jit(solution)/shard_map/ppermute | solution.py:617
  105.3 8.3 %collective-permute-start.12 = (f32[32,8,128]{2,1,0:T(8,128)S(1)}, f32[32,8,128]{2,1,0:T(8,128)S(1)}, u32[]{:S(2)}, u32[]{:S(2)}) collective-permute-start(f32[32,8,128]{2,1,0:T(8,128)S(1)} %all_to_all.10.b2_all), channel_id=1, source_target_pairs={{0,32},{8,40},{16,48},{24,56},{32,64},{40,72},{48,80},{56,88},{64,... | collective-permute-start | bytes 393224 | tf_op jit(solution)/shard_map/ppermute | solution.py:617
  108.3 5.3 %copy-start.10 = (f32[32,8,128]{2,1,0:T(8,128)}, f32[32,8,128]{2,1,0:T(8,128)S(1)}, u32[]{:S(2)}) copy-start(f32[32,8,128]{2,1,0:T(8,128)S(1)} %collective-permute-done.13.after) | copy-start | bytes 393220
  113.7 0.7 copy-start.12
  120.2 10.9 %collective-permute-start.14 = (f32[11,16,256]{2,1,0:T(8,128)}, f32[11,16,256]{2,1,0:T(8,128)S(1)}, u32[]{:S(2)}, u32[]{:S(2)}) collective-permute-start(f32[11,16,256]{2,1,0:T(8,128)} %get-tuple-element.44), channel_id=1, source_target_pairs={{0,8},{8,16},{16,24},{24,32},{32,40},{40,48},{48,56},{56,64},{64,7... | collective-permute-start | bytes 540680 | tf_op jit(solution)/shard_map/ppermute | solution.py:617
  122.7 10.0 %collective-permute-start.15 = (f32[11,16,256]{2,1,0:T(8,128)}, f32[11,16,256]{2,1,0:T(8,128)S(1)}, u32[]{:S(2)}, u32[]{:S(2)}) collective-permute-start(f32[11,16,256]{2,1,0:T(8,128)} %get-tuple-element.45), channel_id=1, source_target_pairs={{8,0},{16,8},{24,16},{32,24},{40,32},{48,40},{56,48},{64,56},{72,6... | collective-permute-start | bytes 540680 | tf_op jit(solution)/shard_map/ppermute | solution.py:617
  133.3 4.4 %collective-permute-start.17 = (f32[38,16,256]{2,1,0:T(8,128)}, f32[38,16,256]{2,1,0:T(8,128)S(1)}, u32[]{:S(2)}, u32[]{:S(2)}) collective-permute-start(f32[38,16,256]{2,1,0:T(8,128)} %constant_dynamic-update-slice_fusion.mid), channel_id=1, source_target_pairs={{1,0},{2,1},{3,2},{4,3},{5,4},{6,5},{7,6},{9,8},{10,9},{11,10},{12... | collective-permute-start | bytes 1867784 | tf_op jit(solution)/shard_map/ppermute | solution.py:617
  134.6 4.9 %collective-permute-start.16 = (f32[38,16,256]{2,1,0:T(8,128)}, f32[38,16,256]{2,1,0:T(8,128)S(1)}, u32[]{:S(2)}, u32[]{:S(2)}) collective-permute-start(f32[38,16,256]{2,1,0:T(8,128)} %constant_dynamic-update-slice_fusion.mid), channel_id=1, source_target_pairs={{0,1},{1,2},{2,3},{3,4},{4,5},{5,6},{6,7},{8,9},{9,10},{10,11},{11... | collective-permute-start | bytes 1867784 | tf_op jit(solution)/shard_map/ppermute | solution.py:617
  137.7 1.8 copy-start
  139.5 0.8 copy-start.1
  165.3 15.6 %copy-start.5 = (f32[32,8,128]{2,1,0:T(8,128)}, f32[32,8,128]{2,1,0:T(8,128)S(1)}, u32[]{:S(2)}) copy-start(f32[32,8,128]{2,1,0:T(8,128)S(1)} %all_to_all.11.b2_all) | copy-start | bytes 393220
  165.3 10.3 %collective-permute-start.19 = (f32[32,8,128]{2,1,0:T(8,128)S(1)}, f32[32,8,128]{2,1,0:T(8,128)S(1)}, u32[]{:S(2)}, u32[]{:S(2)}) collective-permute-start(f32[32,8,128]{2,1,0:T(8,128)S(1)} %all_to_all.11.b2_all), channel_id=1, source_target_pairs={{32,0},{40,8},{48,16},{56,24},{64,32},{72,40},{80,48},{88,56},{96,... | collective-permute-start | bytes 393224 | tf_op jit(solution)/shard_map/ppermute | solution.py:617
  172.6 8.3 %collective-permute-start.18 = (f32[32,8,128]{2,1,0:T(8,128)S(1)}, f32[32,8,128]{2,1,0:T(8,128)S(1)}, u32[]{:S(2)}, u32[]{:S(2)}) collective-permute-start(f32[32,8,128]{2,1,0:T(8,128)S(1)} %all_to_all.11.b2_all), channel_id=1, source_target_pairs={{0,32},{8,40},{16,48},{24,56},{32,64},{40,72},{48,80},{56,88},{64,... | collective-permute-start | bytes 393224 | tf_op jit(solution)/shard_map/ppermute | solution.py:617
  175.6 5.3 %copy-start.11 = (f32[32,8,128]{2,1,0:T(8,128)}, f32[32,8,128]{2,1,0:T(8,128)S(1)}, u32[]{:S(2)}) copy-start(f32[32,8,128]{2,1,0:T(8,128)S(1)} %collective-permute-done.19.after) | copy-start | bytes 393220
  180.9 0.7 copy-start.13

commit v3 on v2

v3 whole, which is shorter than its diff:
```python
import functools

import jax
import jax.numpy as jnp
from jax import lax
from jax.experimental import pallas as pl
from jax.experimental.pallas import tpu as pltpu
from jax.sharding import PartitionSpec as P

DELTA_SQ = 0.0025
WENO_EPS = 0.01
SIDE = 0.8 / 6.0
F32 = jnp.float32
HIGHEST = lax.Precision.HIGHEST

HALO = 14
KEEP = 4
NEAR = 4
GROUP = 4


def iota(shape, dim):
    return lax.broadcasted_iota(jnp.int32, shape, dim)


def roll(v, shift, axis):
    return pltpu.roll(v, shift % v.shape[axis], axis)


def z_shifted(v):
    lane = iota(v.shape, 1)
    last = v.shape[1] - 1
    lower = jnp.where(lane == 0, 0.0, roll(v, 1, 1))
    upper = jnp.where(lane == last, 0.0, roll(v, -1, 1))
    return lower, upper


def z_pair(v):
    lower, upper = z_shifted(v)
    return lower + upper


def y_pair(v):
    return roll(v, 1, 0) + roll(v, -1, 0)


def beside(ref, i):
    c = ref[i]
    return c, (ref[i - 1] + ref[i + 1]) + y_pair(c) + z_pair(c)


def inside(first, count):
    return jnp.logical_and(first >= 0, first < count)


def row_mask(shape, first, count):
    rows = iota(shape, 0) + first
    return jnp.where(inside(rows, count), 1.0, 0.0).astype(F32)


def plane_factor(index, count):
    return jnp.where(inside(index, count), 1.0, 0.0).astype(F32)


def dot(a, b):
    return lax.dot_general(
        a, b, (((1,), (0,)), ((), ())), precision=HIGHEST, preferred_element_type=F32
    )


def pair_matrix(rows, cols, value):
    return jnp.where((iota((rows, cols), 0) >> 1) == iota((rows, cols), 1), value, 0.0).astype(F32)


def copy_matrix(rows, cols):
    return jnp.where(iota((rows, cols), 0) == (iota((rows, cols), 1) >> 1), 1.0, 0.0).astype(F32)


def words(shape):
    *lead, rows, lanes = (1,) * (3 - len(shape)) + tuple(shape)
    size = -(-rows // 8) * 8 * (-(-lanes // 128) * 128)
    for n in lead:
        size *= n
    return size


def call(body, outs, scratch, args, flops):
    vmem = pl.BlockSpec(memory_space=pltpu.VMEM)
    smem = pl.BlockSpec(memory_space=pltpu.SMEM)
    total = sum(words(a.shape) for a in args) + sum(map(words, outs)) + sum(map(words, scratch))
    return pl.pallas_call(
        body,
        out_shape=[jax.ShapeDtypeStruct(s, F32) for s in outs],
        in_specs=[smem if a.dtype == jnp.int32 and a.ndim == 1 else vmem for a in args],
        out_specs=[vmem] * len(outs),
        scratch_shapes=[pltpu.VMEM(s, F32) for s in scratch],
        compiler_params=pltpu.CompilerParams(vmem_limit_bytes=4 * total + (6 << 20)),
        cost_estimate=pl.CostEstimate(flops=flops, bytes_accessed=4000000, transcendentals=0),
    )(*args)


def pick_sides(at, chip, link):
    odd = lax.rem(at[1], 2) == 1
    lower = lambda *k: jnp.where(odd, chip[k], link[k])
    upper = lambda *k: jnp.where(odd, link[k], chip[k])
    return lower, upper


def send_shapes(planes):
    return [(16 + 2 * planes, 16, 256), (planes, 16, 256), (planes, 16, 256)]


def send(block, wider, low, high, planes):
    for i in range(16):
        wider[planes + i] = block[i]
    for i in range(planes):
        low[i] = block[i]
        high[i] = block[16 - planes + i]


def prepare_body(at, phase, distance, velocity, psi, x_low, x_high, chip, link):
    odd = lax.rem(at[1], 2) == 1

    def plane(i, carry):
        orient = 2.0 * phase[i].astype(F32) - 1.0
        psi[i] = 1.0 / (1.0 + jnp.exp(-orient * distance[i]))
        first = jnp.concatenate([psi[i, 0:3, :], velocity[1, i, 0:1, :]], axis=0)
        final = jnp.concatenate([psi[i, 13:16, :], velocity[1, i, 15:16, :]], axis=0)
        chip[i] = jnp.where(odd, first, final)
        link[i] = jnp.where(odd, final, first)
        return carry

    lax.fori_loop(0, 16, plane, 0, unroll=True)
    for k in range(3):
        x_low[k] = psi[k]
        x_high[k] = psi[13 + k]
    x_low[3] = velocity[0, 0]
    x_high[3] = velocity[0, 15]


def prepare(at, phase, distance, velocity):
    outs = [(16, 16, 256), (4, 16, 256), (4, 16, 256), (16, 4, 256), (16, 4, 256)]
    return call(prepare_body, outs, [], [at, phase, distance, velocity], 1000000)


def indicators(a, b, c):
    d = a - c
    curve = (a + c) - 2.0 * b
    twice = 2.0 * curve
    base = (13.0 / 12.0) * (curve * curve) + WENO_EPS
    up, down = twice - d, twice + d
    p = base + 0.25 * (up * up)
    q = base + 0.25 * (d * d)
    r = base + 0.25 * (down * down)
    return p * p, q * q, r * r


def upwind_flux(s, l, p_left, q_left, r_left, p_right, q_right, r_right):
    ahead = s > 0.0
    pick = lambda x, y: jnp.where(ahead, x, y)
    a, b, c, e, f = pick(l[0], l[5]), pick(l[1], l[4]), pick(l[2], l[3]), pick(l[3], l[2]), pick(l[4], l[1])
    p, q, r = pick(p_left, r_right), pick(q_left, q_right), pick(r_left, p_right)
    w0, w1, w2 = 0.1 * (q * r), 0.6 * (p * r), 0.3 * (p * q)
    g0 = 2.0 * a - 7.0 * b + 11.0 * c
    g1 = 5.0 * c + 2.0 * e - b
    g2 = 2.0 * c + 5.0 * e - f
    top = w0 * g0 + w1 * g1 + w2 * g2
    return (s * top) / (6.0 * (w0 + w1 + w2))


def transport_body(at, psi, velocity, xl, xh, chip, link, moved, wider, low, high, ext, p_x, q_x, r_x, rows, speed):
    lower, upper = pick_sides(at, chip, link)
    for k in range(3):
        ext[k] = xl[k]
        ext[19 + k] = xh[k]

    def fill(i, carry):
        ext[3 + i] = psi[i]
        return carry

    lax.fori_loop(0, 16, fill, 0, unroll=True)

    def marks(i, carry):
        p, q, r = indicators(ext[i], ext[i + 1], ext[i + 2])
        p_x[i], q_x[i], r_x[i] = p, q, r
        return carry

    lax.fori_loop(0, 20, marks, 0, unroll=True)

    def x_flux(j, v_low, v_high):
        s = 0.5 * (v_low + v_high)
        l = [ext[j + k] for k in range(6)]
        return upwind_flux(
            s, l, p_x[j], q_x[j + 1], r_x[j + 2], p_x[j + 1], q_x[j + 2], r_x[j + 3]
        )

    def plane(i, below):
        here = velocity[0, i]
        following = jnp.where(i == 15, xh[3], velocity[0, jnp.minimum(i + 1, 15)])
        above = x_flux(i + 1, here, following)
        change = above - below
        y_low, y_high = lower(i), upper(i)
        rows[1:4, :] = y_low[0:3, :]
        rows[4:20, :] = psi[i]
        rows[20:23, :] = y_high[0:3, :]
        speed[3:4, :] = y_low[3:4, :]
        speed[4:20, :] = velocity[1, i]
        speed[20:21, :] = y_high[3:4, :]
        v = rows[...]
        u = speed[...]
        s = 0.5 * (u + roll(u, -1, 0))
        l = [roll(v, 2 - k, 0) for k in range(6)]
        p, q, r = indicators(l[1], l[2], l[3])
        q_next, r_next = roll(q, -1, 0), roll(r, -1, 0)
        flux = upwind_flux(s, l, roll(p, 1, 0), q, r_next, p, q_next, roll(r, -2, 0))
        rows_change = flux - roll(flux, 1, 0)
        change = change + rows_change[4:20, :]
        v = psi[i]
        w = velocity[2, i]
        lane = iota(v.shape, 1)

        def ahead(x, k):
            return jnp.where(lane > 255 - k, 0.0, roll(x, -k, 1))

        def behind(x, k):
            return jnp.where(lane < k, 0.0, roll(x, k, 1))

        l = [behind(v, 2), behind(v, 1), v, ahead(v, 1), ahead(v, 2), ahead(v, 3)]
        s = 0.5 * (w + ahead(w, 1))
        p, q, r = indicators(l[1], l[2], l[3])
        p1, q1, r1 = indicators(l[2], l[3], l[4])
        _, _, r2 = indicators(l[3], l[4], l[5])
        p0, _, _ = indicators(l[0], l[1], l[2])
        flux = upwind_flux(s, l, p0, q, r1, p, q1, r2)
        low = v[:, 0:128]
        none = jnp.zeros_like(low)
        l = [none, none, none, low, roll(low, -1, 1), roll(low, -2, 1)]
        p, q, r = indicators(l[1], l[2], l[3])
        p1, q1, r1 = indicators(l[2], l[3], l[4])
        _, _, r2 = indicators(l[3], l[4], l[5])
        p0, _, _ = indicators(none, none, none)
        wall = upwind_flux(0.5 * w[:, 0:128], l, p0, q, r1, p, q1, r2)
        wall = jnp.concatenate([wall, wall], axis=1)
        change = change + (flux - jnp.where(lane == 0, wall, roll(flux, 1, 1)))
        moved[i] = v - 0.25 * change
        return above

    rows[...] = jnp.zeros_like(rows)
    speed[...] = jnp.zeros_like(speed)
    lax.fori_loop(0, 16, plane, x_flux(0, xl[3], velocity[0, 0]), unroll=True)
    send(moved, wider, low, high, 3)


def transport(at, psi, velocity, xl, xh, chip, link):
    planes = (20, 16, 256)
    scratch = [(22, 16, 256), planes, planes, planes, (24, 256), (24, 256)]
    outs = [(16, 16, 256)] + send_shapes(3)
    return call(transport_body, outs, scratch, [at, psi, velocity, xl, xh, chip, link], 10000000)


def force_body(nx, ny, at, mid, chip, link, velocity, xl, xh, v_chip, v_link, wider, low, high, m, n_x, n_y, n_z, s_x, part, pad, source):
    lower, upper = pick_sides(at, chip, link)
    v_lower, v_upper = pick_sides(at, v_chip, v_link)
    x0, y0 = at[0] * 16, at[1] * 16
    shape = (32, 256)
    lane = iota(shape, 1)

    def fill(i, carry):
        m[i] = jnp.zeros(shape, F32)
        m[i, 5:8, :] = lower(i)
        m[i, 8:24, :] = mid[i]
        m[i, 24:27, :] = upper(i)
        return carry

    lax.fori_loop(0, 22, fill, 0, unroll=True)

    def gradient(i):
        c = m[i]
        below, above = z_shifted(c)
        gx = 0.5 * (m[i + 1] - m[i - 1])
        gy = 0.5 * (roll(c, -1, 0) - roll(c, 1, 0))
        return gx, gy, 0.5 * (above - below)

    def normals(i, carry):
        gx, gy, gz = gradient(i + 1)
        inverse = lax.rsqrt(gx * gx + gy * gy + gz * gz + DELTA_SQ)
        n_x[i], n_y[i], n_z[i] = gx * inverse, gy * inverse, gz * inverse
        return carry

    lax.fori_loop(0, 20, normals, 0, unroll=True)
    mask_y = row_mask(shape, y0 - 8, ny)

    def stars(i, carry):
        gx, gy, gz = gradient(i + 2)
        c = m[i + 2]
        edge = 0.5 * c
        edge = edge * lax.rsqrt(edge * edge + DELTA_SQ)
        nz = n_z[i + 1]
        above = jnp.where(lane == 255, -edge, roll(nz, -1, 1))
        below = jnp.where(lane == 0, edge, roll(nz, 1, 1))
        nn = n_y[i + 1]
        bending = -0.5 * (
            (n_x[i + 2] - n_x[i]) + (roll(nn, -1, 0) - roll(nn, 1, 0)) + (above - below)
        )
        keep = mask_y * plane_factor(x0 + i - 1, nx)
        bending = bending * keep
        fx, fy, fz = bending * gx, bending * gy, bending * gz
        k = jnp.clip(i - 1, 0, 15)
        vx = jnp.where(i == 0, xl[3], jnp.where(i == 17, xh[3], velocity[0, k]))
        s_x[i] = fx[8:24, :] + vx
        pad[7:8, :] = v_lower(k)[3:4, :]
        pad[8:24, :] = velocity[1, k]
        pad[24:25, :] = v_upper(k)[3:4, :]
        sy = fy + pad[...]
        dy = roll(sy, -1, 0) - roll(sy, 1, 0)
        sz = fz[8:24, :] + velocity[2, k]
        below, above = z_shifted(sz)
        part[i] = dy[8:24, :] + (above - below)
        return carry

    pad[...] = jnp.zeros_like(pad)
    lax.fori_loop(0, 18, stars, 0, unroll=True)

    def finish(i, carry):
        source[i] = -0.5 * (part[i + 1] + (s_x[i + 2] - s_x[i]))
        return carry

    lax.fori_loop(0, 16, finish, 0, unroll=True)
    send(source, wider, low, high, HALO)


def force(nx, ny, at, mid, chip, link, velocity, xl, xh, v_chip, v_link):
    n = (20, 32, 256)
    scratch = [(22, 32, 256), n, n, n, (18, 16, 256), (18, 16, 256), (32, 256), (16, 16, 256)]
    args = [at, mid, chip, link, velocity, xl, xh, v_chip, v_link]
    return call(functools.partial(force_body, nx, ny), send_shapes(HALO), scratch, args, 10000000)


class Field:
    def __init__(self, ref, lead):
        self.ref, self.lead = ref, lead

    def __getitem__(self, p):
        return self.ref[p + self.lead]

    def __setitem__(self, p, value):
        self.ref[p + self.lead] = value

    def beside(self, p):
        return beside(self.ref, p + self.lead)


def wall(at, nx, level, p, value):
    own = 16 >> level
    if 0 <= p < own:
        return value
    return value * plane_factor(at[0] * own + p, nx >> level)


def first_smooth(b, v, planes, weight, mask, at, nx, level):
    for p in planes:
        c, around = b.beside(p)
        v[p] = wall(at, nx, level, p, (weight * mask) * (1.2 * c + SIDE * around))


def sweep(src, dst, b, planes, factor, mask, at, nx, level):
    keep = SIDE * mask
    for p in planes:
        c, around = src.beside(p)
        near = around + (b[p] if factor == 1 else factor * b[p])
        dst[p] = 0.2 * c + wall(at, nx, level, p, keep) * near


def coarsen_level0(at, nx, ny, b, v, b1, planes, pair, t):
    first = planes[0]

    def residual(p):
        c, around = v.beside(p)
        return b[p] - (6.0 * c - around)

    for p in planes:
        total = residual(2 * p) + residual(2 * p + 1)
        for half in range(2):
            lanes = slice(128 * half, 128 * half + 128)
            pair[p - first, half] = total[:, lanes]
            even = pair[p - first, half, pl.ds(0, 24, stride=2), :]
            odd = pair[p - first, half, pl.ds(1, 24, stride=2), :]
            t[p - first, :, lanes] = even + odd
    count = len(planes)
    full = dot(t[...].reshape(count * 24, 256), pair_matrix(256, 128, 0.125))
    full = full.reshape(count, 24, 128)
    mask = row_mask((24, 128), at[1] * 8 - 8, ny // 2)
    for p in planes:
        b1[p] = wall(at, nx, 1, p, full[p - first] * mask)


def coarsen_level1(at, nx, ny, b1, u, planes, b2_out, s1, t1):
    mask = row_mask((24, 128), at[1] * 8 - 8, ny // 2)
    first_smooth(b1, u, planes, 4.0 * SIDE, mask, at, nx, 1)
    t1[...] = jnp.zeros_like(t1)
    for k in range(4):
        total = 0.0
        for p in (2 * k, 2 * k + 1):
            c, around = u.beside(p)
            total = total + (b1[p] - 0.25 * (6.0 * c - around))
        s1[k] = total
        t1[k, 0:4, :] = s1[k, pl.ds(8, 4, stride=2), :] + s1[k, pl.ds(9, 4, stride=2), :]
    small = dot(t1[...].reshape(32, 128), pair_matrix(128, 128, 0.125)).reshape(4, 8, 128)
    tile = jnp.concatenate([small[0, 0:4], small[1, 0:4]], axis=0) + roll(
        jnp.concatenate([small[2, 0:4], small[3, 0:4]], axis=0), 64, 1
    )
    for k in range(b2_out.shape[0]):
        b2_out[k] = tile


def reach(extra):
    e0 = extra + 2
    r1 = -(-e0 // 2)
    e1 = r1 + 2
    r2 = -(-e1 // 2)
    e2 = r2 + 2
    r3 = -(-e2 // 2)
    return e0, r1, e1, r2, e2, r3


E0, R1, E1, R2, E2, R3 = reach(KEEP)


def first_down_body(nx, ny, at, mid, chip, link, b_out, v_out, b1_out, u_out, b2_out, b, v, pair, t, s1, t1):
    lower, upper = pick_sides(at, chip, link)
    for i in range(16 + 2 * HALO):
        b[i, 0:16, :] = lower(i)
        b[i, 16:32, :] = mid[i]
        b[i, 32:48, :] = upper(i)
    b, v = Field(b, HALO), Field(v, HALO - 1)
    mask = row_mask((48, 256), at[1] * 16 - 16, ny)
    first_smooth(b, v, range(1 - HALO, 15 + HALO), SIDE, mask, at, nx, 0)
    v_out, b_out = Field(v_out, E0), Field(b_out, E0 - 1)
    for p in range(-E0, 16 + E0):
        v_out[p] = v[p]
    for p in range(1 - E0, 15 + E0):
        b_out[p] = b[p]
    b1, u = Field(b1_out, E1 + 1), Field(u_out, E1)
    coarsen_level0(at, nx, ny, b, v, b1, range(-E1 - 1, 9 + E1), pair, t)
    coarsen_level1(at, nx, ny, b1, u, range(-E1, 8 + E1), b2_out, s1, t1)


def tiles(ny):
    return (GROUP * ny // 16, 8, 128)


def around_block(size, extra, rows, lanes):
    return (size + 2 * extra, rows, lanes)


def first_down(nx, ny, at, mid, chip, link):
    level1 = around_block(8, E1 + 1, 24, 128)
    outs = [
        around_block(16, E0 - 1, 48, 256),
        around_block(16, E0, 48, 256),
        level1,
        around_block(8, E1, 24, 128),
        tiles(ny),
    ]
    scratch = [
        around_block(16, HALO, 48, 256),
        around_block(16, HALO - 1, 48, 256),
        (level1[0], 2, 48, 128),
        (level1[0], 24, 256),
        (4, 24, 128),
        (4, 8, 128),
    ]
    args = [at, mid, chip, link]
    return call(functools.partial(first_down_body, nx, ny), outs, scratch, args, 20000000)


def second_down_body(nx, ny, at, mid, chip, link, b1_out, u_out, b2_out, s1, t1):
    lower, upper = pick_sides(at, chip, link)
    for i in range(8 + 2 * NEAR):
        b1_out[i, 0:8, :] = lower(i)
        b1_out[i, 8:16, :] = mid[i]
        b1_out[i, 16:24, :] = upper(i)
    b1, u = Field(b1_out, NEAR), Field(u_out, NEAR - 1)
    coarsen_level1(at, nx, ny, b1, u, range(1 - NEAR, 7 + NEAR), b2_out, s1, t1)


def second_down(nx, ny, at, mid, chip, link):
    outs = [around_block(8, NEAR, 24, 128), around_block(8, NEAR - 1, 24, 128), tiles(ny)]
    scratch = [(4, 24, 128), (4, 8, 128)]
    args = [at, mid, chip, link]
    return call(functools.partial(second_down_body, nx, ny), outs, scratch, args, 2000000)


def solve_coarse(nx, ny, extra, at, coarse, s2, v2, w2, t3, b3, c3, d3, dup, row2):
    here, before, after = coarse
    _, _, _, r2, e2, r3 = reach(extra)
    spot = at[0] % GROUP
    rows2 = ny // 4
    rows3 = rows2 // 2
    count = rows2 // 4
    lead = 2 * (r3 + 3) + 2
    blocks = -(-lead // 4)
    s2, v2, w2 = Field(s2, 4 * blocks), Field(v2, lead - 1), Field(w2, e2)
    lane8 = iota((8, 128), 1) < 64
    for j in range(-blocks, blocks + 1):
        block = spot + GROUP + j
        layer, place = block // GROUP, block % GROUP
        for n in range(count):
            k = place * count + n
            tile = jnp.where(layer == 0, before[k], jnp.where(layer == 1, here[k], after[k]))
            halves = (jnp.where(lane8, tile, 0.0), jnp.where(lane8, roll(tile, 64, 1), 0.0))
            for p in range(4):
                part = halves[p // 2][4 * (p % 2) : 4 * (p % 2) + 4, :]
                s2.ref[4 * (j + blocks) + p, 4 * n : 4 * n + 4, :] = part

    def around(f, p):
        c = f[p]
        row = iota(c.shape, 0)
        lower = jnp.where(row == 0, 0.0, roll(c, 1, 0))
        upper = jnp.where(row == c.shape[0] - 1, 0.0, roll(c, -1, 0))
        beside = (lower + upper) + (roll(c, 1, 1) + roll(c, -1, 1))
        return c, (f[p - 1] + f[p + 1]) + beside

    def lanes_below(rows, lanes):
        return jnp.where(iota((rows, 128), 1) < lanes, 1.0, 0.0).astype(F32)

    mask2 = lanes_below(rows2, 64)
    for p in range(1 - lead, 3 + lead):
        c, near = around(s2, p)
        v2[p] = wall(at, nx, 2, p, (16.0 * SIDE) * mask2 * (1.2 * c + SIDE * near))

    def residual2(p):
        c, near = around(v2, p)
        return s2[p] - (1.0 / 16.0) * (6.0 * c - near)

    planes3 = range(-r3 - 3, 2 + r3 + 3)
    for i, p in enumerate(planes3):
        row2[i] = residual2(2 * p) + residual2(2 * p + 1)
        t3[i] = row2[i, pl.ds(0, rows3, stride=2), :] + row2[i, pl.ds(1, rows3, stride=2), :]
    total3 = len(planes3)
    full = dot(t3[...].reshape(total3 * rows3, 128), pair_matrix(128, 128, 0.125))
    full = full.reshape(total3, rows3, 128)
    mask3 = lanes_below(rows3, 32)
    b3, c3, d3 = Field(b3, r3 + 3), Field(c3, r3 + 3), Field(d3, r3 + 3)
    for i, p in enumerate(planes3):
        value = wall(at, nx, 3, p, full[i] * ((64.0 * SIDE) * mask3))
        b3[p] = value
    src, dst = b3, c3
    for step in (2, 1, 0):
        for p in range(-r3 - step, 2 + r3 + step):
            c, near = around(src, p)
            dst[p] = wall(at, nx, 3, p, mask3 * (0.2 * c + SIDE * near)) + b3[p]
        src, dst = dst, (d3 if dst is c3 else c3)
    final = src
    planes = range(-r3, 2 + r3)
    flat = jnp.concatenate([final[p] for p in planes], axis=0)
    spread = dot(flat, copy_matrix(128, 128)).reshape(len(planes), rows3, 128)
    for i, p in enumerate(planes):
        dup[i, pl.ds(0, rows3, stride=2), :] = spread[i]
        dup[i, pl.ds(1, rows3, stride=2), :] = spread[i]
        for q in (2 * p, 2 * p + 1):
            if -e2 <= q < 4 + e2:
                v2[q] = v2[q] + wall(at, nx, 2, q, dup[i, 0:rows2, :] * mask2)
    keep = SIDE * mask2
    for src, dst, step in ((v2, w2, 1), (w2, v2, 0)):
        for p in range(-r2 - step, 4 + r2 + step):
            c, near = around(src, p)
            dst[p] = 0.2 * c + wall(at, nx, 2, p, keep) * (near + 16.0 * s2[p])
    return v2


def coarse_scratch(ny, extra):
    _, _, _, _, e2, r3 = reach(extra)
    rows2 = ny // 4
    rows3 = rows2 // 2
    lead = 2 * (r3 + 3) + 2
    small = around_block(2, r3 + 3, rows3, 128)
    return [
        around_block(4, -(-lead // 4) * 4, rows2, 128),
        around_block(4, lead - 1, rows2, 128),
        around_block(4, e2, rows2, 128),
        small, small, small, small,
        (8, 48, 128),
        around_block(2, r3 + 3, rows2, 128),
    ]


def climb(nx, ny, extra, at, v2, b1, u, b, v_down, m1, n1, m0, n0, dup):
    e0, r1, e1, r2, _, _ = reach(extra)
    rows2 = ny // 4
    turn = lax.rem(rows2 + 4 - 4 * at[1] + rows2, rows2)
    planes = range(-r2, 4 + r2)
    picked = jnp.concatenate([pltpu.roll(v2[p], turn, 0)[0:16, :] for p in planes], axis=0)
    spread = dot(picked, copy_matrix(128, 128)).reshape(len(planes), 16, 128)
    mask1 = row_mask((24, 128), at[1] * 8 - 8, ny // 2)
    m1, n1 = Field(m1, e1), Field(n1, e1)
    for i, p in enumerate(planes):
        dup[i, 0, pl.ds(0, 12, stride=2), :] = spread[i, 0:12, :]
        dup[i, 0, pl.ds(1, 12, stride=2), :] = spread[i, 0:12, :]
        for q in (2 * p, 2 * p + 1):
            if -e1 <= q < 8 + e1:
                m1[q] = u[q] + wall(at, nx, 1, q, dup[i, 0, 0:24, :] * mask1)
    sweep(m1, n1, b1, range(1 - e1, 7 + e1), 4.0, mask1, at, nx, 1)
    sweep(n1, m1, b1, range(2 - e1, 6 + e1), 4.0, mask1, at, nx, 1)
    planes = range(-r1, 8 + r1)
    flat = jnp.concatenate([m1[p] for p in planes], axis=0)
    spread = dot(flat, copy_matrix(128, 256)).reshape(len(planes), 24, 256)
    mask0 = row_mask((48, 256), at[1] * 16 - 16, ny)
    m0, n0 = Field(m0, e0), Field(n0, e0)
    for i, p in enumerate(planes):
        for half in range(2):
            value = spread[i, :, 128 * half : 128 * half + 128]
            dup[i, half, pl.ds(0, 24, stride=2), :] = value
            dup[i, half, pl.ds(1, 24, stride=2), :] = value
        value = jnp.concatenate([dup[i, 0], dup[i, 1]], axis=1) * mask0
        for q in (2 * p, 2 * p + 1):
            if -e0 <= q < 16 + e0:
                m0[q] = v_down[q] + wall(at, nx, 0, q, value)
    sweep(m0, n0, b, range(1 - e0, 15 + e0), 1, mask0, at, nx, 0)
    if extra:
        sweep(n0, m0, b, range(2 - e0, 14 + e0), 1, mask0, at, nx, 0)
        return m0
    return n0


def climb_scratch(extra):
    e0, r1, e1, r2, _, _ = reach(extra)
    level1 = around_block(8, e1, 24, 128)
    level0 = around_block(16, e0, 48, 256)
    return [level1, level1, level0, level0, (max(8 + 2 * r1, 4 + 2 * r2), 2, 48, 128)]


def turn_body(nx, ny, at, here, before, after, b1, u, b, v_down, v_out, wider, low, high, own, pair, t, *scratch):
    v2 = solve_coarse(nx, ny, KEEP, at, (here, before, after), *scratch[:9])
    b = Field(b, E0 - 1)
    v = climb(nx, ny, KEEP, at, v2, Field(b1, E1 + 1), Field(u, E1), b, Field(v_down, E0), *scratch[9:])
    mask = row_mask((48, 256), at[1] * 16 - 16, ny)
    once, twice = Field(scratch[12], E0), Field(v_out, KEEP - 2)
    sweep(v, once, b, range(1 - KEEP, 15 + KEEP), 1, mask, at, nx, 0)
    sweep(once, twice, b, range(2 - KEEP, 14 + KEEP), 1, mask, at, nx, 0)
    coarsen_level0(at, nx, ny, b, twice, Field(own, 0), range(8), pair, t)
    for i in range(8):
        wider[NEAR + i] = own[i, 8:16, :]
    for i in range(NEAR):
        low[i] = own[i, 8:16, :]
        high[i] = own[8 - NEAR + i, 8:16, :]


def turn(nx, ny, at, coarse, b1, u, b, v_down):
    outs = [
        around_block(16, KEEP - 2, 48, 256),
        around_block(8, NEAR, 8, 128),
        (NEAR, 8, 128),
        (NEAR, 8, 128),
    ]
    scratch = [(8, 24, 128), (8, 2, 48, 128), (8, 24, 256)]
    scratch += coarse_scratch(ny, KEEP) + climb_scratch(KEEP)
    args = [at, *coarse, b1, u, b, v_down]
    return call(functools.partial(turn_body, nx, ny), outs, scratch, args, 30000000)


def finish_body(nx, ny, at, here, before, after, b1, u, b, v_down, out, *scratch):
    v2 = solve_coarse(nx, ny, 0, at, (here, before, after), *scratch[:9])
    b, v_down = Field(b, E0 - 1), Field(v_down, KEEP - 2)
    v = climb(nx, ny, 0, at, v2, Field(b1, NEAR), Field(u, NEAR - 1), b, v_down, *scratch[9:])
    for p in range(16):
        c, around = v.beside(p)
        out[p] = (0.2 * c + SIDE * (around + b[p]))[16:32, :]


def finish(nx, ny, at, coarse, b1, u, b, v_down):
    scratch = coarse_scratch(ny, 0) + climb_scratch(0)
    args = [at, *coarse, b1, u, b, v_down]
    return call(functools.partial(finish_body, nx, ny), [(16, 16, 256)], scratch, args, 20000000)[0]


def shifted(array, axis, step):
    count = lax.axis_size(axis)
    return lax.ppermute(
        array, axis, [(i, i + step) for i in range(count) if 0 <= i + step < count]
    )


def swapped(array, first):
    count = lax.axis_size("narrow")
    pairs = [(i, i + 1) for i in range(first, count - 1, 2)]
    return lax.ppermute(array, "narrow", pairs + [(j, i) for i, j in pairs])


def widen(wider, low, high):
    planes = low.shape[0]
    wider = lax.dynamic_update_slice(wider, shifted(high, "wide", 1), (0, 0, 0))
    upper = wider.shape[0] - planes
    return lax.dynamic_update_slice(wider, shifted(low, "wide", -1), (upper, 0, 0))


def surround(wider, low, high):
    mid = widen(wider, low, high)
    link = swapped(mid, 1)
    return mid, swapped(mid, 0), link


def spread_coarse(b2):
    wide, size = lax.axis_size("wide"), b2.shape[0]
    groups = [[g * size + k for k in range(size)] for g in range(wide // GROUP)]
    here = lax.all_to_all(b2, ("wide", "narrow"), 0, 0, axis_index_groups=groups)
    return here, shifted(here, "wide", GROUP), shifted(here, "wide", -GROUP)


def on_device(phase, distance, velocity):
    nx, ny = 16 * lax.axis_size("wide"), 16 * lax.axis_size("narrow")
    narrow = lax.axis_index("narrow")
    at = jnp.stack([lax.axis_index("wide"), narrow]).astype(jnp.int32)
    psi, x_low, x_high, chip, link = prepare(at, phase, distance, velocity)
    xl = shifted(x_high, "wide", 1)
    xh = shifted(x_low, "wide", -1)
    v_link = swapped(link, 1)
    v_chip = swapped(chip, 0)
    moved, *sends = transport(at, psi, velocity, xl, xh, v_chip, v_link)
    mid = widen(*sends)
    odd = lax.rem(narrow, 2) == 1
    first, final = mid[:, :3, :], mid[:, 13:, :]
    link = swapped(jnp.where(odd, final, first), 1)
    chip = swapped(jnp.where(odd, first, final), 0)
    sends = force(nx, ny, at, mid, chip, link, velocity, xl, xh, v_chip, v_link)
    b, v, b1, u, b2 = first_down(nx, ny, at, *surround(*sends))
    v, *sends = turn(nx, ny, at, spread_coarse(b2), b1, u, b, v)
    b1, u, b2 = second_down(nx, ny, at, *surround(*sends))
    pressure = finish(nx, ny, at, spread_coarse(b2), b1, u, b, v)
    return (moved, pressure)


def solution(mesh):
    blocks = P("wide", "narrow", None)
    return jax.shard_map(
        on_device,
        mesh=mesh,
        in_specs=(blocks, blocks, P(None, "wide", "narrow", None)),
        out_specs=(blocks, blocks),
        check_vma=False,
    )
```

time: 188 us -> 162 us (0.86)
  the two profiles are of different devices: /device:TPU:128 before, /device:TPU:384 now
where the time goes in v3:
time: 162 us
  starting transfers between devices  78.4 us (48%)
  blocking collectives  29.2 us (18%)
  waiting for transfers between devices  25.2 us (16%)
  Pallas kernels  24.8 us (15%)
  local copies, waits for them, and re-layouts  3.08 us (2%)
    ppermute x12, starting transfers between devices, shifted(): lax.ppermute(array, axis, [(i, i + step) for i in range(count) if 0 <= i...  55.9 us
    all_to_all x2, blocking collectives, spread_coarse(): lax.all_to_all(b2, ('wide', 'narrow'), 0, 0, axis_index_groups=groups)  29.2 us
    pallas_call x7, Pallas kernels, call(): pl.pallas_call(body, out_shape=[jax.ShapeDtypeStruct(s, F32) for s in out...  24.8 us
    ppermute x8, starting transfers between devices, swapped(): return lax.ppermute(array, 'narrow', pairs + [(j, i) for i, j in pairs])  22.4 us
    ppermute x12, waiting for transfers between devices, shifted(): lax.ppermute(array, axis, [(i, i + step) for i in range(count) if 0 <= i...  21.1 us
    ppermute x8, waiting for transfers between devices, swapped(): return lax.ppermute(array, 'narrow', pairs + [(j, i) for i, j in pairs])  4.09 us
  transfers between devices with their start and end apart: 20, of which 13 were waited for; matrix products, arithmetic and copies ran while one was open for 0% of the time, Pallas kernels for 0%

profile of v3, /device:TPU:384, one launch (start us, length us, event | category | flops | bytes accessed | tf_op | source)
XLA Modules:
  0.0 161.7 jit_solution(17805229945668983878)
XLA Ops:
  0.6 0.1 pad_add_fusion.at
  0.7 1.1 copy-done
  1.8 0.9 copy-done.2
  2.8 0.9 copy-done.3
  3.7 0.7 shard_map.50
  4.4 3.4 %collective-permute-start = (f32[4,16,256]{2,1,0:T(8,128)S(1)}, f32[4,16,256]{2,1,0:T(8,128)S(1)}, u32[]{:S(2)}, u32[]{:S(2)}) collective-permute-start(f32[4,16,256]{2,1,0:T(8,128)S(1)} %get-tuple-element.27), channel_id=1, source_target_pairs={{0,8},{8,16},{16,24},{24,32},{32,40},{40,48},{48,56},{56,64},{64,7... | collective-permute-start | bytes 196616 | tf_op jit(solution)/shard_map/ppermute | solution.py:679
  7.8 5.8 %collective-permute-start.1 = (f32[4,16,256]{2,1,0:T(8,128)S(1)}, f32[4,16,256]{2,1,0:T(8,128)S(1)}, u32[]{:S(2)}, u32[]{:S(2)}) collective-permute-start(f32[4,16,256]{2,1,0:T(8,128)S(1)} %get-tuple-element.28), channel_id=1, source_target_pairs={{8,0},{16,8},{24,16},{32,24},{40,32},{48,40},{56,48},{64,56},{72,6... | collective-permute-start | bytes 196616 | tf_op jit(solution)/shard_map/ppermute | solution.py:679
  13.6 1.9 %collective-permute-start.2 = (f32[16,4,256]{2,1,0:T(4,128)S(1)}, f32[16,4,256]{2,1,0:T(4,128)S(1)}, u32[]{:S(2)}, u32[]{:S(2)}) collective-permute-start(f32[16,4,256]{2,1,0:T(4,128)S(1)} %get-tuple-element.29), channel_id=1, source_target_pairs={{0,1},{2,3},{4,5},{6,7},{1,0},{3,2},{5,4},{7,6},{8,9},{10,11},{12,... | collective-permute-start | bytes 196616 | tf_op jit(solution)/shard_map/ppermute | solution.py:687
  15.5 0.7 collective-permute-start.3
  16.2 0.0 collective-permute-done.1.xh
  16.2 0.5 collective-permute-done.2.chip.v_chip
  16.8 4.8 %shard_map.51 = (f32[16,16,256]{2,1,0:T(8,128)}, f32[22,16,256]{2,1,0:T(8,128)S(1)}, f32[3,16,256]{2,1,0:T(8,128)S(1)}, f32[3,16,256]{2,1,0:T(8,128)S(1)}) custom-call(s32[2]{0:T(128)S(1)} %pad_add_fusion.at, f32[16,16,256]{2,1,0:T(8,128)S(1)} %get-tuple-element.26.psi, f32[3,16,16,256]{3,2,1,0:T(8,128)S(1)} %copy-done.1, ...), custom_call_target="tpu_custom_call" | custom-call | flops 10000000 | bytes 4000000 | tf_op jit(solution)/shard_map/pallas_call | solution.py:91
  21.6 1.9 %collective-permute-start.4 = (f32[3,16,256]{2,1,0:T(8,128)S(1)}, f32[3,16,256]{2,1,0:T(8,128)S(1)}, u32[]{:S(2)}, u32[]{:S(2)}) collective-permute-start(f32[3,16,256]{2,1,0:T(8,128)S(1)} %get-tuple-element.33), channel_id=1, source_target_pairs={{0,8},{8,16},{16,24},{24,32},{32,40},{40,48},{48,56},{56,64},{64,7... | collective-permute-start | bytes 147464 | tf_op jit(solution)/shard_map/ppermute | solution.py:679
  23.5 7.2 %collective-permute-start.5 = (f32[3,16,256]{2,1,0:T(8,128)S(1)}, f32[3,16,256]{2,1,0:T(8,128)S(1)}, u32[]{:S(2)}, u32[]{:S(2)}) collective-permute-start(f32[3,16,256]{2,1,0:T(8,128)S(1)} %get-tuple-element.34), channel_id=1, source_target_pairs={{8,0},{16,8},{24,16},{32,24},{40,32},{48,40},{56,48},{64,56},{72,6... | collective-permute-start | bytes 147464 | tf_op jit(solution)/shard_map/ppermute | solution.py:679
  30.8 0.1 collective-permute-done.4
  30.9 1.6 collective-permute-done.5
  32.5 0.7 collective-permute-start.7
  33.2 9.2 %collective-permute-start.6 = (f32[22,3,256]{2,1,0:T(4,128)S(1)}, f32[22,3,256]{2,1,0:T(4,128)S(1)}, u32[]{:S(2)}, u32[]{:S(2)}) collective-permute-start(f32[22,3,256]{2,1,0:T(4,128)S(1)} %get-tuple-element.51), channel_id=1, source_target_pairs={{0,1},{2,3},{4,5},{6,7},{1,0},{3,2},{5,4},{7,6},{8,9},{10,11},{12,... | collective-permute-start | bytes 202760 | tf_op jit(solution)/shard_map/ppermute | solution.py:687
  42.4 0.0 collective-permute-done.7.link
  42.4 0.9 collective-permute-done.6.chip
  43.3 2.7 %shard_map.52 = (f32[44,16,256]{2,1,0:T(8,128)S(1)}, f32[14,16,256]{2,1,0:T(8,128)S(1)}, f32[14,16,256]{2,1,0:T(8,128)S(1)}) custom-call(s32[2]{0:T(128)S(1)} %pad_add_fusion.at, f32[22,16,256]{2,1,0:T(8,128)S(1)} %constant_dynamic-update-slice_fusion.4.mid, f32[22,3,256]{2,1,0:T(4,128)S(1)} %collective-permute-done.6.chip, ...), custom_call_target="tpu_custom_call" | custom-call | flops 10000000 | bytes 4000000 | tf_op jit(solution)/shard_map/pallas_call | solution.py:91
  46.1 1.9 %collective-permute-start.8 = (f32[14,16,256]{2,1,0:T(8,128)S(1)}, f32[14,16,256]{2,1,0:T(8,128)S(1)}, u32[]{:S(2)}, u32[]{:S(2)}) collective-permute-start(f32[14,16,256]{2,1,0:T(8,128)S(1)} %get-tuple-element.36), channel_id=1, source_target_pairs={{0,8},{8,16},{16,24},{24,32},{32,40},{40,48},{48,56},{56,64},{64,7... | collective-permute-start | bytes 688136 | tf_op jit(solution)/shard_map/ppermute | solution.py:679
  48.0 7.6 %collective-permute-start.9 = (f32[14,16,256]{2,1,0:T(8,128)S(1)}, f32[14,16,256]{2,1,0:T(8,128)S(1)}, u32[]{:S(2)}, u32[]{:S(2)}) collective-permute-start(f32[14,16,256]{2,1,0:T(8,128)S(1)} %get-tuple-element.37), channel_id=1, source_target_pairs={{8,0},{16,8},{24,16},{32,24},{40,32},{48,40},{56,48},{64,56},{72,6... | collective-permute-start | bytes 688136 | tf_op jit(solution)/shard_map/ppermute | solution.py:679
  55.6 4.2 %collective-permute-done.8 = f32[14,16,256]{2,1,0:T(8,128)S(1)} collective-permute-done((f32[14,16,256]{2,1,0:T(8,128)S(1)}, f32[14,16,256]{2,1,0:T(8,128)S(1)}, u32[]{:S(2)}, u32[]{:S(2)}) %collective-permute-start.8) | collective-permute-done | bytes 229408 | tf_op jit(solution)/shard_map/ppermute | solution.py:679
  59.8 1.2 collective-permute-done.9
  60.9 0.7 collective-permute-start.11
  61.7 4.8 %collective-permute-start.10 = (f32[44,16,256]{2,1,0:T(8,128)S(1)}, f32[44,16,256]{2,1,0:T(8,128)S(1)}, u32[]{:S(2)}, u32[]{:S(2)}) collective-permute-start(f32[44,16,256]{2,1,0:T(8,128)S(1)} %constant_dynamic-update-slice_fusion.2.mid), channel_id=1, source_target_pairs={{0,1},{2,3},{4,5},{6,7},{1,0},{3,2},{5,4},{7,6},{8,9},{10,11},{12,... | collective-permute-start | bytes 2162696 | tf_op jit(solution)/shard_map/ppermute | solution.py:687
  66.5 1.8 %collective-permute-done.10.chip = f32[44,16,256]{2,1,0:T(8,128)S(1)} collective-permute-done((f32[44,16,256]{2,1,0:T(8,128)S(1)}, f32[44,16,256]{2,1,0:T(8,128)S(1)}, u32[]{:S(2)}, u32[]{:S(2)}) %collective-permute-start.10) | collective-permute-done | bytes 720928 | tf_op jit(solution)/shard_map/ppermute | solution.py:687
  68.3 4.4 %shard_map.53 = (f32[26,48,256]{2,1,0:T(8,128)S(1)}, f32[28,48,256]{2,1,0:T(8,128)S(1)}, f32[20,24,128]{2,1,0:T(8,128)S(1)}, f32[18,24,128]{2,1,0:T(8,128)S(1)}, f32[32,8,128]{2,1,0:T(8,128)S(1)}) custom-call(s32[2]{0:T(128)S(1)} %pad_add_fusion.at, f32[44,16,256]{2,1,0:T(8,128)S(1)} %constant_dynamic-update-slice_fusion.2.mid, ...), custom_call_target="tpu_custom_call" | custom-call | flops 20000000 | bytes 4000000 | tf_op jit(solution)/shard_map/pallas_call | solution.py:91
  72.6 17.5 %all_to_all.10.here = f32[32,8,128]{2,1,0:T(8,128)S(1)} all-to-all(f32[32,8,128]{2,1,0:T(8,128)S(1)} %get-tuple-element.38), channel_id=1, replica_groups={{0,1,2,3,4,5,6,7,8,9,10,11,12,13,14,15,16,17,18,19,20,21,22,23,24,25,26..., dimensions={0} | all-to-all | bytes 262144 | tf_op jit(solution)/shard_map/all_to_all | solution.py:706
  90.1 7.7 %collective-permute-start.13 = (f32[32,8,128]{2,1,0:T(8,128)S(1)}, f32[32,8,128]{2,1,0:T(8,128)S(1)}, u32[]{:S(2)}, u32[]{:S(2)}) collective-permute-start(f32[32,8,128]{2,1,0:T(8,128)S(1)} %all_to_all.10.here), channel_id=1, source_target_pairs={{32,0},{40,8},{48,16},{56,24},{64,32},{72,40},{80,48},{88,56},{96,... | collective-permute-start | bytes 393224 | tf_op jit(solution)/shard_map/ppermute | solution.py:679
  97.9 2.1 %collective-permute-start.12 = (f32[32,8,128]{2,1,0:T(8,128)S(1)}, f32[32,8,128]{2,1,0:T(8,128)S(1)}, u32[]{:S(2)}, u32[]{:S(2)}) collective-permute-start(f32[32,8,128]{2,1,0:T(8,128)S(1)} %all_to_all.10.here), channel_id=1, source_target_pairs={{0,32},{8,40},{16,48},{24,56},{32,64},{40,72},{48,80},{56,88},{64,... | collective-permute-start | bytes 393224 | tf_op jit(solution)/shard_map/ppermute | solution.py:679
  100.0 0.9 collective-permute-done.13.after
  100.9 5.3 %collective-permute-done.12.before = f32[32,8,128]{2,1,0:T(8,128)S(1)} collective-permute-done((f32[32,8,128]{2,1,0:T(8,128)S(1)}, f32[32,8,128]{2,1,0:T(8,128)S(1)}, u32[]{:S(2)}, u32[]{:S(2)}) %collective-permute-start.12) | collective-permute-done | bytes 131104 | tf_op jit(solution)/shard_map/ppermute | solution.py:679
  106.2 7.1 %shard_map.54 = (f32[20,48,256]{2,1,0:T(8,128)S(1)}, f32[16,8,128]{2,1,0:T(8,128)S(1)}, f32[4,8,128]{2,1,0:T(8,128)S(1)}, f32[4,8,128]{2,1,0:T(8,128)S(1)}) custom-call(s32[2]{0:T(128)S(1)} %pad_add_fusion.at, f32[32,8,128]{2,1,0:T(8,128)S(1)} %all_to_all.10.here, f32[32,8,128]{2,1,0:T(8,128)S(1)} %collective-permute-done.12.before, ...), custom_call_target="tpu_custom_call" | custom-call | flops 30000000 | bytes 4000000 | tf_op jit(solution)/shard_map/pallas_call | solution.py:91
  113.3 2.5 %collective-permute-start.14 = (f32[4,8,128]{2,1,0:T(8,128)S(1)}, f32[4,8,128]{2,1,0:T(8,128)S(1)}, u32[]{:S(2)}, u32[]{:S(2)}) collective-permute-start(f32[4,8,128]{2,1,0:T(8,128)S(1)} %get-tuple-element.44), channel_id=1, source_target_pairs={{0,8},{8,16},{16,24},{24,32},{32,40},{40,48},{48,56},{56,64},{64,7... | collective-permute-start | bytes 49160 | tf_op jit(solution)/shard_map/ppermute | solution.py:679
  115.8 6.7 %collective-permute-start.15 = (f32[4,8,128]{2,1,0:T(8,128)S(1)}, f32[4,8,128]{2,1,0:T(8,128)S(1)}, u32[]{:S(2)}, u32[]{:S(2)}) collective-permute-start(f32[4,8,128]{2,1,0:T(8,128)S(1)} %get-tuple-element.45), channel_id=1, source_target_pairs={{8,0},{16,8},{24,16},{32,24},{40,32},{48,40},{56,48},{64,56},{72,6... | collective-permute-start | bytes 49160 | tf_op jit(solution)/shard_map/ppermute | solution.py:679
  122.5 1.4 collective-permute-done.15
  123.9 0.7 collective-permute-start.17
  124.6 3.8 %collective-permute-start.16 = (f32[16,8,128]{2,1,0:T(8,128)S(1)}, f32[16,8,128]{2,1,0:T(8,128)S(1)}, u32[]{:S(2)}, u32[]{:S(2)}) collective-permute-start(f32[16,8,128]{2,1,0:T(8,128)S(1)} %constant_dynamic-update-slice_fusion.mid), channel_id=1, source_target_pairs={{0,1},{2,3},{4,5},{6,7},{1,0},{3,2},{5,4},{7,6},{8,9},{10,11},{12,... | collective-permute-start | bytes 196616 | tf_op jit(solution)/shard_map/ppermute | solution.py:687
  128.4 0.9 collective-permute-done.16.chip
  129.3 1.0 shard_map.55
  130.2 11.7 %all_to_all.11.here = f32[32,8,128]{2,1,0:T(8,128)S(1)} all-to-all(f32[32,8,128]{2,1,0:T(8,128)S(1)} %get-tuple-element.46), channel_id=1, replica_groups={{0,1,2,3,4,5,6,7,8,9,10,11,12,13,14,15,16,17,18,19,20,21,22,23,24,25,26..., dimensions={0} | all-to-all | bytes 262144 | tf_op jit(solution)/shard_map/all_to_all | solution.py:706
  141.9 7.3 %collective-permute-start.19 = (f32[32,8,128]{2,1,0:T(8,128)S(1)}, f32[32,8,128]{2,1,0:T(8,128)S(1)}, u32[]{:S(2)}, u32[]{:S(2)}) collective-permute-start(f32[32,8,128]{2,1,0:T(8,128)S(1)} %all_to_all.11.here), channel_id=1, source_target_pairs={{32,0},{40,8},{48,16},{56,24},{64,32},{72,40},{80,48},{88,56},{96,... | collective-permute-start | bytes 393224 | tf_op jit(solution)/shard_map/ppermute | solution.py:679
  149.2 1.9 %collective-permute-start.18 = (f32[32,8,128]{2,1,0:T(8,128)S(1)}, f32[32,8,128]{2,1,0:T(8,128)S(1)}, u32[]{:S(2)}, u32[]{:S(2)}) collective-permute-start(f32[32,8,128]{2,1,0:T(8,128)S(1)} %all_to_all.11.here), channel_id=1, source_target_pairs={{0,32},{8,40},{16,48},{24,56},{32,64},{40,72},{48,80},{56,88},{64,... | collective-permute-start | bytes 393224 | tf_op jit(solution)/shard_map/ppermute | solution.py:679
  151.1 1.1 collective-permute-done.19.after
  152.2 5.3 %collective-permute-done.18.before = f32[32,8,128]{2,1,0:T(8,128)S(1)} collective-permute-done((f32[32,8,128]{2,1,0:T(8,128)S(1)}, f32[32,8,128]{2,1,0:T(8,128)S(1)}, u32[]{:S(2)}, u32[]{:S(2)}) %collective-permute-start.18) | collective-permute-done | bytes 131104 | tf_op jit(solution)/shard_map/ppermute | solution.py:679
  157.5 4.1 %shard_map.56 = f32[16,16,256]{2,1,0:T(8,128)} custom-call(s32[2]{0:T(128)S(1)} %pad_add_fusion.at, f32[32,8,128]{2,1,0:T(8,128)S(1)} %all_to_all.11.here, f32[32,8,128]{2,1,0:T(8,128)S(1)} %collective-permute-done.18.before, f32[32,8,128]{2,1,0:T(8,128)S(1)} %collective-permute-done.19.after, f32[16,24,128]{2,1,0:T(8,128)S(1)} %get-tuple-element.47.b1, ...), custom_call_target="tpu_custom_call" | custom-call | flops 20000000 | bytes 4000000 | tf_op jit(solution)/shard_map/pallas_call | solution.py:91
  (17 shorter events, 0.1 us)
Async XLA Ops:
  0.7 1.1 copy-start
  1.8 0.9 copy-start.2
  2.8 0.9 copy-start.3
  3.7 13.0 %copy-start.1 = (f32[3,16,16,256]{3,2,1,0:T(8,128)S(1)}, f32[3,16,16,256]{3,2,1,0:T(8,128)}, u32[]{:S(2)}) copy-start(f32[3,16,16,256]{3,2,1,0:T(8,128)} %velocity.5) | copy-start | bytes 2359300
  4.4 11.8 %collective-permute-start = (f32[4,16,256]{2,1,0:T(8,128)S(1)}, f32[4,16,256]{2,1,0:T(8,128)S(1)}, u32[]{:S(2)}, u32[]{:S(2)}) collective-permute-start(f32[4,16,256]{2,1,0:T(8,128)S(1)} %get-tuple-element.27), channel_id=1, source_target_pairs={{0,8},{8,16},{16,24},{24,32},{32,40},{40,48},{48,56},{56,64},{64,7... | collective-permute-start | bytes 196616 | tf_op jit(solution)/shard_map/ppermute | solution.py:679
  7.8 8.4 %collective-permute-start.1 = (f32[4,16,256]{2,1,0:T(8,128)S(1)}, f32[4,16,256]{2,1,0:T(8,128)S(1)}, u32[]{:S(2)}, u32[]{:S(2)}) collective-permute-start(f32[4,16,256]{2,1,0:T(8,128)S(1)} %get-tuple-element.28), channel_id=1, source_target_pairs={{8,0},{16,8},{24,16},{32,24},{40,32},{48,40},{56,48},{64,56},{72,6... | collective-permute-start | bytes 196616 | tf_op jit(solution)/shard_map/ppermute | solution.py:679
  13.6 3.1 %collective-permute-start.2 = (f32[16,4,256]{2,1,0:T(4,128)S(1)}, f32[16,4,256]{2,1,0:T(4,128)S(1)}, u32[]{:S(2)}, u32[]{:S(2)}) collective-permute-start(f32[16,4,256]{2,1,0:T(4,128)S(1)} %get-tuple-element.29), channel_id=1, source_target_pairs={{0,1},{2,3},{4,5},{6,7},{1,0},{3,2},{5,4},{7,6},{8,9},{10,11},{12,... | collective-permute-start | bytes 196616 | tf_op jit(solution)/shard_map/ppermute | solution.py:687
  15.5 1.2 collective-permute-start.3
  21.6 9.3 %collective-permute-start.4 = (f32[3,16,256]{2,1,0:T(8,128)S(1)}, f32[3,16,256]{2,1,0:T(8,128)S(1)}, u32[]{:S(2)}, u32[]{:S(2)}) collective-permute-start(f32[3,16,256]{2,1,0:T(8,128)S(1)} %get-tuple-element.33), channel_id=1, source_target_pairs={{0,8},{8,16},{16,24},{24,32},{32,40},{40,48},{48,56},{56,64},{64,7... | collective-permute-start | bytes 147464 | tf_op jit(solution)/shard_map/ppermute | solution.py:679
  23.5 9.0 %collective-permute-start.5 = (f32[3,16,256]{2,1,0:T(8,128)S(1)}, f32[3,16,256]{2,1,0:T(8,128)S(1)}, u32[]{:S(2)}, u32[]{:S(2)}) collective-permute-start(f32[3,16,256]{2,1,0:T(8,128)S(1)} %get-tuple-element.34), channel_id=1, source_target_pairs={{8,0},{16,8},{24,16},{32,24},{40,32},{48,40},{56,48},{64,56},{72,6... | collective-permute-start | bytes 147464 | tf_op jit(solution)/shard_map/ppermute | solution.py:679
  32.5 9.9 %collective-permute-start.7 = (f32[22,3,256]{2,1,0:T(4,128)S(1)}, f32[22,3,256]{2,1,0:T(4,128)S(1)}, u32[]{:S(2)}, u32[]{:S(2)}) collective-permute-start(f32[22,3,256]{2,1,0:T(4,128)S(1)} %get-tuple-element.50), channel_id=1, source_target_pairs={{1,2},{3,4},{5,6},{2,1},{4,3},{6,5},{9,10},{11,12},{13,14},{10,9},... | collective-permute-start | bytes 202760 | tf_op jit(solution)/shard_map/ppermute | solution.py:687
  33.2 10.1 %collective-permute-start.6 = (f32[22,3,256]{2,1,0:T(4,128)S(1)}, f32[22,3,256]{2,1,0:T(4,128)S(1)}, u32[]{:S(2)}, u32[]{:S(2)}) collective-permute-start(f32[22,3,256]{2,1,0:T(4,128)S(1)} %get-tuple-element.51), channel_id=1, source_target_pairs={{0,1},{2,3},{4,5},{6,7},{1,0},{3,2},{5,4},{7,6},{8,9},{10,11},{12,... | collective-permute-start | bytes 202760 | tf_op jit(solution)/shard_map/ppermute | solution.py:687
  46.1 13.7 %collective-permute-start.8 = (f32[14,16,256]{2,1,0:T(8,128)S(1)}, f32[14,16,256]{2,1,0:T(8,128)S(1)}, u32[]{:S(2)}, u32[]{:S(2)}) collective-permute-start(f32[14,16,256]{2,1,0:T(8,128)S(1)} %get-tuple-element.36), channel_id=1, source_target_pairs={{0,8},{8,16},{16,24},{24,32},{32,40},{40,48},{48,56},{56,64},{64,7... | collective-permute-start | bytes 688136 | tf_op jit(solution)/shard_map/ppermute | solution.py:679
  48.0 12.9 %collective-permute-start.9 = (f32[14,16,256]{2,1,0:T(8,128)S(1)}, f32[14,16,256]{2,1,0:T(8,128)S(1)}, u32[]{:S(2)}, u32[]{:S(2)}) collective-permute-start(f32[14,16,256]{2,1,0:T(8,128)S(1)} %get-tuple-element.37), channel_id=1, source_target_pairs={{8,0},{16,8},{24,16},{32,24},{40,32},{48,40},{56,48},{64,56},{72,6... | collective-permute-start | bytes 688136 | tf_op jit(solution)/shard_map/ppermute | solution.py:679
  60.9 5.5 %collective-permute-start.11 = (f32[44,16,256]{2,1,0:T(8,128)S(1)}, f32[44,16,256]{2,1,0:T(8,128)S(1)}, u32[]{:S(2)}, u32[]{:S(2)}) collective-permute-start(f32[44,16,256]{2,1,0:T(8,128)S(1)} %constant_dynamic-update-slice_fusion.2.mid), channel_id=1, source_target_pairs={{1,2},{3,4},{5,6},{2,1},{4,3},{6,5},{9,10},{11,12},{13,14},{10,9},... | collective-permute-start | bytes 2162696 | tf_op jit(solution)/shard_map/ppermute | solution.py:687
  61.7 6.6 %collective-permute-start.10 = (f32[44,16,256]{2,1,0:T(8,128)S(1)}, f32[44,16,256]{2,1,0:T(8,128)S(1)}, u32[]{:S(2)}, u32[]{:S(2)}) collective-permute-start(f32[44,16,256]{2,1,0:T(8,128)S(1)} %constant_dynamic-update-slice_fusion.2.mid), channel_id=1, source_target_pairs={{0,1},{2,3},{4,5},{6,7},{1,0},{3,2},{5,4},{7,6},{8,9},{10,11},{12,... | collective-permute-start | bytes 2162696 | tf_op jit(solution)/shard_map/ppermute | solution.py:687
  90.1 10.7 %collective-permute-start.13 = (f32[32,8,128]{2,1,0:T(8,128)S(1)}, f32[32,8,128]{2,1,0:T(8,128)S(1)}, u32[]{:S(2)}, u32[]{:S(2)}) collective-permute-start(f32[32,8,128]{2,1,0:T(8,128)S(1)} %all_to_all.10.here), channel_id=1, source_target_pairs={{32,0},{40,8},{48,16},{56,24},{64,32},{72,40},{80,48},{88,56},{96,... | collective-permute-start | bytes 393224 | tf_op jit(solution)/shard_map/ppermute | solution.py:679
  97.9 8.3 %collective-permute-start.12 = (f32[32,8,128]{2,1,0:T(8,128)S(1)}, f32[32,8,128]{2,1,0:T(8,128)S(1)}, u32[]{:S(2)}, u32[]{:S(2)}) collective-permute-start(f32[32,8,128]{2,1,0:T(8,128)S(1)} %all_to_all.10.here), channel_id=1, source_target_pairs={{0,32},{8,40},{16,48},{24,56},{32,64},{40,72},{48,80},{56,88},{64,... | collective-permute-start | bytes 393224 | tf_op jit(solution)/shard_map/ppermute | solution.py:679
  113.3 9.2 %collective-permute-start.14 = (f32[4,8,128]{2,1,0:T(8,128)S(1)}, f32[4,8,128]{2,1,0:T(8,128)S(1)}, u32[]{:S(2)}, u32[]{:S(2)}) collective-permute-start(f32[4,8,128]{2,1,0:T(8,128)S(1)} %get-tuple-element.44), channel_id=1, source_target_pairs={{0,8},{8,16},{16,24},{24,32},{32,40},{40,48},{48,56},{56,64},{64,7... | collective-permute-start | bytes 49160 | tf_op jit(solution)/shard_map/ppermute | solution.py:679
  115.8 8.1 %collective-permute-start.15 = (f32[4,8,128]{2,1,0:T(8,128)S(1)}, f32[4,8,128]{2,1,0:T(8,128)S(1)}, u32[]{:S(2)}, u32[]{:S(2)}) collective-permute-start(f32[4,8,128]{2,1,0:T(8,128)S(1)} %get-tuple-element.45), channel_id=1, source_target_pairs={{8,0},{16,8},{24,16},{32,24},{40,32},{48,40},{56,48},{64,56},{72,6... | collective-permute-start | bytes 49160 | tf_op jit(solution)/shard_map/ppermute | solution.py:679
  123.9 4.5 %collective-permute-start.17 = (f32[16,8,128]{2,1,0:T(8,128)S(1)}, f32[16,8,128]{2,1,0:T(8,128)S(1)}, u32[]{:S(2)}, u32[]{:S(2)}) collective-permute-start(f32[16,8,128]{2,1,0:T(8,128)S(1)} %constant_dynamic-update-slice_fusion.mid), channel_id=1, source_target_pairs={{1,2},{3,4},{5,6},{2,1},{4,3},{6,5},{9,10},{11,12},{13,14},{10,9},... | collective-permute-start | bytes 196616 | tf_op jit(solution)/shard_map/ppermute | solution.py:687
  124.6 4.7 %collective-permute-start.16 = (f32[16,8,128]{2,1,0:T(8,128)S(1)}, f32[16,8,128]{2,1,0:T(8,128)S(1)}, u32[]{:S(2)}, u32[]{:S(2)}) collective-permute-start(f32[16,8,128]{2,1,0:T(8,128)S(1)} %constant_dynamic-update-slice_fusion.mid), channel_id=1, source_target_pairs={{0,1},{2,3},{4,5},{6,7},{1,0},{3,2},{5,4},{7,6},{8,9},{10,11},{12,... | collective-permute-start | bytes 196616 | tf_op jit(solution)/shard_map/ppermute | solution.py:687
  141.9 10.3 %collective-permute-start.19 = (f32[32,8,128]{2,1,0:T(8,128)S(1)}, f32[32,8,128]{2,1,0:T(8,128)S(1)}, u32[]{:S(2)}, u32[]{:S(2)}) collective-permute-start(f32[32,8,128]{2,1,0:T(8,128)S(1)} %all_to_all.11.here), channel_id=1, source_target_pairs={{32,0},{40,8},{48,16},{56,24},{64,32},{72,40},{80,48},{88,56},{96,... | collective-permute-start | bytes 393224 | tf_op jit(solution)/shard_map/ppermute | solution.py:679
  149.2 8.3 %collective-permute-start.18 = (f32[32,8,128]{2,1,0:T(8,128)S(1)}, f32[32,8,128]{2,1,0:T(8,128)S(1)}, u32[]{:S(2)}, u32[]{:S(2)}) collective-permute-start(f32[32,8,128]{2,1,0:T(8,128)S(1)} %all_to_all.11.here), channel_id=1, source_target_pairs={{0,32},{8,40},{16,48},{24,56},{32,64},{40,72},{48,80},{56,88},{64,... | collective-permute-start | bytes 393224 | tf_op jit(solution)/shard_map/ppermute | solution.py:679

commit v4 on v3

--- a/solution.py
+++ b/solution.py
@@ -118,29 +118,67 @@
         high[i] = block[16 - planes + i]
 
 
-def prepare_body(at, phase, distance, velocity, psi, x_low, x_high, chip, link):
+PARTS = 4
+
+
+def prepare_body(at, phase, distance, velocity, psi, x_low, x_high, chip, link, kind, away, x_face, y_face, sems):
     odd = lax.rem(at[1], 2) == 1
-
-    def plane(i, carry):
-        orient = 2.0 * phase[i].astype(F32) - 1.0
-        psi[i] = 1.0 / (1.0 + jnp.exp(-orient * distance[i]))
-        first = jnp.concatenate([psi[i, 0:3, :], velocity[1, i, 0:1, :]], axis=0)
-        final = jnp.concatenate([psi[i, 13:16, :], velocity[1, i, 15:16, :]], axis=0)
+    step = 16 // PARTS
+    copies = []
+
+    def copy(src, dst):
+        started = pltpu.make_async_copy(src, dst, sems.at[len(copies)])
+        started.start()
+        copies.append(started)
+
+    for k in range(PARTS):
+        planes = pl.ds(step * k, step)
+        copy(phase.at[planes], kind.at[planes])
+        copy(distance.at[planes], away.at[planes])
+    copy(velocity.at[0, 0], x_face.at[0])
+    copy(velocity.at[0, 15], x_face.at[1])
+    copy(velocity.at[1, :, pl.ds(0, 8), :], y_face.at[0])
+    copy(velocity.at[1, :, pl.ds(8, 8), :], y_face.at[1])
+    for k in range(PARTS):
+        copies[2 * k].wait()
+        copies[2 * k + 1].wait()
+        for i in range(step * k, step * k + step):
+            orient = 2.0 * kind[i].astype(F32) - 1.0
+            psi[i] = 1.0 / (1.0 + jnp.exp(-orient * away[i]))
+    for started in copies[2 * PARTS :]:
+        started.wait()
+    for i in range(16):
+        first = jnp.concatenate([psi[i, 0:3, :], y_face[0, i, 0:1, :]], axis=0)
+        final = jnp.concatenate([psi[i, 13:16, :], y_face[1, i, 7:8, :]], axis=0)
         chip[i] = jnp.where(odd, first, final)
         link[i] = jnp.where(odd, final, first)
-        return carry
-
-    lax.fori_loop(0, 16, plane, 0, unroll=True)
     for k in range(3):
         x_low[k] = psi[k]
         x_high[k] = psi[13 + k]
-    x_low[3] = velocity[0, 0]
-    x_high[3] = velocity[0, 15]
+    x_low[3] = x_face[0]
+    x_high[3] = x_face[1]
 
 
 def prepare(at, phase, distance, velocity):
+    vmem = pl.BlockSpec(memory_space=pltpu.VMEM)
+    smem = pl.BlockSpec(memory_space=pltpu.SMEM)
+    hbm = pl.BlockSpec(memory_space=pltpu.HBM)
     outs = [(16, 16, 256), (4, 16, 256), (4, 16, 256), (16, 4, 256), (16, 4, 256)]
-    return call(prepare_body, outs, [], [at, phase, distance, velocity], 1000000)
+    return pl.pallas_call(
+        prepare_body,
+        out_shape=[jax.ShapeDtypeStruct(s, F32) for s in outs],
+        in_specs=[smem, hbm, hbm, hbm],
+        out_specs=[vmem] * len(outs),
+        scratch_shapes=[
+            pltpu.VMEM((16, 16, 256), jnp.int32),
+            pltpu.VMEM((16, 16, 256), F32),
+            pltpu.VMEM((2, 16, 256), F32),
+            pltpu.VMEM((2, 16, 8, 256), F32),
+            pltpu.SemaphoreType.DMA((2 * PARTS + 4,)),
+        ],
+        compiler_params=pltpu.CompilerParams(vmem_limit_bytes=8 << 20),
+        cost_estimate=pl.CostEstimate(flops=1000000, bytes_accessed=1000000, transcendentals=0),
+    )(at, *(pltpu.with_memory_space_constraint(a, pltpu.HBM) for a in (phase, distance, velocity)))
 
 
 def indicators(a, b, c):
@@ -228,18 +266,23 @@
         l = [behind(v, 2), behind(v, 1), v, ahead(v, 1), ahead(v, 2), ahead(v, 3)]
         s = 0.5 * (w + ahead(w, 1))
         p, q, r = indicators(l[1], l[2], l[3])
-        p1, q1, r1 = indicators(l[2], l[3], l[4])
-        _, _, r2 = indicators(l[3], l[4], l[5])
-        p0, _, _ = indicators(l[0], l[1], l[2])
-        flux = upwind_flux(s, l, p0, q, r1, p, q1, r2)
-        low = v[:, 0:128]
-        none = jnp.zeros_like(low)
-        l = [none, none, none, low, roll(low, -1, 1), roll(low, -2, 1)]
-        p, q, r = indicators(l[1], l[2], l[3])
-        p1, q1, r1 = indicators(l[2], l[3], l[4])
-        _, _, r2 = indicators(l[3], l[4], l[5])
-        p0, _, _ = indicators(none, none, none)
-        wall = upwind_flux(0.5 * w[:, 0:128], l, p0, q, r1, p, q1, r2)
+        square = v * v
+        edge = WENO_EPS + (13.0 / 12.0 + 9.0 / 4.0) * square
+        edge = edge * edge
+        level = WENO_EPS + (13.0 / 12.0 + 1.0 / 4.0) * square
+        level = level * level
+        p_below = jnp.where(lane == 0, edge, roll(p, 1, 1))
+        q_above = jnp.where(lane == 255, level, roll(q, -1, 1))
+        r_above = jnp.where(lane == 255, edge, roll(r, -1, 1))
+        r_far = jnp.where(lane == 255, WENO_EPS * WENO_EPS, roll(r_above, -1, 1))
+        flux = upwind_flux(s, l, p_below, q, r_above, p, q_above, r_far)
+        low = slice(0, 128)
+        none = jnp.zeros((v.shape[0], 128), F32)
+        l = [none, none, none, v[:, low], l[3][:, low], l[4][:, low]]
+        wall = upwind_flux(
+            0.5 * w[:, low], l, none + WENO_EPS * WENO_EPS, level[:, low], r[:, low],
+            edge[:, low], q[:, low], r_above[:, low],
+        )
         wall = jnp.concatenate([wall, wall], axis=1)
         change = change + (flux - jnp.where(lane == 0, wall, roll(flux, 1, 1)))
         moved[i] = v - 0.25 * change
@@ -373,6 +416,7 @@
 
 def coarsen_level0(at, nx, ny, b, v, b1, planes, pair, t):
     first = planes[0]
+    rows = t.shape[1]
 
     def residual(p):
         c, around = v.beside(p)
@@ -383,20 +427,25 @@
         for half in range(2):
             lanes = slice(128 * half, 128 * half + 128)
             pair[p - first, half] = total[:, lanes]
-            even = pair[p - first, half, pl.ds(0, 24, stride=2), :]
-            odd = pair[p - first, half, pl.ds(1, 24, stride=2), :]
+            even = pair[p - first, half, pl.ds(0, rows, stride=2), :]
+            odd = pair[p - first, half, pl.ds(1, rows, stride=2), :]
             t[p - first, :, lanes] = even + odd
     count = len(planes)
-    full = dot(t[...].reshape(count * 24, 256), pair_matrix(256, 128, 0.125))
-    full = full.reshape(count, 24, 128)
-    mask = row_mask((24, 128), at[1] * 8 - 8, ny // 2)
+    full = dot(t[...].reshape(count * rows, 256), pair_matrix(256, 128, 0.125))
+    full = full.reshape(count, rows, 128)
+    mask = row_mask((rows, 128), at[1] * 8 + 4 - rows // 2, ny // 2)
     for p in planes:
         b1[p] = wall(at, nx, 1, p, full[p - first] * mask)
 
 
-def coarsen_level1(at, nx, ny, b1, u, planes, b2_out, s1, t1):
-    mask = row_mask((24, 128), at[1] * 8 - 8, ny // 2)
+def smooth_level1(at, nx, ny, b1, u, planes):
+    rows = b1.ref.shape[1]
+    mask = row_mask((rows, 128), at[1] * 8 + 4 - rows // 2, ny // 2)
     first_smooth(b1, u, planes, 4.0 * SIDE, mask, at, nx, 1)
+
+
+def coarsen_level1(b1, u, b2_out, s1, t1):
+    start = b1.ref.shape[1] // 2 - 4
     t1[...] = jnp.zeros_like(t1)
     for k in range(4):
         total = 0.0
@@ -404,7 +453,7 @@
             c, around = u.beside(p)
             total = total + (b1[p] - 0.25 * (6.0 * c - around))
         s1[k] = total
-        t1[k, 0:4, :] = s1[k, pl.ds(8, 4, stride=2), :] + s1[k, pl.ds(9, 4, stride=2), :]
+        t1[k, 0:4, :] = s1[k, pl.ds(start, 4, stride=2), :] + s1[k, pl.ds(start + 1, 4, stride=2), :]
     small = dot(t1[...].reshape(32, 128), pair_matrix(128, 128, 0.125)).reshape(4, 8, 128)
     tile = jnp.concatenate([small[0, 0:4], small[1, 0:4]], axis=0) + roll(
         jnp.concatenate([small[2, 0:4], small[3, 0:4]], axis=0), 64, 1
@@ -424,9 +473,40 @@
 
 
 E0, R1, E1, R2, E2, R3 = reach(KEEP)
-
-
-def first_down_body(nx, ny, at, mid, chip, link, b_out, v_out, b1_out, u_out, b2_out, b, v, pair, t, s1, t1):
+SHORT = 6
+
+
+def first_source_body(nx, ny, at, mid, chip, link, b2_out, b, v, b1, u, pair, t, s1, t1):
+    lower, upper = pick_sides(at, chip, link)
+    b, v = Field(b, SHORT), Field(v, SHORT - 1)
+    for p in range(-SHORT, 16 + SHORT):
+        b.ref[p + SHORT, 0:8, :] = lower(p + HALO, slice(8, 16))
+        b.ref[p + SHORT, 8:24, :] = mid[p + HALO]
+        b.ref[p + SHORT, 24:32, :] = upper(p + HALO, slice(0, 8))
+    mask = row_mask((32, 256), at[1] * 16 - 8, ny)
+    first_smooth(b, v, range(1 - SHORT, 15 + SHORT), SIDE, mask, at, nx, 0)
+    b1, u = Field(b1, 2), Field(u, 1)
+    coarsen_level0(at, nx, ny, b, v, b1, range(-2, 10), pair, t)
+    smooth_level1(at, nx, ny, b1, u, range(-1, 9))
+    coarsen_level1(b1, u, b2_out, s1, t1)
+
+
+def first_source(nx, ny, at, mid, chip, link):
+    scratch = [
+        around_block(16, SHORT, 32, 256),
+        around_block(16, SHORT - 1, 32, 256),
+        (12, 16, 128),
+        (10, 16, 128),
+        (12, 2, 32, 128),
+        (12, 16, 256),
+        (4, 16, 128),
+        (4, 8, 128),
+    ]
+    args = [at, mid, chip, link]
+    return call(functools.partial(first_source_body, nx, ny), [tiles(ny)], scratch, args, 6000000)[0]
+
+
+def first_down_body(nx, ny, at, mid, chip, link, b_out, v_out, b1_out, u_out, b, v, pair, t):
     lower, upper = pick_sides(at, chip, link)
     for i in range(16 + 2 * HALO):
         b[i, 0:16, :] = lower(i)
@@ -437,12 +517,12 @@
     first_smooth(b, v, range(1 - HALO, 15 + HALO), SIDE, mask, at, nx, 0)
     v_out, b_out = Field(v_out, E0), Field(b_out, E0 - 1)
     for p in range(-E0, 16 + E0):
-        v_out[p] = v[p]
+        v_out[p] = v[p][8:40, :]
     for p in range(1 - E0, 15 + E0):
-        b_out[p] = b[p]
+        b_out[p] = b[p][8:40, :]
     b1, u = Field(b1_out, E1 + 1), Field(u_out, E1)
     coarsen_level0(at, nx, ny, b, v, b1, range(-E1 - 1, 9 + E1), pair, t)
-    coarsen_level1(at, nx, ny, b1, u, range(-E1, 8 + E1), b2_out, s1, t1)
+    smooth_level1(at, nx, ny, b1, u, range(-E1, 8 + E1))
 
 
 def tiles(ny):
@@ -456,19 +536,16 @@
 def first_down(nx, ny, at, mid, chip, link):
     level1 = around_block(8, E1 + 1, 24, 128)
     outs = [
-        around_block(16, E0 - 1, 48, 256),
-        around_block(16, E0, 48, 256),
+        around_block(16, E0 - 1, 32, 256),
+        around_block(16, E0, 32, 256),
         level1,
         around_block(8, E1, 24, 128),
-        tiles(ny),
     ]
     scratch = [
         around_block(16, HALO, 48, 256),
         around_block(16, HALO - 1, 48, 256),
         (level1[0], 2, 48, 128),
         (level1[0], 24, 256),
-        (4, 24, 128),
-        (4, 8, 128),
     ]
     args = [at, mid, chip, link]
     return call(functools.partial(first_down_body, nx, ny), outs, scratch, args, 20000000)
@@ -481,7 +558,8 @@
         b1_out[i, 8:16, :] = mid[i]
         b1_out[i, 16:24, :] = upper(i)
     b1, u = Field(b1_out, NEAR), Field(u_out, NEAR - 1)
-    coarsen_level1(at, nx, ny, b1, u, range(1 - NEAR, 7 + NEAR), b2_out, s1, t1)
+    smooth_level1(at, nx, ny, b1, u, range(1 - NEAR, 7 + NEAR))
+    coarsen_level1(b1, u, b2_out, s1, t1)
 
 
 def second_down(nx, ny, at, mid, chip, link):
@@ -603,15 +681,15 @@
     sweep(m1, n1, b1, range(1 - e1, 7 + e1), 4.0, mask1, at, nx, 1)
     sweep(n1, m1, b1, range(2 - e1, 6 + e1), 4.0, mask1, at, nx, 1)
     planes = range(-r1, 8 + r1)
-    flat = jnp.concatenate([m1[p] for p in planes], axis=0)
-    spread = dot(flat, copy_matrix(128, 256)).reshape(len(planes), 24, 256)
-    mask0 = row_mask((48, 256), at[1] * 16 - 16, ny)
+    flat = jnp.concatenate([m1[p][4:20, :] for p in planes], axis=0)
+    spread = dot(flat, copy_matrix(128, 256)).reshape(len(planes), 16, 256)
+    mask0 = row_mask((32, 256), at[1] * 16 - 8, ny)
     m0, n0 = Field(m0, e0), Field(n0, e0)
     for i, p in enumerate(planes):
         for half in range(2):
             value = spread[i, :, 128 * half : 128 * half + 128]
-            dup[i, half, pl.ds(0, 24, stride=2), :] = value
-            dup[i, half, pl.ds(1, 24, stride=2), :] = value
+            dup[i, half, pl.ds(0, 16, stride=2), :] = value
+            dup[i, half, pl.ds(1, 16, stride=2), :] = value
         value = jnp.concatenate([dup[i, 0], dup[i, 1]], axis=1) * mask0
         for q in (2 * p, 2 * p + 1):
             if -e0 <= q < 16 + e0:
@@ -626,34 +704,34 @@
 def climb_scratch(extra):
     e0, r1, e1, r2, _, _ = reach(extra)
     level1 = around_block(8, e1, 24, 128)
-    level0 = around_block(16, e0, 48, 256)
-    return [level1, level1, level0, level0, (max(8 + 2 * r1, 4 + 2 * r2), 2, 48, 128)]
+    level0 = around_block(16, e0, 32, 256)
+    return [level1, level1, level0, level0, (max(8 + 2 * r1, 4 + 2 * r2), 2, 32, 128)]
 
 
 def turn_body(nx, ny, at, here, before, after, b1, u, b, v_down, v_out, wider, low, high, own, pair, t, *scratch):
     v2 = solve_coarse(nx, ny, KEEP, at, (here, before, after), *scratch[:9])
     b = Field(b, E0 - 1)
     v = climb(nx, ny, KEEP, at, v2, Field(b1, E1 + 1), Field(u, E1), b, Field(v_down, E0), *scratch[9:])
-    mask = row_mask((48, 256), at[1] * 16 - 16, ny)
+    mask = row_mask((32, 256), at[1] * 16 - 8, ny)
     once, twice = Field(scratch[12], E0), Field(v_out, KEEP - 2)
     sweep(v, once, b, range(1 - KEEP, 15 + KEEP), 1, mask, at, nx, 0)
     sweep(once, twice, b, range(2 - KEEP, 14 + KEEP), 1, mask, at, nx, 0)
     coarsen_level0(at, nx, ny, b, twice, Field(own, 0), range(8), pair, t)
     for i in range(8):
-        wider[NEAR + i] = own[i, 8:16, :]
+        wider[NEAR + i] = own[i, 4:12, :]
     for i in range(NEAR):
-        low[i] = own[i, 8:16, :]
-        high[i] = own[8 - NEAR + i, 8:16, :]
+        low[i] = own[i, 4:12, :]
+        high[i] = own[8 - NEAR + i, 4:12, :]
 
 
 def turn(nx, ny, at, coarse, b1, u, b, v_down):
     outs = [
-        around_block(16, KEEP - 2, 48, 256),
+        around_block(16, KEEP - 2, 32, 256),
         around_block(8, NEAR, 8, 128),
         (NEAR, 8, 128),
         (NEAR, 8, 128),
     ]
-    scratch = [(8, 24, 128), (8, 2, 48, 128), (8, 24, 256)]
+    scratch = [(8, 16, 128), (8, 2, 32, 128), (8, 16, 256)]
     scratch += coarse_scratch(ny, KEEP) + climb_scratch(KEEP)
     args = [at, *coarse, b1, u, b, v_down]
     return call(functools.partial(turn_body, nx, ny), outs, scratch, args, 30000000)
@@ -665,7 +743,7 @@
     v = climb(nx, ny, 0, at, v2, Field(b1, NEAR), Field(u, NEAR - 1), b, v_down, *scratch[9:])
     for p in range(16):
         c, around = v.beside(p)
-        out[p] = (0.2 * c + SIDE * (around + b[p]))[16:32, :]
+        out[p] = (0.2 * c + SIDE * (around + b[p]))[8:24, :]
 
 
 def finish(nx, ny, at, coarse, b1, u, b, v_down):
@@ -723,8 +801,10 @@
     link = swapped(jnp.where(odd, final, first), 1)
     chip = swapped(jnp.where(odd, first, final), 0)
     sends = force(nx, ny, at, mid, chip, link, velocity, xl, xh, v_chip, v_link)
-    b, v, b1, u, b2 = first_down(nx, ny, at, *surround(*sends))
-    v, *sends = turn(nx, ny, at, spread_coarse(b2), b1, u, b, v)
+    parts = surround(*sends)
+    coarse = spread_coarse(first_source(nx, ny, at, *parts))
+    b, v, b1, u = first_down(nx, ny, at, *parts)
+    v, *sends = turn(nx, ny, at, coarse, b1, u, b, v)
     b1, u, b2 = second_down(nx, ny, at, *surround(*sends))
     pressure = finish(nx, ny, at, spread_coarse(b2), b1, u, b, v)
     return (moved, pressure)

time: 162 us -> 158 us (0.975)
  the two profiles are of different devices: /device:TPU:384 before, /device:TPU:256 now
where the time goes in v4:
time: 158 us; the launch traced here: 157 us
  starting transfers between devices  78.4 us (50%)
  blocking collectives  29.2 us (18%)
  Pallas kernels  27.2 us (17%)
  waiting for transfers between devices  21.3 us (13%)
    ppermute x12, starting transfers between devices, shifted(): lax.ppermute(array, axis, [(i, i + step) for i in range(count) if 0 <= i...  55.9 us
    all_to_all x2, blocking collectives, spread_coarse(): lax.all_to_all(b2, ('wide', 'narrow'), 0, 0, axis_index_groups=groups)  29.2 us
    pallas_call x7, Pallas kernels, call(): pl.pallas_call(body, out_shape=[jax.ShapeDtypeStruct(s, F32) for s in out...  25.2 us
    ppermute x8, starting transfers between devices, swapped(): return lax.ppermute(array, 'narrow', pairs + [(j, i) for i, j in pairs])  22.4 us
    ppermute x12, waiting for transfers between devices, shifted(): lax.ppermute(array, axis, [(i, i + step) for i in range(count) if 0 <= i...  17.2 us
    ppermute x8, waiting for transfers between devices, swapped(): return lax.ppermute(array, 'narrow', pairs + [(j, i) for i, j in pairs])  4.09 us
  transfers between devices with their start and end apart: 20, of which 12 were waited for; matrix products, arithmetic and copies ran while one was open for 0% of the time, Pallas kernels for 2%

profile of v4, /device:TPU:256, one launch (start us, length us, event | category | flops | bytes accessed | tf_op | source)
XLA Modules:
  0.0 157.1 jit_solution(6373254965480885256)
XLA Ops:
  0.6 0.0 copy-start
  0.6 0.1 pad_add_fusion.at
  0.7 1.9 %shard_map.50 = (f32[16,16,256]{2,1,0:T(8,128)S(1)}, f32[4,16,256]{2,1,0:T(8,128)S(1)}, f32[4,16,256]{2,1,0:T(8,128)S(1)}, f32[16,4,256]{2,1,0:T(4,128)S(1)}, f32[16,4,256]{2,1,0:T(4,128)S(1)}) custom-call(s32[2]{0:T(128)S(1)} %pad_add_fusion.at, s32[16,16,256]{2,1,0:T(8,128)} %phase.1, f32[16,16,256]{2,1,0:T(8,128)} %distance.1, f32[3,16,16,256]{3,2,1,0:T(8,128)} %velocity.5), custom_call_target="tpu_custom_call" | custom-call | flops 1000000 | bytes 1000000 | tf_op jit(solution)/shard_map/pallas_call | solution.py:167
  2.6 3.4 %collective-permute-start = (f32[4,16,256]{2,1,0:T(8,128)S(1)}, f32[4,16,256]{2,1,0:T(8,128)S(1)}, u32[]{:S(2)}, u32[]{:S(2)}) collective-permute-start(f32[4,16,256]{2,1,0:T(8,128)S(1)} %get-tuple-element.26), channel_id=1, source_target_pairs={{0,8},{8,16},{16,24},{24,32},{32,40},{40,48},{48,56},{56,64},{64,7... | collective-permute-start | bytes 196616 | tf_op jit(solution)/shard_map/ppermute | solution.py:757
  6.0 5.8 %collective-permute-start.1 = (f32[4,16,256]{2,1,0:T(8,128)S(1)}, f32[4,16,256]{2,1,0:T(8,128)S(1)}, u32[]{:S(2)}, u32[]{:S(2)}) collective-permute-start(f32[4,16,256]{2,1,0:T(8,128)S(1)} %get-tuple-element.27), channel_id=1, source_target_pairs={{8,0},{16,8},{24,16},{32,24},{40,32},{48,40},{56,48},{64,56},{72,6... | collective-permute-start | bytes 196616 | tf_op jit(solution)/shard_map/ppermute | solution.py:757
  11.8 1.9 %collective-permute-start.2 = (f32[16,4,256]{2,1,0:T(4,128)S(1)}, f32[16,4,256]{2,1,0:T(4,128)S(1)}, u32[]{:S(2)}, u32[]{:S(2)}) collective-permute-start(f32[16,4,256]{2,1,0:T(4,128)S(1)} %get-tuple-element.28), channel_id=1, source_target_pairs={{0,1},{2,3},{4,5},{6,7},{1,0},{3,2},{5,4},{7,6},{8,9},{10,11},{12,... | collective-permute-start | bytes 196616 | tf_op jit(solution)/shard_map/ppermute | solution.py:765
  13.7 0.7 collective-permute-start.3
  14.4 0.0 collective-permute-done.xl
  14.4 0.5 collective-permute-done.2.chip.v_chip
  15.0 0.0 collective-permute-done.3.link.v_link
  15.0 5.5 %shard_map.51 = (f32[16,16,256]{2,1,0:T(8,128)}, f32[22,16,256]{2,1,0:T(8,128)S(1)}, f32[3,16,256]{2,1,0:T(8,128)S(1)}, f32[3,16,256]{2,1,0:T(8,128)S(1)}) custom-call(s32[2]{0:T(128)S(1)} %pad_add_fusion.at, f32[16,16,256]{2,1,0:T(8,128)S(1)} %get-tuple-element.25.psi, f32[3,16,16,256]{3,2,1,0:T(8,128)S(1)} %copy-done, ...), custom_call_target="tpu_custom_call" | custom-call | flops 10000000 | bytes 4000000 | tf_op jit(solution)/shard_map/pallas_call | solution.py:91
  20.5 1.9 %collective-permute-start.4 = (f32[3,16,256]{2,1,0:T(8,128)S(1)}, f32[3,16,256]{2,1,0:T(8,128)S(1)}, u32[]{:S(2)}, u32[]{:S(2)}) collective-permute-start(f32[3,16,256]{2,1,0:T(8,128)S(1)} %get-tuple-element.32), channel_id=1, source_target_pairs={{0,8},{8,16},{16,24},{24,32},{32,40},{40,48},{48,56},{56,64},{64,7... | collective-permute-start | bytes 147464 | tf_op jit(solution)/shard_map/ppermute | solution.py:757
  22.4 7.2 %collective-permute-start.5 = (f32[3,16,256]{2,1,0:T(8,128)S(1)}, f32[3,16,256]{2,1,0:T(8,128)S(1)}, u32[]{:S(2)}, u32[]{:S(2)}) collective-permute-start(f32[3,16,256]{2,1,0:T(8,128)S(1)} %get-tuple-element.33), channel_id=1, source_target_pairs={{8,0},{16,8},{24,16},{32,24},{40,32},{48,40},{56,48},{64,56},{72,6... | collective-permute-start | bytes 147464 | tf_op jit(solution)/shard_map/ppermute | solution.py:757
  29.6 0.1 collective-permute-done.4
  29.8 1.6 %collective-permute-done.5 = f32[3,16,256]{2,1,0:T(8,128)S(1)} collective-permute-done((f32[3,16,256]{2,1,0:T(8,128)S(1)}, f32[3,16,256]{2,1,0:T(8,128)S(1)}, u32[]{:S(2)}, u32[]{:S(2)}) %collective-permute-start.5) | collective-permute-done | bytes 49184 | tf_op jit(solution)/shard_map/ppermute | solution.py:757
  31.4 0.7 collective-permute-start.7
  32.1 9.2 %collective-permute-start.6 = (f32[22,3,256]{2,1,0:T(4,128)S(1)}, f32[22,3,256]{2,1,0:T(4,128)S(1)}, u32[]{:S(2)}, u32[]{:S(2)}) collective-permute-start(f32[22,3,256]{2,1,0:T(4,128)S(1)} %get-tuple-element.49), channel_id=1, source_target_pairs={{0,1},{2,3},{4,5},{6,7},{1,0},{3,2},{5,4},{7,6},{8,9},{10,11},{12,... | collective-permute-start | bytes 202760 | tf_op jit(solution)/shard_map/ppermute | solution.py:765
  41.3 0.9 collective-permute-done.6.chip
  42.2 2.7 %shard_map.52 = (f32[44,16,256]{2,1,0:T(8,128)S(1)}, f32[14,16,256]{2,1,0:T(8,128)S(1)}, f32[14,16,256]{2,1,0:T(8,128)S(1)}) custom-call(s32[2]{0:T(128)S(1)} %pad_add_fusion.at, f32[22,16,256]{2,1,0:T(8,128)S(1)} %constant_dynamic-update-slice_fusion.4.mid, f32[22,3,256]{2,1,0:T(4,128)S(1)} %collective-permute-done.6.chip, ...), custom_call_target="tpu_custom_call" | custom-call | flops 10000000 | bytes 4000000 | tf_op jit(solution)/shard_map/pallas_call | solution.py:91
  44.9 1.9 %collective-permute-start.8 = (f32[14,16,256]{2,1,0:T(8,128)S(1)}, f32[14,16,256]{2,1,0:T(8,128)S(1)}, u32[]{:S(2)}, u32[]{:S(2)}) collective-permute-start(f32[14,16,256]{2,1,0:T(8,128)S(1)} %get-tuple-element.35), channel_id=1, source_target_pairs={{0,8},{8,16},{16,24},{24,32},{32,40},{40,48},{48,56},{56,64},{64,7... | collective-permute-start | bytes 688136 | tf_op jit(solution)/shard_map/ppermute | solution.py:757
  46.9 7.6 %collective-permute-start.9 = (f32[14,16,256]{2,1,0:T(8,128)S(1)}, f32[14,16,256]{2,1,0:T(8,128)S(1)}, u32[]{:S(2)}, u32[]{:S(2)}) collective-permute-start(f32[14,16,256]{2,1,0:T(8,128)S(1)} %get-tuple-element.36), channel_id=1, source_target_pairs={{8,0},{16,8},{24,16},{32,24},{40,32},{48,40},{56,48},{64,56},{72,6... | collective-permute-start | bytes 688136 | tf_op jit(solution)/shard_map/ppermute | solution.py:757
  54.4 4.2 %collective-permute-done.8 = f32[14,16,256]{2,1,0:T(8,128)S(1)} collective-permute-done((f32[14,16,256]{2,1,0:T(8,128)S(1)}, f32[14,16,256]{2,1,0:T(8,128)S(1)}, u32[]{:S(2)}, u32[]{:S(2)}) %collective-permute-start.8) | collective-permute-done | bytes 229408 | tf_op jit(solution)/shard_map/ppermute | solution.py:757
  58.6 1.2 collective-permute-done.9
  59.8 0.7 collective-permute-start.11
  60.5 4.8 %collective-permute-start.10 = (f32[44,16,256]{2,1,0:T(8,128)S(1)}, f32[44,16,256]{2,1,0:T(8,128)S(1)}, u32[]{:S(2)}, u32[]{:S(2)}) collective-permute-start(f32[44,16,256]{2,1,0:T(8,128)S(1)} %constant_dynamic-update-slice_fusion.2.mid), channel_id=1, source_target_pairs={{0,1},{2,3},{4,5},{6,7},{1,0},{3,2},{5,4},{7,6},{8,9},{10,11},{12,... | collective-permute-start | bytes 2162696 | tf_op jit(solution)/shard_map/ppermute | solution.py:765
  65.3 0.0 collective-permute-done.11.link
  65.4 1.8 %collective-permute-done.10.chip = f32[44,16,256]{2,1,0:T(8,128)S(1)} collective-permute-done((f32[44,16,256]{2,1,0:T(8,128)S(1)}, f32[44,16,256]{2,1,0:T(8,128)S(1)}, u32[]{:S(2)}, u32[]{:S(2)}) %collective-permute-start.10) | collective-permute-done | bytes 720928 | tf_op jit(solution)/shard_map/ppermute | solution.py:765
  67.1 2.4 %shard_map.53 = f32[32,8,128]{2,1,0:T(8,128)S(1)} custom-call(s32[2]{0:T(128)S(1)} %pad_add_fusion.at, f32[44,16,256]{2,1,0:T(8,128)S(1)} %constant_dynamic-update-slice_fusion.2.mid, f32[44,16,256]{2,1,0:T(8,128)S(1)} %collective-permute-done.10.chip, f32[44,16,256]{2,1,0:T(8,128)S(1)} %collective-permute-done.11.link), custom_call_target="tpu_custom_call" | custom-call | flops 6000000 | bytes 4000000 | tf_op jit(solution)/shard_map/pallas_call | solution.py:91
  69.6 17.5 %all_to_all.10.here = f32[32,8,128]{2,1,0:T(8,128)S(1)} all-to-all(f32[32,8,128]{2,1,0:T(8,128)S(1)} %shard_map.53), channel_id=1, replica_groups={{0,1,2,3,4,5,6,7,8,9,10,11,12,13,14,15,16,17,18,19,20,21,22,23,24,25,26..., dimensions={0} | all-to-all | bytes 262144 | tf_op jit(solution)/shard_map/all_to_all | solution.py:784
  87.1 7.7 %collective-permute-start.13 = (f32[32,8,128]{2,1,0:T(8,128)S(1)}, f32[32,8,128]{2,1,0:T(8,128)S(1)}, u32[]{:S(2)}, u32[]{:S(2)}) collective-permute-start(f32[32,8,128]{2,1,0:T(8,128)S(1)} %all_to_all.10.here), channel_id=1, source_target_pairs={{32,0},{40,8},{48,16},{56,24},{64,32},{72,40},{80,48},{88,56},{96,... | collective-permute-start | bytes 393224 | tf_op jit(solution)/shard_map/ppermute | solution.py:757
  94.8 2.1 %collective-permute-start.12 = (f32[32,8,128]{2,1,0:T(8,128)S(1)}, f32[32,8,128]{2,1,0:T(8,128)S(1)}, u32[]{:S(2)}, u32[]{:S(2)}) collective-permute-start(f32[32,8,128]{2,1,0:T(8,128)S(1)} %all_to_all.10.here), channel_id=1, source_target_pairs={{0,32},{8,40},{16,48},{24,56},{32,64},{40,72},{48,80},{56,88},{64,... | collective-permute-start | bytes 393224 | tf_op jit(solution)/shard_map/ppermute | solution.py:757
  96.9 3.9 %shard_map.54 = (f32[26,32,256]{2,1,0:T(8,128)S(1)}, f32[28,32,256]{2,1,0:T(8,128)S(1)}, f32[20,24,128]{2,1,0:T(8,128)S(1)}, f32[18,24,128]{2,1,0:T(8,128)S(1)}) custom-call(s32[2]{0:T(128)S(1)} %pad_add_fusion.at, f32[44,16,256]{2,1,0:T(8,128)S(1)} %constant_dynamic-update-slice_fusion.2.mid, f32[44,16,256]{2,1,0:T(8,128)S(1)} %collective-permute-done.10.chip, ...), custom_call_target="tpu_custom_call" | custom-call | flops 20000000 | bytes 4000000 | tf_op jit(solution)/shard_map/pallas_call | solution.py:91
  100.8 2.3 %collective-permute-done.12.before = f32[32,8,128]{2,1,0:T(8,128)S(1)} collective-permute-done((f32[32,8,128]{2,1,0:T(8,128)S(1)}, f32[32,8,128]{2,1,0:T(8,128)S(1)}, u32[]{:S(2)}, u32[]{:S(2)}) %collective-permute-start.12) | collective-permute-done | bytes 131104 | tf_op jit(solution)/shard_map/ppermute | solution.py:757
  103.2 5.7 %shard_map.55 = (f32[20,32,256]{2,1,0:T(8,128)S(1)}, f32[16,8,128]{2,1,0:T(8,128)S(1)}, f32[4,8,128]{2,1,0:T(8,128)S(1)}, f32[4,8,128]{2,1,0:T(8,128)S(1)}) custom-call(s32[2]{0:T(128)S(1)} %pad_add_fusion.at, f32[32,8,128]{2,1,0:T(8,128)S(1)} %all_to_all.10.here, f32[32,8,128]{2,1,0:T(8,128)S(1)} %collective-permute-done.12.before, ...), custom_call_target="tpu_custom_call" | custom-call | flops 30000000 | bytes 4000000 | tf_op jit(solution)/shard_map/pallas_call | solution.py:91
  108.8 2.5 %collective-permute-start.14 = (f32[4,8,128]{2,1,0:T(8,128)S(1)}, f32[4,8,128]{2,1,0:T(8,128)S(1)}, u32[]{:S(2)}, u32[]{:S(2)}) collective-permute-start(f32[4,8,128]{2,1,0:T(8,128)S(1)} %get-tuple-element.42), channel_id=1, source_target_pairs={{0,8},{8,16},{16,24},{24,32},{32,40},{40,48},{48,56},{56,64},{64,7... | collective-permute-start | bytes 49160 | tf_op jit(solution)/shard_map/ppermute | solution.py:757
  111.3 6.7 %collective-permute-start.15 = (f32[4,8,128]{2,1,0:T(8,128)S(1)}, f32[4,8,128]{2,1,0:T(8,128)S(1)}, u32[]{:S(2)}, u32[]{:S(2)}) collective-permute-start(f32[4,8,128]{2,1,0:T(8,128)S(1)} %get-tuple-element.43), channel_id=1, source_target_pairs={{8,0},{16,8},{24,16},{32,24},{40,32},{48,40},{56,48},{64,56},{72,6... | collective-permute-start | bytes 49160 | tf_op jit(solution)/shard_map/ppermute | solution.py:757
  118.0 0.0 collective-permute-done.14
  118.0 1.4 collective-permute-done.15
  119.4 0.7 collective-permute-start.17
  120.1 3.8 %collective-permute-start.16 = (f32[16,8,128]{2,1,0:T(8,128)S(1)}, f32[16,8,128]{2,1,0:T(8,128)S(1)}, u32[]{:S(2)}, u32[]{:S(2)}) collective-permute-start(f32[16,8,128]{2,1,0:T(8,128)S(1)} %constant_dynamic-update-slice_fusion.mid), channel_id=1, source_target_pairs={{0,1},{2,3},{4,5},{6,7},{1,0},{3,2},{5,4},{7,6},{8,9},{10,11},{12,... | collective-permute-start | bytes 196616 | tf_op jit(solution)/shard_map/ppermute | solution.py:765
  123.9 0.9 collective-permute-done.16.chip
  124.8 1.0 shard_map.56
  125.8 11.7 %all_to_all.11.here = f32[32,8,128]{2,1,0:T(8,128)S(1)} all-to-all(f32[32,8,128]{2,1,0:T(8,128)S(1)} %get-tuple-element.44), channel_id=1, replica_groups={{0,1,2,3,4,5,6,7,8,9,10,11,12,13,14,15,16,17,18,19,20,21,22,23,24,25,26..., dimensions={0} | all-to-all | bytes 262144 | tf_op jit(solution)/shard_map/all_to_all | solution.py:784
  137.5 7.3 %collective-permute-start.19 = (f32[32,8,128]{2,1,0:T(8,128)S(1)}, f32[32,8,128]{2,1,0:T(8,128)S(1)}, u32[]{:S(2)}, u32[]{:S(2)}) collective-permute-start(f32[32,8,128]{2,1,0:T(8,128)S(1)} %all_to_all.11.here), channel_id=1, source_target_pairs={{32,0},{40,8},{48,16},{56,24},{64,32},{72,40},{80,48},{88,56},{96,... | collective-permute-start | bytes 393224 | tf_op jit(solution)/shard_map/ppermute | solution.py:757
  144.7 1.9 %collective-permute-start.18 = (f32[32,8,128]{2,1,0:T(8,128)S(1)}, f32[32,8,128]{2,1,0:T(8,128)S(1)}, u32[]{:S(2)}, u32[]{:S(2)}) collective-permute-start(f32[32,8,128]{2,1,0:T(8,128)S(1)} %all_to_all.11.here), channel_id=1, source_target_pairs={{0,32},{8,40},{16,48},{24,56},{32,64},{40,72},{48,80},{56,88},{64,... | collective-permute-start | bytes 393224 | tf_op jit(solution)/shard_map/ppermute | solution.py:757
  146.7 1.1 collective-permute-done.19.after
  147.7 5.3 %collective-permute-done.18.before = f32[32,8,128]{2,1,0:T(8,128)S(1)} collective-permute-done((f32[32,8,128]{2,1,0:T(8,128)S(1)}, f32[32,8,128]{2,1,0:T(8,128)S(1)}, u32[]{:S(2)}, u32[]{:S(2)}) %collective-permute-start.18) | collective-permute-done | bytes 131104 | tf_op jit(solution)/shard_map/ppermute | solution.py:757
  153.1 4.0 %shard_map.57 = f32[16,16,256]{2,1,0:T(8,128)} custom-call(s32[2]{0:T(128)S(1)} %pad_add_fusion.at, f32[32,8,128]{2,1,0:T(8,128)S(1)} %all_to_all.11.here, f32[32,8,128]{2,1,0:T(8,128)S(1)} %collective-permute-done.18.before, f32[32,8,128]{2,1,0:T(8,128)S(1)} %collective-permute-done.19.after, f32[16,24,128]{2,1,0:T(8,128)S(1)} %get-tuple-element.45.b1, ...), custom_call_target="tpu_custom_call" | custom-call | flops 20000000 | bytes 4000000 | tf_op jit(solution)/shard_map/pallas_call | solution.py:91
  (12 shorter events, 0.1 us)
Async XLA Ops:
  0.6 14.3 %copy-start = (f32[3,16,16,256]{3,2,1,0:T(8,128)S(1)}, f32[3,16,16,256]{3,2,1,0:T(8,128)}, u32[]{:S(2)}) copy-start(f32[3,16,16,256]{3,2,1,0:T(8,128)} %velocity.5) | copy-start | bytes 2359300
  2.6 11.8 %collective-permute-start = (f32[4,16,256]{2,1,0:T(8,128)S(1)}, f32[4,16,256]{2,1,0:T(8,128)S(1)}, u32[]{:S(2)}, u32[]{:S(2)}) collective-permute-start(f32[4,16,256]{2,1,0:T(8,128)S(1)} %get-tuple-element.26), channel_id=1, source_target_pairs={{0,8},{8,16},{16,24},{24,32},{32,40},{40,48},{48,56},{56,64},{64,7... | collective-permute-start | bytes 196616 | tf_op jit(solution)/shard_map/ppermute | solution.py:757
  6.0 8.4 %collective-permute-start.1 = (f32[4,16,256]{2,1,0:T(8,128)S(1)}, f32[4,16,256]{2,1,0:T(8,128)S(1)}, u32[]{:S(2)}, u32[]{:S(2)}) collective-permute-start(f32[4,16,256]{2,1,0:T(8,128)S(1)} %get-tuple-element.27), channel_id=1, source_target_pairs={{8,0},{16,8},{24,16},{32,24},{40,32},{48,40},{56,48},{64,56},{72,6... | collective-permute-start | bytes 196616 | tf_op jit(solution)/shard_map/ppermute | solution.py:757
  11.8 3.1 %collective-permute-start.2 = (f32[16,4,256]{2,1,0:T(4,128)S(1)}, f32[16,4,256]{2,1,0:T(4,128)S(1)}, u32[]{:S(2)}, u32[]{:S(2)}) collective-permute-start(f32[16,4,256]{2,1,0:T(4,128)S(1)} %get-tuple-element.28), channel_id=1, source_target_pairs={{0,1},{2,3},{4,5},{6,7},{1,0},{3,2},{5,4},{7,6},{8,9},{10,11},{12,... | collective-permute-start | bytes 196616 | tf_op jit(solution)/shard_map/ppermute | solution.py:765
  13.7 1.2 collective-permute-start.3
  20.5 9.3 %collective-permute-start.4 = (f32[3,16,256]{2,1,0:T(8,128)S(1)}, f32[3,16,256]{2,1,0:T(8,128)S(1)}, u32[]{:S(2)}, u32[]{:S(2)}) collective-permute-start(f32[3,16,256]{2,1,0:T(8,128)S(1)} %get-tuple-element.32), channel_id=1, source_target_pairs={{0,8},{8,16},{16,24},{24,32},{32,40},{40,48},{48,56},{56,64},{64,7... | collective-permute-start | bytes 147464 | tf_op jit(solution)/shard_map/ppermute | solution.py:757
  22.4 9.0 %collective-permute-start.5 = (f32[3,16,256]{2,1,0:T(8,128)S(1)}, f32[3,16,256]{2,1,0:T(8,128)S(1)}, u32[]{:S(2)}, u32[]{:S(2)}) collective-permute-start(f32[3,16,256]{2,1,0:T(8,128)S(1)} %get-tuple-element.33), channel_id=1, source_target_pairs={{8,0},{16,8},{24,16},{32,24},{40,32},{48,40},{56,48},{64,56},{72,6... | collective-permute-start | bytes 147464 | tf_op jit(solution)/shard_map/ppermute | solution.py:757
  31.4 9.9 %collective-permute-start.7 = (f32[22,3,256]{2,1,0:T(4,128)S(1)}, f32[22,3,256]{2,1,0:T(4,128)S(1)}, u32[]{:S(2)}, u32[]{:S(2)}) collective-permute-start(f32[22,3,256]{2,1,0:T(4,128)S(1)} %get-tuple-element.48), channel_id=1, source_target_pairs={{1,2},{3,4},{5,6},{2,1},{4,3},{6,5},{9,10},{11,12},{13,14},{10,9},... | collective-permute-start | bytes 202760 | tf_op jit(solution)/shard_map/ppermute | solution.py:765
  32.1 10.1 %collective-permute-start.6 = (f32[22,3,256]{2,1,0:T(4,128)S(1)}, f32[22,3,256]{2,1,0:T(4,128)S(1)}, u32[]{:S(2)}, u32[]{:S(2)}) collective-permute-start(f32[22,3,256]{2,1,0:T(4,128)S(1)} %get-tuple-element.49), channel_id=1, source_target_pairs={{0,1},{2,3},{4,5},{6,7},{1,0},{3,2},{5,4},{7,6},{8,9},{10,11},{12,... | collective-permute-start | bytes 202760 | tf_op jit(solution)/shard_map/ppermute | solution.py:765
  44.9 13.7 %collective-permute-start.8 = (f32[14,16,256]{2,1,0:T(8,128)S(1)}, f32[14,16,256]{2,1,0:T(8,128)S(1)}, u32[]{:S(2)}, u32[]{:S(2)}) collective-permute-start(f32[14,16,256]{2,1,0:T(8,128)S(1)} %get-tuple-element.35), channel_id=1, source_target_pairs={{0,8},{8,16},{16,24},{24,32},{32,40},{40,48},{48,56},{56,64},{64,7... | collective-permute-start | bytes 688136 | tf_op jit(solution)/shard_map/ppermute | solution.py:757
  46.9 12.9 %collective-permute-start.9 = (f32[14,16,256]{2,1,0:T(8,128)S(1)}, f32[14,16,256]{2,1,0:T(8,128)S(1)}, u32[]{:S(2)}, u32[]{:S(2)}) collective-permute-start(f32[14,16,256]{2,1,0:T(8,128)S(1)} %get-tuple-element.36), channel_id=1, source_target_pairs={{8,0},{16,8},{24,16},{32,24},{40,32},{48,40},{56,48},{64,56},{72,6... | collective-permute-start | bytes 688136 | tf_op jit(solution)/shard_map/ppermute | solution.py:757
  59.8 5.5 %collective-permute-start.11 = (f32[44,16,256]{2,1,0:T(8,128)S(1)}, f32[44,16,256]{2,1,0:T(8,128)S(1)}, u32[]{:S(2)}, u32[]{:S(2)}) collective-permute-start(f32[44,16,256]{2,1,0:T(8,128)S(1)} %constant_dynamic-update-slice_fusion.2.mid), channel_id=1, source_target_pairs={{1,2},{3,4},{5,6},{2,1},{4,3},{6,5},{9,10},{11,12},{13,14},{10,9},... | collective-permute-start | bytes 2162696 | tf_op jit(solution)/shard_map/ppermute | solution.py:765
  60.5 6.6 %collective-permute-start.10 = (f32[44,16,256]{2,1,0:T(8,128)S(1)}, f32[44,16,256]{2,1,0:T(8,128)S(1)}, u32[]{:S(2)}, u32[]{:S(2)}) collective-permute-start(f32[44,16,256]{2,1,0:T(8,128)S(1)} %constant_dynamic-update-slice_fusion.2.mid), channel_id=1, source_target_pairs={{0,1},{2,3},{4,5},{6,7},{1,0},{3,2},{5,4},{7,6},{8,9},{10,11},{12,... | collective-permute-start | bytes 2162696 | tf_op jit(solution)/shard_map/ppermute | solution.py:765
  87.1 13.7 %collective-permute-start.13 = (f32[32,8,128]{2,1,0:T(8,128)S(1)}, f32[32,8,128]{2,1,0:T(8,128)S(1)}, u32[]{:S(2)}, u32[]{:S(2)}) collective-permute-start(f32[32,8,128]{2,1,0:T(8,128)S(1)} %all_to_all.10.here), channel_id=1, source_target_pairs={{32,0},{40,8},{48,16},{56,24},{64,32},{72,40},{80,48},{88,56},{96,... | collective-permute-start | bytes 393224 | tf_op jit(solution)/shard_map/ppermute | solution.py:757
  94.8 8.3 %collective-permute-start.12 = (f32[32,8,128]{2,1,0:T(8,128)S(1)}, f32[32,8,128]{2,1,0:T(8,128)S(1)}, u32[]{:S(2)}, u32[]{:S(2)}) collective-permute-start(f32[32,8,128]{2,1,0:T(8,128)S(1)} %all_to_all.10.here), channel_id=1, source_target_pairs={{0,32},{8,40},{16,48},{24,56},{32,64},{40,72},{48,80},{56,88},{64,... | collective-permute-start | bytes 393224 | tf_op jit(solution)/shard_map/ppermute | solution.py:757
  108.8 9.2 %collective-permute-start.14 = (f32[4,8,128]{2,1,0:T(8,128)S(1)}, f32[4,8,128]{2,1,0:T(8,128)S(1)}, u32[]{:S(2)}, u32[]{:S(2)}) collective-permute-start(f32[4,8,128]{2,1,0:T(8,128)S(1)} %get-tuple-element.42), channel_id=1, source_target_pairs={{0,8},{8,16},{16,24},{24,32},{32,40},{40,48},{48,56},{56,64},{64,7... | collective-permute-start | bytes 49160 | tf_op jit(solution)/shard_map/ppermute | solution.py:757
  111.3 8.1 %collective-permute-start.15 = (f32[4,8,128]{2,1,0:T(8,128)S(1)}, f32[4,8,128]{2,1,0:T(8,128)S(1)}, u32[]{:S(2)}, u32[]{:S(2)}) collective-permute-start(f32[4,8,128]{2,1,0:T(8,128)S(1)} %get-tuple-element.43), channel_id=1, source_target_pairs={{8,0},{16,8},{24,16},{32,24},{40,32},{48,40},{56,48},{64,56},{72,6... | collective-permute-start | bytes 49160 | tf_op jit(solution)/shard_map/ppermute | solution.py:757
  119.4 4.5 %collective-permute-start.17 = (f32[16,8,128]{2,1,0:T(8,128)S(1)}, f32[16,8,128]{2,1,0:T(8,128)S(1)}, u32[]{:S(2)}, u32[]{:S(2)}) collective-permute-start(f32[16,8,128]{2,1,0:T(8,128)S(1)} %constant_dynamic-update-slice_fusion.mid), channel_id=1, source_target_pairs={{1,2},{3,4},{5,6},{2,1},{4,3},{6,5},{9,10},{11,12},{13,14},{10,9},... | collective-permute-start | bytes 196616 | tf_op jit(solution)/shard_map/ppermute | solution.py:765
  120.1 4.7 %collective-permute-start.16 = (f32[16,8,128]{2,1,0:T(8,128)S(1)}, f32[16,8,128]{2,1,0:T(8,128)S(1)}, u32[]{:S(2)}, u32[]{:S(2)}) collective-permute-start(f32[16,8,128]{2,1,0:T(8,128)S(1)} %constant_dynamic-update-slice_fusion.mid), channel_id=1, source_target_pairs={{0,1},{2,3},{4,5},{6,7},{1,0},{3,2},{5,4},{7,6},{8,9},{10,11},{12,... | collective-permute-start | bytes 196616 | tf_op jit(solution)/shard_map/ppermute | solution.py:765
  137.5 10.3 %collective-permute-start.19 = (f32[32,8,128]{2,1,0:T(8,128)S(1)}, f32[32,8,128]{2,1,0:T(8,128)S(1)}, u32[]{:S(2)}, u32[]{:S(2)}) collective-permute-start(f32[32,8,128]{2,1,0:T(8,128)S(1)} %all_to_all.11.here), channel_id=1, source_target_pairs={{32,0},{40,8},{48,16},{56,24},{64,32},{72,40},{80,48},{88,56},{96,... | collective-permute-start | bytes 393224 | tf_op jit(solution)/shard_map/ppermute | solution.py:757
  144.7 8.3 %collective-permute-start.18 = (f32[32,8,128]{2,1,0:T(8,128)S(1)}, f32[32,8,128]{2,1,0:T(8,128)S(1)}, u32[]{:S(2)}, u32[]{:S(2)}) collective-permute-start(f32[32,8,128]{2,1,0:T(8,128)S(1)} %all_to_all.11.here), channel_id=1, source_target_pairs={{0,32},{8,40},{16,48},{24,56},{32,64},{40,72},{48,80},{56,88},{64,... | collective-permute-start | bytes 393224 | tf_op jit(solution)/shard_map/ppermute | solution.py:757

commit v5 on v4

--- a/solution.py
+++ b/solution.py
@@ -11,7 +11,6 @@
 WENO_EPS = 0.01
 SIDE = 0.8 / 6.0
 F32 = jnp.float32
-HIGHEST = lax.Precision.HIGHEST
 
 HALO = 14
 KEEP = 4
@@ -63,9 +62,10 @@
 
 
 def dot(a, b):
-    return lax.dot_general(
-        a, b, (((1,), (0,)), ((), ())), precision=HIGHEST, preferred_element_type=F32
-    )
+    b = b.astype(jnp.bfloat16)
+    high = a.astype(jnp.bfloat16)
+    low = (a - high.astype(F32)).astype(jnp.bfloat16)
+    return jnp.dot(high, b, preferred_element_type=F32) + jnp.dot(low, b, preferred_element_type=F32)
 
 
 def pair_matrix(rows, cols, value):
@@ -266,22 +266,21 @@
         l = [behind(v, 2), behind(v, 1), v, ahead(v, 1), ahead(v, 2), ahead(v, 3)]
         s = 0.5 * (w + ahead(w, 1))
         p, q, r = indicators(l[1], l[2], l[3])
-        square = v * v
+        _, q1, r1 = indicators(l[2], l[3], l[4])
+        _, _, r2 = indicators(l[3], l[4], l[5])
+        p0, _, _ = indicators(l[0], l[1], l[2])
+        flux = upwind_flux(s, l, p0, q, r1, p, q1, r2)
+        low = slice(0, 128)
+        c = v[:, low]
+        none = jnp.zeros_like(c)
+        square = c * c
         edge = WENO_EPS + (13.0 / 12.0 + 9.0 / 4.0) * square
-        edge = edge * edge
         level = WENO_EPS + (13.0 / 12.0 + 1.0 / 4.0) * square
-        level = level * level
-        p_below = jnp.where(lane == 0, edge, roll(p, 1, 1))
-        q_above = jnp.where(lane == 255, level, roll(q, -1, 1))
-        r_above = jnp.where(lane == 255, edge, roll(r, -1, 1))
-        r_far = jnp.where(lane == 255, WENO_EPS * WENO_EPS, roll(r_above, -1, 1))
-        flux = upwind_flux(s, l, p_below, q, r_above, p, q_above, r_far)
-        low = slice(0, 128)
-        none = jnp.zeros((v.shape[0], 128), F32)
-        l = [none, none, none, v[:, low], l[3][:, low], l[4][:, low]]
         wall = upwind_flux(
-            0.5 * w[:, low], l, none + WENO_EPS * WENO_EPS, level[:, low], r[:, low],
-            edge[:, low], q[:, low], r_above[:, low],
+            0.5 * w[:, low],
+            [none, none, none, c, l[3][:, low], l[4][:, low]],
+            none + WENO_EPS * WENO_EPS, level * level, r[:, low],
+            edge * edge, q[:, low], r1[:, low],
         )
         wall = jnp.concatenate([wall, wall], axis=1)
         change = change + (flux - jnp.where(lane == 0, wall, roll(flux, 1, 1)))
@@ -570,7 +569,8 @@
 
 
 def solve_coarse(nx, ny, extra, at, coarse, s2, v2, w2, t3, b3, c3, d3, dup, row2):
-    here, before, after = coarse
+    here, fetched, other = coarse
+    odd = lax.rem(at[1], 2) == 1
     _, _, _, r2, e2, r3 = reach(extra)
     spot = at[0] % GROUP
     rows2 = ny // 4
@@ -585,7 +585,9 @@
         layer, place = block // GROUP, block % GROUP
         for n in range(count):
             k = place * count + n
-            tile = jnp.where(layer == 0, before[k], jnp.where(layer == 1, here[k], after[k]))
+            tile = jnp.where(
+                layer == 1, here[k], jnp.where((layer == 2) == odd, fetched[k], other[k])
+            )
             halves = (jnp.where(lane8, tile, 0.0), jnp.where(lane8, roll(tile, 64, 1), 0.0))
             for p in range(4):
                 part = halves[p // 2][4 * (p % 2) : 4 * (p % 2) + 4, :]
@@ -708,8 +710,8 @@
     return [level1, level1, level0, level0, (max(8 + 2 * r1, 4 + 2 * r2), 2, 32, 128)]
 
 
-def turn_body(nx, ny, at, here, before, after, b1, u, b, v_down, v_out, wider, low, high, own, pair, t, *scratch):
-    v2 = solve_coarse(nx, ny, KEEP, at, (here, before, after), *scratch[:9])
+def turn_body(nx, ny, at, here, fetched, other, b1, u, b, v_down, v_out, wider, low, high, own, pair, t, *scratch):
+    v2 = solve_coarse(nx, ny, KEEP, at, (here, fetched, other), *scratch[:9])
     b = Field(b, E0 - 1)
     v = climb(nx, ny, KEEP, at, v2, Field(b1, E1 + 1), Field(u, E1), b, Field(v_down, E0), *scratch[9:])
     mask = row_mask((32, 256), at[1] * 16 - 8, ny)
@@ -737,8 +739,8 @@
     return call(functools.partial(turn_body, nx, ny), outs, scratch, args, 30000000)
 
 
-def finish_body(nx, ny, at, here, before, after, b1, u, b, v_down, out, *scratch):
-    v2 = solve_coarse(nx, ny, 0, at, (here, before, after), *scratch[:9])
+def finish_body(nx, ny, at, here, fetched, other, b1, u, b, v_down, out, *scratch):
+    v2 = solve_coarse(nx, ny, 0, at, (here, fetched, other), *scratch[:9])
     b, v_down = Field(b, E0 - 1), Field(v_down, KEEP - 2)
     v = climb(nx, ny, 0, at, v2, Field(b1, NEAR), Field(u, NEAR - 1), b, v_down, *scratch[9:])
     for p in range(16):
@@ -782,7 +784,14 @@
     wide, size = lax.axis_size("wide"), b2.shape[0]
     groups = [[g * size + k for k in range(size)] for g in range(wide // GROUP)]
     here = lax.all_to_all(b2, ("wide", "narrow"), 0, 0, axis_index_groups=groups)
-    return here, shifted(here, "wide", GROUP), shifted(here, "wide", -GROUP)
+    cores, pairs = lax.axis_size("narrow"), []
+    for i in range(wide):
+        for j in range(cores):
+            k = i + (GROUP if j % 2 == 0 else -GROUP)
+            if 0 <= k < wide:
+                pairs.append((i * cores + j, k * cores + j))
+    fetched = lax.ppermute(here, ("wide", "narrow"), pairs)
+    return here, fetched, swapped(fetched, 0)
 
 
 def on_device(phase, distance, velocity):

time: 158 us -> 156 us (0.987)
  the two profiles are of different devices: /device:TPU:256 before, /device:TPU:1 now
where the time goes in v5:
time: 156 us; the launch traced here: 154 us
  starting transfers between devices  50.2 us (32%)
  waiting for transfers between devices  42.8 us (27%)
  blocking collectives  35.9 us (23%)
  Pallas kernels  24.6 us (16%)
    all_to_all x2, blocking collectives, spread_coarse(): lax.all_to_all(b2, ('wide', 'narrow'), 0, 0, axis_index_groups=groups)  35.9 us
    ppermute x10, starting transfers between devices, swapped(): return lax.ppermute(array, 'narrow', pairs + [(j, i) for i, j in pairs])  30.4 us
    pallas_call x7, Pallas kernels, call(): pl.pallas_call(body, out_shape=[jax.ShapeDtypeStruct(s, F32) for s in out...  22.7 us
    ppermute x8, starting transfers between devices, shifted(): lax.ppermute(array, axis, [(i, i + step) for i in range(count) if 0 <= i...  17.2 us
    ppermute x8, waiting for transfers between devices, shifted(): lax.ppermute(array, axis, [(i, i + step) for i in range(count) if 0 <= i...  15.1 us
    ppermute x10, waiting for transfers between devices, swapped(): return lax.ppermute(array, 'narrow', pairs + [(j, i) for i, j in pairs])  14.1 us
    ppermute x2, waiting for transfers between devices, spread_coarse(): fetched = lax.ppermute(here, ('wide', 'narrow'), pairs)  13.5 us
  transfers between devices with their start and end apart: 20, of which 13 were waited for; matrix products, arithmetic and copies ran while one was open for 0% of the time, Pallas kernels for 2%

profile of v5, /device:TPU:1, one launch (start us, length us, event | category | flops | bytes accessed | tf_op | source)
XLA Modules:
  0.0 154.5 jit_solution(18308386801778803080)
XLA Ops:
  0.6 0.0 copy-start
  0.6 0.1 pad_add_fusion.at
  0.7 1.9 %shard_map.50 = (f32[16,16,256]{2,1,0:T(8,128)S(1)}, f32[4,16,256]{2,1,0:T(8,128)S(1)}, f32[4,16,256]{2,1,0:T(8,128)S(1)}, f32[16,4,256]{2,1,0:T(4,128)S(1)}, f32[16,4,256]{2,1,0:T(4,128)S(1)}) custom-call(s32[2]{0:T(128)S(1)} %pad_add_fusion.at, s32[16,16,256]{2,1,0:T(8,128)} %phase.1, f32[16,16,256]{2,1,0:T(8,128)} %distance.1, f32[3,16,16,256]{3,2,1,0:T(8,128)} %velocity.5), custom_call_target="tpu_custom_call" | custom-call | flops 1000000 | bytes 1000000 | tf_op jit(solution)/shard_map/pallas_call | solution.py:167
  2.6 3.9 %collective-permute-start = (f32[4,16,256]{2,1,0:T(8,128)S(1)}, f32[4,16,256]{2,1,0:T(8,128)S(1)}, u32[]{:S(2)}, u32[]{:S(2)}) collective-permute-start(f32[4,16,256]{2,1,0:T(8,128)S(1)} %get-tuple-element.26), channel_id=1, source_target_pairs={{0,8},{8,16},{16,24},{24,32},{32,40},{40,48},{48,56},{56,64},{64,7... | collective-permute-start | bytes 196616 | tf_op jit(solution)/shard_map/ppermute | solution.py:759
  6.6 1.3 collective-permute-start.1
  7.9 6.1 %collective-permute-start.2 = (f32[16,4,256]{2,1,0:T(4,128)S(1)}, f32[16,4,256]{2,1,0:T(4,128)S(1)}, u32[]{:S(2)}, u32[]{:S(2)}) collective-permute-start(f32[16,4,256]{2,1,0:T(4,128)S(1)} %get-tuple-element.28), channel_id=1, source_target_pairs={{0,1},{2,3},{4,5},{6,7},{1,0},{3,2},{5,4},{7,6},{8,9},{10,11},{12,... | collective-permute-start | bytes 196616 | tf_op jit(solution)/shard_map/ppermute | solution.py:767
  14.0 1.9 %collective-permute-start.3 = (f32[16,4,256]{2,1,0:T(4,128)S(1)}, f32[16,4,256]{2,1,0:T(4,128)S(1)}, u32[]{:S(2)}, u32[]{:S(2)}) collective-permute-start(f32[16,4,256]{2,1,0:T(4,128)S(1)} %get-tuple-element.29), channel_id=1, source_target_pairs={{1,2},{3,4},{5,6},{2,1},{4,3},{6,5},{9,10},{11,12},{13,14},{10,9},... | collective-permute-start | bytes 196616 | tf_op jit(solution)/shard_map/ppermute | solution.py:767
  16.0 0.0 collective-permute-done.1.xh
  16.0 0.0 collective-permute-done.2.chip.v_chip
  16.0 3.6 %collective-permute-done.3.link.v_link = f32[16,4,256]{2,1,0:T(4,128)S(1)} collective-permute-done((f32[16,4,256]{2,1,0:T(4,128)S(1)}, f32[16,4,256]{2,1,0:T(4,128)S(1)}, u32[]{:S(2)}, u32[]{:S(2)}) %collective-permute-start.3) | collective-permute-done | bytes 65568 | tf_op jit(solution)/shard_map/ppermute | solution.py:767
  19.6 4.7 %shard_map.51 = (f32[16,16,256]{2,1,0:T(8,128)}, f32[22,16,256]{2,1,0:T(8,128)S(1)}, f32[3,16,256]{2,1,0:T(8,128)S(1)}, f32[3,16,256]{2,1,0:T(8,128)S(1)}) custom-call(s32[2]{0:T(128)S(1)} %pad_add_fusion.at, f32[16,16,256]{2,1,0:T(8,128)S(1)} %get-tuple-element.25.psi, f32[3,16,16,256]{3,2,1,0:T(8,128)S(1)} %copy-done, ...), custom_call_target="tpu_custom_call" | custom-call | flops 10000000 | bytes 4000000 | tf_op jit(solution)/shard_map/pallas_call | solution.py:91
  24.3 4.3 %collective-permute-start.4 = (f32[3,16,256]{2,1,0:T(8,128)S(1)}, f32[3,16,256]{2,1,0:T(8,128)S(1)}, u32[]{:S(2)}, u32[]{:S(2)}) collective-permute-start(f32[3,16,256]{2,1,0:T(8,128)S(1)} %get-tuple-element.32), channel_id=1, source_target_pairs={{0,8},{8,16},{16,24},{24,32},{32,40},{40,48},{48,56},{56,64},{64,7... | collective-permute-start | bytes 147464 | tf_op jit(solution)/shard_map/ppermute | solution.py:759
  28.6 1.3 collective-permute-start.5
  29.9 3.5 %collective-permute-done.5 = f32[3,16,256]{2,1,0:T(8,128)S(1)} collective-permute-done((f32[3,16,256]{2,1,0:T(8,128)S(1)}, f32[3,16,256]{2,1,0:T(8,128)S(1)}, u32[]{:S(2)}, u32[]{:S(2)}) %collective-permute-start.5) | collective-permute-done | bytes 49184 | tf_op jit(solution)/shard_map/ppermute | solution.py:759
  33.5 3.4 %collective-permute-start.7 = (f32[22,3,256]{2,1,0:T(4,128)S(1)}, f32[22,3,256]{2,1,0:T(4,128)S(1)}, u32[]{:S(2)}, u32[]{:S(2)}) collective-permute-start(f32[22,3,256]{2,1,0:T(4,128)S(1)} %get-tuple-element.48), channel_id=1, source_target_pairs={{1,2},{3,4},{5,6},{2,1},{4,3},{6,5},{9,10},{11,12},{13,14},{10,9},... | collective-permute-start | bytes 202760 | tf_op jit(solution)/shard_map/ppermute | solution.py:767
  36.8 1.9 %collective-permute-start.6 = (f32[22,3,256]{2,1,0:T(4,128)S(1)}, f32[22,3,256]{2,1,0:T(4,128)S(1)}, u32[]{:S(2)}, u32[]{:S(2)}) collective-permute-start(f32[22,3,256]{2,1,0:T(4,128)S(1)} %get-tuple-element.49), channel_id=1, source_target_pairs={{0,1},{2,3},{4,5},{6,7},{1,0},{3,2},{5,4},{7,6},{8,9},{10,11},{12,... | collective-permute-start | bytes 202760 | tf_op jit(solution)/shard_map/ppermute | solution.py:767
  38.7 0.6 collective-permute-done.7.link
  39.3 0.7 collective-permute-done.6.chip
  40.0 2.7 %shard_map.52 = (f32[44,16,256]{2,1,0:T(8,128)S(1)}, f32[14,16,256]{2,1,0:T(8,128)S(1)}, f32[14,16,256]{2,1,0:T(8,128)S(1)}) custom-call(s32[2]{0:T(128)S(1)} %pad_add_fusion.at, f32[22,16,256]{2,1,0:T(8,128)S(1)} %constant_dynamic-update-slice_fusion.4.mid, f32[22,3,256]{2,1,0:T(4,128)S(1)} %collective-permute-done.6.chip, ...), custom_call_target="tpu_custom_call" | custom-call | flops 10000000 | bytes 4000000 | tf_op jit(solution)/shard_map/pallas_call | solution.py:91
  42.7 1.7 %collective-permute-start.8 = (f32[14,16,256]{2,1,0:T(8,128)S(1)}, f32[14,16,256]{2,1,0:T(8,128)S(1)}, u32[]{:S(2)}, u32[]{:S(2)}) collective-permute-start(f32[14,16,256]{2,1,0:T(8,128)S(1)} %get-tuple-element.35), channel_id=1, source_target_pairs={{0,8},{8,16},{16,24},{24,32},{32,40},{40,48},{48,56},{56,64},{64,7... | collective-permute-start | bytes 688136 | tf_op jit(solution)/shard_map/ppermute | solution.py:759
  44.4 1.3 collective-permute-start.9
  45.7 3.5 %collective-permute-done.8 = f32[14,16,256]{2,1,0:T(8,128)S(1)} collective-permute-done((f32[14,16,256]{2,1,0:T(8,128)S(1)}, f32[14,16,256]{2,1,0:T(8,128)S(1)}, u32[]{:S(2)}, u32[]{:S(2)}) %collective-permute-start.8) | collective-permute-done | bytes 229408 | tf_op jit(solution)/shard_map/ppermute | solution.py:759
  49.3 4.9 %collective-permute-done.9 = f32[14,16,256]{2,1,0:T(8,128)S(1)} collective-permute-done((f32[14,16,256]{2,1,0:T(8,128)S(1)}, f32[14,16,256]{2,1,0:T(8,128)S(1)}, u32[]{:S(2)}, u32[]{:S(2)}) %collective-permute-start.9) | collective-permute-done | bytes 229408 | tf_op jit(solution)/shard_map/ppermute | solution.py:759
  54.2 4.0 %collective-permute-start.11 = (f32[44,16,256]{2,1,0:T(8,128)S(1)}, f32[44,16,256]{2,1,0:T(8,128)S(1)}, u32[]{:S(2)}, u32[]{:S(2)}) collective-permute-start(f32[44,16,256]{2,1,0:T(8,128)S(1)} %constant_dynamic-update-slice_fusion.2.mid), channel_id=1, source_target_pairs={{1,2},{3,4},{5,6},{2,1},{4,3},{6,5},{9,10},{11,12},{13,14},{10,9},... | collective-permute-start | bytes 2162696 | tf_op jit(solution)/shard_map/ppermute | solution.py:767
  58.3 1.9 %collective-permute-start.10 = (f32[44,16,256]{2,1,0:T(8,128)S(1)}, f32[44,16,256]{2,1,0:T(8,128)S(1)}, u32[]{:S(2)}, u32[]{:S(2)}) collective-permute-start(f32[44,16,256]{2,1,0:T(8,128)S(1)} %constant_dynamic-update-slice_fusion.2.mid), channel_id=1, source_target_pairs={{0,1},{2,3},{4,5},{6,7},{1,0},{3,2},{5,4},{7,6},{8,9},{10,11},{12,... | collective-permute-start | bytes 2162696 | tf_op jit(solution)/shard_map/ppermute | solution.py:767
  60.2 7.0 %collective-permute-done.11.link = f32[44,16,256]{2,1,0:T(8,128)S(1)} collective-permute-done((f32[44,16,256]{2,1,0:T(8,128)S(1)}, f32[44,16,256]{2,1,0:T(8,128)S(1)}, u32[]{:S(2)}, u32[]{:S(2)}) %collective-permute-start.11) | collective-permute-done | bytes 720928 | tf_op jit(solution)/shard_map/ppermute | solution.py:767
  67.2 0.0 collective-permute-done.10.chip
  67.2 2.1 %shard_map.53 = f32[32,8,128]{2,1,0:T(8,128)S(1)} custom-call(s32[2]{0:T(128)S(1)} %pad_add_fusion.at, f32[44,16,256]{2,1,0:T(8,128)S(1)} %constant_dynamic-update-slice_fusion.2.mid, f32[44,16,256]{2,1,0:T(8,128)S(1)} %collective-permute-done.10.chip, f32[44,16,256]{2,1,0:T(8,128)S(1)} %collective-permute-done.11.link), custom_call_target="tpu_custom_call" | custom-call | flops 6000000 | bytes 4000000 | tf_op jit(solution)/shard_map/pallas_call | solution.py:91
  69.3 18.6 %all_to_all.10.here = f32[32,8,128]{2,1,0:T(8,128)S(1)} all-to-all(f32[32,8,128]{2,1,0:T(8,128)S(1)} %shard_map.53), channel_id=1, replica_groups={{0,1,2,3,4,5,6,7,8,9,10,11,12,13,14,15,16,17,18,19,20,21,22,23,24,25,26..., dimensions={0} | all-to-all | bytes 262144 | tf_op jit(solution)/shard_map/all_to_all | solution.py:786
  87.9 1.3 collective-permute-start.12
  89.2 4.6 %collective-permute-done.12.fetched = f32[32,8,128]{2,1,0:T(8,128)S(1)} collective-permute-done((f32[32,8,128]{2,1,0:T(8,128)S(1)}, f32[32,8,128]{2,1,0:T(8,128)S(1)}, u32[]{:S(2)}, u32[]{:S(2)}) %collective-permute-start.12) | collective-permute-done | bytes 131104 | tf_op jit(solution)/shard_map/ppermute | solution.py:793
  93.8 2.9 %collective-permute-start.13 = (f32[32,8,128]{2,1,0:T(8,128)S(1)}, f32[32,8,128]{2,1,0:T(8,128)S(1)}, u32[]{:S(2)}, u32[]{:S(2)}) collective-permute-start(f32[32,8,128]{2,1,0:T(8,128)S(1)} %collective-permute-done.12.fetched), channel_id=1, source_target_pairs={{0,1},{2,3},{4,5},{6,7},{1,0},{3,2},{5,4},{7,6},{8,9},{10,11},{12,... | collective-permute-start | bytes 393224 | tf_op jit(solution)/shard_map/ppermute | solution.py:767
  96.7 3.5 %shard_map.54 = (f32[26,32,256]{2,1,0:T(8,128)S(1)}, f32[28,32,256]{2,1,0:T(8,128)S(1)}, f32[20,24,128]{2,1,0:T(8,128)S(1)}, f32[18,24,128]{2,1,0:T(8,128)S(1)}) custom-call(s32[2]{0:T(128)S(1)} %pad_add_fusion.at, f32[44,16,256]{2,1,0:T(8,128)S(1)} %constant_dynamic-update-slice_fusion.2.mid, f32[44,16,256]{2,1,0:T(8,128)S(1)} %collective-permute-done.10.chip, ...), custom_call_target="tpu_custom_call" | custom-call | flops 20000000 | bytes 4000000 | tf_op jit(solution)/shard_map/pallas_call | solution.py:91
  100.3 5.0 %shard_map.55 = (f32[20,32,256]{2,1,0:T(8,128)S(1)}, f32[16,8,128]{2,1,0:T(8,128)S(1)}, f32[4,8,128]{2,1,0:T(8,128)S(1)}, f32[4,8,128]{2,1,0:T(8,128)S(1)}) custom-call(s32[2]{0:T(128)S(1)} %pad_add_fusion.at, f32[32,8,128]{2,1,0:T(8,128)S(1)} %all_to_all.10.here, f32[32,8,128]{2,1,0:T(8,128)S(1)} %collective-permute-done.12.fetched, ...), custom_call_target="tpu_custom_call" | custom-call | flops 30000000 | bytes 4000000 | tf_op jit(solution)/shard_map/pallas_call | solution.py:91
  105.3 2.2 %collective-permute-start.14 = (f32[4,8,128]{2,1,0:T(8,128)S(1)}, f32[4,8,128]{2,1,0:T(8,128)S(1)}, u32[]{:S(2)}, u32[]{:S(2)}) collective-permute-start(f32[4,8,128]{2,1,0:T(8,128)S(1)} %get-tuple-element.42), channel_id=1, source_target_pairs={{0,8},{8,16},{16,24},{24,32},{32,40},{40,48},{48,56},{56,64},{64,7... | collective-permute-start | bytes 49160 | tf_op jit(solution)/shard_map/ppermute | solution.py:759
  107.5 1.3 collective-permute-start.15
  108.8 3.2 %collective-permute-done.15 = f32[4,8,128]{2,1,0:T(8,128)S(1)} collective-permute-done((f32[4,8,128]{2,1,0:T(8,128)S(1)}, f32[4,8,128]{2,1,0:T(8,128)S(1)}, u32[]{:S(2)}, u32[]{:S(2)}) %collective-permute-start.15) | collective-permute-done | bytes 16416 | tf_op jit(solution)/shard_map/ppermute | solution.py:759
  112.0 3.5 %collective-permute-start.17 = (f32[16,8,128]{2,1,0:T(8,128)S(1)}, f32[16,8,128]{2,1,0:T(8,128)S(1)}, u32[]{:S(2)}, u32[]{:S(2)}) collective-permute-start(f32[16,8,128]{2,1,0:T(8,128)S(1)} %constant_dynamic-update-slice_fusion.mid), channel_id=1, source_target_pairs={{1,2},{3,4},{5,6},{2,1},{4,3},{6,5},{9,10},{11,12},{13,14},{10,9},... | collective-permute-start | bytes 196616 | tf_op jit(solution)/shard_map/ppermute | solution.py:767
  115.5 1.9 %collective-permute-start.16 = (f32[16,8,128]{2,1,0:T(8,128)S(1)}, f32[16,8,128]{2,1,0:T(8,128)S(1)}, u32[]{:S(2)}, u32[]{:S(2)}) collective-permute-start(f32[16,8,128]{2,1,0:T(8,128)S(1)} %constant_dynamic-update-slice_fusion.mid), channel_id=1, source_target_pairs={{0,1},{2,3},{4,5},{6,7},{1,0},{3,2},{5,4},{7,6},{8,9},{10,11},{12,... | collective-permute-start | bytes 196616 | tf_op jit(solution)/shard_map/ppermute | solution.py:767
  117.5 0.1 collective-permute-done.17.link
  117.6 1.1 collective-permute-done.16.chip
  118.7 0.9 shard_map.56
  119.6 17.3 %all_to_all.11.here = f32[32,8,128]{2,1,0:T(8,128)S(1)} all-to-all(f32[32,8,128]{2,1,0:T(8,128)S(1)} %get-tuple-element.44), channel_id=1, replica_groups={{0,1,2,3,4,5,6,7,8,9,10,11,12,13,14,15,16,17,18,19,20,21,22,23,24,25,26..., dimensions={0} | all-to-all | bytes 262144 | tf_op jit(solution)/shard_map/all_to_all | solution.py:786
  136.9 1.3 collective-permute-start.18
  138.2 8.9 %collective-permute-done.18.fetched = f32[32,8,128]{2,1,0:T(8,128)S(1)} collective-permute-done((f32[32,8,128]{2,1,0:T(8,128)S(1)}, f32[32,8,128]{2,1,0:T(8,128)S(1)}, u32[]{:S(2)}, u32[]{:S(2)}) %collective-permute-start.18) | collective-permute-done | bytes 131104 | tf_op jit(solution)/shard_map/ppermute | solution.py:793
  147.1 2.7 %collective-permute-start.19 = (f32[32,8,128]{2,1,0:T(8,128)S(1)}, f32[32,8,128]{2,1,0:T(8,128)S(1)}, u32[]{:S(2)}, u32[]{:S(2)}) collective-permute-start(f32[32,8,128]{2,1,0:T(8,128)S(1)} %collective-permute-done.18.fetched), channel_id=1, source_target_pairs={{0,1},{2,3},{4,5},{6,7},{1,0},{3,2},{5,4},{7,6},{8,9},{10,11},{12,... | collective-permute-start | bytes 393224 | tf_op jit(solution)/shard_map/ppermute | solution.py:767
  149.8 1.0 collective-permute-done.19.other
  150.8 3.7 %shard_map.57 = f32[16,16,256]{2,1,0:T(8,128)} custom-call(s32[2]{0:T(128)S(1)} %pad_add_fusion.at, f32[32,8,128]{2,1,0:T(8,128)S(1)} %all_to_all.11.here, f32[32,8,128]{2,1,0:T(8,128)S(1)} %collective-permute-done.18.fetched, f32[32,8,128]{2,1,0:T(8,128)S(1)} %collective-permute-done.19.other, f32[16,24,128]{2,1,0:T(8,128)S(1)} %get-tuple-element.45.b1, ...), custom_call_target="tpu_custom_call" | custom-call | flops 20000000 | bytes 4000000 | tf_op jit(solution)/shard_map/pallas_call | solution.py:91
  (12 shorter events, 0.1 us)
Async XLA Ops:
  0.6 19.0 %copy-start = (f32[3,16,16,256]{3,2,1,0:T(8,128)S(1)}, f32[3,16,16,256]{3,2,1,0:T(8,128)}, u32[]{:S(2)}) copy-start(f32[3,16,16,256]{3,2,1,0:T(8,128)} %velocity.5) | copy-start | bytes 2359300
  2.6 13.3 %collective-permute-start = (f32[4,16,256]{2,1,0:T(8,128)S(1)}, f32[4,16,256]{2,1,0:T(8,128)S(1)}, u32[]{:S(2)}, u32[]{:S(2)}) collective-permute-start(f32[4,16,256]{2,1,0:T(8,128)S(1)} %get-tuple-element.26), channel_id=1, source_target_pairs={{0,8},{8,16},{16,24},{24,32},{32,40},{40,48},{48,56},{56,64},{64,7... | collective-permute-start | bytes 196616 | tf_op jit(solution)/shard_map/ppermute | solution.py:759
  6.6 9.4 %collective-permute-start.1 = (f32[4,16,256]{2,1,0:T(8,128)S(1)}, f32[4,16,256]{2,1,0:T(8,128)S(1)}, u32[]{:S(2)}, u32[]{:S(2)}) collective-permute-start(f32[4,16,256]{2,1,0:T(8,128)S(1)} %get-tuple-element.27), channel_id=1, source_target_pairs={{8,0},{16,8},{24,16},{32,24},{40,32},{48,40},{56,48},{64,56},{72,6... | collective-permute-start | bytes 196616 | tf_op jit(solution)/shard_map/ppermute | solution.py:759
  7.9 8.1 %collective-permute-start.2 = (f32[16,4,256]{2,1,0:T(4,128)S(1)}, f32[16,4,256]{2,1,0:T(4,128)S(1)}, u32[]{:S(2)}, u32[]{:S(2)}) collective-permute-start(f32[16,4,256]{2,1,0:T(4,128)S(1)} %get-tuple-element.28), channel_id=1, source_target_pairs={{0,1},{2,3},{4,5},{6,7},{1,0},{3,2},{5,4},{7,6},{8,9},{10,11},{12,... | collective-permute-start | bytes 196616 | tf_op jit(solution)/shard_map/ppermute | solution.py:767
  14.0 5.6 %collective-permute-start.3 = (f32[16,4,256]{2,1,0:T(4,128)S(1)}, f32[16,4,256]{2,1,0:T(4,128)S(1)}, u32[]{:S(2)}, u32[]{:S(2)}) collective-permute-start(f32[16,4,256]{2,1,0:T(4,128)S(1)} %get-tuple-element.29), channel_id=1, source_target_pairs={{1,2},{3,4},{5,6},{2,1},{4,3},{6,5},{9,10},{11,12},{13,14},{10,9},... | collective-permute-start | bytes 196616 | tf_op jit(solution)/shard_map/ppermute | solution.py:767
  24.3 5.6 %collective-permute-start.4 = (f32[3,16,256]{2,1,0:T(8,128)S(1)}, f32[3,16,256]{2,1,0:T(8,128)S(1)}, u32[]{:S(2)}, u32[]{:S(2)}) collective-permute-start(f32[3,16,256]{2,1,0:T(8,128)S(1)} %get-tuple-element.32), channel_id=1, source_target_pairs={{0,8},{8,16},{16,24},{24,32},{32,40},{40,48},{48,56},{56,64},{64,7... | collective-permute-start | bytes 147464 | tf_op jit(solution)/shard_map/ppermute | solution.py:759
  28.6 4.8 %collective-permute-start.5 = (f32[3,16,256]{2,1,0:T(8,128)S(1)}, f32[3,16,256]{2,1,0:T(8,128)S(1)}, u32[]{:S(2)}, u32[]{:S(2)}) collective-permute-start(f32[3,16,256]{2,1,0:T(8,128)S(1)} %get-tuple-element.33), channel_id=1, source_target_pairs={{8,0},{16,8},{24,16},{32,24},{40,32},{48,40},{56,48},{64,56},{72,6... | collective-permute-start | bytes 147464 | tf_op jit(solution)/shard_map/ppermute | solution.py:759
  33.5 5.8 %collective-permute-start.7 = (f32[22,3,256]{2,1,0:T(4,128)S(1)}, f32[22,3,256]{2,1,0:T(4,128)S(1)}, u32[]{:S(2)}, u32[]{:S(2)}) collective-permute-start(f32[22,3,256]{2,1,0:T(4,128)S(1)} %get-tuple-element.48), channel_id=1, source_target_pairs={{1,2},{3,4},{5,6},{2,1},{4,3},{6,5},{9,10},{11,12},{13,14},{10,9},... | collective-permute-start | bytes 202760 | tf_op jit(solution)/shard_map/ppermute | solution.py:767
  36.8 3.2 %collective-permute-start.6 = (f32[22,3,256]{2,1,0:T(4,128)S(1)}, f32[22,3,256]{2,1,0:T(4,128)S(1)}, u32[]{:S(2)}, u32[]{:S(2)}) collective-permute-start(f32[22,3,256]{2,1,0:T(4,128)S(1)} %get-tuple-element.49), channel_id=1, source_target_pairs={{0,1},{2,3},{4,5},{6,7},{1,0},{3,2},{5,4},{7,6},{8,9},{10,11},{12,... | collective-permute-start | bytes 202760 | tf_op jit(solution)/shard_map/ppermute | solution.py:767
  42.7 6.5 %collective-permute-start.8 = (f32[14,16,256]{2,1,0:T(8,128)S(1)}, f32[14,16,256]{2,1,0:T(8,128)S(1)}, u32[]{:S(2)}, u32[]{:S(2)}) collective-permute-start(f32[14,16,256]{2,1,0:T(8,128)S(1)} %get-tuple-element.35), channel_id=1, source_target_pairs={{0,8},{8,16},{16,24},{24,32},{32,40},{40,48},{48,56},{56,64},{64,7... | collective-permute-start | bytes 688136 | tf_op jit(solution)/shard_map/ppermute | solution.py:759
  44.4 9.8 %collective-permute-start.9 = (f32[14,16,256]{2,1,0:T(8,128)S(1)}, f32[14,16,256]{2,1,0:T(8,128)S(1)}, u32[]{:S(2)}, u32[]{:S(2)}) collective-permute-start(f32[14,16,256]{2,1,0:T(8,128)S(1)} %get-tuple-element.36), channel_id=1, source_target_pairs={{8,0},{16,8},{24,16},{32,24},{40,32},{48,40},{56,48},{64,56},{72,6... | collective-permute-start | bytes 688136 | tf_op jit(solution)/shard_map/ppermute | solution.py:759
  54.2 13.0 %collective-permute-start.11 = (f32[44,16,256]{2,1,0:T(8,128)S(1)}, f32[44,16,256]{2,1,0:T(8,128)S(1)}, u32[]{:S(2)}, u32[]{:S(2)}) collective-permute-start(f32[44,16,256]{2,1,0:T(8,128)S(1)} %constant_dynamic-update-slice_fusion.2.mid), channel_id=1, source_target_pairs={{1,2},{3,4},{5,6},{2,1},{4,3},{6,5},{9,10},{11,12},{13,14},{10,9},... | collective-permute-start | bytes 2162696 | tf_op jit(solution)/shard_map/ppermute | solution.py:767
  58.3 9.0 %collective-permute-start.10 = (f32[44,16,256]{2,1,0:T(8,128)S(1)}, f32[44,16,256]{2,1,0:T(8,128)S(1)}, u32[]{:S(2)}, u32[]{:S(2)}) collective-permute-start(f32[44,16,256]{2,1,0:T(8,128)S(1)} %constant_dynamic-update-slice_fusion.2.mid), channel_id=1, source_target_pairs={{0,1},{2,3},{4,5},{6,7},{1,0},{3,2},{5,4},{7,6},{8,9},{10,11},{12,... | collective-permute-start | bytes 2162696 | tf_op jit(solution)/shard_map/ppermute | solution.py:767
  87.9 5.9 %collective-permute-start.12 = (f32[32,8,128]{2,1,0:T(8,128)S(1)}, f32[32,8,128]{2,1,0:T(8,128)S(1)}, u32[]{:S(2)}, u32[]{:S(2)}) collective-permute-start(f32[32,8,128]{2,1,0:T(8,128)S(1)} %all_to_all.10.here), channel_id=1, source_target_pairs={{0,32},{2,34},{4,36},{6,38},{8,40},{10,42},{12,44},{14,46},{16,48}... | collective-permute-start | bytes 393224 | tf_op jit(solution)/shard_map/ppermute | solution.py:793
  93.8 6.4 %collective-permute-start.13 = (f32[32,8,128]{2,1,0:T(8,128)S(1)}, f32[32,8,128]{2,1,0:T(8,128)S(1)}, u32[]{:S(2)}, u32[]{:S(2)}) collective-permute-start(f32[32,8,128]{2,1,0:T(8,128)S(1)} %collective-permute-done.12.fetched), channel_id=1, source_target_pairs={{0,1},{2,3},{4,5},{6,7},{1,0},{3,2},{5,4},{7,6},{8,9},{10,11},{12,... | collective-permute-start | bytes 393224 | tf_op jit(solution)/shard_map/ppermute | solution.py:767
  105.3 3.5 %collective-permute-start.14 = (f32[4,8,128]{2,1,0:T(8,128)S(1)}, f32[4,8,128]{2,1,0:T(8,128)S(1)}, u32[]{:S(2)}, u32[]{:S(2)}) collective-permute-start(f32[4,8,128]{2,1,0:T(8,128)S(1)} %get-tuple-element.42), channel_id=1, source_target_pairs={{0,8},{8,16},{16,24},{24,32},{32,40},{40,48},{48,56},{56,64},{64,7... | collective-permute-start | bytes 49160 | tf_op jit(solution)/shard_map/ppermute | solution.py:759
  107.5 4.5 %collective-permute-start.15 = (f32[4,8,128]{2,1,0:T(8,128)S(1)}, f32[4,8,128]{2,1,0:T(8,128)S(1)}, u32[]{:S(2)}, u32[]{:S(2)}) collective-permute-start(f32[4,8,128]{2,1,0:T(8,128)S(1)} %get-tuple-element.43), channel_id=1, source_target_pairs={{8,0},{16,8},{24,16},{32,24},{40,32},{48,40},{56,48},{64,56},{72,6... | collective-permute-start | bytes 49160 | tf_op jit(solution)/shard_map/ppermute | solution.py:759
  112.0 5.6 %collective-permute-start.17 = (f32[16,8,128]{2,1,0:T(8,128)S(1)}, f32[16,8,128]{2,1,0:T(8,128)S(1)}, u32[]{:S(2)}, u32[]{:S(2)}) collective-permute-start(f32[16,8,128]{2,1,0:T(8,128)S(1)} %constant_dynamic-update-slice_fusion.mid), channel_id=1, source_target_pairs={{1,2},{3,4},{5,6},{2,1},{4,3},{6,5},{9,10},{11,12},{13,14},{10,9},... | collective-permute-start | bytes 196616 | tf_op jit(solution)/shard_map/ppermute | solution.py:767
  115.5 3.1 %collective-permute-start.16 = (f32[16,8,128]{2,1,0:T(8,128)S(1)}, f32[16,8,128]{2,1,0:T(8,128)S(1)}, u32[]{:S(2)}, u32[]{:S(2)}) collective-permute-start(f32[16,8,128]{2,1,0:T(8,128)S(1)} %constant_dynamic-update-slice_fusion.mid), channel_id=1, source_target_pairs={{0,1},{2,3},{4,5},{6,7},{1,0},{3,2},{5,4},{7,6},{8,9},{10,11},{12,... | collective-permute-start | bytes 196616 | tf_op jit(solution)/shard_map/ppermute | solution.py:767
  136.9 10.2 %collective-permute-start.18 = (f32[32,8,128]{2,1,0:T(8,128)S(1)}, f32[32,8,128]{2,1,0:T(8,128)S(1)}, u32[]{:S(2)}, u32[]{:S(2)}) collective-permute-start(f32[32,8,128]{2,1,0:T(8,128)S(1)} %all_to_all.11.here), channel_id=1, source_target_pairs={{0,32},{2,34},{4,36},{6,38},{8,40},{10,42},{12,44},{14,46},{16,48}... | collective-permute-start | bytes 393224 | tf_op jit(solution)/shard_map/ppermute | solution.py:793
  147.1 3.7 %collective-permute-start.19 = (f32[32,8,128]{2,1,0:T(8,128)S(1)}, f32[32,8,128]{2,1,0:T(8,128)S(1)}, u32[]{:S(2)}, u32[]{:S(2)}) collective-permute-start(f32[32,8,128]{2,1,0:T(8,128)S(1)} %collective-permute-done.18.fetched), channel_id=1, source_target_pairs={{0,1},{2,3},{4,5},{6,7},{1,0},{3,2},{5,4},{7,6},{8,9},{10,11},{12,... | collective-permute-start | bytes 393224 | tf_op jit(solution)/shard_map/ppermute | solution.py:767

commit v6 on v5

--- a/solution.py
+++ b/solution.py
@@ -457,8 +457,7 @@
     tile = jnp.concatenate([small[0, 0:4], small[1, 0:4]], axis=0) + roll(
         jnp.concatenate([small[2, 0:4], small[3, 0:4]], axis=0), 64, 1
     )
-    for k in range(b2_out.shape[0]):
-        b2_out[k] = tile
+    b2_out[...] = tile
 
 
 def reach(extra):
@@ -472,40 +471,9 @@
 
 
 E0, R1, E1, R2, E2, R3 = reach(KEEP)
-SHORT = 6
-
-
-def first_source_body(nx, ny, at, mid, chip, link, b2_out, b, v, b1, u, pair, t, s1, t1):
-    lower, upper = pick_sides(at, chip, link)
-    b, v = Field(b, SHORT), Field(v, SHORT - 1)
-    for p in range(-SHORT, 16 + SHORT):
-        b.ref[p + SHORT, 0:8, :] = lower(p + HALO, slice(8, 16))
-        b.ref[p + SHORT, 8:24, :] = mid[p + HALO]
-        b.ref[p + SHORT, 24:32, :] = upper(p + HALO, slice(0, 8))
-    mask = row_mask((32, 256), at[1] * 16 - 8, ny)
-    first_smooth(b, v, range(1 - SHORT, 15 + SHORT), SIDE, mask, at, nx, 0)
-    b1, u = Field(b1, 2), Field(u, 1)
-    coarsen_level0(at, nx, ny, b, v, b1, range(-2, 10), pair, t)
-    smooth_level1(at, nx, ny, b1, u, range(-1, 9))
-    coarsen_level1(b1, u, b2_out, s1, t1)
-
-
-def first_source(nx, ny, at, mid, chip, link):
-    scratch = [
-        around_block(16, SHORT, 32, 256),
-        around_block(16, SHORT - 1, 32, 256),
-        (12, 16, 128),
-        (10, 16, 128),
-        (12, 2, 32, 128),
-        (12, 16, 256),
-        (4, 16, 128),
-        (4, 8, 128),
-    ]
-    args = [at, mid, chip, link]
-    return call(functools.partial(first_source_body, nx, ny), [tiles(ny)], scratch, args, 6000000)[0]
-
-
-def first_down_body(nx, ny, at, mid, chip, link, b_out, v_out, b1_out, u_out, b, v, pair, t):
+
+
+def first_down_body(nx, ny, at, mid, chip, link, b_out, v_out, b1_out, u_out, b2_out, b, v, pair, t, s1, t1):
     lower, upper = pick_sides(at, chip, link)
     for i in range(16 + 2 * HALO):
         b[i, 0:16, :] = lower(i)
@@ -522,10 +490,7 @@
     b1, u = Field(b1_out, E1 + 1), Field(u_out, E1)
     coarsen_level0(at, nx, ny, b, v, b1, range(-E1 - 1, 9 + E1), pair, t)
     smooth_level1(at, nx, ny, b1, u, range(-E1, 8 + E1))
-
-
-def tiles(ny):
-    return (GROUP * ny // 16, 8, 128)
+    coarsen_level1(b1, u, b2_out, s1, t1)
 
 
 def around_block(size, extra, rows, lanes):
@@ -539,12 +504,15 @@
         around_block(16, E0, 32, 256),
         level1,
         around_block(8, E1, 24, 128),
+        (8, 128),
     ]
     scratch = [
         around_block(16, HALO, 48, 256),
         around_block(16, HALO - 1, 48, 256),
         (level1[0], 2, 48, 128),
         (level1[0], 24, 256),
+        (4, 24, 128),
+        (4, 8, 128),
     ]
     args = [at, mid, chip, link]
     return call(functools.partial(first_down_body, nx, ny), outs, scratch, args, 20000000)
@@ -562,15 +530,16 @@
 
 
 def second_down(nx, ny, at, mid, chip, link):
-    outs = [around_block(8, NEAR, 24, 128), around_block(8, NEAR - 1, 24, 128), tiles(ny)]
+    outs = [around_block(8, NEAR, 24, 128), around_block(8, NEAR - 1, 24, 128), (8, 128)]
     scratch = [(4, 24, 128), (4, 8, 128)]
     args = [at, mid, chip, link]
     return call(functools.partial(second_down_body, nx, ny), outs, scratch, args, 2000000)
 
 
 def solve_coarse(nx, ny, extra, at, coarse, s2, v2, w2, t3, b3, c3, d3, dup, row2):
-    here, fetched, other = coarse
+    fetched, other = coarse
     odd = lax.rem(at[1], 2) == 1
+    odd_layer = lax.rem(at[0] // GROUP, 2)
     _, _, _, r2, e2, r3 = reach(extra)
     spot = at[0] % GROUP
     rows2 = ny // 4
@@ -583,11 +552,15 @@
     for j in range(-blocks, blocks + 1):
         block = spot + GROUP + j
         layer, place = block // GROUP, block % GROUP
+        first_cores = jnp.where(odd_layer == 1, layer <= 1, layer >= 1)
+        mine = first_cores != odd
+        inner = inside(at[0] + j, nx // 16)
+        start = ((layer + odd_layer) // 2) * (GROUP * count // 2) + place * (count // 2)
         for n in range(count):
-            k = place * count + n
-            tile = jnp.where(
-                layer == 1, here[k], jnp.where((layer == 2) == odd, fetched[k], other[k])
-            )
+            rows = slice(8 * (n % 2), 8 * (n % 2) + 8)
+            k = start + n // 2
+            tile = jnp.where(mine, fetched[k, rows, :], other[k, rows, :])
+            tile = jnp.where(inner, tile, 0.0)
             halves = (jnp.where(lane8, tile, 0.0), jnp.where(lane8, roll(tile, 64, 1), 0.0))
             for p in range(4):
                 part = halves[p // 2][4 * (p % 2) : 4 * (p % 2) + 4, :]
@@ -710,8 +683,8 @@
     return [level1, level1, level0, level0, (max(8 + 2 * r1, 4 + 2 * r2), 2, 32, 128)]
 
 
-def turn_body(nx, ny, at, here, fetched, other, b1, u, b, v_down, v_out, wider, low, high, own, pair, t, *scratch):
-    v2 = solve_coarse(nx, ny, KEEP, at, (here, fetched, other), *scratch[:9])
+def turn_body(nx, ny, at, fetched, other, b1, u, b, v_down, v_out, wider, low, high, own, pair, t, *scratch):
+    v2 = solve_coarse(nx, ny, KEEP, at, (fetched, other), *scratch[:9])
     b = Field(b, E0 - 1)
     v = climb(nx, ny, KEEP, at, v2, Field(b1, E1 + 1), Field(u, E1), b, Field(v_down, E0), *scratch[9:])
     mask = row_mask((32, 256), at[1] * 16 - 8, ny)
@@ -739,8 +712,8 @@
     return call(functools.partial(turn_body, nx, ny), outs, scratch, args, 30000000)
 
 
-def finish_body(nx, ny, at, here, fetched, other, b1, u, b, v_down, out, *scratch):
-    v2 = solve_coarse(nx, ny, 0, at, (here, fetched, other), *scratch[:9])
+def finish_body(nx, ny, at, fetched, other, b1, u, b, v_down, out, *scratch):
+    v2 = solve_coarse(nx, ny, 0, at, (fetched, other), *scratch[:9])
     b, v_down = Field(b, E0 - 1), Field(v_down, KEEP - 2)
     v = climb(nx, ny, 0, at, v2, Field(b1, NEAR), Field(u, NEAR - 1), b, v_down, *scratch[9:])
     for p in range(16):
@@ -781,17 +754,24 @@
 
 
 def spread_coarse(b2):
-    wide, size = lax.axis_size("wide"), b2.shape[0]
-    groups = [[g * size + k for k in range(size)] for g in range(wide // GROUP)]
-    here = lax.all_to_all(b2, ("wide", "narrow"), 0, 0, axis_index_groups=groups)
-    cores, pairs = lax.axis_size("narrow"), []
-    for i in range(wide):
-        for j in range(cores):
-            k = i + (GROUP if j % 2 == 0 else -GROUP)
-            if 0 <= k < wide:
-                pairs.append((i * cores + j, k * cores + j))
-    fetched = lax.ppermute(here, ("wide", "narrow"), pairs)
-    return here, fetched, swapped(fetched, 0)
+    wide, cores = lax.axis_size("wide"), lax.axis_size("narrow")
+    layers = wide // GROUP
+    odd = lax.rem(lax.axis_index("narrow"), 2) == 1
+    other = swapped(b2, 0)
+    pair = jnp.concatenate([jnp.where(odd, other, b2), jnp.where(odd, b2, other)], axis=0)
+    groups = [
+        [
+            (((2 * k + core + i) % layers) * GROUP + x) * cores + y
+            for i in range(2)
+            for x in range(GROUP)
+            for y in range(core, cores, 2)
+        ]
+        for core in range(2)
+        for k in range(layers // 2)
+    ]
+    pieces = jnp.broadcast_to(pair[None], (len(groups[0]),) + pair.shape)
+    fetched = lax.all_to_all(pieces, ("wide", "narrow"), 0, 0, axis_index_groups=groups)
+    return fetched, swapped(fetched, 0)
 
 
 def on_device(phase, distance, velocity):
@@ -810,10 +790,8 @@
     link = swapped(jnp.where(odd, final, first), 1)
     chip = swapped(jnp.where(odd, first, final), 0)
     sends = force(nx, ny, at, mid, chip, link, velocity, xl, xh, v_chip, v_link)
-    parts = surround(*sends)
-    coarse = spread_coarse(first_source(nx, ny, at, *parts))
-    b, v, b1, u = first_down(nx, ny, at, *parts)
-    v, *sends = turn(nx, ny, at, coarse, b1, u, b, v)
+    b, v, b1, u, b2 = first_down(nx, ny, at, *surround(*sends))
+    v, *sends = turn(nx, ny, at, spread_coarse(b2), b1, u, b, v)
     b1, u, b2 = second_down(nx, ny, at, *surround(*sends))
     pressure = finish(nx, ny, at, spread_coarse(b2), b1, u, b, v)
     return (moved, pressure)

time: 156 us -> 154 us (0.987)
  waiting for transfers between devices: 42.8 us -> 32.9 us
  starting transfers between devices: 50.2 us -> 55.8 us
  blocking collectives: 35.9 us -> 40.4 us
  Pallas kernels: 24.6 us -> 23 us
    ppermute x2 -> x0, waiting for transfers between devices: 13.5 us -> none  [spread_coarse(): fetched = lax.ppermute(here, ('wide', 'narrow'), pairs)]
    ppermute x10 -> x12, starting transfers between devices: 30.4 us -> 38.6 us  [swapped(): return lax.ppermute(array, 'narrow', pairs + [(j, i) for i, j in pairs])]
    all_to_all x2, blocking collectives: 35.9 us -> 40.4 us  [spread_coarse(): lax.all_to_all(pieces, ('wide', 'narrow'), 0, 0, axis_index_groups=groups)]
    ppermute x10 -> x12, waiting for transfers between devices: 14.1 us -> 17.7 us  [swapped(): return lax.ppermute(array, 'narrow', pairs + [(j, i) for i, j in pairs])]
    ppermute x2 -> x0, starting transfers between devices: 2.56 us -> none  [spread_coarse(): fetched = lax.ppermute(here, ('wide', 'narrow'), pairs)]
    pallas_call x7 -> x6, Pallas kernels: 22.7 us -> 21.1 us  [call(): pl.pallas_call(body, out_shape=[jax.ShapeDtypeStruct(s, F32) for s in out...]
  transfers between devices with their start and end apart: 20 -> 20, of which waited for: 13 -> 14; matrix products, arithmetic and copies ran while one was open for 0% -> 0% of each run, Pallas kernels for 2% -> 0%
where the time goes in v6:
time: 154 us; the launch traced here: 153 us
  starting transfers between devices  55.8 us (36%)
  blocking collectives  40.4 us (26%)
  waiting for transfers between devices  32.9 us (21%)
  Pallas kernels  23 us (15%)
    all_to_all x2, blocking collectives, spread_coarse(): lax.all_to_all(pieces, ('wide', 'narrow'), 0, 0, axis_index_groups=groups)  40.4 us
    ppermute x12, starting transfers between devices, swapped(): return lax.ppermute(array, 'narrow', pairs + [(j, i) for i, j in pairs])  38.6 us
    pallas_call x6, Pallas kernels, call(): pl.pallas_call(body, out_shape=[jax.ShapeDtypeStruct(s, F32) for s in out...  21.1 us
    ppermute x12, waiting for transfers between devices, swapped(): return lax.ppermute(array, 'narrow', pairs + [(j, i) for i, j in pairs])  17.7 us
    ppermute x8, starting transfers between devices, shifted(): lax.ppermute(array, axis, [(i, i + step) for i in range(count) if 0 <= i...  17.2 us
    ppermute x8, waiting for transfers between devices, shifted(): lax.ppermute(array, axis, [(i, i + step) for i in range(count) if 0 <= i...  15.1 us
  transfers between devices with their start and end apart: 20, of which 14 were waited for; matrix products, arithmetic and copies ran while one was open for 0% of the time, Pallas kernels for 0%

profile of v6, /device:TPU:1, one launch (start us, length us, event | category | flops | bytes accessed | tf_op | source)
XLA Modules:
  0.0 153.3 jit_solution(9215910982471681685)
XLA Ops:
  0.6 0.0 copy-start
  0.6 0.1 pad_add_fusion.at
  0.7 1.9 %shard_map.50 = (f32[16,16,256]{2,1,0:T(8,128)S(1)}, f32[4,16,256]{2,1,0:T(8,128)S(1)}, f32[4,16,256]{2,1,0:T(8,128)S(1)}, f32[16,4,256]{2,1,0:T(4,128)S(1)}, f32[16,4,256]{2,1,0:T(4,128)S(1)}) custom-call(s32[2]{0:T(128)S(1)} %pad_add_fusion.at, s32[16,16,256]{2,1,0:T(8,128)} %phase.1, f32[16,16,256]{2,1,0:T(8,128)} %distance.1, f32[3,16,16,256]{3,2,1,0:T(8,128)} %velocity.5), custom_call_target="tpu_custom_call" | custom-call | flops 1000000 | bytes 1000000 | tf_op jit(solution)/shard_map/pallas_call | solution.py:167
  2.6 3.9 %collective-permute-start = (f32[4,16,256]{2,1,0:T(8,128)S(1)}, f32[4,16,256]{2,1,0:T(8,128)S(1)}, u32[]{:S(2)}, u32[]{:S(2)}) collective-permute-start(f32[4,16,256]{2,1,0:T(8,128)S(1)} %get-tuple-element.27), channel_id=1, source_target_pairs={{0,8},{8,16},{16,24},{24,32},{32,40},{40,48},{48,56},{56,64},{64,7... | collective-permute-start | bytes 196616 | tf_op jit(solution)/shard_map/ppermute | solution.py:732
  6.6 1.3 collective-permute-start.1
  7.9 6.1 %collective-permute-start.2 = (f32[16,4,256]{2,1,0:T(4,128)S(1)}, f32[16,4,256]{2,1,0:T(4,128)S(1)}, u32[]{:S(2)}, u32[]{:S(2)}) collective-permute-start(f32[16,4,256]{2,1,0:T(4,128)S(1)} %get-tuple-element.29), channel_id=1, source_target_pairs={{0,1},{2,3},{4,5},{6,7},{1,0},{3,2},{5,4},{7,6},{8,9},{10,11},{12,... | collective-permute-start | bytes 196616 | tf_op jit(solution)/shard_map/ppermute | solution.py:740
  14.0 1.9 %collective-permute-start.3 = (f32[16,4,256]{2,1,0:T(4,128)S(1)}, f32[16,4,256]{2,1,0:T(4,128)S(1)}, u32[]{:S(2)}, u32[]{:S(2)}) collective-permute-start(f32[16,4,256]{2,1,0:T(4,128)S(1)} %get-tuple-element.30), channel_id=1, source_target_pairs={{1,2},{3,4},{5,6},{2,1},{4,3},{6,5},{9,10},{11,12},{13,14},{10,9},... | collective-permute-start | bytes 196616 | tf_op jit(solution)/shard_map/ppermute | solution.py:740
  16.0 0.0 collective-permute-done.xl
  16.0 0.0 collective-permute-done.2.chip.v_chip
  16.0 3.6 %collective-permute-done.3.link.v_link = f32[16,4,256]{2,1,0:T(4,128)S(1)} collective-permute-done((f32[16,4,256]{2,1,0:T(4,128)S(1)}, f32[16,4,256]{2,1,0:T(4,128)S(1)}, u32[]{:S(2)}, u32[]{:S(2)}) %collective-permute-start.3) | collective-permute-done | bytes 65568 | tf_op jit(solution)/shard_map/ppermute | solution.py:740
  19.6 4.7 %shard_map.51 = (f32[16,16,256]{2,1,0:T(8,128)}, f32[22,16,256]{2,1,0:T(8,128)S(1)}, f32[3,16,256]{2,1,0:T(8,128)S(1)}, f32[3,16,256]{2,1,0:T(8,128)S(1)}) custom-call(s32[2]{0:T(128)S(1)} %pad_add_fusion.at, f32[16,16,256]{2,1,0:T(8,128)S(1)} %get-tuple-element.26.psi, f32[3,16,16,256]{3,2,1,0:T(8,128)S(1)} %copy-done, ...), custom_call_target="tpu_custom_call" | custom-call | flops 10000000 | bytes 4000000 | tf_op jit(solution)/shard_map/pallas_call | solution.py:91
  24.3 4.3 %collective-permute-start.4 = (f32[3,16,256]{2,1,0:T(8,128)S(1)}, f32[3,16,256]{2,1,0:T(8,128)S(1)}, u32[]{:S(2)}, u32[]{:S(2)}) collective-permute-start(f32[3,16,256]{2,1,0:T(8,128)S(1)} %get-tuple-element.33), channel_id=1, source_target_pairs={{0,8},{8,16},{16,24},{24,32},{32,40},{40,48},{48,56},{56,64},{64,7... | collective-permute-start | bytes 147464 | tf_op jit(solution)/shard_map/ppermute | solution.py:732
  28.6 1.3 collective-permute-start.5
  29.9 0.0 collective-permute-done.4
  29.9 3.5 %collective-permute-done.5 = f32[3,16,256]{2,1,0:T(8,128)S(1)} collective-permute-done((f32[3,16,256]{2,1,0:T(8,128)S(1)}, f32[3,16,256]{2,1,0:T(8,128)S(1)}, u32[]{:S(2)}, u32[]{:S(2)}) %collective-permute-start.5) | collective-permute-done | bytes 49184 | tf_op jit(solution)/shard_map/ppermute | solution.py:732
  33.5 3.4 %collective-permute-start.7 = (f32[22,3,256]{2,1,0:T(4,128)S(1)}, f32[22,3,256]{2,1,0:T(4,128)S(1)}, u32[]{:S(2)}, u32[]{:S(2)}) collective-permute-start(f32[22,3,256]{2,1,0:T(4,128)S(1)} %get-tuple-element.50), channel_id=1, source_target_pairs={{1,2},{3,4},{5,6},{2,1},{4,3},{6,5},{9,10},{11,12},{13,14},{10,9},... | collective-permute-start | bytes 202760 | tf_op jit(solution)/shard_map/ppermute | solution.py:740
  36.8 1.9 %collective-permute-start.6 = (f32[22,3,256]{2,1,0:T(4,128)S(1)}, f32[22,3,256]{2,1,0:T(4,128)S(1)}, u32[]{:S(2)}, u32[]{:S(2)}) collective-permute-start(f32[22,3,256]{2,1,0:T(4,128)S(1)} %get-tuple-element.51), channel_id=1, source_target_pairs={{0,1},{2,3},{4,5},{6,7},{1,0},{3,2},{5,4},{7,6},{8,9},{10,11},{12,... | collective-permute-start | bytes 202760 | tf_op jit(solution)/shard_map/ppermute | solution.py:740
  38.8 0.6 collective-permute-done.7.link
  39.3 0.7 collective-permute-done.6.chip
  40.0 2.7 %shard_map.52 = (f32[44,16,256]{2,1,0:T(8,128)S(1)}, f32[14,16,256]{2,1,0:T(8,128)S(1)}, f32[14,16,256]{2,1,0:T(8,128)S(1)}) custom-call(s32[2]{0:T(128)S(1)} %pad_add_fusion.at, f32[22,16,256]{2,1,0:T(8,128)S(1)} %constant_dynamic-update-slice_fusion.4.mid, f32[22,3,256]{2,1,0:T(4,128)S(1)} %collective-permute-done.6.chip, ...), custom_call_target="tpu_custom_call" | custom-call | flops 10000000 | bytes 4000000 | tf_op jit(solution)/shard_map/pallas_call | solution.py:91
  42.7 1.7 %collective-permute-start.8 = (f32[14,16,256]{2,1,0:T(8,128)S(1)}, f32[14,16,256]{2,1,0:T(8,128)S(1)}, u32[]{:S(2)}, u32[]{:S(2)}) collective-permute-start(f32[14,16,256]{2,1,0:T(8,128)S(1)} %get-tuple-element.36), channel_id=1, source_target_pairs={{0,8},{8,16},{16,24},{24,32},{32,40},{40,48},{48,56},{56,64},{64,7... | collective-permute-start | bytes 688136 | tf_op jit(solution)/shard_map/ppermute | solution.py:732
  44.4 1.3 collective-permute-start.9
  45.7 3.5 %collective-permute-done.8 = f32[14,16,256]{2,1,0:T(8,128)S(1)} collective-permute-done((f32[14,16,256]{2,1,0:T(8,128)S(1)}, f32[14,16,256]{2,1,0:T(8,128)S(1)}, u32[]{:S(2)}, u32[]{:S(2)}) %collective-permute-start.8) | collective-permute-done | bytes 229408 | tf_op jit(solution)/shard_map/ppermute | solution.py:732
  49.3 4.9 %collective-permute-done.9 = f32[14,16,256]{2,1,0:T(8,128)S(1)} collective-permute-done((f32[14,16,256]{2,1,0:T(8,128)S(1)}, f32[14,16,256]{2,1,0:T(8,128)S(1)}, u32[]{:S(2)}, u32[]{:S(2)}) %collective-permute-start.9) | collective-permute-done | bytes 229408 | tf_op jit(solution)/shard_map/ppermute | solution.py:732
  54.2 4.0 %collective-permute-start.11 = (f32[44,16,256]{2,1,0:T(8,128)S(1)}, f32[44,16,256]{2,1,0:T(8,128)S(1)}, u32[]{:S(2)}, u32[]{:S(2)}) collective-permute-start(f32[44,16,256]{2,1,0:T(8,128)S(1)} %constant_dynamic-update-slice_fusion.2.mid), channel_id=1, source_target_pairs={{1,2},{3,4},{5,6},{2,1},{4,3},{6,5},{9,10},{11,12},{13,14},{10,9},... | collective-permute-start | bytes 2162696 | tf_op jit(solution)/shard_map/ppermute | solution.py:740
  58.3 1.9 %collective-permute-start.10 = (f32[44,16,256]{2,1,0:T(8,128)S(1)}, f32[44,16,256]{2,1,0:T(8,128)S(1)}, u32[]{:S(2)}, u32[]{:S(2)}) collective-permute-start(f32[44,16,256]{2,1,0:T(8,128)S(1)} %constant_dynamic-update-slice_fusion.2.mid), channel_id=1, source_target_pairs={{0,1},{2,3},{4,5},{6,7},{1,0},{3,2},{5,4},{7,6},{8,9},{10,11},{12,... | collective-permute-start | bytes 2162696 | tf_op jit(solution)/shard_map/ppermute | solution.py:740
  60.2 7.0 %collective-permute-done.11.link = f32[44,16,256]{2,1,0:T(8,128)S(1)} collective-permute-done((f32[44,16,256]{2,1,0:T(8,128)S(1)}, f32[44,16,256]{2,1,0:T(8,128)S(1)}, u32[]{:S(2)}, u32[]{:S(2)}) %collective-permute-start.11) | collective-permute-done | bytes 720928 | tf_op jit(solution)/shard_map/ppermute | solution.py:740
  67.2 3.9 %shard_map.53 = (f32[26,32,256]{2,1,0:T(8,128)S(1)}, f32[28,32,256]{2,1,0:T(8,128)S(1)}, f32[20,24,128]{2,1,0:T(8,128)S(1)}, f32[18,24,128]{2,1,0:T(8,128)S(1)}, f32[8,128]{1,0:T(8,128)S(1)}) custom-call(s32[2]{0:T(128)S(1)} %pad_add_fusion.at, f32[44,16,256]{2,1,0:T(8,128)S(1)} %constant_dynamic-update-slice_fusion.2.mid, ...), custom_call_target="tpu_custom_call" | custom-call | flops 20000000 | bytes 4000000 | tf_op jit(solution)/shard_map/pallas_call | solution.py:91
  71.1 1.9 %collective-permute-start.12 = (f32[8,128]{1,0:T(8,128)S(1)}, f32[8,128]{1,0:T(8,128)S(1)}, u32[]{:S(2)}, u32[]{:S(2)}) collective-permute-start(f32[8,128]{1,0:T(8,128)S(1)} %get-tuple-element.38), channel_id=1, source_target_pairs={{0,1},{2,3},{4,5},{6,7},{1,0},{3,2},{5,4},{7,6},{8,9},{10,11},{12,... | collective-permute-start | bytes 12296 | tf_op jit(solution)/shard_map/ppermute | solution.py:740
  73.0 1.1 collective-permute-done.12
  74.2 22.3 %all_to_all.10.fetched = f32[32,16,128]{2,1,0:T(8,128)S(1)} all-to-all(f32[32,16,128]{2,1,0:T(8,128)S(1)} %broadcast_in_dim.4), channel_id=1, replica_groups={{0,2,4,6,8,10,12,14,16,18,20,22,24,26,28,30,32,34,36,38,40,42,44,46,48,..., dimensions={0} | all-to-all | bytes 524288 | tf_op jit(solution)/shard_map/all_to_all | solution.py:773
  96.5 2.1 %collective-permute-start.13 = (f32[32,16,128]{2,1,0:T(8,128)S(1)}, f32[32,16,128]{2,1,0:T(8,128)S(1)}, u32[]{:S(2)}, u32[]{:S(2)}) collective-permute-start(f32[32,16,128]{2,1,0:T(8,128)S(1)} %all_to_all.10.fetched), channel_id=1, source_target_pairs={{0,1},{2,3},{4,5},{6,7},{1,0},{3,2},{5,4},{7,6},{8,9},{10,11},{12,... | collective-permute-start | bytes 786440 | tf_op jit(solution)/shard_map/ppermute | solution.py:740
  98.6 1.3 collective-permute-done.13.other
  99.9 5.1 %shard_map.54 = (f32[20,32,256]{2,1,0:T(8,128)S(1)}, f32[16,8,128]{2,1,0:T(8,128)S(1)}, f32[4,8,128]{2,1,0:T(8,128)S(1)}, f32[4,8,128]{2,1,0:T(8,128)S(1)}) custom-call(s32[2]{0:T(128)S(1)} %pad_add_fusion.at, f32[32,16,128]{2,1,0:T(8,128)S(1)} %all_to_all.10.fetched, f32[32,16,128]{2,1,0:T(8,128)S(1)} %collective-permute-done.13.other, ...), custom_call_target="tpu_custom_call" | custom-call | flops 30000000 | bytes 4000000 | tf_op jit(solution)/shard_map/pallas_call | solution.py:91
  105.1 2.2 %collective-permute-start.14 = (f32[4,8,128]{2,1,0:T(8,128)S(1)}, f32[4,8,128]{2,1,0:T(8,128)S(1)}, u32[]{:S(2)}, u32[]{:S(2)}) collective-permute-start(f32[4,8,128]{2,1,0:T(8,128)S(1)} %get-tuple-element.44), channel_id=1, source_target_pairs={{0,8},{8,16},{16,24},{24,32},{32,40},{40,48},{48,56},{56,64},{64,7... | collective-permute-start | bytes 49160 | tf_op jit(solution)/shard_map/ppermute | solution.py:732
  107.3 1.3 collective-permute-start.15
  108.6 3.2 %collective-permute-done.15 = f32[4,8,128]{2,1,0:T(8,128)S(1)} collective-permute-done((f32[4,8,128]{2,1,0:T(8,128)S(1)}, f32[4,8,128]{2,1,0:T(8,128)S(1)}, u32[]{:S(2)}, u32[]{:S(2)}) %collective-permute-start.15) | collective-permute-done | bytes 16416 | tf_op jit(solution)/shard_map/ppermute | solution.py:732
  111.8 3.3 %collective-permute-start.17 = (f32[16,8,128]{2,1,0:T(8,128)S(1)}, f32[16,8,128]{2,1,0:T(8,128)S(1)}, u32[]{:S(2)}, u32[]{:S(2)}) collective-permute-start(f32[16,8,128]{2,1,0:T(8,128)S(1)} %constant_dynamic-update-slice_fusion.mid), channel_id=1, source_target_pairs={{1,2},{3,4},{5,6},{2,1},{4,3},{6,5},{9,10},{11,12},{13,14},{10,9},... | collective-permute-start | bytes 196616 | tf_op jit(solution)/shard_map/ppermute | solution.py:740
  115.1 1.9 %collective-permute-start.16 = (f32[16,8,128]{2,1,0:T(8,128)S(1)}, f32[16,8,128]{2,1,0:T(8,128)S(1)}, u32[]{:S(2)}, u32[]{:S(2)}) collective-permute-start(f32[16,8,128]{2,1,0:T(8,128)S(1)} %constant_dynamic-update-slice_fusion.mid), channel_id=1, source_target_pairs={{0,1},{2,3},{4,5},{6,7},{1,0},{3,2},{5,4},{7,6},{8,9},{10,11},{12,... | collective-permute-start | bytes 196616 | tf_op jit(solution)/shard_map/ppermute | solution.py:740
  117.1 0.3 collective-permute-done.17.link
  117.4 0.9 collective-permute-done.16.chip
  118.3 0.9 shard_map.55
  119.2 2.1 %collective-permute-start.18 = (f32[8,128]{1,0:T(8,128)S(1)}, f32[8,128]{1,0:T(8,128)S(1)}, u32[]{:S(2)}, u32[]{:S(2)}) collective-permute-start(f32[8,128]{1,0:T(8,128)S(1)} %get-tuple-element.46), channel_id=1, source_target_pairs={{0,1},{2,3},{4,5},{6,7},{1,0},{3,2},{5,4},{7,6},{8,9},{10,11},{12,... | collective-permute-start | bytes 12296 | tf_op jit(solution)/shard_map/ppermute | solution.py:740
  121.3 1.0 collective-permute-done.18
  122.3 18.1 %all_to_all.11.fetched = f32[32,16,128]{2,1,0:T(8,128)S(1)} all-to-all(f32[32,16,128]{2,1,0:T(8,128)S(1)} %broadcast_in_dim.5), channel_id=1, replica_groups={{0,2,4,6,8,10,12,14,16,18,20,22,24,26,28,30,32,34,36,38,40,42,44,46,48,..., dimensions={0} | all-to-all | bytes 524288 | tf_op jit(solution)/shard_map/all_to_all | solution.py:773
  140.4 8.0 %collective-permute-start.19 = (f32[32,16,128]{2,1,0:T(8,128)S(1)}, f32[32,16,128]{2,1,0:T(8,128)S(1)}, u32[]{:S(2)}, u32[]{:S(2)}) collective-permute-start(f32[32,16,128]{2,1,0:T(8,128)S(1)} %all_to_all.11.fetched), channel_id=1, source_target_pairs={{0,1},{2,3},{4,5},{6,7},{1,0},{3,2},{5,4},{7,6},{8,9},{10,11},{12,... | collective-permute-start | bytes 786440 | tf_op jit(solution)/shard_map/ppermute | solution.py:740
  148.3 1.1 collective-permute-done.19.other
  149.5 3.8 %shard_map.56 = f32[16,16,256]{2,1,0:T(8,128)} custom-call(s32[2]{0:T(128)S(1)} %pad_add_fusion.at, f32[32,16,128]{2,1,0:T(8,128)S(1)} %all_to_all.11.fetched, f32[32,16,128]{2,1,0:T(8,128)S(1)} %collective-permute-done.19.other, f32[16,24,128]{2,1,0:T(8,128)S(1)} %get-tuple-element.47.b1, f32[14,24,128]{2,1,0:T(8,128)S(1)} %get-tuple-element.48.u, ...), custom_call_target="tpu_custom_call" | custom-call | flops 20000000 | bytes 4000000 | tf_op jit(solution)/shard_map/pallas_call | solution.py:91
  (17 shorter events, 0.2 us)
Async XLA Ops:
  0.6 19.0 %copy-start = (f32[3,16,16,256]{3,2,1,0:T(8,128)S(1)}, f32[3,16,16,256]{3,2,1,0:T(8,128)}, u32[]{:S(2)}) copy-start(f32[3,16,16,256]{3,2,1,0:T(8,128)} %velocity.5) | copy-start | bytes 2359300
  2.6 13.3 %collective-permute-start = (f32[4,16,256]{2,1,0:T(8,128)S(1)}, f32[4,16,256]{2,1,0:T(8,128)S(1)}, u32[]{:S(2)}, u32[]{:S(2)}) collective-permute-start(f32[4,16,256]{2,1,0:T(8,128)S(1)} %get-tuple-element.27), channel_id=1, source_target_pairs={{0,8},{8,16},{16,24},{24,32},{32,40},{40,48},{48,56},{56,64},{64,7... | collective-permute-start | bytes 196616 | tf_op jit(solution)/shard_map/ppermute | solution.py:732
  6.6 9.4 %collective-permute-start.1 = (f32[4,16,256]{2,1,0:T(8,128)S(1)}, f32[4,16,256]{2,1,0:T(8,128)S(1)}, u32[]{:S(2)}, u32[]{:S(2)}) collective-permute-start(f32[4,16,256]{2,1,0:T(8,128)S(1)} %get-tuple-element.28), channel_id=1, source_target_pairs={{8,0},{16,8},{24,16},{32,24},{40,32},{48,40},{56,48},{64,56},{72,6... | collective-permute-start | bytes 196616 | tf_op jit(solution)/shard_map/ppermute | solution.py:732
  7.9 8.1 %collective-permute-start.2 = (f32[16,4,256]{2,1,0:T(4,128)S(1)}, f32[16,4,256]{2,1,0:T(4,128)S(1)}, u32[]{:S(2)}, u32[]{:S(2)}) collective-permute-start(f32[16,4,256]{2,1,0:T(4,128)S(1)} %get-tuple-element.29), channel_id=1, source_target_pairs={{0,1},{2,3},{4,5},{6,7},{1,0},{3,2},{5,4},{7,6},{8,9},{10,11},{12,... | collective-permute-start | bytes 196616 | tf_op jit(solution)/shard_map/ppermute | solution.py:740
  14.0 5.6 %collective-permute-start.3 = (f32[16,4,256]{2,1,0:T(4,128)S(1)}, f32[16,4,256]{2,1,0:T(4,128)S(1)}, u32[]{:S(2)}, u32[]{:S(2)}) collective-permute-start(f32[16,4,256]{2,1,0:T(4,128)S(1)} %get-tuple-element.30), channel_id=1, source_target_pairs={{1,2},{3,4},{5,6},{2,1},{4,3},{6,5},{9,10},{11,12},{13,14},{10,9},... | collective-permute-start | bytes 196616 | tf_op jit(solution)/shard_map/ppermute | solution.py:740
  24.3 5.6 %collective-permute-start.4 = (f32[3,16,256]{2,1,0:T(8,128)S(1)}, f32[3,16,256]{2,1,0:T(8,128)S(1)}, u32[]{:S(2)}, u32[]{:S(2)}) collective-permute-start(f32[3,16,256]{2,1,0:T(8,128)S(1)} %get-tuple-element.33), channel_id=1, source_target_pairs={{0,8},{8,16},{16,24},{24,32},{32,40},{40,48},{48,56},{56,64},{64,7... | collective-permute-start | bytes 147464 | tf_op jit(solution)/shard_map/ppermute | solution.py:732
  28.6 4.8 %collective-permute-start.5 = (f32[3,16,256]{2,1,0:T(8,128)S(1)}, f32[3,16,256]{2,1,0:T(8,128)S(1)}, u32[]{:S(2)}, u32[]{:S(2)}) collective-permute-start(f32[3,16,256]{2,1,0:T(8,128)S(1)} %get-tuple-element.34), channel_id=1, source_target_pairs={{8,0},{16,8},{24,16},{32,24},{40,32},{48,40},{56,48},{64,56},{72,6... | collective-permute-start | bytes 147464 | tf_op jit(solution)/shard_map/ppermute | solution.py:732
  33.5 5.8 %collective-permute-start.7 = (f32[22,3,256]{2,1,0:T(4,128)S(1)}, f32[22,3,256]{2,1,0:T(4,128)S(1)}, u32[]{:S(2)}, u32[]{:S(2)}) collective-permute-start(f32[22,3,256]{2,1,0:T(4,128)S(1)} %get-tuple-element.50), channel_id=1, source_target_pairs={{1,2},{3,4},{5,6},{2,1},{4,3},{6,5},{9,10},{11,12},{13,14},{10,9},... | collective-permute-start | bytes 202760 | tf_op jit(solution)/shard_map/ppermute | solution.py:740
  36.8 3.2 %collective-permute-start.6 = (f32[22,3,256]{2,1,0:T(4,128)S(1)}, f32[22,3,256]{2,1,0:T(4,128)S(1)}, u32[]{:S(2)}, u32[]{:S(2)}) collective-permute-start(f32[22,3,256]{2,1,0:T(4,128)S(1)} %get-tuple-element.51), channel_id=1, source_target_pairs={{0,1},{2,3},{4,5},{6,7},{1,0},{3,2},{5,4},{7,6},{8,9},{10,11},{12,... | collective-permute-start | bytes 202760 | tf_op jit(solution)/shard_map/ppermute | solution.py:740
  42.7 6.5 %collective-permute-start.8 = (f32[14,16,256]{2,1,0:T(8,128)S(1)}, f32[14,16,256]{2,1,0:T(8,128)S(1)}, u32[]{:S(2)}, u32[]{:S(2)}) collective-permute-start(f32[14,16,256]{2,1,0:T(8,128)S(1)} %get-tuple-element.36), channel_id=1, source_target_pairs={{0,8},{8,16},{16,24},{24,32},{32,40},{40,48},{48,56},{56,64},{64,7... | collective-permute-start | bytes 688136 | tf_op jit(solution)/shard_map/ppermute | solution.py:732
  44.4 9.8 %collective-permute-start.9 = (f32[14,16,256]{2,1,0:T(8,128)S(1)}, f32[14,16,256]{2,1,0:T(8,128)S(1)}, u32[]{:S(2)}, u32[]{:S(2)}) collective-permute-start(f32[14,16,256]{2,1,0:T(8,128)S(1)} %get-tuple-element.37), channel_id=1, source_target_pairs={{8,0},{16,8},{24,16},{32,24},{40,32},{48,40},{56,48},{64,56},{72,6... | collective-permute-start | bytes 688136 | tf_op jit(solution)/shard_map/ppermute | solution.py:732
  54.2 13.0 %collective-permute-start.11 = (f32[44,16,256]{2,1,0:T(8,128)S(1)}, f32[44,16,256]{2,1,0:T(8,128)S(1)}, u32[]{:S(2)}, u32[]{:S(2)}) collective-permute-start(f32[44,16,256]{2,1,0:T(8,128)S(1)} %constant_dynamic-update-slice_fusion.2.mid), channel_id=1, source_target_pairs={{1,2},{3,4},{5,6},{2,1},{4,3},{6,5},{9,10},{11,12},{13,14},{10,9},... | collective-permute-start | bytes 2162696 | tf_op jit(solution)/shard_map/ppermute | solution.py:740
  58.3 9.0 %collective-permute-start.10 = (f32[44,16,256]{2,1,0:T(8,128)S(1)}, f32[44,16,256]{2,1,0:T(8,128)S(1)}, u32[]{:S(2)}, u32[]{:S(2)}) collective-permute-start(f32[44,16,256]{2,1,0:T(8,128)S(1)} %constant_dynamic-update-slice_fusion.2.mid), channel_id=1, source_target_pairs={{0,1},{2,3},{4,5},{6,7},{1,0},{3,2},{5,4},{7,6},{8,9},{10,11},{12,... | collective-permute-start | bytes 2162696 | tf_op jit(solution)/shard_map/ppermute | solution.py:740
  71.1 3.1 %collective-permute-start.12 = (f32[8,128]{1,0:T(8,128)S(1)}, f32[8,128]{1,0:T(8,128)S(1)}, u32[]{:S(2)}, u32[]{:S(2)}) collective-permute-start(f32[8,128]{1,0:T(8,128)S(1)} %get-tuple-element.38), channel_id=1, source_target_pairs={{0,1},{2,3},{4,5},{6,7},{1,0},{3,2},{5,4},{7,6},{8,9},{10,11},{12,... | collective-permute-start | bytes 12296 | tf_op jit(solution)/shard_map/ppermute | solution.py:740
  96.5 3.4 %collective-permute-start.13 = (f32[32,16,128]{2,1,0:T(8,128)S(1)}, f32[32,16,128]{2,1,0:T(8,128)S(1)}, u32[]{:S(2)}, u32[]{:S(2)}) collective-permute-start(f32[32,16,128]{2,1,0:T(8,128)S(1)} %all_to_all.10.fetched), channel_id=1, source_target_pairs={{0,1},{2,3},{4,5},{6,7},{1,0},{3,2},{5,4},{7,6},{8,9},{10,11},{12,... | collective-permute-start | bytes 786440 | tf_op jit(solution)/shard_map/ppermute | solution.py:740
  105.1 3.5 %collective-permute-start.14 = (f32[4,8,128]{2,1,0:T(8,128)S(1)}, f32[4,8,128]{2,1,0:T(8,128)S(1)}, u32[]{:S(2)}, u32[]{:S(2)}) collective-permute-start(f32[4,8,128]{2,1,0:T(8,128)S(1)} %get-tuple-element.44), channel_id=1, source_target_pairs={{0,8},{8,16},{16,24},{24,32},{32,40},{40,48},{48,56},{56,64},{64,7... | collective-permute-start | bytes 49160 | tf_op jit(solution)/shard_map/ppermute | solution.py:732
  107.3 4.5 %collective-permute-start.15 = (f32[4,8,128]{2,1,0:T(8,128)S(1)}, f32[4,8,128]{2,1,0:T(8,128)S(1)}, u32[]{:S(2)}, u32[]{:S(2)}) collective-permute-start(f32[4,8,128]{2,1,0:T(8,128)S(1)} %get-tuple-element.45), channel_id=1, source_target_pairs={{8,0},{16,8},{24,16},{32,24},{40,32},{48,40},{56,48},{64,56},{72,6... | collective-permute-start | bytes 49160 | tf_op jit(solution)/shard_map/ppermute | solution.py:732
  111.8 5.6 %collective-permute-start.17 = (f32[16,8,128]{2,1,0:T(8,128)S(1)}, f32[16,8,128]{2,1,0:T(8,128)S(1)}, u32[]{:S(2)}, u32[]{:S(2)}) collective-permute-start(f32[16,8,128]{2,1,0:T(8,128)S(1)} %constant_dynamic-update-slice_fusion.mid), channel_id=1, source_target_pairs={{1,2},{3,4},{5,6},{2,1},{4,3},{6,5},{9,10},{11,12},{13,14},{10,9},... | collective-permute-start | bytes 196616 | tf_op jit(solution)/shard_map/ppermute | solution.py:740
  115.1 3.1 %collective-permute-start.16 = (f32[16,8,128]{2,1,0:T(8,128)S(1)}, f32[16,8,128]{2,1,0:T(8,128)S(1)}, u32[]{:S(2)}, u32[]{:S(2)}) collective-permute-start(f32[16,8,128]{2,1,0:T(8,128)S(1)} %constant_dynamic-update-slice_fusion.mid), channel_id=1, source_target_pairs={{0,1},{2,3},{4,5},{6,7},{1,0},{3,2},{5,4},{7,6},{8,9},{10,11},{12,... | collective-permute-start | bytes 196616 | tf_op jit(solution)/shard_map/ppermute | solution.py:740
  119.2 3.1 %collective-permute-start.18 = (f32[8,128]{1,0:T(8,128)S(1)}, f32[8,128]{1,0:T(8,128)S(1)}, u32[]{:S(2)}, u32[]{:S(2)}) collective-permute-start(f32[8,128]{1,0:T(8,128)S(1)} %get-tuple-element.46), channel_id=1, source_target_pairs={{0,1},{2,3},{4,5},{6,7},{1,0},{3,2},{5,4},{7,6},{8,9},{10,11},{12,... | collective-permute-start | bytes 12296 | tf_op jit(solution)/shard_map/ppermute | solution.py:740
  140.4 9.1 %collective-permute-start.19 = (f32[32,16,128]{2,1,0:T(8,128)S(1)}, f32[32,16,128]{2,1,0:T(8,128)S(1)}, u32[]{:S(2)}, u32[]{:S(2)}) collective-permute-start(f32[32,16,128]{2,1,0:T(8,128)S(1)} %all_to_all.11.fetched), channel_id=1, source_target_pairs={{0,1},{2,3},{4,5},{6,7},{1,0},{3,2},{5,4},{7,6},{8,9},{10,11},{12,... | collective-permute-start | bytes 786440 | tf_op jit(solution)/shard_map/ppermute | solution.py:740

commit v7 on v6

--- a/solution.py
+++ b/solution.py
@@ -119,10 +119,20 @@
 
 
 PARTS = 4
-
-
-def prepare_body(at, phase, distance, velocity, psi, x_low, x_high, chip, link, kind, away, x_face, y_face, sems):
-    odd = lax.rem(at[1], 2) == 1
+FAR, ALONG, ACROSS = 6, 4, 3
+SENT = FAR + ALONG + 2 * ACROSS
+
+
+def layer_cuts(dim):
+    cuts, offset = [], FAR
+    for component in range(3):
+        layers = ALONG if component == dim else ACROSS
+        cuts.append((component, layers, offset))
+        offset += layers
+    return cuts
+
+
+def prepare_body(phase, distance, velocity, psi, x_low, x_high, kind, away, sems):
     step = 16 // PARTS
     copies = []
 
@@ -135,50 +145,88 @@
         planes = pl.ds(step * k, step)
         copy(phase.at[planes], kind.at[planes])
         copy(distance.at[planes], away.at[planes])
-    copy(velocity.at[0, 0], x_face.at[0])
-    copy(velocity.at[0, 15], x_face.at[1])
-    copy(velocity.at[1, :, pl.ds(0, 8), :], y_face.at[0])
-    copy(velocity.at[1, :, pl.ds(8, 8), :], y_face.at[1])
+    for component, layers, offset in layer_cuts(0):
+        copy(velocity.at[component, pl.ds(0, layers)], x_low.at[pl.ds(offset, layers)])
+        copy(velocity.at[component, pl.ds(16 - layers, layers)], x_high.at[pl.ds(offset, layers)])
     for k in range(PARTS):
         copies[2 * k].wait()
         copies[2 * k + 1].wait()
         for i in range(step * k, step * k + step):
             orient = 2.0 * kind[i].astype(F32) - 1.0
             psi[i] = 1.0 / (1.0 + jnp.exp(-orient * away[i]))
+    for k in range(FAR):
+        x_low[k] = psi[k]
+        x_high[k] = psi[16 - FAR + k]
     for started in copies[2 * PARTS :]:
         started.wait()
-    for i in range(16):
-        first = jnp.concatenate([psi[i, 0:3, :], y_face[0, i, 0:1, :]], axis=0)
-        final = jnp.concatenate([psi[i, 13:16, :], y_face[1, i, 7:8, :]], axis=0)
-        chip[i] = jnp.where(odd, first, final)
-        link[i] = jnp.where(odd, final, first)
-    for k in range(3):
-        x_low[k] = psi[k]
-        x_high[k] = psi[13 + k]
-    x_low[3] = x_face[0]
-    x_high[3] = x_face[1]
-
-
-def prepare(at, phase, distance, velocity):
+
+
+def prepare(phase, distance, velocity):
     vmem = pl.BlockSpec(memory_space=pltpu.VMEM)
-    smem = pl.BlockSpec(memory_space=pltpu.SMEM)
     hbm = pl.BlockSpec(memory_space=pltpu.HBM)
-    outs = [(16, 16, 256), (4, 16, 256), (4, 16, 256), (16, 4, 256), (16, 4, 256)]
+    outs = [(16, 16, 256), (SENT, 16, 256), (SENT, 16, 256)]
     return pl.pallas_call(
         prepare_body,
         out_shape=[jax.ShapeDtypeStruct(s, F32) for s in outs],
-        in_specs=[smem, hbm, hbm, hbm],
+        in_specs=[hbm, hbm, hbm],
         out_specs=[vmem] * len(outs),
         scratch_shapes=[
             pltpu.VMEM((16, 16, 256), jnp.int32),
             pltpu.VMEM((16, 16, 256), F32),
-            pltpu.VMEM((2, 16, 256), F32),
-            pltpu.VMEM((2, 16, 8, 256), F32),
-            pltpu.SemaphoreType.DMA((2 * PARTS + 4,)),
+            pltpu.SemaphoreType.DMA((2 * PARTS + 6,)),
         ],
         compiler_params=pltpu.CompilerParams(vmem_limit_bytes=8 << 20),
         cost_estimate=pl.CostEstimate(flops=1000000, bytes_accessed=1000000, transcendentals=0),
-    )(at, *(pltpu.with_memory_space_constraint(a, pltpu.HBM) for a in (phase, distance, velocity)))
+    )(*(pltpu.with_memory_space_constraint(a, pltpu.HBM) for a in (phase, distance, velocity)))
+
+
+def plane_of(own, low, high, p, offset, layers):
+    if p < 0:
+        return low[offset + layers + p]
+    return own(p) if p < 16 else high[offset + p - 16]
+
+
+def wide_planes(psi, velocity, low, high):
+    def level(p):
+        return plane_of(lambda k: psi[k], low, high, p, 0, FAR)
+
+    def speed(component):
+        _, layers, offset = layer_cuts(0)[component]
+
+        def at_plane(p):
+            if not -layers <= p < 16 + layers:
+                return None
+            return plane_of(lambda k: velocity[component, k], low, high, p, offset, layers)
+
+        return at_plane
+
+    return level, [speed(c) for c in range(3)]
+
+
+def pack_body(at, psi, velocity, low, high, chip, link):
+    odd = lax.rem(at[1], 2) == 1
+    level, speeds = wide_planes(psi, velocity, low, high)
+    for k in range(16 + 2 * FAR):
+        v = level(k - FAR)
+        first, final = [v[0:FAR]], [v[16 - FAR : 16]]
+        for component, layers, _ in layer_cuts(1):
+            w = speeds[component](k - FAR)
+            if w is None:
+                w = jnp.zeros((16, 256), F32)
+            first.append(w[0:layers])
+            final.append(w[16 - layers : 16])
+        first = jnp.concatenate(first, axis=0)
+        final = jnp.concatenate(final, axis=0)
+        chip[k] = jnp.where(odd, first, final)
+        link[k] = jnp.where(odd, final, first)
+
+
+def pack(at, psi, velocity, low, high):
+    outs = [(16 + 2 * FAR, SENT, 256)] * 2
+    return call(pack_body, outs, [], [at, psi, velocity, low, high], 1000000)
+
+
+FACE = 0.25 / 12.0
 
 
 def indicators(a, b, c):
@@ -198,184 +246,166 @@
     pick = lambda x, y: jnp.where(ahead, x, y)
     a, b, c, e, f = pick(l[0], l[5]), pick(l[1], l[4]), pick(l[2], l[3]), pick(l[3], l[2]), pick(l[4], l[1])
     p, q, r = pick(p_left, r_right), pick(q_left, q_right), pick(r_left, p_right)
-    w0, w1, w2 = 0.1 * (q * r), 0.6 * (p * r), 0.3 * (p * q)
+    w0, w1, w2 = q * r, 6.0 * (p * r), 3.0 * (p * q)
     g0 = 2.0 * a - 7.0 * b + 11.0 * c
     g1 = 5.0 * c + 2.0 * e - b
     g2 = 2.0 * c + 5.0 * e - f
     top = w0 * g0 + w1 * g1 + w2 * g2
-    return (s * top) / (6.0 * (w0 + w1 + w2))
-
-
-def transport_body(at, psi, velocity, xl, xh, chip, link, moved, wider, low, high, ext, p_x, q_x, r_x, rows, speed):
+    total = w0 + w1 + w2
+    return (s * top) / total
+
+
+def z_change(v, w):
+    lane = iota(v.shape, 1)
+
+    def ahead(x, k):
+        return jnp.where(lane > 255 - k, 0.0, roll(x, -k, 1))
+
+    def behind(x, k):
+        return jnp.where(lane < k, 0.0, roll(x, k, 1))
+
+    l = [behind(v, 2), behind(v, 1), v, ahead(v, 1), ahead(v, 2), ahead(v, 3)]
+    s = FACE * (w + ahead(w, 1))
+    p, q, r = indicators(l[1], l[2], l[3])
+    _, q1, r1 = indicators(l[2], l[3], l[4])
+    _, _, r2 = indicators(l[3], l[4], l[5])
+    p0, _, _ = indicators(l[0], l[1], l[2])
+    flux = upwind_flux(s, l, p0, q, r1, p, q1, r2)
+    low = slice(0, 128)
+    c = v[:, low]
+    none = jnp.zeros_like(c)
+    square = c * c
+    edge = WENO_EPS + (13.0 / 12.0 + 9.0 / 4.0) * square
+    level = WENO_EPS + (13.0 / 12.0 + 1.0 / 4.0) * square
+    wall_flux = upwind_flux(
+        FACE * w[:, low],
+        [none, none, none, c, l[3][:, low], l[4][:, low]],
+        none + WENO_EPS * WENO_EPS, level * level, r[:, low],
+        edge * edge, q[:, low], r1[:, low],
+    )
+    wall_flux = jnp.concatenate([wall_flux, wall_flux], axis=1)
+    return flux - jnp.where(lane == 0, wall_flux, roll(flux, 1, 1))
+
+
+def y_change(v, w):
+    s = FACE * (w + roll(w, -1, 0))
+    l = [roll(v, 2 - k, 0) for k in range(6)]
+    p, q, r = indicators(l[1], l[2], l[3])
+    q_next, r_next = roll(q, -1, 0), roll(r, -1, 0)
+    flux = upwind_flux(s, l, roll(p, 1, 0), q, r_next, p, q_next, roll(r, -2, 0))
+    return flux - roll(flux, 1, 0)
+
+
+SKIN = 3
+
+
+def advance_body(
+    nx, ny, at, psi, velocity, low, high, chip, link, moved, wider, first, final,
+    v24, v32, u24, u32, w24, p_x, q_x, r_x, m, n_x, n_y, n_z, s_x, part, source,
+):
     lower, upper = pick_sides(at, chip, link)
-    for k in range(3):
-        ext[k] = xl[k]
-        ext[19 + k] = xh[k]
-
-    def fill(i, carry):
-        ext[3 + i] = psi[i]
-        return carry
-
-    lax.fori_loop(0, 16, fill, 0, unroll=True)
-
-    def marks(i, carry):
-        p, q, r = indicators(ext[i], ext[i + 1], ext[i + 2])
-        p_x[i], q_x[i], r_x[i] = p, q, r
-        return carry
-
-    lax.fori_loop(0, 20, marks, 0, unroll=True)
-
-    def x_flux(j, v_low, v_high):
-        s = 0.5 * (v_low + v_high)
-        l = [ext[j + k] for k in range(6)]
+    level, speeds = wide_planes(psi, velocity, low, high)
+    cuts = layer_cuts(1)
+
+    def place(ref, i, start, rows, layers, below, above):
+        total = ref.shape[1]
+        ref[i, start - layers : start, :] = below
+        ref[i, start : start + 16, :] = rows
+        ref[i, start + 16 : start + 16 + layers, :] = above
+        if start - layers:
+            ref[i, 0 : start - layers, :] = jnp.zeros((start - layers, 256), F32)
+        rest = total - start - 16 - layers
+        if rest:
+            ref[i, total - rest : total, :] = jnp.zeros((rest, 256), F32)
+
+    for i in range(16 + 2 * FAR):
+        p = i - FAR
+        below, above = lower(i), upper(i)
+        rows = level(p)
+        place(v24, i, 4, rows, 4, below[FAR - 4 : FAR], above[0:4])
+        if -SKIN <= p < 16 + SKIN:
+            place(v32, p + SKIN, 8, rows, FAR, below[0:FAR], above[0:FAR])
+        for component, ref, start in ((0, u24, 4), (1, u32, 8), (2, w24, 4)):
+            rows = speeds[component](p)
+            if rows is not None:
+                _, count, offset = cuts[component]
+                _, layers, _ = layer_cuts(0)[component]
+                cut = slice(offset, offset + count)
+                place(ref, p + layers, start, rows, count, below[cut], above[cut])
+
+    for i in range(26):
+        p_x[i], q_x[i], r_x[i] = indicators(v24[i], v24[i + 1], v24[i + 2])
+
+    def x_flux(f):
+        s = FACE * (u24[f - 1 + ALONG] + u24[f + ALONG])
+        l = [v24[f - 3 + k + FAR] for k in range(6)]
         return upwind_flux(
-            s, l, p_x[j], q_x[j + 1], r_x[j + 2], p_x[j + 1], q_x[j + 2], r_x[j + 3]
+            s, l, p_x[f + 3], q_x[f + 4], r_x[f + 5], p_x[f + 4], q_x[f + 5], r_x[f + 6]
         )
 
-    def plane(i, below):
-        here = velocity[0, i]
-        following = jnp.where(i == 15, xh[3], velocity[0, jnp.minimum(i + 1, 15)])
-        above = x_flux(i + 1, here, following)
+    shape = (24, 256)
+    mask = row_mask(shape, at[1] * 16 - 4, ny)
+    below = x_flux(-SKIN)
+    for p in range(-SKIN, 16 + SKIN):
+        above = x_flux(p + 1)
+        v = v24[p + FAR]
         change = above - below
-        y_low, y_high = lower(i), upper(i)
-        rows[1:4, :] = y_low[0:3, :]
-        rows[4:20, :] = psi[i]
-        rows[20:23, :] = y_high[0:3, :]
-        speed[3:4, :] = y_low[3:4, :]
-        speed[4:20, :] = velocity[1, i]
-        speed[20:21, :] = y_high[3:4, :]
-        v = rows[...]
-        u = speed[...]
-        s = 0.5 * (u + roll(u, -1, 0))
-        l = [roll(v, 2 - k, 0) for k in range(6)]
-        p, q, r = indicators(l[1], l[2], l[3])
-        q_next, r_next = roll(q, -1, 0), roll(r, -1, 0)
-        flux = upwind_flux(s, l, roll(p, 1, 0), q, r_next, p, q_next, roll(r, -2, 0))
-        rows_change = flux - roll(flux, 1, 0)
-        change = change + rows_change[4:20, :]
-        v = psi[i]
-        w = velocity[2, i]
-        lane = iota(v.shape, 1)
-
-        def ahead(x, k):
-            return jnp.where(lane > 255 - k, 0.0, roll(x, -k, 1))
-
-        def behind(x, k):
-            return jnp.where(lane < k, 0.0, roll(x, k, 1))
-
-        l = [behind(v, 2), behind(v, 1), v, ahead(v, 1), ahead(v, 2), ahead(v, 3)]
-        s = 0.5 * (w + ahead(w, 1))
-        p, q, r = indicators(l[1], l[2], l[3])
-        _, q1, r1 = indicators(l[2], l[3], l[4])
-        _, _, r2 = indicators(l[3], l[4], l[5])
-        p0, _, _ = indicators(l[0], l[1], l[2])
-        flux = upwind_flux(s, l, p0, q, r1, p, q1, r2)
-        low = slice(0, 128)
-        c = v[:, low]
-        none = jnp.zeros_like(c)
-        square = c * c
-        edge = WENO_EPS + (13.0 / 12.0 + 9.0 / 4.0) * square
-        level = WENO_EPS + (13.0 / 12.0 + 1.0 / 4.0) * square
-        wall = upwind_flux(
-            0.5 * w[:, low],
-            [none, none, none, c, l[3][:, low], l[4][:, low]],
-            none + WENO_EPS * WENO_EPS, level * level, r[:, low],
-            edge * edge, q[:, low], r1[:, low],
+        change = change + y_change(v32[p + SKIN], u32[p + ACROSS])[4:28, :]
+        change = change + z_change(v, w24[p + ACROSS])
+        below = above
+        value = wall(at, nx, 0, p, (v - change) * mask)
+        m[p + SKIN] = value
+        if 0 <= p < 16:
+            moved[p] = value[4:20, :]
+
+    lane = iota(shape, 1)
+
+    def gradient(p):
+        c = m[p + SKIN]
+        down, ahead = z_shifted(c)
+        gx = 0.5 * (m[p + SKIN + 1] - m[p + SKIN - 1])
+        gy = 0.5 * (roll(c, -1, 0) - roll(c, 1, 0))
+        return gx, gy, 0.5 * (ahead - down)
+
+    for p in range(-2, 18):
+        gx, gy, gz = gradient(p)
+        inverse = lax.rsqrt(gx * gx + gy * gy + gz * gz + DELTA_SQ)
+        n_x[p + 2], n_y[p + 2], n_z[p + 2] = gx * inverse, gy * inverse, gz * inverse
+    for p in range(-1, 17):
+        gx, gy, gz = gradient(p)
+        edge = 0.5 * m[p + SKIN]
+        edge = edge * lax.rsqrt(edge * edge + DELTA_SQ)
+        nz, ny_here = n_z[p + 2], n_y[p + 2]
+        ahead = jnp.where(lane == 255, -edge, roll(nz, -1, 1))
+        behind = jnp.where(lane == 0, edge, roll(nz, 1, 1))
+        bending = -0.5 * (
+            (n_x[p + 3] - n_x[p + 1])
+            + (roll(ny_here, -1, 0) - roll(ny_here, 1, 0))
+            + (ahead - behind)
         )
-        wall = jnp.concatenate([wall, wall], axis=1)
-        change = change + (flux - jnp.where(lane == 0, wall, roll(flux, 1, 1)))
-        moved[i] = v - 0.25 * change
-        return above
-
-    rows[...] = jnp.zeros_like(rows)
-    speed[...] = jnp.zeros_like(speed)
-    lax.fori_loop(0, 16, plane, x_flux(0, xl[3], velocity[0, 0]), unroll=True)
-    send(moved, wider, low, high, 3)
-
-
-def transport(at, psi, velocity, xl, xh, chip, link):
-    planes = (20, 16, 256)
-    scratch = [(22, 16, 256), planes, planes, planes, (24, 256), (24, 256)]
-    outs = [(16, 16, 256)] + send_shapes(3)
-    return call(transport_body, outs, scratch, [at, psi, velocity, xl, xh, chip, link], 10000000)
-
-
-def force_body(nx, ny, at, mid, chip, link, velocity, xl, xh, v_chip, v_link, wider, low, high, m, n_x, n_y, n_z, s_x, part, pad, source):
-    lower, upper = pick_sides(at, chip, link)
-    v_lower, v_upper = pick_sides(at, v_chip, v_link)
-    x0, y0 = at[0] * 16, at[1] * 16
-    shape = (32, 256)
-    lane = iota(shape, 1)
-
-    def fill(i, carry):
-        m[i] = jnp.zeros(shape, F32)
-        m[i, 5:8, :] = lower(i)
-        m[i, 8:24, :] = mid[i]
-        m[i, 24:27, :] = upper(i)
-        return carry
-
-    lax.fori_loop(0, 22, fill, 0, unroll=True)
-
-    def gradient(i):
-        c = m[i]
-        below, above = z_shifted(c)
-        gx = 0.5 * (m[i + 1] - m[i - 1])
-        gy = 0.5 * (roll(c, -1, 0) - roll(c, 1, 0))
-        return gx, gy, 0.5 * (above - below)
-
-    def normals(i, carry):
-        gx, gy, gz = gradient(i + 1)
-        inverse = lax.rsqrt(gx * gx + gy * gy + gz * gz + DELTA_SQ)
-        n_x[i], n_y[i], n_z[i] = gx * inverse, gy * inverse, gz * inverse
-        return carry
-
-    lax.fori_loop(0, 20, normals, 0, unroll=True)
-    mask_y = row_mask(shape, y0 - 8, ny)
-
-    def stars(i, carry):
-        gx, gy, gz = gradient(i + 2)
-        c = m[i + 2]
-        edge = 0.5 * c
-        edge = edge * lax.rsqrt(edge * edge + DELTA_SQ)
-        nz = n_z[i + 1]
-        above = jnp.where(lane == 255, -edge, roll(nz, -1, 1))
-        below = jnp.where(lane == 0, edge, roll(nz, 1, 1))
-        nn = n_y[i + 1]
-        bending = -0.5 * (
-            (n_x[i + 2] - n_x[i]) + (roll(nn, -1, 0) - roll(nn, 1, 0)) + (above - below)
-        )
-        keep = mask_y * plane_factor(x0 + i - 1, nx)
-        bending = bending * keep
-        fx, fy, fz = bending * gx, bending * gy, bending * gz
-        k = jnp.clip(i - 1, 0, 15)
-        vx = jnp.where(i == 0, xl[3], jnp.where(i == 17, xh[3], velocity[0, k]))
-        s_x[i] = fx[8:24, :] + vx
-        pad[7:8, :] = v_lower(k)[3:4, :]
-        pad[8:24, :] = velocity[1, k]
-        pad[24:25, :] = v_upper(k)[3:4, :]
-        sy = fy + pad[...]
-        dy = roll(sy, -1, 0) - roll(sy, 1, 0)
-        sz = fz[8:24, :] + velocity[2, k]
-        below, above = z_shifted(sz)
-        part[i] = dy[8:24, :] + (above - below)
-        return carry
-
-    pad[...] = jnp.zeros_like(pad)
-    lax.fori_loop(0, 18, stars, 0, unroll=True)
-
-    def finish(i, carry):
-        source[i] = -0.5 * (part[i + 1] + (s_x[i + 2] - s_x[i]))
-        return carry
-
-    lax.fori_loop(0, 16, finish, 0, unroll=True)
-    send(source, wider, low, high, HALO)
-
-
-def force(nx, ny, at, mid, chip, link, velocity, xl, xh, v_chip, v_link):
-    n = (20, 32, 256)
-    scratch = [(22, 32, 256), n, n, n, (18, 16, 256), (18, 16, 256), (32, 256), (16, 16, 256)]
-    args = [at, mid, chip, link, velocity, xl, xh, v_chip, v_link]
-    return call(functools.partial(force_body, nx, ny), send_shapes(HALO), scratch, args, 10000000)
+        bending = wall(at, nx, 0, p, bending * mask)
+        s_x[p + 1] = (bending * gx)[4:20, :] + u24[p + ALONG, 4:20, :]
+        if 0 <= p < 16:
+            sy = bending * gy + u32[p + ACROSS, 4:28, :]
+            dy = roll(sy, -1, 0) - roll(sy, 1, 0)
+            sz = (bending * gz)[4:20, :] + velocity[2, p]
+            behind, ahead = z_shifted(sz)
+            part[p] = dy[4:20, :] + (ahead - behind)
+    for p in range(16):
+        source[p] = -0.5 * (part[p] + (s_x[p + 2] - s_x[p]))
+    send(source, wider, first, final, HALO)
+
+
+def advance(nx, ny, at, psi, velocity, low, high, chip, link):
+    marks, normals, block = (26, 24, 256), (20, 24, 256), (16, 16, 256)
+    scratch = [
+        (16 + 2 * FAR, 24, 256), (16 + 2 * SKIN, 32, 256), (16 + 2 * ALONG, 24, 256),
+        (16 + 2 * ACROSS, 32, 256), (16 + 2 * ACROSS, 24, 256), marks, marks, marks,
+        (16 + 2 * SKIN, 24, 256), normals, normals, normals, (18, 16, 256), block, block,
+    ]
+    args = [at, psi, velocity, low, high, chip, link]
+    outs = [block] + send_shapes(HALO)
+    return call(functools.partial(advance_body, nx, ny), outs, scratch, args, 30000000)
 
 
 class Field:
@@ -776,20 +806,13 @@
 
 def on_device(phase, distance, velocity):
     nx, ny = 16 * lax.axis_size("wide"), 16 * lax.axis_size("narrow")
-    narrow = lax.axis_index("narrow")
-    at = jnp.stack([lax.axis_index("wide"), narrow]).astype(jnp.int32)
-    psi, x_low, x_high, chip, link = prepare(at, phase, distance, velocity)
-    xl = shifted(x_high, "wide", 1)
-    xh = shifted(x_low, "wide", -1)
+    at = jnp.stack([lax.axis_index("wide"), lax.axis_index("narrow")]).astype(jnp.int32)
+    psi, x_low, x_high = prepare(phase, distance, velocity)
+    low, high = shifted(x_high, "wide", 1), shifted(x_low, "wide", -1)
+    chip, link = pack(at, psi, velocity, low, high)
     v_link = swapped(link, 1)
     v_chip = swapped(chip, 0)
-    moved, *sends = transport(at, psi, velocity, xl, xh, v_chip, v_link)
-    mid = widen(*sends)
-    odd = lax.rem(narrow, 2) == 1
-    first, final = mid[:, :3, :], mid[:, 13:, :]
-    link = swapped(jnp.where(odd, final, first), 1)
-    chip = swapped(jnp.where(odd, first, final), 0)
-    sends = force(nx, ny, at, mid, chip, link, velocity, xl, xh, v_chip, v_link)
+    moved, *sends = advance(nx, ny, at, psi, velocity, low, high, v_chip, v_link)
     b, v, b1, u, b2 = first_down(nx, ny, at, *surround(*sends))
     v, *sends = turn(nx, ny, at, spread_coarse(b2), b1, u, b, v)
     b1, u, b2 = second_down(nx, ny, at, *surround(*sends))

time: 154 us -> 149 us (0.968)
  starting transfers between devices: 55.8 us -> 46.7 us
  Pallas kernels: 23 us -> 25.2 us
  waiting for transfers between devices: 32.9 us -> 35 us
    ppermute x8 -> x6, starting transfers between devices: 17.2 us -> 11.3 us  [shifted(): lax.ppermute(array, axis, [(i, i + step) for i in range(count) if 0 <= i...]
    ppermute x12 -> x10, starting transfers between devices: 38.6 us -> 35.4 us  [swapped(): return lax.ppermute(array, 'narrow', pairs + [(j, i) for i, j in pairs])]
    ppermute x12 -> x10, waiting for transfers between devices: 17.7 us -> 20.7 us  [swapped(): return lax.ppermute(array, 'narrow', pairs + [(j, i) for i, j in pairs])]
    pallas_call x6, Pallas kernels: 21.1 us -> 23.8 us  [call(): pl.pallas_call(body, out_shape=[jax.ShapeDtypeStruct(s, F32) for s in out...]
    ppermute x8 -> x6, waiting for transfers between devices: 15.1 us -> 14.3 us  [shifted(): lax.ppermute(array, axis, [(i, i + step) for i in range(count) if 0 <= i...]
  transfers between devices with their start and end apart: 20 -> 16, of which waited for: 14 -> 13; matrix products, arithmetic and copies ran while one was open for 0% -> 0% of each run, Pallas kernels for 0% -> 0%
where the time goes in v7:
time: 149 us; the launch traced here: 148 us
  starting transfers between devices  46.7 us (31%)
  blocking collectives  40.1 us (27%)
  waiting for transfers between devices  35 us (23%)
  Pallas kernels  25.2 us (17%)
    all_to_all x2, blocking collectives, spread_coarse(): lax.all_to_all(pieces, ('wide', 'narrow'), 0, 0, axis_index_groups=groups)  40.1 us
    ppermute x10, starting transfers between devices, swapped(): return lax.ppermute(array, 'narrow', pairs + [(j, i) for i, j in pairs])  35.4 us
    pallas_call x6, Pallas kernels, call(): pl.pallas_call(body, out_shape=[jax.ShapeDtypeStruct(s, F32) for s in out...  23.8 us
    ppermute x10, waiting for transfers between devices, swapped(): return lax.ppermute(array, 'narrow', pairs + [(j, i) for i, j in pairs])  20.7 us
    ppermute x6, waiting for transfers between devices, shifted(): lax.ppermute(array, axis, [(i, i + step) for i in range(count) if 0 <= i...  14.3 us
    ppermute x6, starting transfers between devices, shifted(): lax.ppermute(array, axis, [(i, i + step) for i in range(count) if 0 <= i...  11.3 us
  transfers between devices with their start and end apart: 16, of which 13 were waited for; matrix products, arithmetic and copies ran while one was open for 0% of the time, Pallas kernels for 0%

profile of v7, /device:TPU:1, one launch (start us, length us, event | category | flops | bytes accessed | tf_op | source)
XLA Modules:
  0.0 148.0 jit_solution(16985089616424354384)
XLA Ops:
  0.6 0.0 copy-start
  0.6 1.3 shard_map.50
  2.0 4.0 %collective-permute-start = (f32[16,16,256]{2,1,0:T(8,128)S(1)}, f32[16,16,256]{2,1,0:T(8,128)S(1)}, u32[]{:S(2)}, u32[]{:S(2)}) collective-permute-start(f32[16,16,256]{2,1,0:T(8,128)S(1)} %get-tuple-element.24), channel_id=1, source_target_pairs={{0,8},{8,16},{16,24},{24,32},{32,40},{40,48},{48,56},{56,64},{64,7... | collective-permute-start | bytes 786440 | tf_op jit(solution)/shard_map/ppermute | solution.py:762
  5.9 1.3 collective-permute-start.1
  7.2 0.1 pad_add_fusion.at
  7.3 1.9 %collective-permute-done.low = f32[16,16,256]{2,1,0:T(8,128)S(1)} collective-permute-done((f32[16,16,256]{2,1,0:T(8,128)S(1)}, f32[16,16,256]{2,1,0:T(8,128)S(1)}, u32[]{:S(2)}, u32[]{:S(2)}) %collective-permute-start) | collective-permute-done | bytes 262176 | tf_op jit(solution)/shard_map/ppermute | solution.py:762
  9.2 3.8 %collective-permute-done.1.high = f32[16,16,256]{2,1,0:T(8,128)S(1)} collective-permute-done((f32[16,16,256]{2,1,0:T(8,128)S(1)}, f32[16,16,256]{2,1,0:T(8,128)S(1)}, u32[]{:S(2)}, u32[]{:S(2)}) %collective-permute-start.1) | collective-permute-done | bytes 262176 | tf_op jit(solution)/shard_map/ppermute | solution.py:762
  13.1 0.0 copy-done
  13.1 0.7 shard_map.51
  13.7 7.3 %collective-permute-start.2 = (f32[28,16,256]{2,1,0:T(8,128)S(1)}, f32[28,16,256]{2,1,0:T(8,128)S(1)}, u32[]{:S(2)}, u32[]{:S(2)}) collective-permute-start(f32[28,16,256]{2,1,0:T(8,128)S(1)} %get-tuple-element.26), channel_id=1, source_target_pairs={{0,1},{2,3},{4,5},{6,7},{1,0},{3,2},{5,4},{7,6},{8,9},{10,11},{12,... | collective-permute-start | bytes 1376264 | tf_op jit(solution)/shard_map/ppermute | solution.py:770
  21.0 1.9 %collective-permute-start.3 = (f32[28,16,256]{2,1,0:T(8,128)S(1)}, f32[28,16,256]{2,1,0:T(8,128)S(1)}, u32[]{:S(2)}, u32[]{:S(2)}) collective-permute-start(f32[28,16,256]{2,1,0:T(8,128)S(1)} %get-tuple-element.27), channel_id=1, source_target_pairs={{1,2},{3,4},{5,6},{2,1},{4,3},{6,5},{9,10},{11,12},{13,14},{10,9},... | collective-permute-start | bytes 1376264 | tf_op jit(solution)/shard_map/ppermute | solution.py:770
  22.9 0.0 collective-permute-done.2.chip
  22.9 7.9 %collective-permute-done.3.link = f32[28,16,256]{2,1,0:T(8,128)S(1)} collective-permute-done((f32[28,16,256]{2,1,0:T(8,128)S(1)}, f32[28,16,256]{2,1,0:T(8,128)S(1)}, u32[]{:S(2)}, u32[]{:S(2)}) %collective-permute-start.3) | collective-permute-done | bytes 458784 | tf_op jit(solution)/shard_map/ppermute | solution.py:770
  30.8 9.6 %shard_map.52 = (f32[16,16,256]{2,1,0:T(8,128)}, f32[44,16,256]{2,1,0:T(8,128)S(1)}, f32[14,16,256]{2,1,0:T(8,128)S(1)}, f32[14,16,256]{2,1,0:T(8,128)S(1)}) custom-call(s32[2]{0:T(128)S(1)} %pad_add_fusion.at, f32[16,16,256]{2,1,0:T(8,128)S(1)} %get-tuple-element.23.psi, f32[3,16,16,256]{3,2,1,0:T(8,128)S(1)} %copy-done, ...), custom_call_target="tpu_custom_call" | custom-call | flops 30000000 | bytes 4000000 | tf_op jit(solution)/shard_map/pallas_call | solution.py:91
  40.4 1.3 collective-permute-start.4
  41.7 1.3 collective-permute-start.5
  43.0 1.6 %collective-permute-done.4 = f32[14,16,256]{2,1,0:T(8,128)S(1)} collective-permute-done((f32[14,16,256]{2,1,0:T(8,128)S(1)}, f32[14,16,256]{2,1,0:T(8,128)S(1)}, u32[]{:S(2)}, u32[]{:S(2)}) %collective-permute-start.4) | collective-permute-done | bytes 229408 | tf_op jit(solution)/shard_map/ppermute | solution.py:762
  44.7 3.8 %collective-permute-done.5 = f32[14,16,256]{2,1,0:T(8,128)S(1)} collective-permute-done((f32[14,16,256]{2,1,0:T(8,128)S(1)}, f32[14,16,256]{2,1,0:T(8,128)S(1)}, u32[]{:S(2)}, u32[]{:S(2)}) %collective-permute-start.5) | collective-permute-done | bytes 229408 | tf_op jit(solution)/shard_map/ppermute | solution.py:762
  48.5 6.2 %collective-permute-start.7 = (f32[44,16,256]{2,1,0:T(8,128)S(1)}, f32[44,16,256]{2,1,0:T(8,128)S(1)}, u32[]{:S(2)}, u32[]{:S(2)}) collective-permute-start(f32[44,16,256]{2,1,0:T(8,128)S(1)} %constant_dynamic-update-slice_fusion.2.mid), channel_id=1, source_target_pairs={{1,2},{3,4},{5,6},{2,1},{4,3},{6,5},{9,10},{11,12},{13,14},{10,9},... | collective-permute-start | bytes 2162696 | tf_op jit(solution)/shard_map/ppermute | solution.py:770
  54.7 2.1 %collective-permute-start.6 = (f32[44,16,256]{2,1,0:T(8,128)S(1)}, f32[44,16,256]{2,1,0:T(8,128)S(1)}, u32[]{:S(2)}, u32[]{:S(2)}) collective-permute-start(f32[44,16,256]{2,1,0:T(8,128)S(1)} %constant_dynamic-update-slice_fusion.2.mid), channel_id=1, source_target_pairs={{0,1},{2,3},{4,5},{6,7},{1,0},{3,2},{5,4},{7,6},{8,9},{10,11},{12,... | collective-permute-start | bytes 2162696 | tf_op jit(solution)/shard_map/ppermute | solution.py:770
  56.8 6.8 %collective-permute-done.7.link = f32[44,16,256]{2,1,0:T(8,128)S(1)} collective-permute-done((f32[44,16,256]{2,1,0:T(8,128)S(1)}, f32[44,16,256]{2,1,0:T(8,128)S(1)}, u32[]{:S(2)}, u32[]{:S(2)}) %collective-permute-start.7) | collective-permute-done | bytes 720928 | tf_op jit(solution)/shard_map/ppermute | solution.py:770
  63.7 0.0 collective-permute-done.6.chip
  63.7 3.8 %shard_map.53 = (f32[26,32,256]{2,1,0:T(8,128)S(1)}, f32[28,32,256]{2,1,0:T(8,128)S(1)}, f32[20,24,128]{2,1,0:T(8,128)S(1)}, f32[18,24,128]{2,1,0:T(8,128)S(1)}, f32[8,128]{1,0:T(8,128)S(1)}) custom-call(s32[2]{0:T(128)S(1)} %pad_add_fusion.at, f32[44,16,256]{2,1,0:T(8,128)S(1)} %constant_dynamic-update-slice_fusion.2.mid, ...), custom_call_target="tpu_custom_call" | custom-call | flops 20000000 | bytes 4000000 | tf_op jit(solution)/shard_map/pallas_call | solution.py:91
  67.5 1.9 %collective-permute-start.8 = (f32[8,128]{1,0:T(8,128)S(1)}, f32[8,128]{1,0:T(8,128)S(1)}, u32[]{:S(2)}, u32[]{:S(2)}) collective-permute-start(f32[8,128]{1,0:T(8,128)S(1)} %get-tuple-element.32), channel_id=1, source_target_pairs={{0,1},{2,3},{4,5},{6,7},{1,0},{3,2},{5,4},{7,6},{8,9},{10,11},{12,... | collective-permute-start | bytes 12296 | tf_op jit(solution)/shard_map/ppermute | solution.py:770
  69.4 1.1 collective-permute-done.8
  70.6 22.0 %all_to_all.10.fetched = f32[32,16,128]{2,1,0:T(8,128)S(1)} all-to-all(f32[32,16,128]{2,1,0:T(8,128)S(1)} %broadcast_in_dim.4), channel_id=1, replica_groups={{0,2,4,6,8,10,12,14,16,18,20,22,24,26,28,30,32,34,36,38,40,42,44,46,48,..., dimensions={0} | all-to-all | bytes 524288 | tf_op jit(solution)/shard_map/all_to_all | solution.py:803
  92.5 1.9 %collective-permute-start.9 = (f32[32,16,128]{2,1,0:T(8,128)S(1)}, f32[32,16,128]{2,1,0:T(8,128)S(1)}, u32[]{:S(2)}, u32[]{:S(2)}) collective-permute-start(f32[32,16,128]{2,1,0:T(8,128)S(1)} %all_to_all.10.fetched), channel_id=1, source_target_pairs={{0,1},{2,3},{4,5},{6,7},{1,0},{3,2},{5,4},{7,6},{8,9},{10,11},{12,... | collective-permute-start | bytes 786440 | tf_op jit(solution)/shard_map/ppermute | solution.py:770
  94.4 1.5 %collective-permute-done.9.other = f32[32,16,128]{2,1,0:T(8,128)S(1)} collective-permute-done((f32[32,16,128]{2,1,0:T(8,128)S(1)}, f32[32,16,128]{2,1,0:T(8,128)S(1)}, u32[]{:S(2)}, u32[]{:S(2)}) %collective-permute-start.9) | collective-permute-done | bytes 262176 | tf_op jit(solution)/shard_map/ppermute | solution.py:770
  95.9 5.1 %shard_map.54 = (f32[20,32,256]{2,1,0:T(8,128)S(1)}, f32[16,8,128]{2,1,0:T(8,128)S(1)}, f32[4,8,128]{2,1,0:T(8,128)S(1)}, f32[4,8,128]{2,1,0:T(8,128)S(1)}) custom-call(s32[2]{0:T(128)S(1)} %pad_add_fusion.at, f32[32,16,128]{2,1,0:T(8,128)S(1)} %all_to_all.10.fetched, f32[32,16,128]{2,1,0:T(8,128)S(1)} %collective-permute-done.9.other, ...), custom_call_target="tpu_custom_call" | custom-call | flops 30000000 | bytes 4000000 | tf_op jit(solution)/shard_map/pallas_call | solution.py:91
  101.1 2.2 %collective-permute-start.10 = (f32[4,8,128]{2,1,0:T(8,128)S(1)}, f32[4,8,128]{2,1,0:T(8,128)S(1)}, u32[]{:S(2)}, u32[]{:S(2)}) collective-permute-start(f32[4,8,128]{2,1,0:T(8,128)S(1)} %get-tuple-element.38), channel_id=1, source_target_pairs={{0,8},{8,16},{16,24},{24,32},{32,40},{40,48},{48,56},{56,64},{64,7... | collective-permute-start | bytes 49160 | tf_op jit(solution)/shard_map/ppermute | solution.py:762
  103.3 1.3 collective-permute-start.11
  104.6 0.0 collective-permute-done.10
  104.6 3.2 %collective-permute-done.11 = f32[4,8,128]{2,1,0:T(8,128)S(1)} collective-permute-done((f32[4,8,128]{2,1,0:T(8,128)S(1)}, f32[4,8,128]{2,1,0:T(8,128)S(1)}, u32[]{:S(2)}, u32[]{:S(2)}) %collective-permute-start.11) | collective-permute-done | bytes 16416 | tf_op jit(solution)/shard_map/ppermute | solution.py:762
  107.8 3.3 %collective-permute-start.13 = (f32[16,8,128]{2,1,0:T(8,128)S(1)}, f32[16,8,128]{2,1,0:T(8,128)S(1)}, u32[]{:S(2)}, u32[]{:S(2)}) collective-permute-start(f32[16,8,128]{2,1,0:T(8,128)S(1)} %constant_dynamic-update-slice_fusion.mid), channel_id=1, source_target_pairs={{1,2},{3,4},{5,6},{2,1},{4,3},{6,5},{9,10},{11,12},{13,14},{10,9},... | collective-permute-start | bytes 196616 | tf_op jit(solution)/shard_map/ppermute | solution.py:770
  111.1 1.9 %collective-permute-start.12 = (f32[16,8,128]{2,1,0:T(8,128)S(1)}, f32[16,8,128]{2,1,0:T(8,128)S(1)}, u32[]{:S(2)}, u32[]{:S(2)}) collective-permute-start(f32[16,8,128]{2,1,0:T(8,128)S(1)} %constant_dynamic-update-slice_fusion.mid), channel_id=1, source_target_pairs={{0,1},{2,3},{4,5},{6,7},{1,0},{3,2},{5,4},{7,6},{8,9},{10,11},{12,... | collective-permute-start | bytes 196616 | tf_op jit(solution)/shard_map/ppermute | solution.py:770
  113.0 0.3 collective-permute-done.13.link
  113.3 0.9 collective-permute-done.12.chip
  114.3 0.9 shard_map.55
  115.1 2.1 %collective-permute-start.14 = (f32[8,128]{1,0:T(8,128)S(1)}, f32[8,128]{1,0:T(8,128)S(1)}, u32[]{:S(2)}, u32[]{:S(2)}) collective-permute-start(f32[8,128]{1,0:T(8,128)S(1)} %get-tuple-element.40), channel_id=1, source_target_pairs={{0,1},{2,3},{4,5},{6,7},{1,0},{3,2},{5,4},{7,6},{8,9},{10,11},{12,... | collective-permute-start | bytes 12296 | tf_op jit(solution)/shard_map/ppermute | solution.py:770
  117.2 1.0 collective-permute-done.14
  118.3 18.1 %all_to_all.11.fetched = f32[32,16,128]{2,1,0:T(8,128)S(1)} all-to-all(f32[32,16,128]{2,1,0:T(8,128)S(1)} %broadcast_in_dim.5), channel_id=1, replica_groups={{0,2,4,6,8,10,12,14,16,18,20,22,24,26,28,30,32,34,36,38,40,42,44,46,48,..., dimensions={0} | all-to-all | bytes 524288 | tf_op jit(solution)/shard_map/all_to_all | solution.py:803
  136.3 6.7 %collective-permute-start.15 = (f32[32,16,128]{2,1,0:T(8,128)S(1)}, f32[32,16,128]{2,1,0:T(8,128)S(1)}, u32[]{:S(2)}, u32[]{:S(2)}) collective-permute-start(f32[32,16,128]{2,1,0:T(8,128)S(1)} %all_to_all.11.fetched), channel_id=1, source_target_pairs={{0,1},{2,3},{4,5},{6,7},{1,0},{3,2},{5,4},{7,6},{8,9},{10,11},{12,... | collective-permute-start | bytes 786440 | tf_op jit(solution)/shard_map/ppermute | solution.py:770
  143.1 1.1 collective-permute-done.15.other
  144.2 3.8 %shard_map.56 = f32[16,16,256]{2,1,0:T(8,128)} custom-call(s32[2]{0:T(128)S(1)} %pad_add_fusion.at, f32[32,16,128]{2,1,0:T(8,128)S(1)} %all_to_all.11.fetched, f32[32,16,128]{2,1,0:T(8,128)S(1)} %collective-permute-done.15.other, f32[16,24,128]{2,1,0:T(8,128)S(1)} %get-tuple-element.41.b1, f32[14,24,128]{2,1,0:T(8,128)S(1)} %get-tuple-element.42.u, ...), custom_call_target="tpu_custom_call" | custom-call | flops 20000000 | bytes 4000000 | tf_op jit(solution)/shard_map/pallas_call | solution.py:91
  (10 shorter events, 0.1 us)
Async XLA Ops:
  0.6 12.4 %copy-start = (f32[3,16,16,256]{3,2,1,0:T(8,128)S(1)}, f32[3,16,16,256]{3,2,1,0:T(8,128)}, u32[]{:S(2)}) copy-start(f32[3,16,16,256]{3,2,1,0:T(8,128)} %velocity.5) | copy-start | bytes 2359300
  2.0 7.3 %collective-permute-start = (f32[16,16,256]{2,1,0:T(8,128)S(1)}, f32[16,16,256]{2,1,0:T(8,128)S(1)}, u32[]{:S(2)}, u32[]{:S(2)}) collective-permute-start(f32[16,16,256]{2,1,0:T(8,128)S(1)} %get-tuple-element.24), channel_id=1, source_target_pairs={{0,8},{8,16},{16,24},{24,32},{32,40},{40,48},{48,56},{56,64},{64,7... | collective-permute-start | bytes 786440 | tf_op jit(solution)/shard_map/ppermute | solution.py:762
  5.9 7.1 %collective-permute-start.1 = (f32[16,16,256]{2,1,0:T(8,128)S(1)}, f32[16,16,256]{2,1,0:T(8,128)S(1)}, u32[]{:S(2)}, u32[]{:S(2)}) collective-permute-start(f32[16,16,256]{2,1,0:T(8,128)S(1)} %get-tuple-element.25), channel_id=1, source_target_pairs={{8,0},{16,8},{24,16},{32,24},{40,32},{48,40},{56,48},{64,56},{72,6... | collective-permute-start | bytes 786440 | tf_op jit(solution)/shard_map/ppermute | solution.py:762
  13.7 9.2 %collective-permute-start.2 = (f32[28,16,256]{2,1,0:T(8,128)S(1)}, f32[28,16,256]{2,1,0:T(8,128)S(1)}, u32[]{:S(2)}, u32[]{:S(2)}) collective-permute-start(f32[28,16,256]{2,1,0:T(8,128)S(1)} %get-tuple-element.26), channel_id=1, source_target_pairs={{0,1},{2,3},{4,5},{6,7},{1,0},{3,2},{5,4},{7,6},{8,9},{10,11},{12,... | collective-permute-start | bytes 1376264 | tf_op jit(solution)/shard_map/ppermute | solution.py:770
  21.0 9.8 %collective-permute-start.3 = (f32[28,16,256]{2,1,0:T(8,128)S(1)}, f32[28,16,256]{2,1,0:T(8,128)S(1)}, u32[]{:S(2)}, u32[]{:S(2)}) collective-permute-start(f32[28,16,256]{2,1,0:T(8,128)S(1)} %get-tuple-element.27), channel_id=1, source_target_pairs={{1,2},{3,4},{5,6},{2,1},{4,3},{6,5},{9,10},{11,12},{13,14},{10,9},... | collective-permute-start | bytes 1376264 | tf_op jit(solution)/shard_map/ppermute | solution.py:770
  40.4 4.2 %collective-permute-start.4 = (f32[14,16,256]{2,1,0:T(8,128)S(1)}, f32[14,16,256]{2,1,0:T(8,128)S(1)}, u32[]{:S(2)}, u32[]{:S(2)}) collective-permute-start(f32[14,16,256]{2,1,0:T(8,128)S(1)} %get-tuple-element.30), channel_id=1, source_target_pairs={{0,8},{8,16},{16,24},{24,32},{32,40},{40,48},{48,56},{56,64},{64,7... | collective-permute-start | bytes 688136 | tf_op jit(solution)/shard_map/ppermute | solution.py:762
  41.7 6.8 %collective-permute-start.5 = (f32[14,16,256]{2,1,0:T(8,128)S(1)}, f32[14,16,256]{2,1,0:T(8,128)S(1)}, u32[]{:S(2)}, u32[]{:S(2)}) collective-permute-start(f32[14,16,256]{2,1,0:T(8,128)S(1)} %get-tuple-element.31), channel_id=1, source_target_pairs={{8,0},{16,8},{24,16},{32,24},{40,32},{48,40},{56,48},{64,56},{72,6... | collective-permute-start | bytes 688136 | tf_op jit(solution)/shard_map/ppermute | solution.py:762
  48.5 15.1 %collective-permute-start.7 = (f32[44,16,256]{2,1,0:T(8,128)S(1)}, f32[44,16,256]{2,1,0:T(8,128)S(1)}, u32[]{:S(2)}, u32[]{:S(2)}) collective-permute-start(f32[44,16,256]{2,1,0:T(8,128)S(1)} %constant_dynamic-update-slice_fusion.2.mid), channel_id=1, source_target_pairs={{1,2},{3,4},{5,6},{2,1},{4,3},{6,5},{9,10},{11,12},{13,14},{10,9},... | collective-permute-start | bytes 2162696 | tf_op jit(solution)/shard_map/ppermute | solution.py:770
  54.7 9.0 %collective-permute-start.6 = (f32[44,16,256]{2,1,0:T(8,128)S(1)}, f32[44,16,256]{2,1,0:T(8,128)S(1)}, u32[]{:S(2)}, u32[]{:S(2)}) collective-permute-start(f32[44,16,256]{2,1,0:T(8,128)S(1)} %constant_dynamic-update-slice_fusion.2.mid), channel_id=1, source_target_pairs={{0,1},{2,3},{4,5},{6,7},{1,0},{3,2},{5,4},{7,6},{8,9},{10,11},{12,... | collective-permute-start | bytes 2162696 | tf_op jit(solution)/shard_map/ppermute | solution.py:770
  67.5 3.1 %collective-permute-start.8 = (f32[8,128]{1,0:T(8,128)S(1)}, f32[8,128]{1,0:T(8,128)S(1)}, u32[]{:S(2)}, u32[]{:S(2)}) collective-permute-start(f32[8,128]{1,0:T(8,128)S(1)} %get-tuple-element.32), channel_id=1, source_target_pairs={{0,1},{2,3},{4,5},{6,7},{1,0},{3,2},{5,4},{7,6},{8,9},{10,11},{12,... | collective-permute-start | bytes 12296 | tf_op jit(solution)/shard_map/ppermute | solution.py:770
  92.5 3.4 %collective-permute-start.9 = (f32[32,16,128]{2,1,0:T(8,128)S(1)}, f32[32,16,128]{2,1,0:T(8,128)S(1)}, u32[]{:S(2)}, u32[]{:S(2)}) collective-permute-start(f32[32,16,128]{2,1,0:T(8,128)S(1)} %all_to_all.10.fetched), channel_id=1, source_target_pairs={{0,1},{2,3},{4,5},{6,7},{1,0},{3,2},{5,4},{7,6},{8,9},{10,11},{12,... | collective-permute-start | bytes 786440 | tf_op jit(solution)/shard_map/ppermute | solution.py:770
  101.1 3.5 %collective-permute-start.10 = (f32[4,8,128]{2,1,0:T(8,128)S(1)}, f32[4,8,128]{2,1,0:T(8,128)S(1)}, u32[]{:S(2)}, u32[]{:S(2)}) collective-permute-start(f32[4,8,128]{2,1,0:T(8,128)S(1)} %get-tuple-element.38), channel_id=1, source_target_pairs={{0,8},{8,16},{16,24},{24,32},{32,40},{40,48},{48,56},{56,64},{64,7... | collective-permute-start | bytes 49160 | tf_op jit(solution)/shard_map/ppermute | solution.py:762
  103.3 4.5 %collective-permute-start.11 = (f32[4,8,128]{2,1,0:T(8,128)S(1)}, f32[4,8,128]{2,1,0:T(8,128)S(1)}, u32[]{:S(2)}, u32[]{:S(2)}) collective-permute-start(f32[4,8,128]{2,1,0:T(8,128)S(1)} %get-tuple-element.39), channel_id=1, source_target_pairs={{8,0},{16,8},{24,16},{32,24},{40,32},{48,40},{56,48},{64,56},{72,6... | collective-permute-start | bytes 49160 | tf_op jit(solution)/shard_map/ppermute | solution.py:762
  107.8 5.6 %collective-permute-start.13 = (f32[16,8,128]{2,1,0:T(8,128)S(1)}, f32[16,8,128]{2,1,0:T(8,128)S(1)}, u32[]{:S(2)}, u32[]{:S(2)}) collective-permute-start(f32[16,8,128]{2,1,0:T(8,128)S(1)} %constant_dynamic-update-slice_fusion.mid), channel_id=1, source_target_pairs={{1,2},{3,4},{5,6},{2,1},{4,3},{6,5},{9,10},{11,12},{13,14},{10,9},... | collective-permute-start | bytes 196616 | tf_op jit(solution)/shard_map/ppermute | solution.py:770
  111.1 3.1 %collective-permute-start.12 = (f32[16,8,128]{2,1,0:T(8,128)S(1)}, f32[16,8,128]{2,1,0:T(8,128)S(1)}, u32[]{:S(2)}, u32[]{:S(2)}) collective-permute-start(f32[16,8,128]{2,1,0:T(8,128)S(1)} %constant_dynamic-update-slice_fusion.mid), channel_id=1, source_target_pairs={{0,1},{2,3},{4,5},{6,7},{1,0},{3,2},{5,4},{7,6},{8,9},{10,11},{12,... | collective-permute-start | bytes 196616 | tf_op jit(solution)/shard_map/ppermute | solution.py:770
  115.1 3.1 %collective-permute-start.14 = (f32[8,128]{1,0:T(8,128)S(1)}, f32[8,128]{1,0:T(8,128)S(1)}, u32[]{:S(2)}, u32[]{:S(2)}) collective-permute-start(f32[8,128]{1,0:T(8,128)S(1)} %get-tuple-element.40), channel_id=1, source_target_pairs={{0,1},{2,3},{4,5},{6,7},{1,0},{3,2},{5,4},{7,6},{8,9},{10,11},{12,... | collective-permute-start | bytes 12296 | tf_op jit(solution)/shard_map/ppermute | solution.py:770
  136.3 7.9 %collective-permute-start.15 = (f32[32,16,128]{2,1,0:T(8,128)S(1)}, f32[32,16,128]{2,1,0:T(8,128)S(1)}, u32[]{:S(2)}, u32[]{:S(2)}) collective-permute-start(f32[32,16,128]{2,1,0:T(8,128)S(1)} %all_to_all.11.fetched), channel_id=1, source_target_pairs={{0,1},{2,3},{4,5},{6,7},{1,0},{3,2},{5,4},{7,6},{8,9},{10,11},{12,... | collective-permute-start | bytes 786440 | tf_op jit(solution)/shard_map/ppermute | solution.py:770

commit v8 on v7

--- a/solution.py
+++ b/solution.py
@@ -104,18 +104,6 @@
     lower = lambda *k: jnp.where(odd, chip[k], link[k])
     upper = lambda *k: jnp.where(odd, link[k], chip[k])
     return lower, upper
-
-
-def send_shapes(planes):
-    return [(16 + 2 * planes, 16, 256), (planes, 16, 256), (planes, 16, 256)]
-
-
-def send(block, wider, low, high, planes):
-    for i in range(16):
-        wider[planes + i] = block[i]
-    for i in range(planes):
-        low[i] = block[i]
-        high[i] = block[16 - planes + i]
 
 
 PARTS = 4
@@ -203,18 +191,47 @@
     return level, [speed(c) for c in range(3)]
 
 
+def narrow_segments():
+    reached = (FAR, ALONG, ALONG, ACROSS)
+    rows_own = (FAR, ACROSS, ALONG, ACROSS)
+    found = {}
+    for p in range(16):
+        offset = 0
+        for field, rows in enumerate(rows_own):
+            found[field, p] = (p, offset, rows)
+            offset += rows
+    for side, edge in enumerate((0, 15)):
+        for slot, layers in enumerate(((1, 4, 5), (2, 3))):
+            offset = 0
+            for d in layers:
+                p = edge - d if side == 0 else edge + d
+                for field, reach_of in enumerate(reached):
+                    rows = min(reach_of - d, rows_own[field])
+                    if rows > 0:
+                        found[field, p] = (16 + 2 * side + slot, offset, rows)
+                        offset += rows
+    return found
+
+
+SEGMENTS = narrow_segments()
+SLOTS = 20
+
+
 def pack_body(at, psi, velocity, low, high, chip, link):
     odd = lax.rem(at[1], 2) == 1
     level, speeds = wide_planes(psi, velocity, low, high)
-    for k in range(16 + 2 * FAR):
-        v = level(k - FAR)
-        first, final = [v[0:FAR]], [v[16 - FAR : 16]]
-        for component, layers, _ in layer_cuts(1):
-            w = speeds[component](k - FAR)
-            if w is None:
-                w = jnp.zeros((16, 256), F32)
-            first.append(w[0:layers])
-            final.append(w[16 - layers : 16])
+    fields = [level] + speeds
+    for k in range(SLOTS):
+        inside_slot = [(offset, f, p, rows) for (f, p), (slot, offset, rows) in SEGMENTS.items() if slot == k]
+        first, final, total = [], [], 0
+        for offset, f, p, rows in sorted(inside_slot):
+            v = fields[f](p)
+            first.append(v[0:rows])
+            final.append(v[16 - rows : 16])
+            total += rows
+        if total < SENT:
+            first.append(jnp.zeros((SENT - total, 256), F32))
+            final.append(first[-1])
         first = jnp.concatenate(first, axis=0)
         final = jnp.concatenate(final, axis=0)
         chip[k] = jnp.where(odd, first, final)
@@ -222,7 +239,7 @@
 
 
 def pack(at, psi, velocity, low, high):
-    outs = [(16 + 2 * FAR, SENT, 256)] * 2
+    outs = [(SLOTS, SENT, 256)] * 2
     return call(pack_body, outs, [], [at, psi, velocity, low, high], 1000000)
 
 
@@ -299,62 +316,95 @@
 SKIN = 3
 
 
+def x_marks(v, planes, marks):
+    for i in range(planes):
+        marks[0][i], marks[1][i], marks[2][i] = indicators(v(i - FAR), v(i - FAR + 1), v(i - FAR + 2))
+
+
+def x_flux(f, v, w, marks):
+    p_x, q_x, r_x = marks
+    l = [v(f - 3 + k) for k in range(6)]
+    return upwind_flux(
+        FACE * (w(f - 1) + w(f)), l,
+        p_x[f + 3], q_x[f + 4], r_x[f + 5], p_x[f + 4], q_x[f + 5], r_x[f + 6],
+    )
+
+
+def xz_change(v, u, w, marks, out):
+    x_marks(v, 26, marks)
+    below = x_flux(-SKIN, v, u, marks)
+    for p in range(-SKIN, 16 + SKIN):
+        above = x_flux(p + 1, v, u, marks)
+        out[p + SKIN] = (above - below) + z_change(v(p), w(p))
+        below = above
+
+
+def inner_body(psi, velocity, low, high, out, *marks):
+    level, speeds = wide_planes(psi, velocity, low, high)
+    xz_change(level, speeds[0], speeds[2], marks, out)
+
+
+def inner(psi, velocity, low, high):
+    block = (16 + 2 * SKIN, 16, 256)
+    scratch = [(26, 16, 256)] * 3
+    return call(inner_body, [block], scratch, [psi, velocity, low, high], 8000000)[0]
+
+
 def advance_body(
-    nx, ny, at, psi, velocity, low, high, chip, link, moved, wider, first, final,
-    v24, v32, u24, u32, w24, p_x, q_x, r_x, m, n_x, n_y, n_z, s_x, part, source,
+    nx, ny, at, psi, velocity, low, high, chip, link, change_in, moved, source, first, final,
+    v8, u8, w8, v32, u32, c8, p_x, q_x, r_x, m, n_x, n_y, n_z, s_x, part,
 ):
     lower, upper = pick_sides(at, chip, link)
     level, speeds = wide_planes(psi, velocity, low, high)
-    cuts = layer_cuts(1)
-
-    def place(ref, i, start, rows, layers, below, above):
+    fields = [level] + speeds
+
+    def halo(field, p, most):
+        if (field, p) not in SEGMENTS:
+            return 0, None, None
+        slot, offset, rows = SEGMENTS[field, p]
+        count = min(most, rows)
+        below = lower(slot)[offset + rows - count : offset + rows]
+        return count, below, upper(slot)[offset : offset + count]
+
+    def beside_only(ref, i, field, p):
+        ref[i] = jnp.zeros((8, 256), F32)
+        count, below, above = halo(field, p, 4)
+        if count:
+            ref[i, 4 - count : 4, :] = below
+            ref[i, 4 : 4 + count, :] = above
+
+    def with_rows(ref, i, field, p, start):
         total = ref.shape[1]
-        ref[i, start - layers : start, :] = below
-        ref[i, start : start + 16, :] = rows
-        ref[i, start + 16 : start + 16 + layers, :] = above
-        if start - layers:
-            ref[i, 0 : start - layers, :] = jnp.zeros((start - layers, 256), F32)
-        rest = total - start - 16 - layers
-        if rest:
-            ref[i, total - rest : total, :] = jnp.zeros((rest, 256), F32)
-
-    for i in range(16 + 2 * FAR):
-        p = i - FAR
-        below, above = lower(i), upper(i)
-        rows = level(p)
-        place(v24, i, 4, rows, 4, below[FAR - 4 : FAR], above[0:4])
+        ref[i, 0:start, :] = jnp.zeros((start, 256), F32)
+        ref[i, start + 16 : total, :] = jnp.zeros((total - start - 16, 256), F32)
+        count, below, above = halo(field, p, start)
+        ref[i, start : start + 16, :] = fields[field](p)
+        if count:
+            ref[i, start - count : start, :] = below
+            ref[i, start + 16 : start + 16 + count, :] = above
+
+    for p in range(-FAR, 16 + FAR):
+        beside_only(v8, p + FAR, 0, p)
+        if -ALONG <= p < 16 + ALONG:
+            beside_only(u8, p + ALONG, 1, p)
         if -SKIN <= p < 16 + SKIN:
-            place(v32, p + SKIN, 8, rows, FAR, below[0:FAR], above[0:FAR])
-        for component, ref, start in ((0, u24, 4), (1, u32, 8), (2, w24, 4)):
-            rows = speeds[component](p)
-            if rows is not None:
-                _, count, offset = cuts[component]
-                _, layers, _ = layer_cuts(0)[component]
-                cut = slice(offset, offset + count)
-                place(ref, p + layers, start, rows, count, below[cut], above[cut])
-
-    for i in range(26):
-        p_x[i], q_x[i], r_x[i] = indicators(v24[i], v24[i + 1], v24[i + 2])
-
-    def x_flux(f):
-        s = FACE * (u24[f - 1 + ALONG] + u24[f + ALONG])
-        l = [v24[f - 3 + k + FAR] for k in range(6)]
-        return upwind_flux(
-            s, l, p_x[f + 3], q_x[f + 4], r_x[f + 5], p_x[f + 4], q_x[f + 5], r_x[f + 6]
-        )
-
+            beside_only(w8, p + SKIN, 3, p)
+            with_rows(v32, p + SKIN, 0, p, 8)
+            with_rows(u32, p + SKIN, 2, p, 8)
+
+    xz_change(
+        lambda p: v8[p + FAR], lambda p: u8[p + ALONG], lambda p: w8[p + SKIN], (p_x, q_x, r_x), c8
+    )
     shape = (24, 256)
     mask = row_mask(shape, at[1] * 16 - 4, ny)
-    below = x_flux(-SKIN)
     for p in range(-SKIN, 16 + SKIN):
-        above = x_flux(p + 1)
-        v = v24[p + FAR]
-        change = above - below
-        change = change + y_change(v32[p + SKIN], u32[p + ACROSS])[4:28, :]
-        change = change + z_change(v, w24[p + ACROSS])
-        below = above
-        value = wall(at, nx, 0, p, (v - change) * mask)
-        m[p + SKIN] = value
+        i = p + SKIN
+        sides = c8[i]
+        change = jnp.concatenate([sides[0:4], change_in[i], sides[4:8]], axis=0)
+        v = v32[i]
+        change = change + y_change(v, u32[i])[4:28, :]
+        value = wall(at, nx, 0, p, (v[4:28, :] - change) * mask)
+        m[i] = value
         if 0 <= p < 16:
             moved[p] = value[4:20, :]
 
@@ -384,27 +434,30 @@
             + (ahead - behind)
         )
         bending = wall(at, nx, 0, p, bending * mask)
-        s_x[p + 1] = (bending * gx)[4:20, :] + u24[p + ALONG, 4:20, :]
+        s_x[p + 1] = (bending * gx)[4:20, :] + speeds[0](p)
         if 0 <= p < 16:
-            sy = bending * gy + u32[p + ACROSS, 4:28, :]
+            sy = bending * gy + u32[p + SKIN, 4:28, :]
             dy = roll(sy, -1, 0) - roll(sy, 1, 0)
             sz = (bending * gz)[4:20, :] + velocity[2, p]
             behind, ahead = z_shifted(sz)
             part[p] = dy[4:20, :] + (ahead - behind)
     for p in range(16):
         source[p] = -0.5 * (part[p] + (s_x[p + 2] - s_x[p]))
-    send(source, wider, first, final, HALO)
-
-
-def advance(nx, ny, at, psi, velocity, low, high, chip, link):
-    marks, normals, block = (26, 24, 256), (20, 24, 256), (16, 16, 256)
+    for i in range(HALO):
+        first[i] = source[i]
+        final[i] = source[16 - HALO + i]
+
+
+def advance(nx, ny, at, psi, velocity, low, high, chip, link, change):
+    marks, normals, block = (26, 8, 256), (20, 24, 256), (16, 16, 256)
+    skin = 16 + 2 * SKIN
     scratch = [
-        (16 + 2 * FAR, 24, 256), (16 + 2 * SKIN, 32, 256), (16 + 2 * ALONG, 24, 256),
-        (16 + 2 * ACROSS, 32, 256), (16 + 2 * ACROSS, 24, 256), marks, marks, marks,
-        (16 + 2 * SKIN, 24, 256), normals, normals, normals, (18, 16, 256), block, block,
+        (16 + 2 * FAR, 8, 256), (16 + 2 * ALONG, 8, 256), (skin, 8, 256), (skin, 32, 256),
+        (skin, 32, 256), (skin, 8, 256), marks, marks, marks,
+        (skin, 24, 256), normals, normals, normals, (18, 16, 256), block,
     ]
-    args = [at, psi, velocity, low, high, chip, link]
-    outs = [block] + send_shapes(HALO)
+    args = [at, psi, velocity, low, high, chip, link, change]
+    outs = [block, block, (HALO, 16, 256), (HALO, 16, 256)]
     return call(functools.partial(advance_body, nx, ny), outs, scratch, args, 30000000)
 
 
@@ -503,12 +556,74 @@
 E0, R1, E1, R2, E2, R3 = reach(KEEP)
 
 
-def first_down_body(nx, ny, at, mid, chip, link, b_out, v_out, b1_out, u_out, b2_out, b, v, pair, t, s1, t1):
+def source_segments():
+    whole, parts = [], []
+    for p in range(-HALO, 16 + HALO):
+        d = max(-p, p - 15, 0)
+        rows = 16 - max(d, 2)
+        if rows >= 8:
+            whole.append((p, 0, 8))
+        if rows % 8:
+            parts.append((p, rows // 8 * 8, rows % 8))
+    found = [(p, n, rows, tile, 0) for tile, (p, n, rows) in enumerate(whole)]
+    room = []
+    for p, n, rows in sorted(parts, key=lambda part: (-part[2], part[0])):
+        for k, used in enumerate(room):
+            if used + rows <= 8:
+                break
+        else:
+            k = len(room)
+            room.append(0)
+        found.append((p, n, rows, len(whole) + k, room[k]))
+        room[k] += rows
+    return found, len(whole) + len(room)
+
+
+SOURCE_SEGMENTS, SOURCE_TILES = source_segments()
+
+
+def source_plane(own, low, high, p):
+    return low[p + HALO] if p < 0 else own[p] if p < 16 else high[p - 16]
+
+
+def weave_body(at, own, low, high, chip, link):
+    odd = lax.rem(at[1], 2) == 1
+    for k in range(SOURCE_TILES):
+        first, final, total = [], [], 0
+        for p, n, rows, tile, offset in sorted(SOURCE_SEGMENTS, key=lambda part: part[4]):
+            if tile == k:
+                v = source_plane(own, low, high, p)
+                first.append(v[n : n + rows])
+                final.append(v[16 - n - rows : 16 - n])
+                total += rows
+        if total < 8:
+            first.append(jnp.zeros((8 - total, 256), F32))
+            final.append(first[-1])
+        if len(first) > 1:
+            first = [jnp.concatenate(first, axis=0)]
+            final = [jnp.concatenate(final, axis=0)]
+        chip[k] = jnp.where(odd, first[0], final[0])
+        link[k] = jnp.where(odd, final[0], first[0])
+
+
+def weave(at, own, low, high):
+    outs = [(SOURCE_TILES, 8, 256)] * 2
+    return call(weave_body, outs, [], [at, own, low, high], 1000000)
+
+
+def first_down_body(
+    nx, ny, at, own, low, high, chip, link, b_out, v_out, b1_out, u_out, b2_out, b, v, pair, t, s1, t1
+):
     lower, upper = pick_sides(at, chip, link)
-    for i in range(16 + 2 * HALO):
-        b[i, 0:16, :] = lower(i)
-        b[i, 16:32, :] = mid[i]
-        b[i, 32:48, :] = upper(i)
+    none = jnp.zeros((16, 256), F32)
+    for p in range(-HALO, 16 + HALO):
+        b[p + HALO, 0:16, :] = none
+        b[p + HALO, 16:32, :] = source_plane(own, low, high, p)
+        b[p + HALO, 32:48, :] = none
+    for p, n, rows, tile, offset in SOURCE_SEGMENTS:
+        cut = slice(offset, offset + rows)
+        b[p + HALO, 16 - n - rows : 16 - n, :] = lower(tile)[cut]
+        b[p + HALO, 32 + n : 32 + n + rows, :] = upper(tile)[cut]
     b, v = Field(b, HALO), Field(v, HALO - 1)
     mask = row_mask((48, 256), at[1] * 16 - 16, ny)
     first_smooth(b, v, range(1 - HALO, 15 + HALO), SIDE, mask, at, nx, 0)
@@ -527,7 +642,7 @@
     return (size + 2 * extra, rows, lanes)
 
 
-def first_down(nx, ny, at, mid, chip, link):
+def first_down(nx, ny, at, own, low, high, chip, link):
     level1 = around_block(8, E1 + 1, 24, 128)
     outs = [
         around_block(16, E0 - 1, 32, 256),
@@ -544,7 +659,7 @@
         (4, 24, 128),
         (4, 8, 128),
     ]
-    args = [at, mid, chip, link]
+    args = [at, own, low, high, chip, link]
     return call(functools.partial(first_down_body, nx, ny), outs, scratch, args, 20000000)
 
 
@@ -812,8 +927,15 @@
     chip, link = pack(at, psi, velocity, low, high)
     v_link = swapped(link, 1)
     v_chip = swapped(chip, 0)
-    moved, *sends = advance(nx, ny, at, psi, velocity, low, high, v_chip, v_link)
-    b, v, b1, u, b2 = first_down(nx, ny, at, *surround(*sends))
+    change = inner(psi, velocity, low, high)
+    moved, source, first, final = advance(
+        nx, ny, at, psi, velocity, low, high, v_chip, v_link, change
+    )
+    low, high = shifted(final, "wide", 1), shifted(first, "wide", -1)
+    chip, link = weave(at, source, low, high)
+    b_link = swapped(link, 1)
+    b_chip = swapped(chip, 0)
+    b, v, b1, u, b2 = first_down(nx, ny, at, source, low, high, b_chip, b_link)
     v, *sends = turn(nx, ny, at, spread_coarse(b2), b1, u, b, v)
     b1, u, b2 = second_down(nx, ny, at, *surround(*sends))
     pressure = finish(nx, ny, at, spread_coarse(b2), b1, u, b, v)

time: 149 us -> 145 us (0.973)
  waiting for transfers between devices: 35 us -> 30.4 us
    ppermute x10, waiting for transfers between devices: 20.7 us -> 16 us  [swapped(): return lax.ppermute(array, 'narrow', pairs + [(j, i) for i, j in pairs])]
    pallas_call x6 -> x8, Pallas kernels: 23.8 us -> 25.1 us  [call(): pl.pallas_call(body, out_shape=[jax.ShapeDtypeStruct(s, F32) for s in out...]
  transfers between devices with their start and end apart: 16 -> 16, of which waited for: 13 -> 13; matrix products, arithmetic and copies ran while one was open for 0% -> 0% of each run, Pallas kernels for 0% -> 2%
where the time goes in v8:
time: 145 us
  starting transfers between devices  46.6 us (32%)
  blocking collectives  40.3 us (28%)
  waiting for transfers between devices  30.4 us (21%)
  Pallas kernels  26.4 us (18%)
    all_to_all x2, blocking collectives, spread_coarse(): lax.all_to_all(pieces, ('wide', 'narrow'), 0, 0, axis_index_groups=groups)  40.3 us
    ppermute x10, starting transfers between devices, swapped(): return lax.ppermute(array, 'narrow', pairs + [(j, i) for i, j in pairs])  35.3 us
    pallas_call x8, Pallas kernels, call(): pl.pallas_call(body, out_shape=[jax.ShapeDtypeStruct(s, F32) for s in out...  25.1 us
    ppermute x10, waiting for transfers between devices, swapped(): return lax.ppermute(array, 'narrow', pairs + [(j, i) for i, j in pairs])  16 us
    ppermute x6, waiting for transfers between devices, shifted(): lax.ppermute(array, axis, [(i, i + step) for i in range(count) if 0 <= i...  14.4 us
    ppermute x6, starting transfers between devices, shifted(): lax.ppermute(array, axis, [(i, i + step) for i in range(count) if 0 <= i...  11.3 us
  transfers between devices with their start and end apart: 16, of which 13 were waited for; matrix products, arithmetic and copies ran while one was open for 0% of the time, Pallas kernels for 2%

profile of v8, /device:TPU:1, one launch (start us, length us, event | category | flops | bytes accessed | tf_op | source)
XLA Modules:
  0.0 144.7 jit_solution(9180544785761299214)
XLA Ops:
  0.6 0.0 copy-start
  0.6 1.3 shard_map.50
  2.0 4.0 %collective-permute-start = (f32[16,16,256]{2,1,0:T(8,128)S(1)}, f32[16,16,256]{2,1,0:T(8,128)S(1)}, u32[]{:S(2)}, u32[]{:S(2)}) collective-permute-start(f32[16,16,256]{2,1,0:T(8,128)S(1)} %get-tuple-element.26), channel_id=1, source_target_pairs={{0,8},{8,16},{16,24},{24,32},{32,40},{40,48},{48,56},{56,64},{64,7... | collective-permute-start | bytes 786440 | tf_op jit(solution)/shard_map/ppermute | solution.py:877
  5.9 1.3 collective-permute-start.1
  7.2 0.1 pad_add_fusion.at
  7.3 1.9 %collective-permute-done.low = f32[16,16,256]{2,1,0:T(8,128)S(1)} collective-permute-done((f32[16,16,256]{2,1,0:T(8,128)S(1)}, f32[16,16,256]{2,1,0:T(8,128)S(1)}, u32[]{:S(2)}, u32[]{:S(2)}) %collective-permute-start) | collective-permute-done | bytes 262176 | tf_op jit(solution)/shard_map/ppermute | solution.py:877
  9.2 3.8 %collective-permute-done.1.high = f32[16,16,256]{2,1,0:T(8,128)S(1)} collective-permute-done((f32[16,16,256]{2,1,0:T(8,128)S(1)}, f32[16,16,256]{2,1,0:T(8,128)S(1)}, u32[]{:S(2)}, u32[]{:S(2)}) %collective-permute-start.1) | collective-permute-done | bytes 262176 | tf_op jit(solution)/shard_map/ppermute | solution.py:877
  13.1 0.0 copy-done
  13.1 0.6 shard_map.51
  13.7 7.3 %collective-permute-start.2 = (f32[20,16,256]{2,1,0:T(8,128)S(1)}, f32[20,16,256]{2,1,0:T(8,128)S(1)}, u32[]{:S(2)}, u32[]{:S(2)}) collective-permute-start(f32[20,16,256]{2,1,0:T(8,128)S(1)} %get-tuple-element.28), channel_id=1, source_target_pairs={{0,1},{2,3},{4,5},{6,7},{1,0},{3,2},{5,4},{7,6},{8,9},{10,11},{12,... | collective-permute-start | bytes 983048 | tf_op jit(solution)/shard_map/ppermute | solution.py:885
  21.0 1.9 %collective-permute-start.3 = (f32[20,16,256]{2,1,0:T(8,128)S(1)}, f32[20,16,256]{2,1,0:T(8,128)S(1)}, u32[]{:S(2)}, u32[]{:S(2)}) collective-permute-start(f32[20,16,256]{2,1,0:T(8,128)S(1)} %get-tuple-element.29), channel_id=1, source_target_pairs={{1,2},{3,4},{5,6},{2,1},{4,3},{6,5},{9,10},{11,12},{13,14},{10,9},... | collective-permute-start | bytes 983048 | tf_op jit(solution)/shard_map/ppermute | solution.py:885
  22.9 2.9 %shard_map.52.change_in = f32[22,16,256]{2,1,0:T(8,128)S(1)} custom-call(f32[16,16,256]{2,1,0:T(8,128)S(1)} %get-tuple-element.25.psi, f32[3,16,16,256]{3,2,1,0:T(8,128)S(1)} %copy-done, f32[16,16,256]{2,1,0:T(8,128)S(1)} %collective-permute-done.low, f32[16,16,256]{2,1,0:T(8,128)S(1)} %collective-permute-done.1.high), custom_call_target="tpu_custom_call" | custom-call | flops 8000000 | bytes 4000000 | tf_op jit(solution)/shard_map/pallas_call | solution.py:91
  25.9 0.0 collective-permute-done.2.chip
  25.9 3.5 %collective-permute-done.3.link = f32[20,16,256]{2,1,0:T(8,128)S(1)} collective-permute-done((f32[20,16,256]{2,1,0:T(8,128)S(1)}, f32[20,16,256]{2,1,0:T(8,128)S(1)}, u32[]{:S(2)}, u32[]{:S(2)}) %collective-permute-start.3) | collective-permute-done | bytes 327712 | tf_op jit(solution)/shard_map/ppermute | solution.py:885
  29.4 7.3 %shard_map.53 = (f32[16,16,256]{2,1,0:T(8,128)}, f32[16,16,256]{2,1,0:T(8,128)S(1)}, f32[14,16,256]{2,1,0:T(8,128)S(1)}, f32[14,16,256]{2,1,0:T(8,128)S(1)}) custom-call(s32[2]{0:T(128)S(1)} %pad_add_fusion.at, f32[16,16,256]{2,1,0:T(8,128)S(1)} %get-tuple-element.25.psi, f32[3,16,16,256]{3,2,1,0:T(8,128)S(1)} %copy-done, ...), custom_call_target="tpu_custom_call" | custom-call | flops 30000000 | bytes 4000000 | tf_op jit(solution)/shard_map/pallas_call | solution.py:91
  36.7 1.3 collective-permute-start.4
  38.0 1.3 collective-permute-start.5
  39.2 1.6 %collective-permute-done.4.low = f32[14,16,256]{2,1,0:T(8,128)S(1)} collective-permute-done((f32[14,16,256]{2,1,0:T(8,128)S(1)}, f32[14,16,256]{2,1,0:T(8,128)S(1)}, u32[]{:S(2)}, u32[]{:S(2)}) %collective-permute-start.4) | collective-permute-done | bytes 229408 | tf_op jit(solution)/shard_map/ppermute | solution.py:877
  40.9 3.8 %collective-permute-done.5.high = f32[14,16,256]{2,1,0:T(8,128)S(1)} collective-permute-done((f32[14,16,256]{2,1,0:T(8,128)S(1)}, f32[14,16,256]{2,1,0:T(8,128)S(1)}, u32[]{:S(2)}, u32[]{:S(2)}) %collective-permute-start.5) | collective-permute-done | bytes 229408 | tf_op jit(solution)/shard_map/ppermute | solution.py:877
  44.7 0.6 shard_map.54
  45.4 1.9 %collective-permute-start.6 = (f32[62,8,256]{2,1,0:T(8,128)S(1)}, f32[62,8,256]{2,1,0:T(8,128)S(1)}, u32[]{:S(2)}, u32[]{:S(2)}) collective-permute-start(f32[62,8,256]{2,1,0:T(8,128)S(1)} %get-tuple-element.34), channel_id=1, source_target_pairs={{0,1},{2,3},{4,5},{6,7},{1,0},{3,2},{5,4},{7,6},{8,9},{10,11},{12,... | collective-permute-start | bytes 1523720 | tf_op jit(solution)/shard_map/ppermute | solution.py:885
  47.3 6.4 %collective-permute-start.7 = (f32[62,8,256]{2,1,0:T(8,128)S(1)}, f32[62,8,256]{2,1,0:T(8,128)S(1)}, u32[]{:S(2)}, u32[]{:S(2)}) collective-permute-start(f32[62,8,256]{2,1,0:T(8,128)S(1)} %get-tuple-element.35), channel_id=1, source_target_pairs={{1,2},{3,4},{5,6},{2,1},{4,3},{6,5},{9,10},{11,12},{13,14},{10,9},... | collective-permute-start | bytes 1523720 | tf_op jit(solution)/shard_map/ppermute | solution.py:885
  53.6 0.0 collective-permute-done.6.chip
  53.7 6.5 %collective-permute-done.7.link = f32[62,8,256]{2,1,0:T(8,128)S(1)} collective-permute-done((f32[62,8,256]{2,1,0:T(8,128)S(1)}, f32[62,8,256]{2,1,0:T(8,128)S(1)}, u32[]{:S(2)}, u32[]{:S(2)}) %collective-permute-start.7) | collective-permute-done | bytes 507936 | tf_op jit(solution)/shard_map/ppermute | solution.py:885
  60.1 3.8 %shard_map.55 = (f32[26,32,256]{2,1,0:T(8,128)S(1)}, f32[28,32,256]{2,1,0:T(8,128)S(1)}, f32[20,24,128]{2,1,0:T(8,128)S(1)}, f32[18,24,128]{2,1,0:T(8,128)S(1)}, f32[8,128]{1,0:T(8,128)S(1)}) custom-call(s32[2]{0:T(128)S(1)} %pad_add_fusion.at, f32[16,16,256]{2,1,0:T(8,128)S(1)} %get-tuple-element.31.own, f32[14,16,256]{2,1,0:T(8,128)S(1)} %collective-permute-done.4.low, ...), custom_call_target="tpu_custom_call" | custom-call | flops 20000000 | bytes 4000000 | tf_op jit(solution)/shard_map/pallas_call | solution.py:91
  64.0 1.9 %collective-permute-start.8 = (f32[8,128]{1,0:T(8,128)S(1)}, f32[8,128]{1,0:T(8,128)S(1)}, u32[]{:S(2)}, u32[]{:S(2)}) collective-permute-start(f32[8,128]{1,0:T(8,128)S(1)} %get-tuple-element.36), channel_id=1, source_target_pairs={{0,1},{2,3},{4,5},{6,7},{1,0},{3,2},{5,4},{7,6},{8,9},{10,11},{12,... | collective-permute-start | bytes 12296 | tf_op jit(solution)/shard_map/ppermute | solution.py:885
  65.9 1.1 collective-permute-done.8
  67.1 22.2 %all_to_all.10.fetched = f32[32,16,128]{2,1,0:T(8,128)S(1)} all-to-all(f32[32,16,128]{2,1,0:T(8,128)S(1)} %broadcast_in_dim.4), channel_id=1, replica_groups={{0,2,4,6,8,10,12,14,16,18,20,22,24,26,28,30,32,34,36,38,40,42,44,46,48,..., dimensions={0} | all-to-all | bytes 524288 | tf_op jit(solution)/shard_map/all_to_all | solution.py:918
  89.3 1.9 %collective-permute-start.9 = (f32[32,16,128]{2,1,0:T(8,128)S(1)}, f32[32,16,128]{2,1,0:T(8,128)S(1)}, u32[]{:S(2)}, u32[]{:S(2)}) collective-permute-start(f32[32,16,128]{2,1,0:T(8,128)S(1)} %all_to_all.10.fetched), channel_id=1, source_target_pairs={{0,1},{2,3},{4,5},{6,7},{1,0},{3,2},{5,4},{7,6},{8,9},{10,11},{12,... | collective-permute-start | bytes 786440 | tf_op jit(solution)/shard_map/ppermute | solution.py:885
  91.2 1.5 %collective-permute-done.9.other = f32[32,16,128]{2,1,0:T(8,128)S(1)} collective-permute-done((f32[32,16,128]{2,1,0:T(8,128)S(1)}, f32[32,16,128]{2,1,0:T(8,128)S(1)}, u32[]{:S(2)}, u32[]{:S(2)}) %collective-permute-start.9) | collective-permute-done | bytes 262176 | tf_op jit(solution)/shard_map/ppermute | solution.py:885
  92.7 5.1 %shard_map.56 = (f32[20,32,256]{2,1,0:T(8,128)S(1)}, f32[16,8,128]{2,1,0:T(8,128)S(1)}, f32[4,8,128]{2,1,0:T(8,128)S(1)}, f32[4,8,128]{2,1,0:T(8,128)S(1)}) custom-call(s32[2]{0:T(128)S(1)} %pad_add_fusion.at, f32[32,16,128]{2,1,0:T(8,128)S(1)} %all_to_all.10.fetched, f32[32,16,128]{2,1,0:T(8,128)S(1)} %collective-permute-done.9.other, ...), custom_call_target="tpu_custom_call" | custom-call | flops 30000000 | bytes 4000000 | tf_op jit(solution)/shard_map/pallas_call | solution.py:91
  97.8 2.2 %collective-permute-start.10 = (f32[4,8,128]{2,1,0:T(8,128)S(1)}, f32[4,8,128]{2,1,0:T(8,128)S(1)}, u32[]{:S(2)}, u32[]{:S(2)}) collective-permute-start(f32[4,8,128]{2,1,0:T(8,128)S(1)} %get-tuple-element.42), channel_id=1, source_target_pairs={{0,8},{8,16},{16,24},{24,32},{32,40},{40,48},{48,56},{56,64},{64,7... | collective-permute-start | bytes 49160 | tf_op jit(solution)/shard_map/ppermute | solution.py:877
  100.1 1.3 collective-permute-start.11
  101.4 0.0 collective-permute-done.10
  101.4 3.2 %collective-permute-done.11 = f32[4,8,128]{2,1,0:T(8,128)S(1)} collective-permute-done((f32[4,8,128]{2,1,0:T(8,128)S(1)}, f32[4,8,128]{2,1,0:T(8,128)S(1)}, u32[]{:S(2)}, u32[]{:S(2)}) %collective-permute-start.11) | collective-permute-done | bytes 16416 | tf_op jit(solution)/shard_map/ppermute | solution.py:877
  104.5 3.3 %collective-permute-start.13 = (f32[16,8,128]{2,1,0:T(8,128)S(1)}, f32[16,8,128]{2,1,0:T(8,128)S(1)}, u32[]{:S(2)}, u32[]{:S(2)}) collective-permute-start(f32[16,8,128]{2,1,0:T(8,128)S(1)} %constant_dynamic-update-slice_fusion.mid), channel_id=1, source_target_pairs={{1,2},{3,4},{5,6},{2,1},{4,3},{6,5},{9,10},{11,12},{13,14},{10,9},... | collective-permute-start | bytes 196616 | tf_op jit(solution)/shard_map/ppermute | solution.py:885
  107.8 1.9 %collective-permute-start.12 = (f32[16,8,128]{2,1,0:T(8,128)S(1)}, f32[16,8,128]{2,1,0:T(8,128)S(1)}, u32[]{:S(2)}, u32[]{:S(2)}) collective-permute-start(f32[16,8,128]{2,1,0:T(8,128)S(1)} %constant_dynamic-update-slice_fusion.mid), channel_id=1, source_target_pairs={{0,1},{2,3},{4,5},{6,7},{1,0},{3,2},{5,4},{7,6},{8,9},{10,11},{12,... | collective-permute-start | bytes 196616 | tf_op jit(solution)/shard_map/ppermute | solution.py:885
  109.7 0.4 collective-permute-done.13.link
  110.1 0.8 collective-permute-done.12.chip
  111.0 0.9 shard_map.57
  111.9 2.1 %collective-permute-start.14 = (f32[8,128]{1,0:T(8,128)S(1)}, f32[8,128]{1,0:T(8,128)S(1)}, u32[]{:S(2)}, u32[]{:S(2)}) collective-permute-start(f32[8,128]{1,0:T(8,128)S(1)} %get-tuple-element.44), channel_id=1, source_target_pairs={{0,1},{2,3},{4,5},{6,7},{1,0},{3,2},{5,4},{7,6},{8,9},{10,11},{12,... | collective-permute-start | bytes 12296 | tf_op jit(solution)/shard_map/ppermute | solution.py:885
  113.9 1.0 collective-permute-done.14
  115.0 18.1 %all_to_all.11.fetched = f32[32,16,128]{2,1,0:T(8,128)S(1)} all-to-all(f32[32,16,128]{2,1,0:T(8,128)S(1)} %broadcast_in_dim.5), channel_id=1, replica_groups={{0,2,4,6,8,10,12,14,16,18,20,22,24,26,28,30,32,34,36,38,40,42,44,46,48,..., dimensions={0} | all-to-all | bytes 524288 | tf_op jit(solution)/shard_map/all_to_all | solution.py:918
  133.0 6.7 %collective-permute-start.15 = (f32[32,16,128]{2,1,0:T(8,128)S(1)}, f32[32,16,128]{2,1,0:T(8,128)S(1)}, u32[]{:S(2)}, u32[]{:S(2)}) collective-permute-start(f32[32,16,128]{2,1,0:T(8,128)S(1)} %all_to_all.11.fetched), channel_id=1, source_target_pairs={{0,1},{2,3},{4,5},{6,7},{1,0},{3,2},{5,4},{7,6},{8,9},{10,11},{12,... | collective-permute-start | bytes 786440 | tf_op jit(solution)/shard_map/ppermute | solution.py:885
  139.8 1.1 collective-permute-done.15.other
  140.9 3.8 %shard_map.58 = f32[16,16,256]{2,1,0:T(8,128)} custom-call(s32[2]{0:T(128)S(1)} %pad_add_fusion.at, f32[32,16,128]{2,1,0:T(8,128)S(1)} %all_to_all.11.fetched, f32[32,16,128]{2,1,0:T(8,128)S(1)} %collective-permute-done.15.other, f32[16,24,128]{2,1,0:T(8,128)S(1)} %get-tuple-element.45.b1, f32[14,24,128]{2,1,0:T(8,128)S(1)} %get-tuple-element.46.u, ...), custom_call_target="tpu_custom_call" | custom-call | flops 20000000 | bytes 4000000 | tf_op jit(solution)/shard_map/pallas_call | solution.py:91
  (8 shorter events, 0.1 us)
Async XLA Ops:
  0.6 12.4 %copy-start = (f32[3,16,16,256]{3,2,1,0:T(8,128)S(1)}, f32[3,16,16,256]{3,2,1,0:T(8,128)}, u32[]{:S(2)}) copy-start(f32[3,16,16,256]{3,2,1,0:T(8,128)} %velocity.7) | copy-start | bytes 2359300
  2.0 7.3 %collective-permute-start = (f32[16,16,256]{2,1,0:T(8,128)S(1)}, f32[16,16,256]{2,1,0:T(8,128)S(1)}, u32[]{:S(2)}, u32[]{:S(2)}) collective-permute-start(f32[16,16,256]{2,1,0:T(8,128)S(1)} %get-tuple-element.26), channel_id=1, source_target_pairs={{0,8},{8,16},{16,24},{24,32},{32,40},{40,48},{48,56},{56,64},{64,7... | collective-permute-start | bytes 786440 | tf_op jit(solution)/shard_map/ppermute | solution.py:877
  5.9 7.1 %collective-permute-start.1 = (f32[16,16,256]{2,1,0:T(8,128)S(1)}, f32[16,16,256]{2,1,0:T(8,128)S(1)}, u32[]{:S(2)}, u32[]{:S(2)}) collective-permute-start(f32[16,16,256]{2,1,0:T(8,128)S(1)} %get-tuple-element.27), channel_id=1, source_target_pairs={{8,0},{16,8},{24,16},{32,24},{40,32},{48,40},{56,48},{64,56},{72,6... | collective-permute-start | bytes 786440 | tf_op jit(solution)/shard_map/ppermute | solution.py:877
  13.7 12.2 %collective-permute-start.2 = (f32[20,16,256]{2,1,0:T(8,128)S(1)}, f32[20,16,256]{2,1,0:T(8,128)S(1)}, u32[]{:S(2)}, u32[]{:S(2)}) collective-permute-start(f32[20,16,256]{2,1,0:T(8,128)S(1)} %get-tuple-element.28), channel_id=1, source_target_pairs={{0,1},{2,3},{4,5},{6,7},{1,0},{3,2},{5,4},{7,6},{8,9},{10,11},{12,... | collective-permute-start | bytes 983048 | tf_op jit(solution)/shard_map/ppermute | solution.py:885
  21.0 8.4 %collective-permute-start.3 = (f32[20,16,256]{2,1,0:T(8,128)S(1)}, f32[20,16,256]{2,1,0:T(8,128)S(1)}, u32[]{:S(2)}, u32[]{:S(2)}) collective-permute-start(f32[20,16,256]{2,1,0:T(8,128)S(1)} %get-tuple-element.29), channel_id=1, source_target_pairs={{1,2},{3,4},{5,6},{2,1},{4,3},{6,5},{9,10},{11,12},{13,14},{10,9},... | collective-permute-start | bytes 983048 | tf_op jit(solution)/shard_map/ppermute | solution.py:885
  36.7 4.2 %collective-permute-start.4 = (f32[14,16,256]{2,1,0:T(8,128)S(1)}, f32[14,16,256]{2,1,0:T(8,128)S(1)}, u32[]{:S(2)}, u32[]{:S(2)}) collective-permute-start(f32[14,16,256]{2,1,0:T(8,128)S(1)} %get-tuple-element.32), channel_id=1, source_target_pairs={{0,8},{8,16},{16,24},{24,32},{32,40},{40,48},{48,56},{56,64},{64,7... | collective-permute-start | bytes 688136 | tf_op jit(solution)/shard_map/ppermute | solution.py:877
  38.0 6.8 %collective-permute-start.5 = (f32[14,16,256]{2,1,0:T(8,128)S(1)}, f32[14,16,256]{2,1,0:T(8,128)S(1)}, u32[]{:S(2)}, u32[]{:S(2)}) collective-permute-start(f32[14,16,256]{2,1,0:T(8,128)S(1)} %get-tuple-element.33), channel_id=1, source_target_pairs={{8,0},{16,8},{24,16},{32,24},{40,32},{48,40},{56,48},{64,56},{72,6... | collective-permute-start | bytes 688136 | tf_op jit(solution)/shard_map/ppermute | solution.py:877
  45.4 8.3 %collective-permute-start.6 = (f32[62,8,256]{2,1,0:T(8,128)S(1)}, f32[62,8,256]{2,1,0:T(8,128)S(1)}, u32[]{:S(2)}, u32[]{:S(2)}) collective-permute-start(f32[62,8,256]{2,1,0:T(8,128)S(1)} %get-tuple-element.34), channel_id=1, source_target_pairs={{0,1},{2,3},{4,5},{6,7},{1,0},{3,2},{5,4},{7,6},{8,9},{10,11},{12,... | collective-permute-start | bytes 1523720 | tf_op jit(solution)/shard_map/ppermute | solution.py:885
  47.3 12.9 %collective-permute-start.7 = (f32[62,8,256]{2,1,0:T(8,128)S(1)}, f32[62,8,256]{2,1,0:T(8,128)S(1)}, u32[]{:S(2)}, u32[]{:S(2)}) collective-permute-start(f32[62,8,256]{2,1,0:T(8,128)S(1)} %get-tuple-element.35), channel_id=1, source_target_pairs={{1,2},{3,4},{5,6},{2,1},{4,3},{6,5},{9,10},{11,12},{13,14},{10,9},... | collective-permute-start | bytes 1523720 | tf_op jit(solution)/shard_map/ppermute | solution.py:885
  64.0 3.1 %collective-permute-start.8 = (f32[8,128]{1,0:T(8,128)S(1)}, f32[8,128]{1,0:T(8,128)S(1)}, u32[]{:S(2)}, u32[]{:S(2)}) collective-permute-start(f32[8,128]{1,0:T(8,128)S(1)} %get-tuple-element.36), channel_id=1, source_target_pairs={{0,1},{2,3},{4,5},{6,7},{1,0},{3,2},{5,4},{7,6},{8,9},{10,11},{12,... | collective-permute-start | bytes 12296 | tf_op jit(solution)/shard_map/ppermute | solution.py:885
  89.3 3.4 %collective-permute-start.9 = (f32[32,16,128]{2,1,0:T(8,128)S(1)}, f32[32,16,128]{2,1,0:T(8,128)S(1)}, u32[]{:S(2)}, u32[]{:S(2)}) collective-permute-start(f32[32,16,128]{2,1,0:T(8,128)S(1)} %all_to_all.10.fetched), channel_id=1, source_target_pairs={{0,1},{2,3},{4,5},{6,7},{1,0},{3,2},{5,4},{7,6},{8,9},{10,11},{12,... | collective-permute-start | bytes 786440 | tf_op jit(solution)/shard_map/ppermute | solution.py:885
  97.8 3.5 %collective-permute-start.10 = (f32[4,8,128]{2,1,0:T(8,128)S(1)}, f32[4,8,128]{2,1,0:T(8,128)S(1)}, u32[]{:S(2)}, u32[]{:S(2)}) collective-permute-start(f32[4,8,128]{2,1,0:T(8,128)S(1)} %get-tuple-element.42), channel_id=1, source_target_pairs={{0,8},{8,16},{16,24},{24,32},{32,40},{40,48},{48,56},{56,64},{64,7... | collective-permute-start | bytes 49160 | tf_op jit(solution)/shard_map/ppermute | solution.py:877
  100.1 4.5 %collective-permute-start.11 = (f32[4,8,128]{2,1,0:T(8,128)S(1)}, f32[4,8,128]{2,1,0:T(8,128)S(1)}, u32[]{:S(2)}, u32[]{:S(2)}) collective-permute-start(f32[4,8,128]{2,1,0:T(8,128)S(1)} %get-tuple-element.43), channel_id=1, source_target_pairs={{8,0},{16,8},{24,16},{32,24},{40,32},{48,40},{56,48},{64,56},{72,6... | collective-permute-start | bytes 49160 | tf_op jit(solution)/shard_map/ppermute | solution.py:877
  104.5 5.6 %collective-permute-start.13 = (f32[16,8,128]{2,1,0:T(8,128)S(1)}, f32[16,8,128]{2,1,0:T(8,128)S(1)}, u32[]{:S(2)}, u32[]{:S(2)}) collective-permute-start(f32[16,8,128]{2,1,0:T(8,128)S(1)} %constant_dynamic-update-slice_fusion.mid), channel_id=1, source_target_pairs={{1,2},{3,4},{5,6},{2,1},{4,3},{6,5},{9,10},{11,12},{13,14},{10,9},... | collective-permute-start | bytes 196616 | tf_op jit(solution)/shard_map/ppermute | solution.py:885
  107.8 3.1 %collective-permute-start.12 = (f32[16,8,128]{2,1,0:T(8,128)S(1)}, f32[16,8,128]{2,1,0:T(8,128)S(1)}, u32[]{:S(2)}, u32[]{:S(2)}) collective-permute-start(f32[16,8,128]{2,1,0:T(8,128)S(1)} %constant_dynamic-update-slice_fusion.mid), channel_id=1, source_target_pairs={{0,1},{2,3},{4,5},{6,7},{1,0},{3,2},{5,4},{7,6},{8,9},{10,11},{12,... | collective-permute-start | bytes 196616 | tf_op jit(solution)/shard_map/ppermute | solution.py:885
  111.9 3.1 %collective-permute-start.14 = (f32[8,128]{1,0:T(8,128)S(1)}, f32[8,128]{1,0:T(8,128)S(1)}, u32[]{:S(2)}, u32[]{:S(2)}) collective-permute-start(f32[8,128]{1,0:T(8,128)S(1)} %get-tuple-element.44), channel_id=1, source_target_pairs={{0,1},{2,3},{4,5},{6,7},{1,0},{3,2},{5,4},{7,6},{8,9},{10,11},{12,... | collective-permute-start | bytes 12296 | tf_op jit(solution)/shard_map/ppermute | solution.py:885
  133.0 7.9 %collective-permute-start.15 = (f32[32,16,128]{2,1,0:T(8,128)S(1)}, f32[32,16,128]{2,1,0:T(8,128)S(1)}, u32[]{:S(2)}, u32[]{:S(2)}) collective-permute-start(f32[32,16,128]{2,1,0:T(8,128)S(1)} %all_to_all.11.fetched), channel_id=1, source_target_pairs={{0,1},{2,3},{4,5},{6,7},{1,0},{3,2},{5,4},{7,6},{8,9},{10,11},{12,... | collective-permute-start | bytes 786440 | tf_op jit(solution)/shard_map/ppermute | solution.py:885

commit v9 on v8

--- a/solution.py
+++ b/solution.py
@@ -217,7 +217,7 @@
 SLOTS = 20
 
 
-def pack_body(at, psi, velocity, low, high, chip, link):
+def pack_body(at, psi, velocity, low, high, link, chip):
     odd = lax.rem(at[1], 2) == 1
     level, speeds = wide_planes(psi, velocity, low, high)
     fields = [level] + speeds
@@ -351,7 +351,7 @@
 
 
 def advance_body(
-    nx, ny, at, psi, velocity, low, high, chip, link, change_in, moved, source, first, final,
+    nx, ny, at, psi, velocity, low, high, link, chip, change_in, moved, source, first, final,
     v8, u8, w8, v32, u32, c8, p_x, q_x, r_x, m, n_x, n_y, n_z, s_x, part,
 ):
     lower, upper = pick_sides(at, chip, link)
@@ -456,7 +456,7 @@
         (skin, 32, 256), (skin, 8, 256), marks, marks, marks,
         (skin, 24, 256), normals, normals, normals, (18, 16, 256), block,
     ]
-    args = [at, psi, velocity, low, high, chip, link, change]
+    args = [at, psi, velocity, low, high, link, chip, change]
     outs = [block, block, (HALO, 16, 256), (HALO, 16, 256)]
     return call(functools.partial(advance_body, nx, ny), outs, scratch, args, 30000000)
 
@@ -586,7 +586,7 @@
     return low[p + HALO] if p < 0 else own[p] if p < 16 else high[p - 16]
 
 
-def weave_body(at, own, low, high, chip, link):
+def weave_body(at, own, low, high, link, chip):
     odd = lax.rem(at[1], 2) == 1
     for k in range(SOURCE_TILES):
         first, final, total = [], [], 0
@@ -612,7 +612,7 @@
 
 
 def first_down_body(
-    nx, ny, at, own, low, high, chip, link, b_out, v_out, b1_out, u_out, b2_out, b, v, pair, t, s1, t1
+    nx, ny, at, own, low, high, link, chip, b_out, v_out, b1_out, u_out, b2_out, b, v, pair, t, s1, t1
 ):
     lower, upper = pick_sides(at, chip, link)
     none = jnp.zeros((16, 256), F32)
@@ -659,7 +659,7 @@
         (4, 24, 128),
         (4, 8, 128),
     ]
-    args = [at, own, low, high, chip, link]
+    args = [at, own, low, high, link, chip]
     return call(functools.partial(first_down_body, nx, ny), outs, scratch, args, 20000000)
 
 
@@ -924,7 +924,7 @@
     at = jnp.stack([lax.axis_index("wide"), lax.axis_index("narrow")]).astype(jnp.int32)
     psi, x_low, x_high = prepare(phase, distance, velocity)
     low, high = shifted(x_high, "wide", 1), shifted(x_low, "wide", -1)
-    chip, link = pack(at, psi, velocity, low, high)
+    link, chip = pack(at, psi, velocity, low, high)
     v_link = swapped(link, 1)
     v_chip = swapped(chip, 0)
     change = inner(psi, velocity, low, high)
@@ -932,7 +932,7 @@
         nx, ny, at, psi, velocity, low, high, v_chip, v_link, change
     )
     low, high = shifted(final, "wide", 1), shifted(first, "wide", -1)
-    chip, link = weave(at, source, low, high)
+    link, chip = weave(at, source, low, high)
     b_link = swapped(link, 1)
     b_chip = swapped(chip, 0)
     b, v, b1, u, b2 = first_down(nx, ny, at, source, low, high, b_chip, b_link)

time: 145 us -> 141 us (0.972)
  waiting for transfers between devices: 30.4 us -> 26.4 us
    ppermute x10, waiting for transfers between devices: 16 us -> 10.6 us  [swapped(): return lax.ppermute(array, 'narrow', pairs + [(j, i) for i, j in pairs])]
    ppermute x10, starting transfers between devices: 35.3 us -> 33.3 us  [swapped(): return lax.ppermute(array, 'narrow', pairs + [(j, i) for i, j in pairs])]
    ppermute x6, starting transfers between devices: 11.3 us -> 13.2 us  [shifted(): lax.ppermute(array, axis, [(i, i + step) for i in range(count) if 0 <= i...]
    ppermute x6, waiting for transfers between devices: 14.4 us -> 15.8 us  [shifted(): lax.ppermute(array, axis, [(i, i + step) for i in range(count) if 0 <= i...]
  transfers between devices with their start and end apart: 16 -> 16, of which waited for: 13 -> 12; matrix products, arithmetic and copies ran while one was open for 0% -> 0% of each run, Pallas kernels for 2% -> 2%
where the time goes in v9:
time: 141 us; the launch traced here: 140 us
  starting transfers between devices  46.4 us (33%)
  blocking collectives  39.9 us (28%)
  Pallas kernels  26.4 us (19%)
  waiting for transfers between devices  26.4 us (19%)
    all_to_all x2, blocking collectives, spread_coarse(): lax.all_to_all(pieces, ('wide', 'narrow'), 0, 0, axis_index_groups=groups)  39.9 us
    ppermute x10, starting transfers between devices, swapped(): return lax.ppermute(array, 'narrow', pairs + [(j, i) for i, j in pairs])  33.3 us
    pallas_call x8, Pallas kernels, call(): pl.pallas_call(body, out_shape=[jax.ShapeDtypeStruct(s, F32) for s in out...  25.1 us
    ppermute x6, waiting for transfers between devices, shifted(): lax.ppermute(array, axis, [(i, i + step) for i in range(count) if 0 <= i...  15.8 us
    ppermute x6, starting transfers between devices, shifted(): lax.ppermute(array, axis, [(i, i + step) for i in range(count) if 0 <= i...  13.2 us
    ppermute x10, waiting for transfers between devices, swapped(): return lax.ppermute(array, 'narrow', pairs + [(j, i) for i, j in pairs])  10.6 us
  transfers between devices with their start and end apart: 16, of which 12 were waited for; matrix products, arithmetic and copies ran while one was open for 0% of the time, Pallas kernels for 2%

profile of v9, /device:TPU:1, one launch (start us, length us, event | category | flops | bytes accessed | tf_op | source)
XLA Modules:
  0.0 140.2 jit_solution(942977600617139105)
XLA Ops:
  0.6 0.0 copy-start
  0.6 1.3 shard_map.50
  2.0 4.0 %collective-permute-start = (f32[16,16,256]{2,1,0:T(8,128)S(1)}, f32[16,16,256]{2,1,0:T(8,128)S(1)}, u32[]{:S(2)}, u32[]{:S(2)}) collective-permute-start(f32[16,16,256]{2,1,0:T(8,128)S(1)} %get-tuple-element.26), channel_id=1, source_target_pairs={{0,8},{8,16},{16,24},{24,32},{32,40},{40,48},{48,56},{56,64},{64,7... | collective-permute-start | bytes 786440 | tf_op jit(solution)/shard_map/ppermute | solution.py:877
  5.9 1.3 collective-permute-start.1
  7.2 0.1 pad_add_fusion.at
  7.3 1.9 %collective-permute-done.low = f32[16,16,256]{2,1,0:T(8,128)S(1)} collective-permute-done((f32[16,16,256]{2,1,0:T(8,128)S(1)}, f32[16,16,256]{2,1,0:T(8,128)S(1)}, u32[]{:S(2)}, u32[]{:S(2)}) %collective-permute-start) | collective-permute-done | bytes 262176 | tf_op jit(solution)/shard_map/ppermute | solution.py:877
  9.2 3.8 %collective-permute-done.1.high = f32[16,16,256]{2,1,0:T(8,128)S(1)} collective-permute-done((f32[16,16,256]{2,1,0:T(8,128)S(1)}, f32[16,16,256]{2,1,0:T(8,128)S(1)}, u32[]{:S(2)}, u32[]{:S(2)}) %collective-permute-start.1) | collective-permute-done | bytes 262176 | tf_op jit(solution)/shard_map/ppermute | solution.py:877
  13.1 0.0 copy-done
  13.1 0.6 shard_map.51
  13.7 6.6 %collective-permute-start.2 = (f32[20,16,256]{2,1,0:T(8,128)S(1)}, f32[20,16,256]{2,1,0:T(8,128)S(1)}, u32[]{:S(2)}, u32[]{:S(2)}) collective-permute-start(f32[20,16,256]{2,1,0:T(8,128)S(1)} %get-tuple-element.28), channel_id=1, source_target_pairs={{1,2},{3,4},{5,6},{2,1},{4,3},{6,5},{9,10},{11,12},{13,14},{10,9},... | collective-permute-start | bytes 983048 | tf_op jit(solution)/shard_map/ppermute | solution.py:885
  20.3 1.9 %collective-permute-start.3 = (f32[20,16,256]{2,1,0:T(8,128)S(1)}, f32[20,16,256]{2,1,0:T(8,128)S(1)}, u32[]{:S(2)}, u32[]{:S(2)}) collective-permute-start(f32[20,16,256]{2,1,0:T(8,128)S(1)} %get-tuple-element.29), channel_id=1, source_target_pairs={{0,1},{2,3},{4,5},{6,7},{1,0},{3,2},{5,4},{7,6},{8,9},{10,11},{12,... | collective-permute-start | bytes 983048 | tf_op jit(solution)/shard_map/ppermute | solution.py:885
  22.2 2.9 %shard_map.52.change_in = f32[22,16,256]{2,1,0:T(8,128)S(1)} custom-call(f32[16,16,256]{2,1,0:T(8,128)S(1)} %get-tuple-element.25.psi, f32[3,16,16,256]{3,2,1,0:T(8,128)S(1)} %copy-done, f32[16,16,256]{2,1,0:T(8,128)S(1)} %collective-permute-done.low, f32[16,16,256]{2,1,0:T(8,128)S(1)} %collective-permute-done.1.high), custom_call_target="tpu_custom_call" | custom-call | flops 8000000 | bytes 4000000 | tf_op jit(solution)/shard_map/pallas_call | solution.py:91
  25.2 0.0 collective-permute-done.2.link
  25.2 0.0 collective-permute-done.3.chip
  25.2 7.3 %shard_map.53 = (f32[16,16,256]{2,1,0:T(8,128)}, f32[16,16,256]{2,1,0:T(8,128)S(1)}, f32[14,16,256]{2,1,0:T(8,128)S(1)}, f32[14,16,256]{2,1,0:T(8,128)S(1)}) custom-call(s32[2]{0:T(128)S(1)} %pad_add_fusion.at, f32[16,16,256]{2,1,0:T(8,128)S(1)} %get-tuple-element.25.psi, f32[3,16,16,256]{3,2,1,0:T(8,128)S(1)} %copy-done, ...), custom_call_target="tpu_custom_call" | custom-call | flops 30000000 | bytes 4000000 | tf_op jit(solution)/shard_map/pallas_call | solution.py:91
  32.4 3.1 %collective-permute-start.4 = (f32[14,16,256]{2,1,0:T(8,128)S(1)}, f32[14,16,256]{2,1,0:T(8,128)S(1)}, u32[]{:S(2)}, u32[]{:S(2)}) collective-permute-start(f32[14,16,256]{2,1,0:T(8,128)S(1)} %get-tuple-element.32), channel_id=1, source_target_pairs={{0,8},{8,16},{16,24},{24,32},{32,40},{40,48},{48,56},{56,64},{64,7... | collective-permute-start | bytes 688136 | tf_op jit(solution)/shard_map/ppermute | solution.py:877
  35.6 1.3 collective-permute-start.5
  36.9 3.1 %collective-permute-done.4.low = f32[14,16,256]{2,1,0:T(8,128)S(1)} collective-permute-done((f32[14,16,256]{2,1,0:T(8,128)S(1)}, f32[14,16,256]{2,1,0:T(8,128)S(1)}, u32[]{:S(2)}, u32[]{:S(2)}) %collective-permute-start.4) | collective-permute-done | bytes 229408 | tf_op jit(solution)/shard_map/ppermute | solution.py:877
  40.0 3.8 %collective-permute-done.5.high = f32[14,16,256]{2,1,0:T(8,128)S(1)} collective-permute-done((f32[14,16,256]{2,1,0:T(8,128)S(1)}, f32[14,16,256]{2,1,0:T(8,128)S(1)}, u32[]{:S(2)}, u32[]{:S(2)}) %collective-permute-start.5) | collective-permute-done | bytes 229408 | tf_op jit(solution)/shard_map/ppermute | solution.py:877
  43.8 0.6 shard_map.54
  44.4 4.8 %collective-permute-start.6 = (f32[62,8,256]{2,1,0:T(8,128)S(1)}, f32[62,8,256]{2,1,0:T(8,128)S(1)}, u32[]{:S(2)}, u32[]{:S(2)}) collective-permute-start(f32[62,8,256]{2,1,0:T(8,128)S(1)} %get-tuple-element.34), channel_id=1, source_target_pairs={{1,2},{3,4},{5,6},{2,1},{4,3},{6,5},{9,10},{11,12},{13,14},{10,9},... | collective-permute-start | bytes 1523720 | tf_op jit(solution)/shard_map/ppermute | solution.py:885
  49.2 2.1 %collective-permute-start.7 = (f32[62,8,256]{2,1,0:T(8,128)S(1)}, f32[62,8,256]{2,1,0:T(8,128)S(1)}, u32[]{:S(2)}, u32[]{:S(2)}) collective-permute-start(f32[62,8,256]{2,1,0:T(8,128)S(1)} %get-tuple-element.35), channel_id=1, source_target_pairs={{0,1},{2,3},{4,5},{6,7},{1,0},{3,2},{5,4},{7,6},{8,9},{10,11},{12,... | collective-permute-start | bytes 1523720 | tf_op jit(solution)/shard_map/ppermute | solution.py:885
  51.3 4.6 %collective-permute-done.6.link = f32[62,8,256]{2,1,0:T(8,128)S(1)} collective-permute-done((f32[62,8,256]{2,1,0:T(8,128)S(1)}, f32[62,8,256]{2,1,0:T(8,128)S(1)}, u32[]{:S(2)}, u32[]{:S(2)}) %collective-permute-start.6) | collective-permute-done | bytes 507936 | tf_op jit(solution)/shard_map/ppermute | solution.py:885
  55.9 0.0 collective-permute-done.7.chip
  55.9 3.8 %shard_map.55 = (f32[26,32,256]{2,1,0:T(8,128)S(1)}, f32[28,32,256]{2,1,0:T(8,128)S(1)}, f32[20,24,128]{2,1,0:T(8,128)S(1)}, f32[18,24,128]{2,1,0:T(8,128)S(1)}, f32[8,128]{1,0:T(8,128)S(1)}) custom-call(s32[2]{0:T(128)S(1)} %pad_add_fusion.at, f32[16,16,256]{2,1,0:T(8,128)S(1)} %get-tuple-element.31.own, f32[14,16,256]{2,1,0:T(8,128)S(1)} %collective-permute-done.4.low, ...), custom_call_target="tpu_custom_call" | custom-call | flops 20000000 | bytes 4000000 | tf_op jit(solution)/shard_map/pallas_call | solution.py:91
  59.8 1.9 %collective-permute-start.8 = (f32[8,128]{1,0:T(8,128)S(1)}, f32[8,128]{1,0:T(8,128)S(1)}, u32[]{:S(2)}, u32[]{:S(2)}) collective-permute-start(f32[8,128]{1,0:T(8,128)S(1)} %get-tuple-element.36), channel_id=1, source_target_pairs={{0,1},{2,3},{4,5},{6,7},{1,0},{3,2},{5,4},{7,6},{8,9},{10,11},{12,... | collective-permute-start | bytes 12296 | tf_op jit(solution)/shard_map/ppermute | solution.py:885
  61.7 1.1 collective-permute-done.8
  62.9 21.8 %all_to_all.10.fetched = f32[32,16,128]{2,1,0:T(8,128)S(1)} all-to-all(f32[32,16,128]{2,1,0:T(8,128)S(1)} %broadcast_in_dim.4), channel_id=1, replica_groups={{0,2,4,6,8,10,12,14,16,18,20,22,24,26,28,30,32,34,36,38,40,42,44,46,48,..., dimensions={0} | all-to-all | bytes 524288 | tf_op jit(solution)/shard_map/all_to_all | solution.py:918
  84.7 1.9 %collective-permute-start.9 = (f32[32,16,128]{2,1,0:T(8,128)S(1)}, f32[32,16,128]{2,1,0:T(8,128)S(1)}, u32[]{:S(2)}, u32[]{:S(2)}) collective-permute-start(f32[32,16,128]{2,1,0:T(8,128)S(1)} %all_to_all.10.fetched), channel_id=1, source_target_pairs={{0,1},{2,3},{4,5},{6,7},{1,0},{3,2},{5,4},{7,6},{8,9},{10,11},{12,... | collective-permute-start | bytes 786440 | tf_op jit(solution)/shard_map/ppermute | solution.py:885
  86.6 1.5 %collective-permute-done.9.other = f32[32,16,128]{2,1,0:T(8,128)S(1)} collective-permute-done((f32[32,16,128]{2,1,0:T(8,128)S(1)}, f32[32,16,128]{2,1,0:T(8,128)S(1)}, u32[]{:S(2)}, u32[]{:S(2)}) %collective-permute-start.9) | collective-permute-done | bytes 262176 | tf_op jit(solution)/shard_map/ppermute | solution.py:885
  88.1 5.1 %shard_map.56 = (f32[20,32,256]{2,1,0:T(8,128)S(1)}, f32[16,8,128]{2,1,0:T(8,128)S(1)}, f32[4,8,128]{2,1,0:T(8,128)S(1)}, f32[4,8,128]{2,1,0:T(8,128)S(1)}) custom-call(s32[2]{0:T(128)S(1)} %pad_add_fusion.at, f32[32,16,128]{2,1,0:T(8,128)S(1)} %all_to_all.10.fetched, f32[32,16,128]{2,1,0:T(8,128)S(1)} %collective-permute-done.9.other, ...), custom_call_target="tpu_custom_call" | custom-call | flops 30000000 | bytes 4000000 | tf_op jit(solution)/shard_map/pallas_call | solution.py:91
  93.2 2.2 %collective-permute-start.10 = (f32[4,8,128]{2,1,0:T(8,128)S(1)}, f32[4,8,128]{2,1,0:T(8,128)S(1)}, u32[]{:S(2)}, u32[]{:S(2)}) collective-permute-start(f32[4,8,128]{2,1,0:T(8,128)S(1)} %get-tuple-element.42), channel_id=1, source_target_pairs={{0,8},{8,16},{16,24},{24,32},{32,40},{40,48},{48,56},{56,64},{64,7... | collective-permute-start | bytes 49160 | tf_op jit(solution)/shard_map/ppermute | solution.py:877
  95.4 1.3 collective-permute-start.11
  96.7 0.0 collective-permute-done.10
  96.8 3.2 %collective-permute-done.11 = f32[4,8,128]{2,1,0:T(8,128)S(1)} collective-permute-done((f32[4,8,128]{2,1,0:T(8,128)S(1)}, f32[4,8,128]{2,1,0:T(8,128)S(1)}, u32[]{:S(2)}, u32[]{:S(2)}) %collective-permute-start.11) | collective-permute-done | bytes 16416 | tf_op jit(solution)/shard_map/ppermute | solution.py:877
  99.9 3.3 %collective-permute-start.13 = (f32[16,8,128]{2,1,0:T(8,128)S(1)}, f32[16,8,128]{2,1,0:T(8,128)S(1)}, u32[]{:S(2)}, u32[]{:S(2)}) collective-permute-start(f32[16,8,128]{2,1,0:T(8,128)S(1)} %constant_dynamic-update-slice_fusion.mid), channel_id=1, source_target_pairs={{1,2},{3,4},{5,6},{2,1},{4,3},{6,5},{9,10},{11,12},{13,14},{10,9},... | collective-permute-start | bytes 196616 | tf_op jit(solution)/shard_map/ppermute | solution.py:885
  103.2 1.9 %collective-permute-start.12 = (f32[16,8,128]{2,1,0:T(8,128)S(1)}, f32[16,8,128]{2,1,0:T(8,128)S(1)}, u32[]{:S(2)}, u32[]{:S(2)}) collective-permute-start(f32[16,8,128]{2,1,0:T(8,128)S(1)} %constant_dynamic-update-slice_fusion.mid), channel_id=1, source_target_pairs={{0,1},{2,3},{4,5},{6,7},{1,0},{3,2},{5,4},{7,6},{8,9},{10,11},{12,... | collective-permute-start | bytes 196616 | tf_op jit(solution)/shard_map/ppermute | solution.py:885
  105.2 0.3 collective-permute-done.13.link
  105.5 0.9 collective-permute-done.12.chip
  106.4 0.9 shard_map.57
  107.3 2.1 %collective-permute-start.14 = (f32[8,128]{1,0:T(8,128)S(1)}, f32[8,128]{1,0:T(8,128)S(1)}, u32[]{:S(2)}, u32[]{:S(2)}) collective-permute-start(f32[8,128]{1,0:T(8,128)S(1)} %get-tuple-element.44), channel_id=1, source_target_pairs={{0,1},{2,3},{4,5},{6,7},{1,0},{3,2},{5,4},{7,6},{8,9},{10,11},{12,... | collective-permute-start | bytes 12296 | tf_op jit(solution)/shard_map/ppermute | solution.py:885
  109.4 1.0 collective-permute-done.14
  110.4 18.1 %all_to_all.11.fetched = f32[32,16,128]{2,1,0:T(8,128)S(1)} all-to-all(f32[32,16,128]{2,1,0:T(8,128)S(1)} %broadcast_in_dim.5), channel_id=1, replica_groups={{0,2,4,6,8,10,12,14,16,18,20,22,24,26,28,30,32,34,36,38,40,42,44,46,48,..., dimensions={0} | all-to-all | bytes 524288 | tf_op jit(solution)/shard_map/all_to_all | solution.py:918
  128.5 6.7 %collective-permute-start.15 = (f32[32,16,128]{2,1,0:T(8,128)S(1)}, f32[32,16,128]{2,1,0:T(8,128)S(1)}, u32[]{:S(2)}, u32[]{:S(2)}) collective-permute-start(f32[32,16,128]{2,1,0:T(8,128)S(1)} %all_to_all.11.fetched), channel_id=1, source_target_pairs={{0,1},{2,3},{4,5},{6,7},{1,0},{3,2},{5,4},{7,6},{8,9},{10,11},{12,... | collective-permute-start | bytes 786440 | tf_op jit(solution)/shard_map/ppermute | solution.py:885
  135.2 1.1 collective-permute-done.15.other
  136.4 3.8 %shard_map.58 = f32[16,16,256]{2,1,0:T(8,128)} custom-call(s32[2]{0:T(128)S(1)} %pad_add_fusion.at, f32[32,16,128]{2,1,0:T(8,128)S(1)} %all_to_all.11.fetched, f32[32,16,128]{2,1,0:T(8,128)S(1)} %collective-permute-done.15.other, f32[16,24,128]{2,1,0:T(8,128)S(1)} %get-tuple-element.45.b1, f32[14,24,128]{2,1,0:T(8,128)S(1)} %get-tuple-element.46.u, ...), custom_call_target="tpu_custom_call" | custom-call | flops 20000000 | bytes 4000000 | tf_op jit(solution)/shard_map/pallas_call | solution.py:91
  (8 shorter events, 0.1 us)
Async XLA Ops:
  0.6 12.4 %copy-start = (f32[3,16,16,256]{3,2,1,0:T(8,128)S(1)}, f32[3,16,16,256]{3,2,1,0:T(8,128)}, u32[]{:S(2)}) copy-start(f32[3,16,16,256]{3,2,1,0:T(8,128)} %velocity.7) | copy-start | bytes 2359300
  2.0 7.3 %collective-permute-start = (f32[16,16,256]{2,1,0:T(8,128)S(1)}, f32[16,16,256]{2,1,0:T(8,128)S(1)}, u32[]{:S(2)}, u32[]{:S(2)}) collective-permute-start(f32[16,16,256]{2,1,0:T(8,128)S(1)} %get-tuple-element.26), channel_id=1, source_target_pairs={{0,8},{8,16},{16,24},{24,32},{32,40},{40,48},{48,56},{56,64},{64,7... | collective-permute-start | bytes 786440 | tf_op jit(solution)/shard_map/ppermute | solution.py:877
  5.9 7.1 %collective-permute-start.1 = (f32[16,16,256]{2,1,0:T(8,128)S(1)}, f32[16,16,256]{2,1,0:T(8,128)S(1)}, u32[]{:S(2)}, u32[]{:S(2)}) collective-permute-start(f32[16,16,256]{2,1,0:T(8,128)S(1)} %get-tuple-element.27), channel_id=1, source_target_pairs={{8,0},{16,8},{24,16},{32,24},{40,32},{48,40},{56,48},{64,56},{72,6... | collective-permute-start | bytes 786440 | tf_op jit(solution)/shard_map/ppermute | solution.py:877
  13.7 11.5 %collective-permute-start.2 = (f32[20,16,256]{2,1,0:T(8,128)S(1)}, f32[20,16,256]{2,1,0:T(8,128)S(1)}, u32[]{:S(2)}, u32[]{:S(2)}) collective-permute-start(f32[20,16,256]{2,1,0:T(8,128)S(1)} %get-tuple-element.28), channel_id=1, source_target_pairs={{1,2},{3,4},{5,6},{2,1},{4,3},{6,5},{9,10},{11,12},{13,14},{10,9},... | collective-permute-start | bytes 983048 | tf_op jit(solution)/shard_map/ppermute | solution.py:885
  20.3 4.9 %collective-permute-start.3 = (f32[20,16,256]{2,1,0:T(8,128)S(1)}, f32[20,16,256]{2,1,0:T(8,128)S(1)}, u32[]{:S(2)}, u32[]{:S(2)}) collective-permute-start(f32[20,16,256]{2,1,0:T(8,128)S(1)} %get-tuple-element.29), channel_id=1, source_target_pairs={{0,1},{2,3},{4,5},{6,7},{1,0},{3,2},{5,4},{7,6},{8,9},{10,11},{12,... | collective-permute-start | bytes 983048 | tf_op jit(solution)/shard_map/ppermute | solution.py:885
  32.4 7.6 %collective-permute-start.4 = (f32[14,16,256]{2,1,0:T(8,128)S(1)}, f32[14,16,256]{2,1,0:T(8,128)S(1)}, u32[]{:S(2)}, u32[]{:S(2)}) collective-permute-start(f32[14,16,256]{2,1,0:T(8,128)S(1)} %get-tuple-element.32), channel_id=1, source_target_pairs={{0,8},{8,16},{16,24},{24,32},{32,40},{40,48},{48,56},{56,64},{64,7... | collective-permute-start | bytes 688136 | tf_op jit(solution)/shard_map/ppermute | solution.py:877
  35.6 8.2 %collective-permute-start.5 = (f32[14,16,256]{2,1,0:T(8,128)S(1)}, f32[14,16,256]{2,1,0:T(8,128)S(1)}, u32[]{:S(2)}, u32[]{:S(2)}) collective-permute-start(f32[14,16,256]{2,1,0:T(8,128)S(1)} %get-tuple-element.33), channel_id=1, source_target_pairs={{8,0},{16,8},{24,16},{32,24},{40,32},{48,40},{56,48},{64,56},{72,6... | collective-permute-start | bytes 688136 | tf_op jit(solution)/shard_map/ppermute | solution.py:877
  44.4 11.5 %collective-permute-start.6 = (f32[62,8,256]{2,1,0:T(8,128)S(1)}, f32[62,8,256]{2,1,0:T(8,128)S(1)}, u32[]{:S(2)}, u32[]{:S(2)}) collective-permute-start(f32[62,8,256]{2,1,0:T(8,128)S(1)} %get-tuple-element.34), channel_id=1, source_target_pairs={{1,2},{3,4},{5,6},{2,1},{4,3},{6,5},{9,10},{11,12},{13,14},{10,9},... | collective-permute-start | bytes 1523720 | tf_op jit(solution)/shard_map/ppermute | solution.py:885
  49.2 6.7 %collective-permute-start.7 = (f32[62,8,256]{2,1,0:T(8,128)S(1)}, f32[62,8,256]{2,1,0:T(8,128)S(1)}, u32[]{:S(2)}, u32[]{:S(2)}) collective-permute-start(f32[62,8,256]{2,1,0:T(8,128)S(1)} %get-tuple-element.35), channel_id=1, source_target_pairs={{0,1},{2,3},{4,5},{6,7},{1,0},{3,2},{5,4},{7,6},{8,9},{10,11},{12,... | collective-permute-start | bytes 1523720 | tf_op jit(solution)/shard_map/ppermute | solution.py:885
  59.8 3.1 %collective-permute-start.8 = (f32[8,128]{1,0:T(8,128)S(1)}, f32[8,128]{1,0:T(8,128)S(1)}, u32[]{:S(2)}, u32[]{:S(2)}) collective-permute-start(f32[8,128]{1,0:T(8,128)S(1)} %get-tuple-element.36), channel_id=1, source_target_pairs={{0,1},{2,3},{4,5},{6,7},{1,0},{3,2},{5,4},{7,6},{8,9},{10,11},{12,... | collective-permute-start | bytes 12296 | tf_op jit(solution)/shard_map/ppermute | solution.py:885
  84.7 3.4 %collective-permute-start.9 = (f32[32,16,128]{2,1,0:T(8,128)S(1)}, f32[32,16,128]{2,1,0:T(8,128)S(1)}, u32[]{:S(2)}, u32[]{:S(2)}) collective-permute-start(f32[32,16,128]{2,1,0:T(8,128)S(1)} %all_to_all.10.fetched), channel_id=1, source_target_pairs={{0,1},{2,3},{4,5},{6,7},{1,0},{3,2},{5,4},{7,6},{8,9},{10,11},{12,... | collective-permute-start | bytes 786440 | tf_op jit(solution)/shard_map/ppermute | solution.py:885
  93.2 3.5 %collective-permute-start.10 = (f32[4,8,128]{2,1,0:T(8,128)S(1)}, f32[4,8,128]{2,1,0:T(8,128)S(1)}, u32[]{:S(2)}, u32[]{:S(2)}) collective-permute-start(f32[4,8,128]{2,1,0:T(8,128)S(1)} %get-tuple-element.42), channel_id=1, source_target_pairs={{0,8},{8,16},{16,24},{24,32},{32,40},{40,48},{48,56},{56,64},{64,7... | collective-permute-start | bytes 49160 | tf_op jit(solution)/shard_map/ppermute | solution.py:877
  95.4 4.5 %collective-permute-start.11 = (f32[4,8,128]{2,1,0:T(8,128)S(1)}, f32[4,8,128]{2,1,0:T(8,128)S(1)}, u32[]{:S(2)}, u32[]{:S(2)}) collective-permute-start(f32[4,8,128]{2,1,0:T(8,128)S(1)} %get-tuple-element.43), channel_id=1, source_target_pairs={{8,0},{16,8},{24,16},{32,24},{40,32},{48,40},{56,48},{64,56},{72,6... | collective-permute-start | bytes 49160 | tf_op jit(solution)/shard_map/ppermute | solution.py:877
  99.9 5.6 %collective-permute-start.13 = (f32[16,8,128]{2,1,0:T(8,128)S(1)}, f32[16,8,128]{2,1,0:T(8,128)S(1)}, u32[]{:S(2)}, u32[]{:S(2)}) collective-permute-start(f32[16,8,128]{2,1,0:T(8,128)S(1)} %constant_dynamic-update-slice_fusion.mid), channel_id=1, source_target_pairs={{1,2},{3,4},{5,6},{2,1},{4,3},{6,5},{9,10},{11,12},{13,14},{10,9},... | collective-permute-start | bytes 196616 | tf_op jit(solution)/shard_map/ppermute | solution.py:885
  103.2 3.1 %collective-permute-start.12 = (f32[16,8,128]{2,1,0:T(8,128)S(1)}, f32[16,8,128]{2,1,0:T(8,128)S(1)}, u32[]{:S(2)}, u32[]{:S(2)}) collective-permute-start(f32[16,8,128]{2,1,0:T(8,128)S(1)} %constant_dynamic-update-slice_fusion.mid), channel_id=1, source_target_pairs={{0,1},{2,3},{4,5},{6,7},{1,0},{3,2},{5,4},{7,6},{8,9},{10,11},{12,... | collective-permute-start | bytes 196616 | tf_op jit(solution)/shard_map/ppermute | solution.py:885
  107.3 3.1 %collective-permute-start.14 = (f32[8,128]{1,0:T(8,128)S(1)}, f32[8,128]{1,0:T(8,128)S(1)}, u32[]{:S(2)}, u32[]{:S(2)}) collective-permute-start(f32[8,128]{1,0:T(8,128)S(1)} %get-tuple-element.44), channel_id=1, source_target_pairs={{0,1},{2,3},{4,5},{6,7},{1,0},{3,2},{5,4},{7,6},{8,9},{10,11},{12,... | collective-permute-start | bytes 12296 | tf_op jit(solution)/shard_map/ppermute | solution.py:885
  128.5 7.9 %collective-permute-start.15 = (f32[32,16,128]{2,1,0:T(8,128)S(1)}, f32[32,16,128]{2,1,0:T(8,128)S(1)}, u32[]{:S(2)}, u32[]{:S(2)}) collective-permute-start(f32[32,16,128]{2,1,0:T(8,128)S(1)} %all_to_all.11.fetched), channel_id=1, source_target_pairs={{0,1},{2,3},{4,5},{6,7},{1,0},{3,2},{5,4},{7,6},{8,9},{10,11},{12,... | collective-permute-start | bytes 786440 | tf_op jit(solution)/shard_map/ppermute | solution.py:885

commit v10 on v9

--- a/solution.py
+++ b/solution.py
@@ -330,24 +330,34 @@
     )
 
 
-def xz_change(v, u, w, marks, out):
+def xz_change(v, u, w, marks, out, known=None):
     x_marks(v, 26, marks)
     below = x_flux(-SKIN, v, u, marks)
     for p in range(-SKIN, 16 + SKIN):
         above = x_flux(p + 1, v, u, marks)
-        out[p + SKIN] = (above - below) + z_change(v(p), w(p))
+        along_z = known[p] if known is not None and 0 <= p < 16 else z_change(v(p), w(p))
+        out[p + SKIN] = (above - below) + along_z
         below = above
 
 
-def inner_body(psi, velocity, low, high, out, *marks):
+def inner_z_body(psi, velocity, out):
+    for p in range(16):
+        out[p] = z_change(psi[p], velocity[2, p])
+
+
+def inner_z(psi, velocity):
+    return call(inner_z_body, [(16, 16, 256)], [], [psi, velocity], 8000000)[0]
+
+
+def inner_body(psi, velocity, low, high, known, out, *marks):
     level, speeds = wide_planes(psi, velocity, low, high)
-    xz_change(level, speeds[0], speeds[2], marks, out)
-
-
-def inner(psi, velocity, low, high):
+    xz_change(level, speeds[0], speeds[2], marks, out, known)
+
+
+def inner(psi, velocity, low, high, known):
     block = (16 + 2 * SKIN, 16, 256)
     scratch = [(26, 16, 256)] * 3
-    return call(inner_body, [block], scratch, [psi, velocity, low, high], 8000000)[0]
+    return call(inner_body, [block], scratch, [psi, velocity, low, high, known], 8000000)[0]
 
 
 def advance_body(
@@ -924,10 +934,11 @@
     at = jnp.stack([lax.axis_index("wide"), lax.axis_index("narrow")]).astype(jnp.int32)
     psi, x_low, x_high = prepare(phase, distance, velocity)
     low, high = shifted(x_high, "wide", 1), shifted(x_low, "wide", -1)
+    known = inner_z(psi, velocity)
     link, chip = pack(at, psi, velocity, low, high)
     v_link = swapped(link, 1)
     v_chip = swapped(chip, 0)
-    change = inner(psi, velocity, low, high)
+    change = inner(psi, velocity, low, high, known)
     moved, source, first, final = advance(
         nx, ny, at, psi, velocity, low, high, v_chip, v_link, change
     )

time: 141 us -> 141 us (level)
    pallas_call x8 -> x9, Pallas kernels: 25.1 us -> 25.4 us  [call(): pl.pallas_call(body, out_shape=[jax.ShapeDtypeStruct(s, F32) for s in out...]
where the time goes in v10:
time: 141 us; the launch traced here: 140 us
  starting transfers between devices  46.4 us (33%)
  blocking collectives  39.8 us (28%)
  Pallas kernels  26.7 us (19%)
  waiting for transfers between devices  26.4 us (19%)
    all_to_all x2, blocking collectives, spread_coarse(): lax.all_to_all(pieces, ('wide', 'narrow'), 0, 0, axis_index_groups=groups)  39.8 us
    ppermute x10, starting transfers between devices, swapped(): return lax.ppermute(array, 'narrow', pairs + [(j, i) for i, j in pairs])  33.3 us
    pallas_call x9, Pallas kernels, call(): pl.pallas_call(body, out_shape=[jax.ShapeDtypeStruct(s, F32) for s in out...  25.4 us
    ppermute x6, waiting for transfers between devices, shifted(): lax.ppermute(array, axis, [(i, i + step) for i in range(count) if 0 <= i...  15.8 us
    ppermute x6, starting transfers between devices, shifted(): lax.ppermute(array, axis, [(i, i + step) for i in range(count) if 0 <= i...  13.2 us
    ppermute x10, waiting for transfers between devices, swapped(): return lax.ppermute(array, 'narrow', pairs + [(j, i) for i, j in pairs])  10.6 us
  transfers between devices with their start and end apart: 16, of which 12 were waited for; matrix products, arithmetic and copies ran while one was open for 0% of the time, Pallas kernels for 2%

profile of v10, /device:TPU:1, one launch (start us, length us, event | category | flops | bytes accessed | tf_op | source)
XLA Modules:
  0.0 140.3 jit_solution(12850108669282468630)
XLA Ops:
  0.6 0.0 copy-start
  0.6 1.3 shard_map.50
  2.0 4.0 %collective-permute-start = (f32[16,16,256]{2,1,0:T(8,128)S(1)}, f32[16,16,256]{2,1,0:T(8,128)S(1)}, u32[]{:S(2)}, u32[]{:S(2)}) collective-permute-start(f32[16,16,256]{2,1,0:T(8,128)S(1)} %get-tuple-element.26), channel_id=1, source_target_pairs={{0,8},{8,16},{16,24},{24,32},{32,40},{40,48},{48,56},{56,64},{64,7... | collective-permute-start | bytes 786440 | tf_op jit(solution)/shard_map/ppermute | solution.py:887
  5.9 1.3 collective-permute-start.1
  7.2 0.1 pad_add_fusion.at
  7.3 1.9 %collective-permute-done.low = f32[16,16,256]{2,1,0:T(8,128)S(1)} collective-permute-done((f32[16,16,256]{2,1,0:T(8,128)S(1)}, f32[16,16,256]{2,1,0:T(8,128)S(1)}, u32[]{:S(2)}, u32[]{:S(2)}) %collective-permute-start) | collective-permute-done | bytes 262176 | tf_op jit(solution)/shard_map/ppermute | solution.py:887
  9.2 3.8 %collective-permute-done.1.high = f32[16,16,256]{2,1,0:T(8,128)S(1)} collective-permute-done((f32[16,16,256]{2,1,0:T(8,128)S(1)}, f32[16,16,256]{2,1,0:T(8,128)S(1)}, u32[]{:S(2)}, u32[]{:S(2)}) %collective-permute-start.1) | collective-permute-done | bytes 262176 | tf_op jit(solution)/shard_map/ppermute | solution.py:887
  13.1 0.0 copy-done
  13.1 0.6 shard_map.51
  13.7 6.6 %collective-permute-start.2 = (f32[20,16,256]{2,1,0:T(8,128)S(1)}, f32[20,16,256]{2,1,0:T(8,128)S(1)}, u32[]{:S(2)}, u32[]{:S(2)}) collective-permute-start(f32[20,16,256]{2,1,0:T(8,128)S(1)} %get-tuple-element.28), channel_id=1, source_target_pairs={{1,2},{3,4},{5,6},{2,1},{4,3},{6,5},{9,10},{11,12},{13,14},{10,9},... | collective-permute-start | bytes 983048 | tf_op jit(solution)/shard_map/ppermute | solution.py:895
  20.3 1.9 %collective-permute-start.3 = (f32[20,16,256]{2,1,0:T(8,128)S(1)}, f32[20,16,256]{2,1,0:T(8,128)S(1)}, u32[]{:S(2)}, u32[]{:S(2)}) collective-permute-start(f32[20,16,256]{2,1,0:T(8,128)S(1)} %get-tuple-element.29), channel_id=1, source_target_pairs={{0,1},{2,3},{4,5},{6,7},{1,0},{3,2},{5,4},{7,6},{8,9},{10,11},{12,... | collective-permute-start | bytes 983048 | tf_op jit(solution)/shard_map/ppermute | solution.py:895
  22.2 1.9 %shard_map.52.known = f32[16,16,256]{2,1,0:T(8,128)S(1)} custom-call(f32[16,16,256]{2,1,0:T(8,128)S(1)} %get-tuple-element.25.psi, f32[3,16,16,256]{3,2,1,0:T(8,128)S(1)} %copy-done), custom_call_target="tpu_custom_call" | custom-call | flops 8000000 | bytes 4000000 | tf_op jit(solution)/shard_map/pallas_call | solution.py:91
  24.1 1.3 shard_map.53.change_in
  25.5 0.0 collective-permute-done.2.link
  25.5 0.0 collective-permute-done.3.chip
  25.5 7.3 %shard_map.54 = (f32[16,16,256]{2,1,0:T(8,128)}, f32[16,16,256]{2,1,0:T(8,128)S(1)}, f32[14,16,256]{2,1,0:T(8,128)S(1)}, f32[14,16,256]{2,1,0:T(8,128)S(1)}) custom-call(s32[2]{0:T(128)S(1)} %pad_add_fusion.at, f32[16,16,256]{2,1,0:T(8,128)S(1)} %get-tuple-element.25.psi, f32[3,16,16,256]{3,2,1,0:T(8,128)S(1)} %copy-done, ...), custom_call_target="tpu_custom_call" | custom-call | flops 30000000 | bytes 4000000 | tf_op jit(solution)/shard_map/pallas_call | solution.py:91
  32.7 3.1 %collective-permute-start.4 = (f32[14,16,256]{2,1,0:T(8,128)S(1)}, f32[14,16,256]{2,1,0:T(8,128)S(1)}, u32[]{:S(2)}, u32[]{:S(2)}) collective-permute-start(f32[14,16,256]{2,1,0:T(8,128)S(1)} %get-tuple-element.32), channel_id=1, source_target_pairs={{0,8},{8,16},{16,24},{24,32},{32,40},{40,48},{48,56},{56,64},{64,7... | collective-permute-start | bytes 688136 | tf_op jit(solution)/shard_map/ppermute | solution.py:887
  35.8 1.3 collective-permute-start.5
  37.1 3.1 %collective-permute-done.4.low = f32[14,16,256]{2,1,0:T(8,128)S(1)} collective-permute-done((f32[14,16,256]{2,1,0:T(8,128)S(1)}, f32[14,16,256]{2,1,0:T(8,128)S(1)}, u32[]{:S(2)}, u32[]{:S(2)}) %collective-permute-start.4) | collective-permute-done | bytes 229408 | tf_op jit(solution)/shard_map/ppermute | solution.py:887
  40.3 3.8 %collective-permute-done.5.high = f32[14,16,256]{2,1,0:T(8,128)S(1)} collective-permute-done((f32[14,16,256]{2,1,0:T(8,128)S(1)}, f32[14,16,256]{2,1,0:T(8,128)S(1)}, u32[]{:S(2)}, u32[]{:S(2)}) %collective-permute-start.5) | collective-permute-done | bytes 229408 | tf_op jit(solution)/shard_map/ppermute | solution.py:887
  44.1 0.6 shard_map.55
  44.7 4.8 %collective-permute-start.6 = (f32[62,8,256]{2,1,0:T(8,128)S(1)}, f32[62,8,256]{2,1,0:T(8,128)S(1)}, u32[]{:S(2)}, u32[]{:S(2)}) collective-permute-start(f32[62,8,256]{2,1,0:T(8,128)S(1)} %get-tuple-element.34), channel_id=1, source_target_pairs={{1,2},{3,4},{5,6},{2,1},{4,3},{6,5},{9,10},{11,12},{13,14},{10,9},... | collective-permute-start | bytes 1523720 | tf_op jit(solution)/shard_map/ppermute | solution.py:895
  49.5 2.1 %collective-permute-start.7 = (f32[62,8,256]{2,1,0:T(8,128)S(1)}, f32[62,8,256]{2,1,0:T(8,128)S(1)}, u32[]{:S(2)}, u32[]{:S(2)}) collective-permute-start(f32[62,8,256]{2,1,0:T(8,128)S(1)} %get-tuple-element.35), channel_id=1, source_target_pairs={{0,1},{2,3},{4,5},{6,7},{1,0},{3,2},{5,4},{7,6},{8,9},{10,11},{12,... | collective-permute-start | bytes 1523720 | tf_op jit(solution)/shard_map/ppermute | solution.py:895
  51.6 4.6 %collective-permute-done.6.link = f32[62,8,256]{2,1,0:T(8,128)S(1)} collective-permute-done((f32[62,8,256]{2,1,0:T(8,128)S(1)}, f32[62,8,256]{2,1,0:T(8,128)S(1)}, u32[]{:S(2)}, u32[]{:S(2)}) %collective-permute-start.6) | collective-permute-done | bytes 507936 | tf_op jit(solution)/shard_map/ppermute | solution.py:895
  56.2 0.0 collective-permute-done.7.chip
  56.2 3.8 %shard_map.56 = (f32[26,32,256]{2,1,0:T(8,128)S(1)}, f32[28,32,256]{2,1,0:T(8,128)S(1)}, f32[20,24,128]{2,1,0:T(8,128)S(1)}, f32[18,24,128]{2,1,0:T(8,128)S(1)}, f32[8,128]{1,0:T(8,128)S(1)}) custom-call(s32[2]{0:T(128)S(1)} %pad_add_fusion.at, f32[16,16,256]{2,1,0:T(8,128)S(1)} %get-tuple-element.31.own, f32[14,16,256]{2,1,0:T(8,128)S(1)} %collective-permute-done.4.low, ...), custom_call_target="tpu_custom_call" | custom-call | flops 20000000 | bytes 4000000 | tf_op jit(solution)/shard_map/pallas_call | solution.py:91
  60.0 1.9 %collective-permute-start.8 = (f32[8,128]{1,0:T(8,128)S(1)}, f32[8,128]{1,0:T(8,128)S(1)}, u32[]{:S(2)}, u32[]{:S(2)}) collective-permute-start(f32[8,128]{1,0:T(8,128)S(1)} %get-tuple-element.36), channel_id=1, source_target_pairs={{0,1},{2,3},{4,5},{6,7},{1,0},{3,2},{5,4},{7,6},{8,9},{10,11},{12,... | collective-permute-start | bytes 12296 | tf_op jit(solution)/shard_map/ppermute | solution.py:895
  62.0 1.1 collective-permute-done.8
  63.1 21.7 %all_to_all.10.fetched = f32[32,16,128]{2,1,0:T(8,128)S(1)} all-to-all(f32[32,16,128]{2,1,0:T(8,128)S(1)} %broadcast_in_dim.4), channel_id=1, replica_groups={{0,2,4,6,8,10,12,14,16,18,20,22,24,26,28,30,32,34,36,38,40,42,44,46,48,..., dimensions={0} | all-to-all | bytes 524288 | tf_op jit(solution)/shard_map/all_to_all | solution.py:928
  84.8 1.9 %collective-permute-start.9 = (f32[32,16,128]{2,1,0:T(8,128)S(1)}, f32[32,16,128]{2,1,0:T(8,128)S(1)}, u32[]{:S(2)}, u32[]{:S(2)}) collective-permute-start(f32[32,16,128]{2,1,0:T(8,128)S(1)} %all_to_all.10.fetched), channel_id=1, source_target_pairs={{0,1},{2,3},{4,5},{6,7},{1,0},{3,2},{5,4},{7,6},{8,9},{10,11},{12,... | collective-permute-start | bytes 786440 | tf_op jit(solution)/shard_map/ppermute | solution.py:895
  86.7 1.5 %collective-permute-done.9.other = f32[32,16,128]{2,1,0:T(8,128)S(1)} collective-permute-done((f32[32,16,128]{2,1,0:T(8,128)S(1)}, f32[32,16,128]{2,1,0:T(8,128)S(1)}, u32[]{:S(2)}, u32[]{:S(2)}) %collective-permute-start.9) | collective-permute-done | bytes 262176 | tf_op jit(solution)/shard_map/ppermute | solution.py:895
  88.2 5.1 %shard_map.57 = (f32[20,32,256]{2,1,0:T(8,128)S(1)}, f32[16,8,128]{2,1,0:T(8,128)S(1)}, f32[4,8,128]{2,1,0:T(8,128)S(1)}, f32[4,8,128]{2,1,0:T(8,128)S(1)}) custom-call(s32[2]{0:T(128)S(1)} %pad_add_fusion.at, f32[32,16,128]{2,1,0:T(8,128)S(1)} %all_to_all.10.fetched, f32[32,16,128]{2,1,0:T(8,128)S(1)} %collective-permute-done.9.other, ...), custom_call_target="tpu_custom_call" | custom-call | flops 30000000 | bytes 4000000 | tf_op jit(solution)/shard_map/pallas_call | solution.py:91
  93.3 2.2 %collective-permute-start.10 = (f32[4,8,128]{2,1,0:T(8,128)S(1)}, f32[4,8,128]{2,1,0:T(8,128)S(1)}, u32[]{:S(2)}, u32[]{:S(2)}) collective-permute-start(f32[4,8,128]{2,1,0:T(8,128)S(1)} %get-tuple-element.42), channel_id=1, source_target_pairs={{0,8},{8,16},{16,24},{24,32},{32,40},{40,48},{48,56},{56,64},{64,7... | collective-permute-start | bytes 49160 | tf_op jit(solution)/shard_map/ppermute | solution.py:887
  95.6 1.3 collective-permute-start.11
  96.9 0.0 collective-permute-done.10
  96.9 3.2 %collective-permute-done.11 = f32[4,8,128]{2,1,0:T(8,128)S(1)} collective-permute-done((f32[4,8,128]{2,1,0:T(8,128)S(1)}, f32[4,8,128]{2,1,0:T(8,128)S(1)}, u32[]{:S(2)}, u32[]{:S(2)}) %collective-permute-start.11) | collective-permute-done | bytes 16416 | tf_op jit(solution)/shard_map/ppermute | solution.py:887
  100.0 3.3 %collective-permute-start.13 = (f32[16,8,128]{2,1,0:T(8,128)S(1)}, f32[16,8,128]{2,1,0:T(8,128)S(1)}, u32[]{:S(2)}, u32[]{:S(2)}) collective-permute-start(f32[16,8,128]{2,1,0:T(8,128)S(1)} %constant_dynamic-update-slice_fusion.mid), channel_id=1, source_target_pairs={{1,2},{3,4},{5,6},{2,1},{4,3},{6,5},{9,10},{11,12},{13,14},{10,9},... | collective-permute-start | bytes 196616 | tf_op jit(solution)/shard_map/ppermute | solution.py:895
  103.4 1.9 %collective-permute-start.12 = (f32[16,8,128]{2,1,0:T(8,128)S(1)}, f32[16,8,128]{2,1,0:T(8,128)S(1)}, u32[]{:S(2)}, u32[]{:S(2)}) collective-permute-start(f32[16,8,128]{2,1,0:T(8,128)S(1)} %constant_dynamic-update-slice_fusion.mid), channel_id=1, source_target_pairs={{0,1},{2,3},{4,5},{6,7},{1,0},{3,2},{5,4},{7,6},{8,9},{10,11},{12,... | collective-permute-start | bytes 196616 | tf_op jit(solution)/shard_map/ppermute | solution.py:895
  105.3 0.3 collective-permute-done.13.link
  105.6 0.9 collective-permute-done.12.chip
  106.5 0.9 shard_map.58
  107.4 2.1 %collective-permute-start.14 = (f32[8,128]{1,0:T(8,128)S(1)}, f32[8,128]{1,0:T(8,128)S(1)}, u32[]{:S(2)}, u32[]{:S(2)}) collective-permute-start(f32[8,128]{1,0:T(8,128)S(1)} %get-tuple-element.44), channel_id=1, source_target_pairs={{0,1},{2,3},{4,5},{6,7},{1,0},{3,2},{5,4},{7,6},{8,9},{10,11},{12,... | collective-permute-start | bytes 12296 | tf_op jit(solution)/shard_map/ppermute | solution.py:895
  109.5 1.0 collective-permute-done.14
  110.5 18.1 %all_to_all.11.fetched = f32[32,16,128]{2,1,0:T(8,128)S(1)} all-to-all(f32[32,16,128]{2,1,0:T(8,128)S(1)} %broadcast_in_dim.5), channel_id=1, replica_groups={{0,2,4,6,8,10,12,14,16,18,20,22,24,26,28,30,32,34,36,38,40,42,44,46,48,..., dimensions={0} | all-to-all | bytes 524288 | tf_op jit(solution)/shard_map/all_to_all | solution.py:928
  128.6 6.7 %collective-permute-start.15 = (f32[32,16,128]{2,1,0:T(8,128)S(1)}, f32[32,16,128]{2,1,0:T(8,128)S(1)}, u32[]{:S(2)}, u32[]{:S(2)}) collective-permute-start(f32[32,16,128]{2,1,0:T(8,128)S(1)} %all_to_all.11.fetched), channel_id=1, source_target_pairs={{0,1},{2,3},{4,5},{6,7},{1,0},{3,2},{5,4},{7,6},{8,9},{10,11},{12,... | collective-permute-start | bytes 786440 | tf_op jit(solution)/shard_map/ppermute | solution.py:895
  135.4 1.1 collective-permute-done.15.other
  136.5 3.8 %shard_map.59 = f32[16,16,256]{2,1,0:T(8,128)} custom-call(s32[2]{0:T(128)S(1)} %pad_add_fusion.at, f32[32,16,128]{2,1,0:T(8,128)S(1)} %all_to_all.11.fetched, f32[32,16,128]{2,1,0:T(8,128)S(1)} %collective-permute-done.15.other, f32[16,24,128]{2,1,0:T(8,128)S(1)} %get-tuple-element.45.b1, f32[14,24,128]{2,1,0:T(8,128)S(1)} %get-tuple-element.46.u, ...), custom_call_target="tpu_custom_call" | custom-call | flops 20000000 | bytes 4000000 | tf_op jit(solution)/shard_map/pallas_call | solution.py:91
  (8 shorter events, 0.1 us)
Async XLA Ops:
  0.6 12.4 %copy-start = (f32[3,16,16,256]{3,2,1,0:T(8,128)S(1)}, f32[3,16,16,256]{3,2,1,0:T(8,128)}, u32[]{:S(2)}) copy-start(f32[3,16,16,256]{3,2,1,0:T(8,128)} %velocity.9) | copy-start | bytes 2359300
  2.0 7.3 %collective-permute-start = (f32[16,16,256]{2,1,0:T(8,128)S(1)}, f32[16,16,256]{2,1,0:T(8,128)S(1)}, u32[]{:S(2)}, u32[]{:S(2)}) collective-permute-start(f32[16,16,256]{2,1,0:T(8,128)S(1)} %get-tuple-element.26), channel_id=1, source_target_pairs={{0,8},{8,16},{16,24},{24,32},{32,40},{40,48},{48,56},{56,64},{64,7... | collective-permute-start | bytes 786440 | tf_op jit(solution)/shard_map/ppermute | solution.py:887
  5.9 7.1 %collective-permute-start.1 = (f32[16,16,256]{2,1,0:T(8,128)S(1)}, f32[16,16,256]{2,1,0:T(8,128)S(1)}, u32[]{:S(2)}, u32[]{:S(2)}) collective-permute-start(f32[16,16,256]{2,1,0:T(8,128)S(1)} %get-tuple-element.27), channel_id=1, source_target_pairs={{8,0},{16,8},{24,16},{32,24},{40,32},{48,40},{56,48},{64,56},{72,6... | collective-permute-start | bytes 786440 | tf_op jit(solution)/shard_map/ppermute | solution.py:887
  13.7 11.7 %collective-permute-start.2 = (f32[20,16,256]{2,1,0:T(8,128)S(1)}, f32[20,16,256]{2,1,0:T(8,128)S(1)}, u32[]{:S(2)}, u32[]{:S(2)}) collective-permute-start(f32[20,16,256]{2,1,0:T(8,128)S(1)} %get-tuple-element.28), channel_id=1, source_target_pairs={{1,2},{3,4},{5,6},{2,1},{4,3},{6,5},{9,10},{11,12},{13,14},{10,9},... | collective-permute-start | bytes 983048 | tf_op jit(solution)/shard_map/ppermute | solution.py:895
  20.3 5.2 %collective-permute-start.3 = (f32[20,16,256]{2,1,0:T(8,128)S(1)}, f32[20,16,256]{2,1,0:T(8,128)S(1)}, u32[]{:S(2)}, u32[]{:S(2)}) collective-permute-start(f32[20,16,256]{2,1,0:T(8,128)S(1)} %get-tuple-element.29), channel_id=1, source_target_pairs={{0,1},{2,3},{4,5},{6,7},{1,0},{3,2},{5,4},{7,6},{8,9},{10,11},{12,... | collective-permute-start | bytes 983048 | tf_op jit(solution)/shard_map/ppermute | solution.py:895
  32.7 7.6 %collective-permute-start.4 = (f32[14,16,256]{2,1,0:T(8,128)S(1)}, f32[14,16,256]{2,1,0:T(8,128)S(1)}, u32[]{:S(2)}, u32[]{:S(2)}) collective-permute-start(f32[14,16,256]{2,1,0:T(8,128)S(1)} %get-tuple-element.32), channel_id=1, source_target_pairs={{0,8},{8,16},{16,24},{24,32},{32,40},{40,48},{48,56},{56,64},{64,7... | collective-permute-start | bytes 688136 | tf_op jit(solution)/shard_map/ppermute | solution.py:887
  35.8 8.2 %collective-permute-start.5 = (f32[14,16,256]{2,1,0:T(8,128)S(1)}, f32[14,16,256]{2,1,0:T(8,128)S(1)}, u32[]{:S(2)}, u32[]{:S(2)}) collective-permute-start(f32[14,16,256]{2,1,0:T(8,128)S(1)} %get-tuple-element.33), channel_id=1, source_target_pairs={{8,0},{16,8},{24,16},{32,24},{40,32},{48,40},{56,48},{64,56},{72,6... | collective-permute-start | bytes 688136 | tf_op jit(solution)/shard_map/ppermute | solution.py:887
  44.7 11.4 %collective-permute-start.6 = (f32[62,8,256]{2,1,0:T(8,128)S(1)}, f32[62,8,256]{2,1,0:T(8,128)S(1)}, u32[]{:S(2)}, u32[]{:S(2)}) collective-permute-start(f32[62,8,256]{2,1,0:T(8,128)S(1)} %get-tuple-element.34), channel_id=1, source_target_pairs={{1,2},{3,4},{5,6},{2,1},{4,3},{6,5},{9,10},{11,12},{13,14},{10,9},... | collective-permute-start | bytes 1523720 | tf_op jit(solution)/shard_map/ppermute | solution.py:895
  49.5 6.7 %collective-permute-start.7 = (f32[62,8,256]{2,1,0:T(8,128)S(1)}, f32[62,8,256]{2,1,0:T(8,128)S(1)}, u32[]{:S(2)}, u32[]{:S(2)}) collective-permute-start(f32[62,8,256]{2,1,0:T(8,128)S(1)} %get-tuple-element.35), channel_id=1, source_target_pairs={{0,1},{2,3},{4,5},{6,7},{1,0},{3,2},{5,4},{7,6},{8,9},{10,11},{12,... | collective-permute-start | bytes 1523720 | tf_op jit(solution)/shard_map/ppermute | solution.py:895
  60.0 3.1 %collective-permute-start.8 = (f32[8,128]{1,0:T(8,128)S(1)}, f32[8,128]{1,0:T(8,128)S(1)}, u32[]{:S(2)}, u32[]{:S(2)}) collective-permute-start(f32[8,128]{1,0:T(8,128)S(1)} %get-tuple-element.36), channel_id=1, source_target_pairs={{0,1},{2,3},{4,5},{6,7},{1,0},{3,2},{5,4},{7,6},{8,9},{10,11},{12,... | collective-permute-start | bytes 12296 | tf_op jit(solution)/shard_map/ppermute | solution.py:895
  84.8 3.4 %collective-permute-start.9 = (f32[32,16,128]{2,1,0:T(8,128)S(1)}, f32[32,16,128]{2,1,0:T(8,128)S(1)}, u32[]{:S(2)}, u32[]{:S(2)}) collective-permute-start(f32[32,16,128]{2,1,0:T(8,128)S(1)} %all_to_all.10.fetched), channel_id=1, source_target_pairs={{0,1},{2,3},{4,5},{6,7},{1,0},{3,2},{5,4},{7,6},{8,9},{10,11},{12,... | collective-permute-start | bytes 786440 | tf_op jit(solution)/shard_map/ppermute | solution.py:895
  93.3 3.5 %collective-permute-start.10 = (f32[4,8,128]{2,1,0:T(8,128)S(1)}, f32[4,8,128]{2,1,0:T(8,128)S(1)}, u32[]{:S(2)}, u32[]{:S(2)}) collective-permute-start(f32[4,8,128]{2,1,0:T(8,128)S(1)} %get-tuple-element.42), channel_id=1, source_target_pairs={{0,8},{8,16},{16,24},{24,32},{32,40},{40,48},{48,56},{56,64},{64,7... | collective-permute-start | bytes 49160 | tf_op jit(solution)/shard_map/ppermute | solution.py:887
  95.6 4.5 %collective-permute-start.11 = (f32[4,8,128]{2,1,0:T(8,128)S(1)}, f32[4,8,128]{2,1,0:T(8,128)S(1)}, u32[]{:S(2)}, u32[]{:S(2)}) collective-permute-start(f32[4,8,128]{2,1,0:T(8,128)S(1)} %get-tuple-element.43), channel_id=1, source_target_pairs={{8,0},{16,8},{24,16},{32,24},{40,32},{48,40},{56,48},{64,56},{72,6... | collective-permute-start | bytes 49160 | tf_op jit(solution)/shard_map/ppermute | solution.py:887
  100.0 5.6 %collective-permute-start.13 = (f32[16,8,128]{2,1,0:T(8,128)S(1)}, f32[16,8,128]{2,1,0:T(8,128)S(1)}, u32[]{:S(2)}, u32[]{:S(2)}) collective-permute-start(f32[16,8,128]{2,1,0:T(8,128)S(1)} %constant_dynamic-update-slice_fusion.mid), channel_id=1, source_target_pairs={{1,2},{3,4},{5,6},{2,1},{4,3},{6,5},{9,10},{11,12},{13,14},{10,9},... | collective-permute-start | bytes 196616 | tf_op jit(solution)/shard_map/ppermute | solution.py:895
  103.4 3.1 %collective-permute-start.12 = (f32[16,8,128]{2,1,0:T(8,128)S(1)}, f32[16,8,128]{2,1,0:T(8,128)S(1)}, u32[]{:S(2)}, u32[]{:S(2)}) collective-permute-start(f32[16,8,128]{2,1,0:T(8,128)S(1)} %constant_dynamic-update-slice_fusion.mid), channel_id=1, source_target_pairs={{0,1},{2,3},{4,5},{6,7},{1,0},{3,2},{5,4},{7,6},{8,9},{10,11},{12,... | collective-permute-start | bytes 196616 | tf_op jit(solution)/shard_map/ppermute | solution.py:895
  107.4 3.1 %collective-permute-start.14 = (f32[8,128]{1,0:T(8,128)S(1)}, f32[8,128]{1,0:T(8,128)S(1)}, u32[]{:S(2)}, u32[]{:S(2)}) collective-permute-start(f32[8,128]{1,0:T(8,128)S(1)} %get-tuple-element.44), channel_id=1, source_target_pairs={{0,1},{2,3},{4,5},{6,7},{1,0},{3,2},{5,4},{7,6},{8,9},{10,11},{12,... | collective-permute-start | bytes 12296 | tf_op jit(solution)/shard_map/ppermute | solution.py:895
  128.6 7.9 %collective-permute-start.15 = (f32[32,16,128]{2,1,0:T(8,128)S(1)}, f32[32,16,128]{2,1,0:T(8,128)S(1)}, u32[]{:S(2)}, u32[]{:S(2)}) collective-permute-start(f32[32,16,128]{2,1,0:T(8,128)S(1)} %all_to_all.11.fetched), channel_id=1, source_target_pairs={{0,1},{2,3},{4,5},{6,7},{1,0},{3,2},{5,4},{7,6},{8,9},{10,11},{12,... | collective-permute-start | bytes 786440 | tf_op jit(solution)/shard_map/ppermute | solution.py:895

commit v11 on v10

--- a/solution.py
+++ b/solution.py
@@ -217,7 +217,7 @@
 SLOTS = 20
 
 
-def pack_body(at, psi, velocity, low, high, link, chip):
+def pack_body(at, psi, velocity, low, high, known, link, chip):
     odd = lax.rem(at[1], 2) == 1
     level, speeds = wide_planes(psi, velocity, low, high)
     fields = [level] + speeds
@@ -238,9 +238,9 @@
         link[k] = jnp.where(odd, final, first)
 
 
-def pack(at, psi, velocity, low, high):
+def pack(at, psi, velocity, low, high, known):
     outs = [(SLOTS, SENT, 256)] * 2
-    return call(pack_body, outs, [], [at, psi, velocity, low, high], 1000000)
+    return call(pack_body, outs, [], [at, psi, velocity, low, high, known], 1000000)
 
 
 FACE = 0.25 / 12.0
@@ -935,7 +935,7 @@
     psi, x_low, x_high = prepare(phase, distance, velocity)
     low, high = shifted(x_high, "wide", 1), shifted(x_low, "wide", -1)
     known = inner_z(psi, velocity)
-    link, chip = pack(at, psi, velocity, low, high)
+    link, chip = pack(at, psi, velocity, low, high, known)
     v_link = swapped(link, 1)
     v_chip = swapped(chip, 0)
     change = inner(psi, velocity, low, high, known)

time: 141 us -> 141 us (level)
    ppermute x10, waiting for transfers between devices: 10.6 us -> 12 us  [swapped(): return lax.ppermute(array, 'narrow', pairs + [(j, i) for i, j in pairs])]
where the time goes in v11:
time: 141 us; the launch traced here: 140 us
  starting transfers between devices  45.8 us (32%)
  blocking collectives  39.9 us (28%)
  waiting for transfers between devices  26.8 us (19%)
  Pallas kernels  26.7 us (19%)
    all_to_all x2, blocking collectives, spread_coarse(): lax.all_to_all(pieces, ('wide', 'narrow'), 0, 0, axis_index_groups=groups)  39.9 us
    ppermute x10, starting transfers between devices, swapped(): return lax.ppermute(array, 'narrow', pairs + [(j, i) for i, j in pairs])  32.6 us
    pallas_call x9, Pallas kernels, call(): pl.pallas_call(body, out_shape=[jax.ShapeDtypeStruct(s, F32) for s in out...  25.4 us
    ppermute x6, waiting for transfers between devices, shifted(): lax.ppermute(array, axis, [(i, i + step) for i in range(count) if 0 <= i...  14.7 us
    ppermute x6, starting transfers between devices, shifted(): lax.ppermute(array, axis, [(i, i + step) for i in range(count) if 0 <= i...  13.2 us
    ppermute x10, waiting for transfers between devices, swapped(): return lax.ppermute(array, 'narrow', pairs + [(j, i) for i, j in pairs])  12 us
  transfers between devices with their start and end apart: 16, of which 12 were waited for; matrix products, arithmetic and copies ran while one was open for 0% of the time, Pallas kernels for 2%

profile of v11, /device:TPU:1, one launch (start us, length us, event | category | flops | bytes accessed | tf_op | source)
XLA Modules:
  0.0 140.2 jit_solution(4059721434627499724)
XLA Ops:
  0.6 0.0 copy-start
  0.6 1.3 shard_map.50
  2.0 4.0 %collective-permute-start = (f32[16,16,256]{2,1,0:T(8,128)S(1)}, f32[16,16,256]{2,1,0:T(8,128)S(1)}, u32[]{:S(2)}, u32[]{:S(2)}) collective-permute-start(f32[16,16,256]{2,1,0:T(8,128)S(1)} %get-tuple-element.26), channel_id=1, source_target_pairs={{0,8},{8,16},{16,24},{24,32},{32,40},{40,48},{48,56},{56,64},{64,7... | collective-permute-start | bytes 786440 | tf_op jit(solution)/shard_map/ppermute | solution.py:887
  5.9 1.3 collective-permute-start.1
  7.2 0.0 copy-done
  7.3 1.9 %shard_map.51.known = f32[16,16,256]{2,1,0:T(8,128)S(1)} custom-call(f32[16,16,256]{2,1,0:T(8,128)S(1)} %get-tuple-element.25.psi, f32[3,16,16,256]{3,2,1,0:T(8,128)S(1)} %copy-done), custom_call_target="tpu_custom_call" | custom-call | flops 8000000 | bytes 4000000 | tf_op jit(solution)/shard_map/pallas_call | solution.py:91
  9.2 0.1 pad_add_fusion.at
  9.2 0.0 collective-permute-done.low
  9.2 3.8 %collective-permute-done.1.high = f32[16,16,256]{2,1,0:T(8,128)S(1)} collective-permute-done((f32[16,16,256]{2,1,0:T(8,128)S(1)}, f32[16,16,256]{2,1,0:T(8,128)S(1)}, u32[]{:S(2)}, u32[]{:S(2)}) %collective-permute-start.1) | collective-permute-done | bytes 262176 | tf_op jit(solution)/shard_map/ppermute | solution.py:887
  13.1 0.6 shard_map.52
  13.7 6.6 %collective-permute-start.2 = (f32[20,16,256]{2,1,0:T(8,128)S(1)}, f32[20,16,256]{2,1,0:T(8,128)S(1)}, u32[]{:S(2)}, u32[]{:S(2)}) collective-permute-start(f32[20,16,256]{2,1,0:T(8,128)S(1)} %get-tuple-element.28), channel_id=1, source_target_pairs={{1,2},{3,4},{5,6},{2,1},{4,3},{6,5},{9,10},{11,12},{13,14},{10,9},... | collective-permute-start | bytes 983048 | tf_op jit(solution)/shard_map/ppermute | solution.py:895
  20.3 1.9 %collective-permute-start.3 = (f32[20,16,256]{2,1,0:T(8,128)S(1)}, f32[20,16,256]{2,1,0:T(8,128)S(1)}, u32[]{:S(2)}, u32[]{:S(2)}) collective-permute-start(f32[20,16,256]{2,1,0:T(8,128)S(1)} %get-tuple-element.29), channel_id=1, source_target_pairs={{0,1},{2,3},{4,5},{6,7},{1,0},{3,2},{5,4},{7,6},{8,9},{10,11},{12,... | collective-permute-start | bytes 983048 | tf_op jit(solution)/shard_map/ppermute | solution.py:895
  22.2 1.3 shard_map.53.change_in
  23.5 1.5 %collective-permute-done.2.link = f32[20,16,256]{2,1,0:T(8,128)S(1)} collective-permute-done((f32[20,16,256]{2,1,0:T(8,128)S(1)}, f32[20,16,256]{2,1,0:T(8,128)S(1)}, u32[]{:S(2)}, u32[]{:S(2)}) %collective-permute-start.2) | collective-permute-done | bytes 327712 | tf_op jit(solution)/shard_map/ppermute | solution.py:895
  25.0 0.0 collective-permute-done.3.chip
  25.0 7.3 %shard_map.54 = (f32[16,16,256]{2,1,0:T(8,128)}, f32[16,16,256]{2,1,0:T(8,128)S(1)}, f32[14,16,256]{2,1,0:T(8,128)S(1)}, f32[14,16,256]{2,1,0:T(8,128)S(1)}) custom-call(s32[2]{0:T(128)S(1)} %pad_add_fusion.at, f32[16,16,256]{2,1,0:T(8,128)S(1)} %get-tuple-element.25.psi, f32[3,16,16,256]{3,2,1,0:T(8,128)S(1)} %copy-done, ...), custom_call_target="tpu_custom_call" | custom-call | flops 30000000 | bytes 4000000 | tf_op jit(solution)/shard_map/pallas_call | solution.py:91
  32.3 3.1 %collective-permute-start.4 = (f32[14,16,256]{2,1,0:T(8,128)S(1)}, f32[14,16,256]{2,1,0:T(8,128)S(1)}, u32[]{:S(2)}, u32[]{:S(2)}) collective-permute-start(f32[14,16,256]{2,1,0:T(8,128)S(1)} %get-tuple-element.32), channel_id=1, source_target_pairs={{0,8},{8,16},{16,24},{24,32},{32,40},{40,48},{48,56},{56,64},{64,7... | collective-permute-start | bytes 688136 | tf_op jit(solution)/shard_map/ppermute | solution.py:887
  35.4 1.3 collective-permute-start.5
  36.7 3.6 %collective-permute-done.4.low = f32[14,16,256]{2,1,0:T(8,128)S(1)} collective-permute-done((f32[14,16,256]{2,1,0:T(8,128)S(1)}, f32[14,16,256]{2,1,0:T(8,128)S(1)}, u32[]{:S(2)}, u32[]{:S(2)}) %collective-permute-start.4) | collective-permute-done | bytes 229408 | tf_op jit(solution)/shard_map/ppermute | solution.py:887
  40.3 4.2 %collective-permute-done.5.high = f32[14,16,256]{2,1,0:T(8,128)S(1)} collective-permute-done((f32[14,16,256]{2,1,0:T(8,128)S(1)}, f32[14,16,256]{2,1,0:T(8,128)S(1)}, u32[]{:S(2)}, u32[]{:S(2)}) %collective-permute-start.5) | collective-permute-done | bytes 229408 | tf_op jit(solution)/shard_map/ppermute | solution.py:887
  44.4 0.6 shard_map.55
  45.1 4.1 %collective-permute-start.6 = (f32[62,8,256]{2,1,0:T(8,128)S(1)}, f32[62,8,256]{2,1,0:T(8,128)S(1)}, u32[]{:S(2)}, u32[]{:S(2)}) collective-permute-start(f32[62,8,256]{2,1,0:T(8,128)S(1)} %get-tuple-element.34), channel_id=1, source_target_pairs={{1,2},{3,4},{5,6},{2,1},{4,3},{6,5},{9,10},{11,12},{13,14},{10,9},... | collective-permute-start | bytes 1523720 | tf_op jit(solution)/shard_map/ppermute | solution.py:895
  49.2 2.1 %collective-permute-start.7 = (f32[62,8,256]{2,1,0:T(8,128)S(1)}, f32[62,8,256]{2,1,0:T(8,128)S(1)}, u32[]{:S(2)}, u32[]{:S(2)}) collective-permute-start(f32[62,8,256]{2,1,0:T(8,128)S(1)} %get-tuple-element.35), channel_id=1, source_target_pairs={{0,1},{2,3},{4,5},{6,7},{1,0},{3,2},{5,4},{7,6},{8,9},{10,11},{12,... | collective-permute-start | bytes 1523720 | tf_op jit(solution)/shard_map/ppermute | solution.py:895
  51.3 4.6 %collective-permute-done.6.link = f32[62,8,256]{2,1,0:T(8,128)S(1)} collective-permute-done((f32[62,8,256]{2,1,0:T(8,128)S(1)}, f32[62,8,256]{2,1,0:T(8,128)S(1)}, u32[]{:S(2)}, u32[]{:S(2)}) %collective-permute-start.6) | collective-permute-done | bytes 507936 | tf_op jit(solution)/shard_map/ppermute | solution.py:895
  55.9 0.0 collective-permute-done.7.chip
  55.9 3.8 %shard_map.56 = (f32[26,32,256]{2,1,0:T(8,128)S(1)}, f32[28,32,256]{2,1,0:T(8,128)S(1)}, f32[20,24,128]{2,1,0:T(8,128)S(1)}, f32[18,24,128]{2,1,0:T(8,128)S(1)}, f32[8,128]{1,0:T(8,128)S(1)}) custom-call(s32[2]{0:T(128)S(1)} %pad_add_fusion.at, f32[16,16,256]{2,1,0:T(8,128)S(1)} %get-tuple-element.31.own, f32[14,16,256]{2,1,0:T(8,128)S(1)} %collective-permute-done.4.low, ...), custom_call_target="tpu_custom_call" | custom-call | flops 20000000 | bytes 4000000 | tf_op jit(solution)/shard_map/pallas_call | solution.py:91
  59.8 1.9 %collective-permute-start.8 = (f32[8,128]{1,0:T(8,128)S(1)}, f32[8,128]{1,0:T(8,128)S(1)}, u32[]{:S(2)}, u32[]{:S(2)}) collective-permute-start(f32[8,128]{1,0:T(8,128)S(1)} %get-tuple-element.36), channel_id=1, source_target_pairs={{0,1},{2,3},{4,5},{6,7},{1,0},{3,2},{5,4},{7,6},{8,9},{10,11},{12,... | collective-permute-start | bytes 12296 | tf_op jit(solution)/shard_map/ppermute | solution.py:895
  61.7 1.1 collective-permute-done.8
  62.8 21.8 %all_to_all.10.fetched = f32[32,16,128]{2,1,0:T(8,128)S(1)} all-to-all(f32[32,16,128]{2,1,0:T(8,128)S(1)} %broadcast_in_dim.4), channel_id=1, replica_groups={{0,2,4,6,8,10,12,14,16,18,20,22,24,26,28,30,32,34,36,38,40,42,44,46,48,..., dimensions={0} | all-to-all | bytes 524288 | tf_op jit(solution)/shard_map/all_to_all | solution.py:928
  84.7 1.9 %collective-permute-start.9 = (f32[32,16,128]{2,1,0:T(8,128)S(1)}, f32[32,16,128]{2,1,0:T(8,128)S(1)}, u32[]{:S(2)}, u32[]{:S(2)}) collective-permute-start(f32[32,16,128]{2,1,0:T(8,128)S(1)} %all_to_all.10.fetched), channel_id=1, source_target_pairs={{0,1},{2,3},{4,5},{6,7},{1,0},{3,2},{5,4},{7,6},{8,9},{10,11},{12,... | collective-permute-start | bytes 786440 | tf_op jit(solution)/shard_map/ppermute | solution.py:895
  86.6 1.5 %collective-permute-done.9.other = f32[32,16,128]{2,1,0:T(8,128)S(1)} collective-permute-done((f32[32,16,128]{2,1,0:T(8,128)S(1)}, f32[32,16,128]{2,1,0:T(8,128)S(1)}, u32[]{:S(2)}, u32[]{:S(2)}) %collective-permute-start.9) | collective-permute-done | bytes 262176 | tf_op jit(solution)/shard_map/ppermute | solution.py:895
  88.1 5.1 %shard_map.57 = (f32[20,32,256]{2,1,0:T(8,128)S(1)}, f32[16,8,128]{2,1,0:T(8,128)S(1)}, f32[4,8,128]{2,1,0:T(8,128)S(1)}, f32[4,8,128]{2,1,0:T(8,128)S(1)}) custom-call(s32[2]{0:T(128)S(1)} %pad_add_fusion.at, f32[32,16,128]{2,1,0:T(8,128)S(1)} %all_to_all.10.fetched, f32[32,16,128]{2,1,0:T(8,128)S(1)} %collective-permute-done.9.other, ...), custom_call_target="tpu_custom_call" | custom-call | flops 30000000 | bytes 4000000 | tf_op jit(solution)/shard_map/pallas_call | solution.py:91
  93.2 2.2 %collective-permute-start.10 = (f32[4,8,128]{2,1,0:T(8,128)S(1)}, f32[4,8,128]{2,1,0:T(8,128)S(1)}, u32[]{:S(2)}, u32[]{:S(2)}) collective-permute-start(f32[4,8,128]{2,1,0:T(8,128)S(1)} %get-tuple-element.42), channel_id=1, source_target_pairs={{0,8},{8,16},{16,24},{24,32},{32,40},{40,48},{48,56},{56,64},{64,7... | collective-permute-start | bytes 49160 | tf_op jit(solution)/shard_map/ppermute | solution.py:887
  95.4 1.3 collective-permute-start.11
  96.7 0.0 collective-permute-done.10
  96.7 3.2 %collective-permute-done.11 = f32[4,8,128]{2,1,0:T(8,128)S(1)} collective-permute-done((f32[4,8,128]{2,1,0:T(8,128)S(1)}, f32[4,8,128]{2,1,0:T(8,128)S(1)}, u32[]{:S(2)}, u32[]{:S(2)}) %collective-permute-start.11) | collective-permute-done | bytes 16416 | tf_op jit(solution)/shard_map/ppermute | solution.py:887
  99.9 3.3 %collective-permute-start.13 = (f32[16,8,128]{2,1,0:T(8,128)S(1)}, f32[16,8,128]{2,1,0:T(8,128)S(1)}, u32[]{:S(2)}, u32[]{:S(2)}) collective-permute-start(f32[16,8,128]{2,1,0:T(8,128)S(1)} %constant_dynamic-update-slice_fusion.mid), channel_id=1, source_target_pairs={{1,2},{3,4},{5,6},{2,1},{4,3},{6,5},{9,10},{11,12},{13,14},{10,9},... | collective-permute-start | bytes 196616 | tf_op jit(solution)/shard_map/ppermute | solution.py:895
  103.2 1.9 %collective-permute-start.12 = (f32[16,8,128]{2,1,0:T(8,128)S(1)}, f32[16,8,128]{2,1,0:T(8,128)S(1)}, u32[]{:S(2)}, u32[]{:S(2)}) collective-permute-start(f32[16,8,128]{2,1,0:T(8,128)S(1)} %constant_dynamic-update-slice_fusion.mid), channel_id=1, source_target_pairs={{0,1},{2,3},{4,5},{6,7},{1,0},{3,2},{5,4},{7,6},{8,9},{10,11},{12,... | collective-permute-start | bytes 196616 | tf_op jit(solution)/shard_map/ppermute | solution.py:895
  105.2 0.3 collective-permute-done.13.link
  105.5 0.9 collective-permute-done.12.chip
  106.4 0.9 shard_map.58
  107.3 2.1 %collective-permute-start.14 = (f32[8,128]{1,0:T(8,128)S(1)}, f32[8,128]{1,0:T(8,128)S(1)}, u32[]{:S(2)}, u32[]{:S(2)}) collective-permute-start(f32[8,128]{1,0:T(8,128)S(1)} %get-tuple-element.44), channel_id=1, source_target_pairs={{0,1},{2,3},{4,5},{6,7},{1,0},{3,2},{5,4},{7,6},{8,9},{10,11},{12,... | collective-permute-start | bytes 12296 | tf_op jit(solution)/shard_map/ppermute | solution.py:895
  109.4 1.0 collective-permute-done.14
  110.4 18.1 %all_to_all.11.fetched = f32[32,16,128]{2,1,0:T(8,128)S(1)} all-to-all(f32[32,16,128]{2,1,0:T(8,128)S(1)} %broadcast_in_dim.5), channel_id=1, replica_groups={{0,2,4,6,8,10,12,14,16,18,20,22,24,26,28,30,32,34,36,38,40,42,44,46,48,..., dimensions={0} | all-to-all | bytes 524288 | tf_op jit(solution)/shard_map/all_to_all | solution.py:928
  128.5 6.7 %collective-permute-start.15 = (f32[32,16,128]{2,1,0:T(8,128)S(1)}, f32[32,16,128]{2,1,0:T(8,128)S(1)}, u32[]{:S(2)}, u32[]{:S(2)}) collective-permute-start(f32[32,16,128]{2,1,0:T(8,128)S(1)} %all_to_all.11.fetched), channel_id=1, source_target_pairs={{0,1},{2,3},{4,5},{6,7},{1,0},{3,2},{5,4},{7,6},{8,9},{10,11},{12,... | collective-permute-start | bytes 786440 | tf_op jit(solution)/shard_map/ppermute | solution.py:895
  135.2 1.1 collective-permute-done.15.other
  136.4 3.8 %shard_map.59 = f32[16,16,256]{2,1,0:T(8,128)} custom-call(s32[2]{0:T(128)S(1)} %pad_add_fusion.at, f32[32,16,128]{2,1,0:T(8,128)S(1)} %all_to_all.11.fetched, f32[32,16,128]{2,1,0:T(8,128)S(1)} %collective-permute-done.15.other, f32[16,24,128]{2,1,0:T(8,128)S(1)} %get-tuple-element.45.b1, f32[14,24,128]{2,1,0:T(8,128)S(1)} %get-tuple-element.46.u, ...), custom_call_target="tpu_custom_call" | custom-call | flops 20000000 | bytes 4000000 | tf_op jit(solution)/shard_map/pallas_call | solution.py:91
  (8 shorter events, 0.1 us)
Async XLA Ops:
  0.6 6.6 %copy-start = (f32[3,16,16,256]{3,2,1,0:T(8,128)S(1)}, f32[3,16,16,256]{3,2,1,0:T(8,128)}, u32[]{:S(2)}) copy-start(f32[3,16,16,256]{3,2,1,0:T(8,128)} %velocity.9) | copy-start | bytes 2359300
  2.0 7.3 %collective-permute-start = (f32[16,16,256]{2,1,0:T(8,128)S(1)}, f32[16,16,256]{2,1,0:T(8,128)S(1)}, u32[]{:S(2)}, u32[]{:S(2)}) collective-permute-start(f32[16,16,256]{2,1,0:T(8,128)S(1)} %get-tuple-element.26), channel_id=1, source_target_pairs={{0,8},{8,16},{16,24},{24,32},{32,40},{40,48},{48,56},{56,64},{64,7... | collective-permute-start | bytes 786440 | tf_op jit(solution)/shard_map/ppermute | solution.py:887
  5.9 7.1 %collective-permute-start.1 = (f32[16,16,256]{2,1,0:T(8,128)S(1)}, f32[16,16,256]{2,1,0:T(8,128)S(1)}, u32[]{:S(2)}, u32[]{:S(2)}) collective-permute-start(f32[16,16,256]{2,1,0:T(8,128)S(1)} %get-tuple-element.27), channel_id=1, source_target_pairs={{8,0},{16,8},{24,16},{32,24},{40,32},{48,40},{56,48},{64,56},{72,6... | collective-permute-start | bytes 786440 | tf_op jit(solution)/shard_map/ppermute | solution.py:887
  13.7 11.3 %collective-permute-start.2 = (f32[20,16,256]{2,1,0:T(8,128)S(1)}, f32[20,16,256]{2,1,0:T(8,128)S(1)}, u32[]{:S(2)}, u32[]{:S(2)}) collective-permute-start(f32[20,16,256]{2,1,0:T(8,128)S(1)} %get-tuple-element.28), channel_id=1, source_target_pairs={{1,2},{3,4},{5,6},{2,1},{4,3},{6,5},{9,10},{11,12},{13,14},{10,9},... | collective-permute-start | bytes 983048 | tf_op jit(solution)/shard_map/ppermute | solution.py:895
  20.3 4.7 %collective-permute-start.3 = (f32[20,16,256]{2,1,0:T(8,128)S(1)}, f32[20,16,256]{2,1,0:T(8,128)S(1)}, u32[]{:S(2)}, u32[]{:S(2)}) collective-permute-start(f32[20,16,256]{2,1,0:T(8,128)S(1)} %get-tuple-element.29), channel_id=1, source_target_pairs={{0,1},{2,3},{4,5},{6,7},{1,0},{3,2},{5,4},{7,6},{8,9},{10,11},{12,... | collective-permute-start | bytes 983048 | tf_op jit(solution)/shard_map/ppermute | solution.py:895
  32.3 8.0 %collective-permute-start.4 = (f32[14,16,256]{2,1,0:T(8,128)S(1)}, f32[14,16,256]{2,1,0:T(8,128)S(1)}, u32[]{:S(2)}, u32[]{:S(2)}) collective-permute-start(f32[14,16,256]{2,1,0:T(8,128)S(1)} %get-tuple-element.32), channel_id=1, source_target_pairs={{0,8},{8,16},{16,24},{24,32},{32,40},{40,48},{48,56},{56,64},{64,7... | collective-permute-start | bytes 688136 | tf_op jit(solution)/shard_map/ppermute | solution.py:887
  35.4 9.0 %collective-permute-start.5 = (f32[14,16,256]{2,1,0:T(8,128)S(1)}, f32[14,16,256]{2,1,0:T(8,128)S(1)}, u32[]{:S(2)}, u32[]{:S(2)}) collective-permute-start(f32[14,16,256]{2,1,0:T(8,128)S(1)} %get-tuple-element.33), channel_id=1, source_target_pairs={{8,0},{16,8},{24,16},{32,24},{40,32},{48,40},{56,48},{64,56},{72,6... | collective-permute-start | bytes 688136 | tf_op jit(solution)/shard_map/ppermute | solution.py:887
  45.1 10.8 %collective-permute-start.6 = (f32[62,8,256]{2,1,0:T(8,128)S(1)}, f32[62,8,256]{2,1,0:T(8,128)S(1)}, u32[]{:S(2)}, u32[]{:S(2)}) collective-permute-start(f32[62,8,256]{2,1,0:T(8,128)S(1)} %get-tuple-element.34), channel_id=1, source_target_pairs={{1,2},{3,4},{5,6},{2,1},{4,3},{6,5},{9,10},{11,12},{13,14},{10,9},... | collective-permute-start | bytes 1523720 | tf_op jit(solution)/shard_map/ppermute | solution.py:895
  49.2 6.7 %collective-permute-start.7 = (f32[62,8,256]{2,1,0:T(8,128)S(1)}, f32[62,8,256]{2,1,0:T(8,128)S(1)}, u32[]{:S(2)}, u32[]{:S(2)}) collective-permute-start(f32[62,8,256]{2,1,0:T(8,128)S(1)} %get-tuple-element.35), channel_id=1, source_target_pairs={{0,1},{2,3},{4,5},{6,7},{1,0},{3,2},{5,4},{7,6},{8,9},{10,11},{12,... | collective-permute-start | bytes 1523720 | tf_op jit(solution)/shard_map/ppermute | solution.py:895
  59.8 3.1 %collective-permute-start.8 = (f32[8,128]{1,0:T(8,128)S(1)}, f32[8,128]{1,0:T(8,128)S(1)}, u32[]{:S(2)}, u32[]{:S(2)}) collective-permute-start(f32[8,128]{1,0:T(8,128)S(1)} %get-tuple-element.36), channel_id=1, source_target_pairs={{0,1},{2,3},{4,5},{6,7},{1,0},{3,2},{5,4},{7,6},{8,9},{10,11},{12,... | collective-permute-start | bytes 12296 | tf_op jit(solution)/shard_map/ppermute | solution.py:895
  84.7 3.4 %collective-permute-start.9 = (f32[32,16,128]{2,1,0:T(8,128)S(1)}, f32[32,16,128]{2,1,0:T(8,128)S(1)}, u32[]{:S(2)}, u32[]{:S(2)}) collective-permute-start(f32[32,16,128]{2,1,0:T(8,128)S(1)} %all_to_all.10.fetched), channel_id=1, source_target_pairs={{0,1},{2,3},{4,5},{6,7},{1,0},{3,2},{5,4},{7,6},{8,9},{10,11},{12,... | collective-permute-start | bytes 786440 | tf_op jit(solution)/shard_map/ppermute | solution.py:895
  93.2 3.5 %collective-permute-start.10 = (f32[4,8,128]{2,1,0:T(8,128)S(1)}, f32[4,8,128]{2,1,0:T(8,128)S(1)}, u32[]{:S(2)}, u32[]{:S(2)}) collective-permute-start(f32[4,8,128]{2,1,0:T(8,128)S(1)} %get-tuple-element.42), channel_id=1, source_target_pairs={{0,8},{8,16},{16,24},{24,32},{32,40},{40,48},{48,56},{56,64},{64,7... | collective-permute-start | bytes 49160 | tf_op jit(solution)/shard_map/ppermute | solution.py:887
  95.4 4.5 %collective-permute-start.11 = (f32[4,8,128]{2,1,0:T(8,128)S(1)}, f32[4,8,128]{2,1,0:T(8,128)S(1)}, u32[]{:S(2)}, u32[]{:S(2)}) collective-permute-start(f32[4,8,128]{2,1,0:T(8,128)S(1)} %get-tuple-element.43), channel_id=1, source_target_pairs={{8,0},{16,8},{24,16},{32,24},{40,32},{48,40},{56,48},{64,56},{72,6... | collective-permute-start | bytes 49160 | tf_op jit(solution)/shard_map/ppermute | solution.py:887
  99.9 5.6 %collective-permute-start.13 = (f32[16,8,128]{2,1,0:T(8,128)S(1)}, f32[16,8,128]{2,1,0:T(8,128)S(1)}, u32[]{:S(2)}, u32[]{:S(2)}) collective-permute-start(f32[16,8,128]{2,1,0:T(8,128)S(1)} %constant_dynamic-update-slice_fusion.mid), channel_id=1, source_target_pairs={{1,2},{3,4},{5,6},{2,1},{4,3},{6,5},{9,10},{11,12},{13,14},{10,9},... | collective-permute-start | bytes 196616 | tf_op jit(solution)/shard_map/ppermute | solution.py:895
  103.2 3.1 %collective-permute-start.12 = (f32[16,8,128]{2,1,0:T(8,128)S(1)}, f32[16,8,128]{2,1,0:T(8,128)S(1)}, u32[]{:S(2)}, u32[]{:S(2)}) collective-permute-start(f32[16,8,128]{2,1,0:T(8,128)S(1)} %constant_dynamic-update-slice_fusion.mid), channel_id=1, source_target_pairs={{0,1},{2,3},{4,5},{6,7},{1,0},{3,2},{5,4},{7,6},{8,9},{10,11},{12,... | collective-permute-start | bytes 196616 | tf_op jit(solution)/shard_map/ppermute | solution.py:895
  107.3 3.1 %collective-permute-start.14 = (f32[8,128]{1,0:T(8,128)S(1)}, f32[8,128]{1,0:T(8,128)S(1)}, u32[]{:S(2)}, u32[]{:S(2)}) collective-permute-start(f32[8,128]{1,0:T(8,128)S(1)} %get-tuple-element.44), channel_id=1, source_target_pairs={{0,1},{2,3},{4,5},{6,7},{1,0},{3,2},{5,4},{7,6},{8,9},{10,11},{12,... | collective-permute-start | bytes 12296 | tf_op jit(solution)/shard_map/ppermute | solution.py:895
  128.5 7.9 %collective-permute-start.15 = (f32[32,16,128]{2,1,0:T(8,128)S(1)}, f32[32,16,128]{2,1,0:T(8,128)S(1)}, u32[]{:S(2)}, u32[]{:S(2)}) collective-permute-start(f32[32,16,128]{2,1,0:T(8,128)S(1)} %all_to_all.11.fetched), channel_id=1, source_target_pairs={{0,1},{2,3},{4,5},{6,7},{1,0},{3,2},{5,4},{7,6},{8,9},{10,11},{12,... | collective-permute-start | bytes 786440 | tf_op jit(solution)/shard_map/ppermute | solution.py:895

commit v12 on v11

--- a/solution.py
+++ b/solution.py
@@ -518,7 +518,7 @@
         total = residual(2 * p) + residual(2 * p + 1)
         for half in range(2):
             lanes = slice(128 * half, 128 * half + 128)
-            pair[p - first, half] = total[:, lanes]
+            pair[p - first, half, 0 : 2 * rows, :] = total[:, lanes]
             even = pair[p - first, half, pl.ds(0, rows, stride=2), :]
             odd = pair[p - first, half, pl.ds(1, rows, stride=2), :]
             t[p - first, :, lanes] = even + odd
@@ -664,7 +664,7 @@
     scratch = [
         around_block(16, HALO, 48, 256),
         around_block(16, HALO - 1, 48, 256),
-        (level1[0], 2, 48, 128),
+        (level1[0], 2, 56, 128),
         (level1[0], 24, 256),
         (4, 24, 128),
         (4, 8, 128),
@@ -743,7 +743,7 @@
 
     planes3 = range(-r3 - 3, 2 + r3 + 3)
     for i, p in enumerate(planes3):
-        row2[i] = residual2(2 * p) + residual2(2 * p + 1)
+        row2[i, 0:rows2, :] = residual2(2 * p) + residual2(2 * p + 1)
         t3[i] = row2[i, pl.ds(0, rows3, stride=2), :] + row2[i, pl.ds(1, rows3, stride=2), :]
     total3 = len(planes3)
     full = dot(t3[...].reshape(total3 * rows3, 128), pair_matrix(128, 128, 0.125))
@@ -789,7 +789,7 @@
         around_block(4, e2, rows2, 128),
         small, small, small, small,
         (8, 48, 128),
-        around_block(2, r3 + 3, rows2, 128),
+        around_block(2, r3 + 3, rows2 + 8, 128),
     ]
 
 
@@ -820,7 +820,7 @@
             value = spread[i, :, 128 * half : 128 * half + 128]
             dup[i, half, pl.ds(0, 16, stride=2), :] = value
             dup[i, half, pl.ds(1, 16, stride=2), :] = value
-        value = jnp.concatenate([dup[i, 0], dup[i, 1]], axis=1) * mask0
+        value = jnp.concatenate([dup[i, 0, 0:32, :], dup[i, 1, 0:32, :]], axis=1) * mask0
         for q in (2 * p, 2 * p + 1):
             if -e0 <= q < 16 + e0:
                 m0[q] = v_down[q] + wall(at, nx, 0, q, value)
@@ -835,7 +835,7 @@
     e0, r1, e1, r2, _, _ = reach(extra)
     level1 = around_block(8, e1, 24, 128)
     level0 = around_block(16, e0, 32, 256)
-    return [level1, level1, level0, level0, (max(8 + 2 * r1, 4 + 2 * r2), 2, 32, 128)]
+    return [level1, level1, level0, level0, (max(8 + 2 * r1, 4 + 2 * r2), 2, 40, 128)]
 
 
 def turn_body(nx, ny, at, fetched, other, b1, u, b, v_down, v_out, wider, low, high, own, pair, t, *scratch):
@@ -861,7 +861,7 @@
         (NEAR, 8, 128),
         (NEAR, 8, 128),
     ]
-    scratch = [(8, 16, 128), (8, 2, 32, 128), (8, 16, 256)]
+    scratch = [(8, 16, 128), (8, 2, 40, 128), (8, 16, 256)]
     scratch += coarse_scratch(ny, KEEP) + climb_scratch(KEEP)
     args = [at, *coarse, b1, u, b, v_down]
     return call(functools.partial(turn_body, nx, ny), outs, scratch, args, 30000000)

time: 141 us -> 141 us (level)
  no operation moved by 1% of the time
where the time goes in v12:
time: 141 us; the launch traced here: 140 us
  starting transfers between devices  45.8 us (32%)
  blocking collectives  39.9 us (28%)
  waiting for transfers between devices  26.8 us (19%)
  Pallas kernels  26.7 us (19%)
    all_to_all x2, blocking collectives, spread_coarse(): lax.all_to_all(pieces, ('wide', 'narrow'), 0, 0, axis_index_groups=groups)  39.9 us
    ppermute x10, starting transfers between devices, swapped(): return lax.ppermute(array, 'narrow', pairs + [(j, i) for i, j in pairs])  32.6 us
    pallas_call x9, Pallas kernels, call(): pl.pallas_call(body, out_shape=[jax.ShapeDtypeStruct(s, F32) for s in out...  25.3 us
    ppermute x6, waiting for transfers between devices, shifted(): lax.ppermute(array, axis, [(i, i + step) for i in range(count) if 0 <= i...  14.7 us
    ppermute x6, starting transfers between devices, shifted(): lax.ppermute(array, axis, [(i, i + step) for i in range(count) if 0 <= i...  13.2 us
    ppermute x10, waiting for transfers between devices, swapped(): return lax.ppermute(array, 'narrow', pairs + [(j, i) for i, j in pairs])  12 us
  transfers between devices with their start and end apart: 16, of which 12 were waited for; matrix products, arithmetic and copies ran while one was open for 0% of the time, Pallas kernels for 2%

profile of v12, /device:TPU:1, one launch (start us, length us, event | category | flops | bytes accessed | tf_op | source)
XLA Modules:
  0.0 140.1 jit_solution(4562946380766797248)
XLA Ops:
  0.6 0.0 copy-start
  0.6 1.3 shard_map.50
  2.0 4.0 %collective-permute-start = (f32[16,16,256]{2,1,0:T(8,128)S(1)}, f32[16,16,256]{2,1,0:T(8,128)S(1)}, u32[]{:S(2)}, u32[]{:S(2)}) collective-permute-start(f32[16,16,256]{2,1,0:T(8,128)S(1)} %get-tuple-element.26), channel_id=1, source_target_pairs={{0,8},{8,16},{16,24},{24,32},{32,40},{40,48},{48,56},{56,64},{64,7... | collective-permute-start | bytes 786440 | tf_op jit(solution)/shard_map/ppermute | solution.py:887
  5.9 1.3 collective-permute-start.1
  7.2 0.0 copy-done
  7.3 1.9 %shard_map.51.known = f32[16,16,256]{2,1,0:T(8,128)S(1)} custom-call(f32[16,16,256]{2,1,0:T(8,128)S(1)} %get-tuple-element.25.psi, f32[3,16,16,256]{3,2,1,0:T(8,128)S(1)} %copy-done), custom_call_target="tpu_custom_call" | custom-call | flops 8000000 | bytes 4000000 | tf_op jit(solution)/shard_map/pallas_call | solution.py:91
  9.2 0.1 pad_add_fusion.at
  9.2 0.0 collective-permute-done.low
  9.2 3.8 %collective-permute-done.1.high = f32[16,16,256]{2,1,0:T(8,128)S(1)} collective-permute-done((f32[16,16,256]{2,1,0:T(8,128)S(1)}, f32[16,16,256]{2,1,0:T(8,128)S(1)}, u32[]{:S(2)}, u32[]{:S(2)}) %collective-permute-start.1) | collective-permute-done | bytes 262176 | tf_op jit(solution)/shard_map/ppermute | solution.py:887
  13.1 0.6 shard_map.52
  13.7 6.6 %collective-permute-start.2 = (f32[20,16,256]{2,1,0:T(8,128)S(1)}, f32[20,16,256]{2,1,0:T(8,128)S(1)}, u32[]{:S(2)}, u32[]{:S(2)}) collective-permute-start(f32[20,16,256]{2,1,0:T(8,128)S(1)} %get-tuple-element.28), channel_id=1, source_target_pairs={{1,2},{3,4},{5,6},{2,1},{4,3},{6,5},{9,10},{11,12},{13,14},{10,9},... | collective-permute-start | bytes 983048 | tf_op jit(solution)/shard_map/ppermute | solution.py:895
  20.3 1.9 %collective-permute-start.3 = (f32[20,16,256]{2,1,0:T(8,128)S(1)}, f32[20,16,256]{2,1,0:T(8,128)S(1)}, u32[]{:S(2)}, u32[]{:S(2)}) collective-permute-start(f32[20,16,256]{2,1,0:T(8,128)S(1)} %get-tuple-element.29), channel_id=1, source_target_pairs={{0,1},{2,3},{4,5},{6,7},{1,0},{3,2},{5,4},{7,6},{8,9},{10,11},{12,... | collective-permute-start | bytes 983048 | tf_op jit(solution)/shard_map/ppermute | solution.py:895
  22.2 1.3 shard_map.53.change_in
  23.5 1.5 %collective-permute-done.2.link = f32[20,16,256]{2,1,0:T(8,128)S(1)} collective-permute-done((f32[20,16,256]{2,1,0:T(8,128)S(1)}, f32[20,16,256]{2,1,0:T(8,128)S(1)}, u32[]{:S(2)}, u32[]{:S(2)}) %collective-permute-start.2) | collective-permute-done | bytes 327712 | tf_op jit(solution)/shard_map/ppermute | solution.py:895
  25.0 0.0 collective-permute-done.3.chip
  25.0 7.3 %shard_map.54 = (f32[16,16,256]{2,1,0:T(8,128)}, f32[16,16,256]{2,1,0:T(8,128)S(1)}, f32[14,16,256]{2,1,0:T(8,128)S(1)}, f32[14,16,256]{2,1,0:T(8,128)S(1)}) custom-call(s32[2]{0:T(128)S(1)} %pad_add_fusion.at, f32[16,16,256]{2,1,0:T(8,128)S(1)} %get-tuple-element.25.psi, f32[3,16,16,256]{3,2,1,0:T(8,128)S(1)} %copy-done, ...), custom_call_target="tpu_custom_call" | custom-call | flops 30000000 | bytes 4000000 | tf_op jit(solution)/shard_map/pallas_call | solution.py:91
  32.3 3.1 %collective-permute-start.4 = (f32[14,16,256]{2,1,0:T(8,128)S(1)}, f32[14,16,256]{2,1,0:T(8,128)S(1)}, u32[]{:S(2)}, u32[]{:S(2)}) collective-permute-start(f32[14,16,256]{2,1,0:T(8,128)S(1)} %get-tuple-element.32), channel_id=1, source_target_pairs={{0,8},{8,16},{16,24},{24,32},{32,40},{40,48},{48,56},{56,64},{64,7... | collective-permute-start | bytes 688136 | tf_op jit(solution)/shard_map/ppermute | solution.py:887
  35.4 1.3 collective-permute-start.5
  36.7 3.6 %collective-permute-done.4.low = f32[14,16,256]{2,1,0:T(8,128)S(1)} collective-permute-done((f32[14,16,256]{2,1,0:T(8,128)S(1)}, f32[14,16,256]{2,1,0:T(8,128)S(1)}, u32[]{:S(2)}, u32[]{:S(2)}) %collective-permute-start.4) | collective-permute-done | bytes 229408 | tf_op jit(solution)/shard_map/ppermute | solution.py:887
  40.3 4.2 %collective-permute-done.5.high = f32[14,16,256]{2,1,0:T(8,128)S(1)} collective-permute-done((f32[14,16,256]{2,1,0:T(8,128)S(1)}, f32[14,16,256]{2,1,0:T(8,128)S(1)}, u32[]{:S(2)}, u32[]{:S(2)}) %collective-permute-start.5) | collective-permute-done | bytes 229408 | tf_op jit(solution)/shard_map/ppermute | solution.py:887
  44.4 0.6 shard_map.55
  45.1 4.1 %collective-permute-start.6 = (f32[62,8,256]{2,1,0:T(8,128)S(1)}, f32[62,8,256]{2,1,0:T(8,128)S(1)}, u32[]{:S(2)}, u32[]{:S(2)}) collective-permute-start(f32[62,8,256]{2,1,0:T(8,128)S(1)} %get-tuple-element.34), channel_id=1, source_target_pairs={{1,2},{3,4},{5,6},{2,1},{4,3},{6,5},{9,10},{11,12},{13,14},{10,9},... | collective-permute-start | bytes 1523720 | tf_op jit(solution)/shard_map/ppermute | solution.py:895
  49.2 2.1 %collective-permute-start.7 = (f32[62,8,256]{2,1,0:T(8,128)S(1)}, f32[62,8,256]{2,1,0:T(8,128)S(1)}, u32[]{:S(2)}, u32[]{:S(2)}) collective-permute-start(f32[62,8,256]{2,1,0:T(8,128)S(1)} %get-tuple-element.35), channel_id=1, source_target_pairs={{0,1},{2,3},{4,5},{6,7},{1,0},{3,2},{5,4},{7,6},{8,9},{10,11},{12,... | collective-permute-start | bytes 1523720 | tf_op jit(solution)/shard_map/ppermute | solution.py:895
  51.3 4.6 %collective-permute-done.6.link = f32[62,8,256]{2,1,0:T(8,128)S(1)} collective-permute-done((f32[62,8,256]{2,1,0:T(8,128)S(1)}, f32[62,8,256]{2,1,0:T(8,128)S(1)}, u32[]{:S(2)}, u32[]{:S(2)}) %collective-permute-start.6) | collective-permute-done | bytes 507936 | tf_op jit(solution)/shard_map/ppermute | solution.py:895
  55.9 0.0 collective-permute-done.7.chip
  55.9 3.8 %shard_map.56 = (f32[26,32,256]{2,1,0:T(8,128)S(1)}, f32[28,32,256]{2,1,0:T(8,128)S(1)}, f32[20,24,128]{2,1,0:T(8,128)S(1)}, f32[18,24,128]{2,1,0:T(8,128)S(1)}, f32[8,128]{1,0:T(8,128)S(1)}) custom-call(s32[2]{0:T(128)S(1)} %pad_add_fusion.at, f32[16,16,256]{2,1,0:T(8,128)S(1)} %get-tuple-element.31.own, f32[14,16,256]{2,1,0:T(8,128)S(1)} %collective-permute-done.4.low, ...), custom_call_target="tpu_custom_call" | custom-call | flops 20000000 | bytes 4000000 | tf_op jit(solution)/shard_map/pallas_call | solution.py:91
  59.7 1.9 %collective-permute-start.8 = (f32[8,128]{1,0:T(8,128)S(1)}, f32[8,128]{1,0:T(8,128)S(1)}, u32[]{:S(2)}, u32[]{:S(2)}) collective-permute-start(f32[8,128]{1,0:T(8,128)S(1)} %get-tuple-element.36), channel_id=1, source_target_pairs={{0,1},{2,3},{4,5},{6,7},{1,0},{3,2},{5,4},{7,6},{8,9},{10,11},{12,... | collective-permute-start | bytes 12296 | tf_op jit(solution)/shard_map/ppermute | solution.py:895
  61.7 1.1 collective-permute-done.8
  62.8 21.8 %all_to_all.10.fetched = f32[32,16,128]{2,1,0:T(8,128)S(1)} all-to-all(f32[32,16,128]{2,1,0:T(8,128)S(1)} %broadcast_in_dim.4), channel_id=1, replica_groups={{0,2,4,6,8,10,12,14,16,18,20,22,24,26,28,30,32,34,36,38,40,42,44,46,48,..., dimensions={0} | all-to-all | bytes 524288 | tf_op jit(solution)/shard_map/all_to_all | solution.py:928
  84.6 1.9 %collective-permute-start.9 = (f32[32,16,128]{2,1,0:T(8,128)S(1)}, f32[32,16,128]{2,1,0:T(8,128)S(1)}, u32[]{:S(2)}, u32[]{:S(2)}) collective-permute-start(f32[32,16,128]{2,1,0:T(8,128)S(1)} %all_to_all.10.fetched), channel_id=1, source_target_pairs={{0,1},{2,3},{4,5},{6,7},{1,0},{3,2},{5,4},{7,6},{8,9},{10,11},{12,... | collective-permute-start | bytes 786440 | tf_op jit(solution)/shard_map/ppermute | solution.py:895
  86.6 1.5 %collective-permute-done.9.other = f32[32,16,128]{2,1,0:T(8,128)S(1)} collective-permute-done((f32[32,16,128]{2,1,0:T(8,128)S(1)}, f32[32,16,128]{2,1,0:T(8,128)S(1)}, u32[]{:S(2)}, u32[]{:S(2)}) %collective-permute-start.9) | collective-permute-done | bytes 262176 | tf_op jit(solution)/shard_map/ppermute | solution.py:895
  88.1 5.1 %shard_map.57 = (f32[20,32,256]{2,1,0:T(8,128)S(1)}, f32[16,8,128]{2,1,0:T(8,128)S(1)}, f32[4,8,128]{2,1,0:T(8,128)S(1)}, f32[4,8,128]{2,1,0:T(8,128)S(1)}) custom-call(s32[2]{0:T(128)S(1)} %pad_add_fusion.at, f32[32,16,128]{2,1,0:T(8,128)S(1)} %all_to_all.10.fetched, f32[32,16,128]{2,1,0:T(8,128)S(1)} %collective-permute-done.9.other, ...), custom_call_target="tpu_custom_call" | custom-call | flops 30000000 | bytes 4000000 | tf_op jit(solution)/shard_map/pallas_call | solution.py:91
  93.2 2.2 %collective-permute-start.10 = (f32[4,8,128]{2,1,0:T(8,128)S(1)}, f32[4,8,128]{2,1,0:T(8,128)S(1)}, u32[]{:S(2)}, u32[]{:S(2)}) collective-permute-start(f32[4,8,128]{2,1,0:T(8,128)S(1)} %get-tuple-element.42), channel_id=1, source_target_pairs={{0,8},{8,16},{16,24},{24,32},{32,40},{40,48},{48,56},{56,64},{64,7... | collective-permute-start | bytes 49160 | tf_op jit(solution)/shard_map/ppermute | solution.py:887
  95.4 1.3 collective-permute-start.11
  96.7 0.0 collective-permute-done.10
  96.7 3.2 %collective-permute-done.11 = f32[4,8,128]{2,1,0:T(8,128)S(1)} collective-permute-done((f32[4,8,128]{2,1,0:T(8,128)S(1)}, f32[4,8,128]{2,1,0:T(8,128)S(1)}, u32[]{:S(2)}, u32[]{:S(2)}) %collective-permute-start.11) | collective-permute-done | bytes 16416 | tf_op jit(solution)/shard_map/ppermute | solution.py:887
  99.9 3.3 %collective-permute-start.13 = (f32[16,8,128]{2,1,0:T(8,128)S(1)}, f32[16,8,128]{2,1,0:T(8,128)S(1)}, u32[]{:S(2)}, u32[]{:S(2)}) collective-permute-start(f32[16,8,128]{2,1,0:T(8,128)S(1)} %constant_dynamic-update-slice_fusion.mid), channel_id=1, source_target_pairs={{1,2},{3,4},{5,6},{2,1},{4,3},{6,5},{9,10},{11,12},{13,14},{10,9},... | collective-permute-start | bytes 196616 | tf_op jit(solution)/shard_map/ppermute | solution.py:895
  103.2 1.9 %collective-permute-start.12 = (f32[16,8,128]{2,1,0:T(8,128)S(1)}, f32[16,8,128]{2,1,0:T(8,128)S(1)}, u32[]{:S(2)}, u32[]{:S(2)}) collective-permute-start(f32[16,8,128]{2,1,0:T(8,128)S(1)} %constant_dynamic-update-slice_fusion.mid), channel_id=1, source_target_pairs={{0,1},{2,3},{4,5},{6,7},{1,0},{3,2},{5,4},{7,6},{8,9},{10,11},{12,... | collective-permute-start | bytes 196616 | tf_op jit(solution)/shard_map/ppermute | solution.py:895
  105.2 0.3 collective-permute-done.13.link
  105.5 0.9 collective-permute-done.12.chip
  106.4 0.9 shard_map.58
  107.3 2.1 %collective-permute-start.14 = (f32[8,128]{1,0:T(8,128)S(1)}, f32[8,128]{1,0:T(8,128)S(1)}, u32[]{:S(2)}, u32[]{:S(2)}) collective-permute-start(f32[8,128]{1,0:T(8,128)S(1)} %get-tuple-element.44), channel_id=1, source_target_pairs={{0,1},{2,3},{4,5},{6,7},{1,0},{3,2},{5,4},{7,6},{8,9},{10,11},{12,... | collective-permute-start | bytes 12296 | tf_op jit(solution)/shard_map/ppermute | solution.py:895
  109.4 1.0 collective-permute-done.14
  110.4 18.1 %all_to_all.11.fetched = f32[32,16,128]{2,1,0:T(8,128)S(1)} all-to-all(f32[32,16,128]{2,1,0:T(8,128)S(1)} %broadcast_in_dim.5), channel_id=1, replica_groups={{0,2,4,6,8,10,12,14,16,18,20,22,24,26,28,30,32,34,36,38,40,42,44,46,48,..., dimensions={0} | all-to-all | bytes 524288 | tf_op jit(solution)/shard_map/all_to_all | solution.py:928
  128.5 6.7 %collective-permute-start.15 = (f32[32,16,128]{2,1,0:T(8,128)S(1)}, f32[32,16,128]{2,1,0:T(8,128)S(1)}, u32[]{:S(2)}, u32[]{:S(2)}) collective-permute-start(f32[32,16,128]{2,1,0:T(8,128)S(1)} %all_to_all.11.fetched), channel_id=1, source_target_pairs={{0,1},{2,3},{4,5},{6,7},{1,0},{3,2},{5,4},{7,6},{8,9},{10,11},{12,... | collective-permute-start | bytes 786440 | tf_op jit(solution)/shard_map/ppermute | solution.py:895
  135.2 1.1 collective-permute-done.15.other
  136.4 3.8 %shard_map.59 = f32[16,16,256]{2,1,0:T(8,128)} custom-call(s32[2]{0:T(128)S(1)} %pad_add_fusion.at, f32[32,16,128]{2,1,0:T(8,128)S(1)} %all_to_all.11.fetched, f32[32,16,128]{2,1,0:T(8,128)S(1)} %collective-permute-done.15.other, f32[16,24,128]{2,1,0:T(8,128)S(1)} %get-tuple-element.45.b1, f32[14,24,128]{2,1,0:T(8,128)S(1)} %get-tuple-element.46.u, ...), custom_call_target="tpu_custom_call" | custom-call | flops 20000000 | bytes 4000000 | tf_op jit(solution)/shard_map/pallas_call | solution.py:91
  (8 shorter events, 0.1 us)
Async XLA Ops:
  0.6 6.6 %copy-start = (f32[3,16,16,256]{3,2,1,0:T(8,128)S(1)}, f32[3,16,16,256]{3,2,1,0:T(8,128)}, u32[]{:S(2)}) copy-start(f32[3,16,16,256]{3,2,1,0:T(8,128)} %velocity.9) | copy-start | bytes 2359300
  2.0 7.3 %collective-permute-start = (f32[16,16,256]{2,1,0:T(8,128)S(1)}, f32[16,16,256]{2,1,0:T(8,128)S(1)}, u32[]{:S(2)}, u32[]{:S(2)}) collective-permute-start(f32[16,16,256]{2,1,0:T(8,128)S(1)} %get-tuple-element.26), channel_id=1, source_target_pairs={{0,8},{8,16},{16,24},{24,32},{32,40},{40,48},{48,56},{56,64},{64,7... | collective-permute-start | bytes 786440 | tf_op jit(solution)/shard_map/ppermute | solution.py:887
  5.9 7.1 %collective-permute-start.1 = (f32[16,16,256]{2,1,0:T(8,128)S(1)}, f32[16,16,256]{2,1,0:T(8,128)S(1)}, u32[]{:S(2)}, u32[]{:S(2)}) collective-permute-start(f32[16,16,256]{2,1,0:T(8,128)S(1)} %get-tuple-element.27), channel_id=1, source_target_pairs={{8,0},{16,8},{24,16},{32,24},{40,32},{48,40},{56,48},{64,56},{72,6... | collective-permute-start | bytes 786440 | tf_op jit(solution)/shard_map/ppermute | solution.py:887
  13.7 11.3 %collective-permute-start.2 = (f32[20,16,256]{2,1,0:T(8,128)S(1)}, f32[20,16,256]{2,1,0:T(8,128)S(1)}, u32[]{:S(2)}, u32[]{:S(2)}) collective-permute-start(f32[20,16,256]{2,1,0:T(8,128)S(1)} %get-tuple-element.28), channel_id=1, source_target_pairs={{1,2},{3,4},{5,6},{2,1},{4,3},{6,5},{9,10},{11,12},{13,14},{10,9},... | collective-permute-start | bytes 983048 | tf_op jit(solution)/shard_map/ppermute | solution.py:895
  20.3 4.7 %collective-permute-start.3 = (f32[20,16,256]{2,1,0:T(8,128)S(1)}, f32[20,16,256]{2,1,0:T(8,128)S(1)}, u32[]{:S(2)}, u32[]{:S(2)}) collective-permute-start(f32[20,16,256]{2,1,0:T(8,128)S(1)} %get-tuple-element.29), channel_id=1, source_target_pairs={{0,1},{2,3},{4,5},{6,7},{1,0},{3,2},{5,4},{7,6},{8,9},{10,11},{12,... | collective-permute-start | bytes 983048 | tf_op jit(solution)/shard_map/ppermute | solution.py:895
  32.3 8.0 %collective-permute-start.4 = (f32[14,16,256]{2,1,0:T(8,128)S(1)}, f32[14,16,256]{2,1,0:T(8,128)S(1)}, u32[]{:S(2)}, u32[]{:S(2)}) collective-permute-start(f32[14,16,256]{2,1,0:T(8,128)S(1)} %get-tuple-element.32), channel_id=1, source_target_pairs={{0,8},{8,16},{16,24},{24,32},{32,40},{40,48},{48,56},{56,64},{64,7... | collective-permute-start | bytes 688136 | tf_op jit(solution)/shard_map/ppermute | solution.py:887
  35.4 9.0 %collective-permute-start.5 = (f32[14,16,256]{2,1,0:T(8,128)S(1)}, f32[14,16,256]{2,1,0:T(8,128)S(1)}, u32[]{:S(2)}, u32[]{:S(2)}) collective-permute-start(f32[14,16,256]{2,1,0:T(8,128)S(1)} %get-tuple-element.33), channel_id=1, source_target_pairs={{8,0},{16,8},{24,16},{32,24},{40,32},{48,40},{56,48},{64,56},{72,6... | collective-permute-start | bytes 688136 | tf_op jit(solution)/shard_map/ppermute | solution.py:887
  45.1 10.8 %collective-permute-start.6 = (f32[62,8,256]{2,1,0:T(8,128)S(1)}, f32[62,8,256]{2,1,0:T(8,128)S(1)}, u32[]{:S(2)}, u32[]{:S(2)}) collective-permute-start(f32[62,8,256]{2,1,0:T(8,128)S(1)} %get-tuple-element.34), channel_id=1, source_target_pairs={{1,2},{3,4},{5,6},{2,1},{4,3},{6,5},{9,10},{11,12},{13,14},{10,9},... | collective-permute-start | bytes 1523720 | tf_op jit(solution)/shard_map/ppermute | solution.py:895
  49.2 6.7 %collective-permute-start.7 = (f32[62,8,256]{2,1,0:T(8,128)S(1)}, f32[62,8,256]{2,1,0:T(8,128)S(1)}, u32[]{:S(2)}, u32[]{:S(2)}) collective-permute-start(f32[62,8,256]{2,1,0:T(8,128)S(1)} %get-tuple-element.35), channel_id=1, source_target_pairs={{0,1},{2,3},{4,5},{6,7},{1,0},{3,2},{5,4},{7,6},{8,9},{10,11},{12,... | collective-permute-start | bytes 1523720 | tf_op jit(solution)/shard_map/ppermute | solution.py:895
  59.7 3.1 %collective-permute-start.8 = (f32[8,128]{1,0:T(8,128)S(1)}, f32[8,128]{1,0:T(8,128)S(1)}, u32[]{:S(2)}, u32[]{:S(2)}) collective-permute-start(f32[8,128]{1,0:T(8,128)S(1)} %get-tuple-element.36), channel_id=1, source_target_pairs={{0,1},{2,3},{4,5},{6,7},{1,0},{3,2},{5,4},{7,6},{8,9},{10,11},{12,... | collective-permute-start | bytes 12296 | tf_op jit(solution)/shard_map/ppermute | solution.py:895
  84.6 3.4 %collective-permute-start.9 = (f32[32,16,128]{2,1,0:T(8,128)S(1)}, f32[32,16,128]{2,1,0:T(8,128)S(1)}, u32[]{:S(2)}, u32[]{:S(2)}) collective-permute-start(f32[32,16,128]{2,1,0:T(8,128)S(1)} %all_to_all.10.fetched), channel_id=1, source_target_pairs={{0,1},{2,3},{4,5},{6,7},{1,0},{3,2},{5,4},{7,6},{8,9},{10,11},{12,... | collective-permute-start | bytes 786440 | tf_op jit(solution)/shard_map/ppermute | solution.py:895
  93.2 3.5 %collective-permute-start.10 = (f32[4,8,128]{2,1,0:T(8,128)S(1)}, f32[4,8,128]{2,1,0:T(8,128)S(1)}, u32[]{:S(2)}, u32[]{:S(2)}) collective-permute-start(f32[4,8,128]{2,1,0:T(8,128)S(1)} %get-tuple-element.42), channel_id=1, source_target_pairs={{0,8},{8,16},{16,24},{24,32},{32,40},{40,48},{48,56},{56,64},{64,7... | collective-permute-start | bytes 49160 | tf_op jit(solution)/shard_map/ppermute | solution.py:887
  95.4 4.5 %collective-permute-start.11 = (f32[4,8,128]{2,1,0:T(8,128)S(1)}, f32[4,8,128]{2,1,0:T(8,128)S(1)}, u32[]{:S(2)}, u32[]{:S(2)}) collective-permute-start(f32[4,8,128]{2,1,0:T(8,128)S(1)} %get-tuple-element.43), channel_id=1, source_target_pairs={{8,0},{16,8},{24,16},{32,24},{40,32},{48,40},{56,48},{64,56},{72,6... | collective-permute-start | bytes 49160 | tf_op jit(solution)/shard_map/ppermute | solution.py:887
  99.9 5.6 %collective-permute-start.13 = (f32[16,8,128]{2,1,0:T(8,128)S(1)}, f32[16,8,128]{2,1,0:T(8,128)S(1)}, u32[]{:S(2)}, u32[]{:S(2)}) collective-permute-start(f32[16,8,128]{2,1,0:T(8,128)S(1)} %constant_dynamic-update-slice_fusion.mid), channel_id=1, source_target_pairs={{1,2},{3,4},{5,6},{2,1},{4,3},{6,5},{9,10},{11,12},{13,14},{10,9},... | collective-permute-start | bytes 196616 | tf_op jit(solution)/shard_map/ppermute | solution.py:895
  103.2 3.1 %collective-permute-start.12 = (f32[16,8,128]{2,1,0:T(8,128)S(1)}, f32[16,8,128]{2,1,0:T(8,128)S(1)}, u32[]{:S(2)}, u32[]{:S(2)}) collective-permute-start(f32[16,8,128]{2,1,0:T(8,128)S(1)} %constant_dynamic-update-slice_fusion.mid), channel_id=1, source_target_pairs={{0,1},{2,3},{4,5},{6,7},{1,0},{3,2},{5,4},{7,6},{8,9},{10,11},{12,... | collective-permute-start | bytes 196616 | tf_op jit(solution)/shard_map/ppermute | solution.py:895
  107.3 3.1 %collective-permute-start.14 = (f32[8,128]{1,0:T(8,128)S(1)}, f32[8,128]{1,0:T(8,128)S(1)}, u32[]{:S(2)}, u32[]{:S(2)}) collective-permute-start(f32[8,128]{1,0:T(8,128)S(1)} %get-tuple-element.44), channel_id=1, source_target_pairs={{0,1},{2,3},{4,5},{6,7},{1,0},{3,2},{5,4},{7,6},{8,9},{10,11},{12,... | collective-permute-start | bytes 12296 | tf_op jit(solution)/shard_map/ppermute | solution.py:895
  128.5 7.9 %collective-permute-start.15 = (f32[32,16,128]{2,1,0:T(8,128)S(1)}, f32[32,16,128]{2,1,0:T(8,128)S(1)}, u32[]{:S(2)}, u32[]{:S(2)}) collective-permute-start(f32[32,16,128]{2,1,0:T(8,128)S(1)} %all_to_all.11.fetched), channel_id=1, source_target_pairs={{0,1},{2,3},{4,5},{6,7},{1,0},{3,2},{5,4},{7,6},{8,9},{10,11},{12,... | collective-permute-start | bytes 786440 | tf_op jit(solution)/shard_map/ppermute | solution.py:895
